TPU v7x, 128 devices: a whole 4x4x4 slice. The times are simulated.
128 devices in a mesh: gx: 4 (over y), gy: 4 (over z), gz: 8 (over x, core).
Axes of the slice: x: 4, y: 4, z: 4, core: 2. Of those that a mesh axis runs over, the one named last changes fastest.
Arguments:
- initial: float32 [128, 128, 1024], P('gx', 'gy', 'gz'), may hold values from -6 to 6
- rhs: float32 [128, 128, 1024], P('gx', 'gy', 'gz'), may hold values from -6 to 6
- kappa: float32 [128, 128, 1024], P('gx', 'gy', 'gz'), may hold values from 0.5 to 2
- sigma: float32 [128, 128, 1024], P('gx', 'gy', 'gz'), may hold values from 0.005 to 0.05
Outputs:
- updated: float32 [128, 128, 1024], P('gx', 'gy', 'gz')
All inputs are finite; a program needn't handle non-finite values.
Results may differ from a plain program's by a relative error of at most 0.00016.
Values sent between devices are 32-bit elements; how exact they have to be, the bound alone decides.
No kernel may reach another device: no remote copies, remote signals or barrier semaphores. Data moves between devices by JAX's collectives and lax.ppermute only.
A program may use at most 192 MiB of HBM per device.

v0:
```python
import jax
import jax.numpy as jnp
from jax import lax
from jax.sharding import PartitionSpec as P

COARSE_SWEEPS = 8


jacobi_weight = 0.8


def extended(block, sides, width):
    for axis, dim in sides:
        count = lax.axis_size(axis)
        forward = [(i, i + 1) for i in range(count - 1)]
        forward.append((count - 1, 0))
        backward = [(target, source) for source, target in forward]
        low = lax.ppermute(
            lax.slice_in_dim(block, block.shape[dim] - width, None, axis=dim), axis, forward
        )
        high = lax.ppermute(lax.slice_in_dim(block, 0, width, axis=dim), axis, backward)
        block = jnp.concatenate([low, block, high], axis=dim)
    return block


def neighbours(padded):
    return [
        padded[2:, 1:-1, 1:-1],
        padded[:-2, 1:-1, 1:-1],
        padded[1:-1, 2:, 1:-1],
        padded[1:-1, :-2, 1:-1],
        padded[1:-1, 1:-1, 2:],
        padded[1:-1, 1:-1, :-2],
    ]


def face_list(kappa_pad):
    center = kappa_pad[1:-1, 1:-1, 1:-1]
    return [0.5 * (center + other) for other in neighbours(kappa_pad)]


def operate(field_pad, faces, shift):
    center = field_pad[1:-1, 1:-1, 1:-1]
    total = shift * center
    for face, other in zip(faces, neighbours(field_pad)):
        total = total + face * (center - other)
    return total


def diagonal_of(faces, shift):
    total = shift
    for face in faces:
        total = total + face
    return total


def coarsen(field):
    sizes = field.shape
    blocks = field.reshape(sizes[0] // 2, 2, sizes[1] // 2, 2, sizes[2] // 2, 2)
    return blocks.mean(axis=(1, 3, 5))


def refine(field):
    return jnp.repeat(jnp.repeat(jnp.repeat(field, 2, 0), 2, 1), 2, 2)


def smooth(source, faces, shift, sweeps, padder):
    diagonal = diagonal_of(faces, shift)
    result = jacobi_weight * source / diagonal
    for sweep in range(sweeps - 1):
        result = (
            result + jacobi_weight * (source - operate(padder(result), faces, shift)) / diagonal
        )
    return result


def fine_rims(stacked):
    return extended(stacked, (("gx", 1), ("gy", 2), ("gz", 3)), 1)


def middle_rims(field):
    return extended(field, (("gx", 0), ("gy", 1), ("gz", 2)), 1)


def group_rims(field):
    padded = extended(field, (("gx", 0), ("gy", 1)), 1)
    return jnp.concatenate([padded[:, :, -1:], padded, padded[:, :, :1]], axis=2)


def line_local(rest, kappa, shift):
    return (
        jnp.mean(rest, axis=2, keepdims=True),
        jnp.mean(kappa, axis=2, keepdims=True),
        jnp.mean(shift, axis=2, keepdims=True),
    )


def coarse_cycle(residual, kappa, shift, padder, depth_levels, liner, line_padder):
    rests = [residual]
    kappas = [kappa]
    shifts = [shift]
    for level in range(depth_levels - 1):
        rests.append(4.0 * coarsen(rests[-1]))
        kappas.append(coarsen(kappas[-1]))
        shifts.append(4.0 * coarsen(shifts[-1]))
    line_rest, line_kappa, line_shift = liner(rests[-1], kappas[-1], shifts[-1])
    total = smooth(
        line_rest, face_list(line_padder(line_kappa)), line_shift, COARSE_SWEEPS, line_padder
    )
    for level in reversed(range(depth_levels)):
        faces = face_list(padder(kappas[level]))
        correction = smooth(rests[level], faces, shifts[level], COARSE_SWEEPS, padder)
        if level == depth_levels - 1:
            total = correction + jnp.broadcast_to(total, correction.shape)
        else:
            total = correction + refine(total)
    return total


def on_device(initial, rhs, kappa, sigma):
    padded = fine_rims(jnp.stack((kappa, initial)))
    faces = face_list(padded[0])
    residual = rhs - operate(padded[1], faces, sigma)
    diagonal = diagonal_of(faces, sigma)
    first = jacobi_weight * residual / diagonal
    first_pad = fine_rims(first[None])[0]
    fine = first + jacobi_weight * (residual - operate(first_pad, faces, sigma)) / diagonal
    rest_two = 4.0 * coarsen(residual)
    kappa_two = coarsen(kappa)
    shift_two = 4.0 * coarsen(sigma)
    rest_three = 4.0 * coarsen(rest_two)
    kappa_three = coarsen(kappa_two)
    shift_three = 4.0 * coarsen(shift_two)
    gathered = (
        lax.all_gather(rest_three, "gz", axis=2, tiled=True),
        lax.all_gather(kappa_three, "gz", axis=2, tiled=True),
        lax.all_gather(shift_three, "gz", axis=2, tiled=True),
    )
    column = coarse_cycle(
        gathered[0], gathered[1], gathered[2], group_rims, 4, line_local, group_rims
    )
    depth = rest_three.shape[2]
    lower = lax.dynamic_slice_in_dim(column, lax.axis_index("gz") * depth, depth, 2)
    middle_faces = face_list(middle_rims(kappa_two))
    middle = smooth(rest_two, middle_faces, shift_two, 2, middle_rims) + refine(lower)
    return initial + (fine + refine(middle))


def solution(mesh):
    in_specs = (P("gx", "gy", "gz"), P("gx", "gy", "gz"), P("gx", "gy", "gz"), P("gx", "gy", "gz"))
    out_specs = P("gx", "gy", "gz")
    return jax.shard_map(
        on_device, mesh=mesh, in_specs=in_specs, out_specs=out_specs, check_vma=False
    )
```

profile of v0, /device:TPU:1, one launch (start us, length us, event | category | flops | bytes accessed | tf_op | source)
XLA Modules:
  0.0 793.5 jit_solution(1181463102496103079)
XLA Ops:
  0.0 35.6 %reshape.152 = f32[16,2,16,2,64,2]{5,4,3,2,1,0:T(8,128)} reshape(f32[32,32,128]{2,1,0:T(8,128)} %param.6) | data formatting | bytes 1048576 | tf_op jit(solution)/shard_map/reshape | solution.py:59
  35.6 12.2 %reduce_sum.185 = f32[16,16,64]{2,1,0:T(8,128)S(1)} reduce(f32[16,2,16,2,64,2]{5,4,3,2,1,0:T(8,128)} %reshape.152, f32[]{:T(128)} %constant.71.clone.1), dimensions={1,3,5}, to_apply=%region_2.0 | reduce | flops 114688 | bytes 589828 | tf_op jit(solution)/shard_map/reduce_sum | solution.py:60
  47.9 5.7 div.183
  56.3 15.4 %all_gather.11 = f32[8,8,256]{1,0,2:T(8,128)S(1)} all-gather(f32[8,8,32]{1,0,2:T(8,128)S(1)} %copy.813), channel_id=1, replica_groups=mesh['gx'=4,'gy'=4,'gz'=8] {'gz'}, dimensions={2}, use_global_device_ids=true | all-gather | bytes 73728 | tf_op jit(solution)/shard_map/all_gather | solution.py:136
  72.0 5.6 reshape.155
  92.0 34.9 %reshape.151 = f32[16,2,16,2,64,2]{5,4,3,2,1,0:T(8,128)} reshape(f32[32,32,128]{2,1,0:T(8,128)S(1)} %copy-done.18) | data formatting | bytes 1048576 | tf_op jit(solution)/shard_map/reshape | solution.py:59
  126.9 12.2 %reduce_sum.184 = f32[16,16,64]{2,1,0:T(8,128)S(1)} reduce(f32[16,2,16,2,64,2]{5,4,3,2,1,0:T(8,128)} %reshape.151, f32[]{:T(128)} %constant.71.clone.1), dimensions={1,3,5}, to_apply=%region_1.0 | reduce | flops 114688 | bytes 589828 | tf_op jit(solution)/shard_map/reduce_sum | solution.py:60
  139.2 5.7 mul.1197
  147.6 16.6 %all_gather.10 = f32[8,8,256]{1,0,2:T(8,128)S(1)} all-gather(f32[8,8,32]{1,0,2:T(8,128)S(1)} %copy.812), channel_id=1, replica_groups=mesh['gx'=4,'gy'=4,'gz'=8] {'gz'}, dimensions={2}, use_global_device_ids=true | all-gather | bytes 73728 | tf_op jit(solution)/shard_map/all_gather | solution.py:137
  164.6 5.6 reshape.154
  177.7 3.8 collective-permute-start.154
  217.0 10.5 %collective-permute-start.16 = (f32[18,18,1]{2,1,0:T(8,128)}, f32[18,18,1]{2,1,0:T(8,128)}, u32[]{:S(2)}, u32[]{:S(2)}) collective-permute-start(f32[18,18,1]{2,1,0:T(8,128)} %get-tuple-element.48), channel_id=1, source_target_pairs={{1,0},{2,1},{3,2},{4,3},{5,4},{6,5},{7,6},{0,7},{9,8},{10,9},{11,1... | collective-permute-start | bytes 3896 | tf_op jit(solution)/shard_map/ppermute | solution.py:21
  251.6 35.6 %reshape.150 = f32[16,2,16,2,64,2]{5,4,3,2,1,0:T(8,128)} reshape(f32[32,32,128]{2,1,0:T(8,128)} %get-tuple-element.6) | data formatting | bytes 1048576 | tf_op jit(solution)/shard_map/reshape | solution.py:59
  287.3 12.2 %reduce_sum.183 = f32[16,16,64]{2,1,0:T(8,128)S(1)} reduce(f32[16,2,16,2,64,2]{5,4,3,2,1,0:T(8,128)} %reshape.150, f32[]{:T(128)} %constant.71.clone.1), dimensions={1,3,5}, to_apply=%region_0.0 | reduce | flops 114688 | bytes 589828 | tf_op jit(solution)/shard_map/reduce_sum | solution.py:60
  299.5 5.7 mul.1193
  308.0 17.6 %all_gather.9 = f32[8,8,256]{1,0,2:T(8,128)} all-gather(f32[8,8,32]{1,0,2:T(8,128)S(1)} %copy.810), channel_id=1, replica_groups=mesh['gx'=4,'gy'=4,'gz'=8] {'gz'}, dimensions={2}, use_global_device_ids=true | all-gather | bytes 73728 | tf_op jit(solution)/shard_map/all_gather | solution.py:135
  327.1 5.6 reshape.153
  520.7 3.5 collective-permute-done.101
  553.2 3.5 collective-permute-done.111
  588.9 68.9 %collective-permute-start.23 = (f32[18,18,1]{2,1,0:T(8,128)}, f32[18,18,1]{2,1,0:T(8,128)}, u32[]{:S(2)}, u32[]{:S(2)}) collective-permute-start(f32[18,18,1]{2,1,0:T(8,128)} %get-tuple-element.46), channel_id=1, source_target_pairs={{0,1},{1,2},{2,3},{3,4},{4,5},{5,6},{6,7},{7,0},{8,9},{9,10},{10,1... | collective-permute-start | bytes 3896 | tf_op jit(solution)/shard_map/ppermute | solution.py:18
  690.6 3.6 collective-permute-done.35
  722.4 18.0 %collective-permute-start.11 = (f32[1,34,34,1]{2,3,1,0:T(1,128)S(1)}, f32[1,34,34,1]{2,3,1,0:T(1,128)}, u32[]{:S(2)}, u32[]{:S(2)}) collective-permute-start(f32[1,34,34,1]{2,3,1,0:T(1,128)S(1)} %copy.807), channel_id=1, source_target_pairs={{1,0},{2,1},{3,2},{4,3},{5,4},{6,5},{7,6},{0,7},{9,8},{10,9},{11,1... | collective-permute-start | bytes 13880 | tf_op jit(solution)/shard_map/ppermute | solution.py:21
  757.2 4.6 collective-permute-start.22
  789.5 3.8 fusion.7
  (878 shorter events, 421.5 us)
Async XLA Ops:
  81.7 108.2 %collective-permute-start.120 = (f32[1,1,32]{2,1,0:T(1,128)S(1)}, f32[1,1,32]{2,1,0:T(1,128)S(1)}, u32[]{:S(2)}, u32[]{:S(2)}) collective-permute-start(f32[1,1,32]{2,1,0:T(1,128)S(1)} %get-tuple-element.220), channel_id=1, source_target_pairs={{32,0},{64,32},{96,64},{0,96},{33,1},{65,33},{97,65},{1,97},{34,2}... | collective-permute-start | bytes 392 | tf_op jit(solution)/shard_map/ppermute | solution.py:21
  84.4 105.6 %collective-permute-start.121 = (f32[1,1,32]{2,1,0:T(1,128)S(1)}, f32[1,1,32]{2,1,0:T(1,128)S(1)}, u32[]{:S(2)}, u32[]{:S(2)}) collective-permute-start(f32[1,1,32]{2,1,0:T(1,128)S(1)} %get-tuple-element.220), channel_id=1, source_target_pairs={{0,32},{32,64},{64,96},{96,0},{1,33},{33,65},{65,97},{97,1},{2,34}... | collective-permute-start | bytes 392 | tf_op jit(solution)/shard_map/ppermute | solution.py:18
  85.1 89.8 %collective-permute-start.152 = (f32[1,1,1]{0,2,1:T(1,128)}, f32[1,1,1]{0,2,1:T(1,128)}, u32[]{:S(2)}, u32[]{:S(2)}) collective-permute-start(f32[1,1,1]{0,2,1:T(1,128)} %bitcast.12), channel_id=1, source_target_pairs={{32,0},{64,32},{96,64},{0,96},{33,1},{65,33},{97,65},{1,97},{34,2}... | collective-permute-start | bytes 20 | tf_op jit(solution)/shard_map/ppermute | solution.py:21
  88.5 87.1 %collective-permute-start.153 = (f32[1,1,1]{0,2,1:T(1,128)}, f32[1,1,1]{0,2,1:T(1,128)}, u32[]{:S(2)}, u32[]{:S(2)}) collective-permute-start(f32[1,1,1]{0,2,1:T(1,128)} %bitcast.12), channel_id=1, source_target_pairs={{0,32},{32,64},{64,96},{96,0},{1,33},{33,65},{65,97},{97,1},{2,34}... | collective-permute-start | bytes 20 | tf_op jit(solution)/shard_map/ppermute | solution.py:18
  89.3 139.3 %collective-permute-start.1 = (f32[2,1,32,128]{3,2,1,0:T(8,128)S(1)}, f32[2,1,32,128]{3,2,1,0:T(8,128)S(1)}, u32[]{:S(2)}, u32[]{:S(2)}) collective-permute-start(f32[2,1,32,128]{3,2,1,0:T(8,128)S(1)} %get-tuple-element.38), channel_id=1, source_target_pairs={{32,0},{64,32},{96,64},{0,96},{33,1},{65,33},{97,65},{1,97},{34,2}... | collective-permute-start | bytes 98312 | tf_op jit(solution)/shard_map/ppermute | solution.py:21
  174.9 53.7 %collective-permute-start = (f32[2,1,32,128]{3,2,1,0:T(8,128)S(1)}, f32[2,1,32,128]{3,2,1,0:T(8,128)S(1)}, u32[]{:S(2)}, u32[]{:S(2)}) collective-permute-start(f32[2,1,32,128]{3,2,1,0:T(8,128)S(1)} %get-tuple-element.37), channel_id=1, source_target_pairs={{0,32},{32,64},{64,96},{96,0},{1,33},{33,65},{65,97},{97,1},{2,34}... | collective-permute-start | bytes 98312 | tf_op jit(solution)/shard_map/ppermute | solution.py:18
  217.0 132.4 %collective-permute-start.16 = (f32[18,18,1]{2,1,0:T(8,128)}, f32[18,18,1]{2,1,0:T(8,128)}, u32[]{:S(2)}, u32[]{:S(2)}) collective-permute-start(f32[18,18,1]{2,1,0:T(8,128)} %get-tuple-element.48), channel_id=1, source_target_pairs={{1,0},{2,1},{3,2},{4,3},{5,4},{6,5},{7,6},{0,7},{9,8},{10,9},{11,1... | collective-permute-start | bytes 3896 | tf_op jit(solution)/shard_map/ppermute | solution.py:21
  227.5 122.7 %collective-permute-start.17 = (f32[18,18,1]{2,1,0:T(8,128)}, f32[18,18,1]{2,1,0:T(8,128)}, u32[]{:S(2)}, u32[]{:S(2)}) collective-permute-start(f32[18,18,1]{2,1,0:T(8,128)} %get-tuple-element.47), channel_id=1, source_target_pairs={{0,1},{1,2},{2,3},{3,4},{4,5},{5,6},{6,7},{7,0},{8,9},{9,10},{10,1... | collective-permute-start | bytes 3896 | tf_op jit(solution)/shard_map/ppermute | solution.py:18
  339.0 115.5 %collective-permute-start.124 = (f32[1,1,32]{2,1,0:T(1,128)}, f32[1,1,32]{2,1,0:T(1,128)}, u32[]{:S(2)}, u32[]{:S(2)}) collective-permute-start(f32[1,1,32]{2,1,0:T(1,128)} %get-tuple-element.17), channel_id=1, source_target_pairs={{32,0},{64,32},{96,64},{0,96},{33,1},{65,33},{97,65},{1,97},{34,2}... | collective-permute-start | bytes 392 | tf_op jit(solution)/shard_map/ppermute | solution.py:21
  341.2 113.3 %collective-permute-start.125 = (f32[1,1,32]{2,1,0:T(1,128)}, f32[1,1,32]{2,1,0:T(1,128)}, u32[]{:S(2)}, u32[]{:S(2)}) collective-permute-start(f32[1,1,32]{2,1,0:T(1,128)} %get-tuple-element.17), channel_id=1, source_target_pairs={{0,32},{32,64},{64,96},{96,0},{1,33},{33,65},{65,97},{97,1},{2,34}... | collective-permute-start | bytes 392 | tf_op jit(solution)/shard_map/ppermute | solution.py:18
  350.1 122.8 %collective-permute-start.92 = (f32[1,2,64]{2,1,0:T(2,128)}, f32[1,2,64]{2,1,0:T(2,128)S(1)}, u32[]{:S(2)}, u32[]{:S(2)}) collective-permute-start(f32[1,2,64]{2,1,0:T(2,128)} %get-tuple-element.216), channel_id=1, source_target_pairs={{32,0},{64,32},{96,64},{0,96},{33,1},{65,33},{97,65},{1,97},{34,2}... | collective-permute-start | bytes 1544 | tf_op jit(solution)/shard_map/ppermute | solution.py:21
  354.9 118.1 %collective-permute-start.93 = (f32[1,2,64]{2,1,0:T(2,128)}, f32[1,2,64]{2,1,0:T(2,128)S(1)}, u32[]{:S(2)}, u32[]{:S(2)}) collective-permute-start(f32[1,2,64]{2,1,0:T(2,128)} %get-tuple-element.215), channel_id=1, source_target_pairs={{0,32},{32,64},{64,96},{96,0},{1,33},{33,65},{65,97},{97,1},{2,34}... | collective-permute-start | bytes 1544 | tf_op jit(solution)/shard_map/ppermute | solution.py:18
  458.0 49.9 %collective-permute-start.60 = (f32[1,4,128]{2,1,0:T(4,128)S(1)}, f32[1,4,128]{2,1,0:T(4,128)S(1)}, u32[]{:S(2)}, u32[]{:S(2)}) collective-permute-start(f32[1,4,128]{2,1,0:T(4,128)S(1)} %copy-done.115), channel_id=1, source_target_pairs={{32,0},{64,32},{96,64},{0,96},{33,1},{65,33},{97,65},{1,97},{34,2}... | collective-permute-start | bytes 6152 | tf_op jit(solution)/shard_map/ppermute | solution.py:21
  470.0 37.9 %collective-permute-start.61 = (f32[1,4,128]{2,1,0:T(4,128)S(1)}, f32[1,4,128]{2,1,0:T(4,128)S(1)}, u32[]{:S(2)}, u32[]{:S(2)}) collective-permute-start(f32[1,4,128]{2,1,0:T(4,128)S(1)} %copy-done.114), channel_id=1, source_target_pairs={{0,32},{32,64},{64,96},{96,0},{1,33},{33,65},{65,97},{97,1},{2,34}... | collective-permute-start | bytes 6152 | tf_op jit(solution)/shard_map/ppermute | solution.py:18
  470.0 87.6 %collective-permute-start.28 = (f32[1,8,256]{2,1,0:T(8,128)}, f32[1,8,256]{2,1,0:T(8,128)S(1)}, u32[]{:S(2)}, u32[]{:S(2)}) collective-permute-start(f32[1,8,256]{2,1,0:T(8,128)} %get-tuple-element.102), channel_id=1, source_target_pairs={{32,0},{64,32},{96,64},{0,96},{33,1},{65,33},{97,65},{1,97},{34,2}... | collective-permute-start | bytes 24584 | tf_op jit(solution)/shard_map/ppermute | solution.py:21
  505.0 54.9 %collective-permute-start.29 = (f32[1,8,256]{2,1,0:T(8,128)}, f32[1,8,256]{2,1,0:T(8,128)S(1)}, u32[]{:S(2)}, u32[]{:S(2)}) collective-permute-start(f32[1,8,256]{2,1,0:T(8,128)} %get-tuple-element.101), channel_id=1, source_target_pairs={{0,32},{32,64},{64,96},{96,0},{1,33},{33,65},{65,97},{97,1},{2,34}... | collective-permute-start | bytes 24584 | tf_op jit(solution)/shard_map/ppermute | solution.py:18
  530.3 128.6 %collective-permute-start.7 = (f32[1,1,32,128]{3,2,1,0:T(8,128)}, f32[1,1,32,128]{3,2,1,0:T(8,128)}, u32[]{:S(2)}, u32[]{:S(2)}) collective-permute-start(f32[1,1,32,128]{3,2,1,0:T(8,128)} %get-tuple-element.44), channel_id=1, source_target_pairs={{32,0},{64,32},{96,64},{0,96},{33,1},{65,33},{97,65},{1,97},{34,2}... | collective-permute-start | bytes 49160 | tf_op jit(solution)/shard_map/ppermute | solution.py:21
  553.1 105.8 %collective-permute-start.6 = (f32[1,1,32,128]{3,2,1,0:T(8,128)}, f32[1,1,32,128]{3,2,1,0:T(8,128)}, u32[]{:S(2)}, u32[]{:S(2)}) collective-permute-start(f32[1,1,32,128]{3,2,1,0:T(8,128)} %get-tuple-element.43), channel_id=1, source_target_pairs={{0,32},{32,64},{64,96},{96,0},{1,33},{33,65},{65,97},{97,1},{2,34}... | collective-permute-start | bytes 49160 | tf_op jit(solution)/shard_map/ppermute | solution.py:18
  574.9 88.4 %collective-permute-start.30 = (f32[10,1,256]{2,1,0:T(1,128)}, f32[10,1,256]{2,1,0:T(1,128)S(1)}, u32[]{:S(2)}, u32[]{:S(2)}) collective-permute-start(f32[10,1,256]{2,1,0:T(1,128)} %get-tuple-element.86), channel_id=1, source_target_pairs={{8,0},{16,8},{24,16},{0,24},{9,1},{17,9},{25,17},{1,25},{10,2},{18... | collective-permute-start | bytes 30728 | tf_op jit(solution)/shard_map/ppermute | solution.py:21
  586.4 79.5 %collective-permute-start.31 = (f32[10,1,256]{2,1,0:T(1,128)}, f32[10,1,256]{2,1,0:T(1,128)S(1)}, u32[]{:S(2)}, u32[]{:S(2)}) collective-permute-start(f32[10,1,256]{2,1,0:T(1,128)} %get-tuple-element.85), channel_id=1, source_target_pairs={{0,8},{8,16},{16,24},{24,0},{1,9},{9,17},{17,25},{25,1},{2,10},{10... | collective-permute-start | bytes 30728 | tf_op jit(solution)/shard_map/ppermute | solution.py:18
  588.9 188.0 %collective-permute-start.23 = (f32[18,18,1]{2,1,0:T(8,128)}, f32[18,18,1]{2,1,0:T(8,128)}, u32[]{:S(2)}, u32[]{:S(2)}) collective-permute-start(f32[18,18,1]{2,1,0:T(8,128)} %get-tuple-element.46), channel_id=1, source_target_pairs={{0,1},{1,2},{2,3},{3,4},{4,5},{5,6},{6,7},{7,0},{8,9},{9,10},{10,1... | collective-permute-start | bytes 3896 | tf_op jit(solution)/shard_map/ppermute | solution.py:18
  661.4 48.5 %collective-permute-start.9 = (f32[1,34,1,128]{3,2,1,0:T(1,128)S(1)}, f32[1,34,1,128]{3,2,1,0:T(1,128)S(1)}, u32[]{:S(2)}, u32[]{:S(2)}) collective-permute-start(f32[1,34,1,128]{3,2,1,0:T(1,128)S(1)} %get-tuple-element.42), channel_id=1, source_target_pairs={{8,0},{16,8},{24,16},{0,24},{9,1},{17,9},{25,17},{1,25},{10,2},{18... | collective-permute-start | bytes 52232 | tf_op jit(solution)/shard_map/ppermute | solution.py:21
  663.1 49.4 %collective-permute-start.8 = (f32[1,34,1,128]{3,2,1,0:T(1,128)S(1)}, f32[1,34,1,128]{3,2,1,0:T(1,128)S(1)}, u32[]{:S(2)}, u32[]{:S(2)}) collective-permute-start(f32[1,34,1,128]{3,2,1,0:T(1,128)S(1)} %get-tuple-element.41), channel_id=1, source_target_pairs={{0,8},{8,16},{16,24},{24,0},{1,9},{9,17},{17,25},{25,1},{2,10},{10... | collective-permute-start | bytes 52232 | tf_op jit(solution)/shard_map/ppermute | solution.py:18
  722.4 34.8 %collective-permute-start.11 = (f32[1,34,34,1]{2,3,1,0:T(1,128)S(1)}, f32[1,34,34,1]{2,3,1,0:T(1,128)}, u32[]{:S(2)}, u32[]{:S(2)}) collective-permute-start(f32[1,34,34,1]{2,3,1,0:T(1,128)S(1)} %copy.807), channel_id=1, source_target_pairs={{1,0},{2,1},{3,2},{4,3},{5,4},{6,5},{7,6},{0,7},{9,8},{10,9},{11,1... | collective-permute-start | bytes 13880 | tf_op jit(solution)/shard_map/ppermute | solution.py:21
  (276 other events, 6518.5 us)
where the time goes:
time: 804 us; the launch traced here: 794 us
  starting transfers between devices  262 us (33%)
  local copies, waits for them, and re-layouts  199 us (25%)
  waiting for transfers between devices  156 us (19%)
  other arithmetic  101 us (13%)
  blocking collectives  49.6 us (6%)
  between operations  25.3 us (3%)
    ppermute x92, starting transfers between devices, extended(): lax.ppermute(lax.slice_in_dim(block, 0, width, axis=dim), axis, backward)  152 us
    reshape x6, local copies, waits for them, and re-layouts, coarsen(): blocks = field.reshape(sizes[0] // 2, 2, sizes[1] // 2, 2, sizes[2] // 2, 2)  123 us
    ppermute x92, waiting for transfers between devices, extended(): lax.ppermute(lax.slice_in_dim(block, block.shape[dim] - width, None, axis...  114 us
    ppermute x92, starting transfers between devices, extended(): lax.ppermute(lax.slice_in_dim(block, block.shape[dim] - width, None, axis...  110 us
    reduce_sum x18, other arithmetic, coarsen(): return blocks.mean(axis=(1, 3, 5))  53.8 us
    ppermute x92, waiting for transfers between devices, extended(): lax.ppermute(lax.slice_in_dim(block, 0, width, axis=dim), axis, backward)  42.4 us
    concatenate x79, other arithmetic, extended(): block = jnp.concatenate([low, block, high], axis=dim)  19.9 us
    all_gather x1, blocking collectives, on_device(): lax.all_gather(rest_three, 'gz', axis=2, tiled=True)  17.6 us
  transfers between devices with their start and end apart: 184, of which 105 were waited for; matrix products, arithmetic and copies ran while one was open for 27% of the time, Pallas kernels for 0%

commit v1 on v0

v1 whole, which is shorter than its diff:
```python
import jax
import jax.numpy as jnp
from jax import lax
from jax.experimental import pallas as pl
from jax.experimental.pallas import tpu as pltpu
from jax.sharding import PartitionSpec as P

COARSE_SWEEPS = 8
WEIGHT = 0.8
LANES = 128
F32 = jnp.float32
BF16 = jnp.bfloat16

Z_FINE, Z_SEC, Z_ROWS = 72, 104, 120
W_SHIFT, W_FOUR, W_FIVE, W_SEC, W_ROWS = 64, 128, 144, 152, 168


def turn(value, shift, axis):
    size = value.shape[axis]
    if isinstance(shift, int):
        shift = shift % size
        if shift == 0:
            return value
    return pltpu.roll(value, shift, axis)


def lanes_of(shape):
    return lax.broadcasted_iota(jnp.int32, shape, len(shape) - 1)


def square(rule):
    row = lax.broadcasted_iota(jnp.int32, (LANES, LANES), 0)
    col = lax.broadcasted_iota(jnp.int32, (LANES, LANES), 1)
    return jnp.where(rule(row, col), 1.0, 0.0).astype(BF16)


def spread(value, chosen):
    total = None
    for part in range(3):
        piece = value.astype(BF16)
        term = jnp.dot(piece, chosen, preferred_element_type=F32)
        total = term if total is None else total + term
        if part < 2:
            value = value - piece.astype(F32)
    return total


def flat(value):
    return value.reshape(-1, LANES)


def faces_kernel(kappa, initial, xp, xm, yp, ym, zs):
    xp[0] = kappa[31]
    xp[1] = kappa[30]
    xp[2] = initial[31]
    xm[0] = kappa[0]
    xm[1] = kappa[1]
    xm[2] = initial[0]
    yp[0] = kappa[:, 31, :]
    yp[1] = kappa[:, 30, :]
    yp[2] = initial[:, 31, :]
    ym[0] = kappa[:, 0, :]
    ym[1] = kappa[:, 1, :]
    ym[2] = initial[:, 0, :]
    lane = lanes_of((32, LANES))

    def body(x, carry):
        first, second = carry
        mine = lane // 4 == x
        shift = 4 * x + 2
        first = jnp.where(mine, turn(kappa[x], shift, 1), first)
        second = jnp.where(mine, turn(initial[x], shift, 1), second)
        return first, second

    zero = jnp.zeros((32, LANES), F32)
    first, second = lax.fori_loop(0, 32, body, (zero, zero), unroll=4)
    zs[0] = first
    zs[1] = second


def z_sides(value, rim, x, lane, period):
    near = turn(rim, 126 - 4 * x, 1)
    if period < LANES:
        other = turn(rim, lax.rem(190 - 4 * x, 128), 1)
        near = jnp.where((lane >= 32) & (lane < 96), other, near)
    inside = lane % period
    above = turn(jnp.where(inside == 0, near, value), LANES - 1, 1)
    below = turn(jnp.where(inside == period - 1, near, value), 1, 1)
    return above, below


def residual_kernel(
    kappa, initial, rhs, sigma, xlo, xhi, ylo, yhi, zlo, zhi,
    kp, ck, scale, first, message, sides, kp2, ck2, scale2, first2, sides2,
    vp, pair_r, pair_k, pair_s, rims, small,
):
    lane = lanes_of((32, LANES))
    inner = pl.ds(8, 32)
    kp[0, inner] = xlo[0]
    kp[33, inner] = xhi[0]
    vp[0, inner] = xlo[2]
    vp[33, inner] = xhi[2]

    def fill(x, carry):
        one = pl.ds(x, 1)
        kp[x + 1, inner] = kappa[x]
        vp[x + 1, inner] = initial[x]
        kp[x + 1, 7:8] = ylo[0, one]
        kp[x + 1, 40:41] = yhi[0, one]
        vp[x + 1, 7:8] = ylo[2, one]
        vp[x + 1, 40:41] = yhi[2, one]
        return carry

    lax.fori_loop(0, 32, fill, 0, unroll=4)
    low_half = lane % 4 < 2
    rim_k = jnp.where(low_half, zlo[0], zhi[0])
    rim_v = jnp.where(low_half, zlo[1], zhi[1])
    ck[...] = rim_k

    def slab(x, packed):
        k = kp[x + 1, inner]
        v = vp[x + 1, inner]
        around = [
            (kp[x, inner], vp[x, inner]),
            (kp[x + 2, inner], vp[x + 2, inner]),
            (kp[x + 1, pl.ds(7, 32)], vp[x + 1, pl.ds(7, 32)]),
            (kp[x + 1, pl.ds(9, 32)], vp[x + 1, pl.ds(9, 32)]),
        ]
        k_up, k_down = z_sides(k, rim_k, x, lane, LANES)
        v_up, v_down = z_sides(v, rim_v, x, lane, LANES)
        around += [(k_up, v_up), (k_down, v_down)]
        k_sum = sum(kn for kn, _ in around)
        v_sum = sum(vn for _, vn in around)
        both = sum(kn * vn for kn, vn in around)
        s = sigma[x]
        diagonal = s + 3.0 * k + 0.5 * k_sum
        r = rhs[x] - diagonal * v + 0.5 * (k * v_sum + both)
        h = WEIGHT / diagonal
        e = h * r
        scale[x] = h
        first[x] = e
        packed = jnp.where(lane // 4 == x, turn(e, 4 * x + 2, 1), packed)
        return r, k, s, packed

    def two(i, packed):
        r0, k0, s0, packed = slab(2 * i, packed)
        r1, k1, s1, packed = slab(2 * i + 1, packed)
        pair_r[i] = r0 + r1
        pair_k[i] = k0 + k1
        pair_s[i] = s0 + s1
        return packed

    packed = lax.fori_loop(0, 16, two, jnp.zeros((32, LANES), F32))
    sides[0] = first[31]
    sides[1] = first[0]
    sides[2] = first[:, 31, :]
    sides[3] = first[:, 0, :]

    even, odd = pl.ds(0, 16, stride=2), pl.ds(1, 16, stride=2)
    to_two = square(lambda row, col: row // 2 == col % 64)

    def level_two(ref, weight):
        summed = ref[:, even, :] + ref[:, odd, :]
        return (spread(flat(summed), to_two) * weight).reshape(16, 16, LANES)

    r2 = level_two(pair_r, 0.5)
    k2 = level_two(pair_k, 0.125)
    s2 = level_two(pair_s, 0.5)
    rims[0] = xlo[0] + xlo[1]
    rims[1] = xhi[0] + xhi[1]
    rims[2] = ylo[0] + ylo[1]
    rims[3] = yhi[0] + yhi[1]
    halo = rims[:, even, :] + rims[:, odd, :]
    halo = (spread(flat(halo), to_two) * 0.125).reshape(4, 16, LANES)
    inner2 = pl.ds(8, 16)
    kp2[1:17, inner2] = k2
    kp2[0, inner2] = halo[0]
    kp2[17, inner2] = halo[1]
    for x in range(16):
        kp2[x + 1, 7:8] = halo[2, x : x + 1]
        kp2[x + 1, 24:25] = halo[3, x : x + 1]
    rims[0] = rim_k
    rim_pair = rims[0, even, :] + rims[0, odd, :]

    def rim_rule(row, col):
        low = (col % 4 == 1) & (row % 4 < 2)
        high = (col % 4 == 2) & (row % 4 >= 2)
        return (row // 8 == col // 4) & (low | high)

    rim_k2 = spread(rim_pair, square(rim_rule)) * 0.125
    ck2[...] = rim_k2
    lane2 = lanes_of((16, LANES))
    packed2 = jnp.zeros((16, LANES), F32)
    for x in range(16):
        k = k2[x]
        up, down = z_sides(k, rim_k2, x, lane2, 64)
        k_sum = (
            kp2[x, inner2] + kp2[x + 2, inner2]
            + kp2[x + 1, pl.ds(7, 16)] + kp2[x + 1, pl.ds(9, 16)] + up + down
        )
        h = WEIGHT / (s2[x] + 3.0 * k + 0.5 * k_sum)
        e = h * r2[x]
        scale2[x] = h
        first2[x] = e
        packed2 = jnp.where(lane2 // 4 == x, turn(e, 4 * x + 2, 1), packed2)
    sides2[0] = first2[15]
    sides2[1] = first2[0]
    sides2[2] = first2[:, 15, :]
    sides2[3] = first2[:, 0, :]

    even8, odd8 = pl.ds(0, 8, stride=2), pl.ds(1, 8, stride=2)

    def level_three(field, part, weight):
        halves = field.reshape(8, 2, 16, LANES)
        small[...] = halves[:, 0] + halves[:, 1]
        summed = small[:, even8, :] + small[:, odd8, :]
        rule = square(lambda row, col: (row < 64) & (row // 2 == col - 32 * part))
        return spread(flat(summed), rule) * weight

    three = level_three(r2, 0, 0.5) + level_three(k2, 1, 0.125) + level_three(s2, 2, 0.5)
    cubes = three.reshape(2, 4, 8, LANES)
    summed = cubes[:, 0] + cubes[:, 1] + cubes[:, 2] + cubes[:, 3]
    small[0:2, 0:8] = summed
    quads = [small[0:2, pl.ds(j, 2, stride=4), :] for j in range(4)]
    quad = quads[0] + quads[1] + quads[2] + quads[3]
    small[2, 0:8] = jnp.zeros((8, LANES), F32)
    small[2, 0:2] = quad[0]
    small[2, 2:4] = quad[1]
    five = spread(small[2, 0:8], square(lambda row, col: (row < 96) & (row // 4 == col)))
    lane8 = lanes_of((8, LANES))
    five = five * jnp.where((lane8 >= 8) & (lane8 < 16), 1.0 / 64.0, 0.25)
    for p in range(8):
        message[p, 0:64] = three
        message[p, 64:72] = five
        message[p, Z_FINE:Z_SEC] = packed
        message[p, Z_SEC:Z_ROWS] = packed2


def window_kernel(place, lines, sides, sides2, out, cf, cf2, small):
    gx, gy, gz = place[0], place[1], place[2]
    before, after = lax.rem(gz + 7, 8), lax.rem(gz + 1, 8)
    a, b, c = lines[before, 0:64], lines[gz, 0:64], lines[after, 0:64]
    lane = lanes_of((64, LANES))

    def join(pieces):
        total = pieces[-1][1]
        for stop, piece in reversed(pieces[:-1]):
            total = jnp.where(lane < stop, piece, total)
        return total

    both = join([
        (16, turn(a, -16, 1)), (48, turn(b, 16, 1)), (64, turn(c, 48, 1)),
        (80, turn(a, 16, 1)), (112, turn(b, 48, 1)), (128, turn(c, 80, 1)),
    ])
    shift = join([
        (16, turn(a, -80, 1)), (48, turn(b, -48, 1)), (64, turn(c, -16, 1)),
        (128, jnp.zeros((64, LANES), F32)),
    ])

    even, odd = pl.ds(0, 4, stride=2), pl.ds(1, 4, stride=2)

    def shrink(field):
        halves = field.reshape(4, 2, 8, LANES)
        small[0:4] = halves[:, 0] + halves[:, 1]
        summed = small[0:4, even, :] + small[0:4, odd, :]
        for i in range(4):
            small[4 + i // 2, 4 * (i % 2) : 4 * (i % 2) + 4] = summed[i]
        return flat(small[4:6])

    lane4 = lanes_of((16, LANES))
    four = spread(shrink(both), square(lambda row, col: row // 2 == col))
    four = four * jnp.where(lane4 < 32, 0.5, 0.125)
    four = four + 0.5 * spread(
        shrink(shift), square(lambda row, col: (row < 64) & (row // 2 + 64 == col))
    )

    lane8 = lanes_of((8, LANES))
    row8 = lax.broadcasted_iota(jnp.int32, (8, LANES), 0)
    five = jnp.zeros((8, LANES), F32)
    five_shift = jnp.zeros((8, LANES), F32)
    for p in range(8):
        piece = lines[p, 64:72]
        five = jnp.where(lane8 // 8 == p, turn(piece, 8 * p, 1), five)
        five = jnp.where(lane8 // 8 == p + 8, turn(piece, 56 + 8 * p, 1), five)
        five_shift = jnp.where(lane8 // 8 == p, turn(piece, 8 * p - 16, 1), five_shift)
    five = jnp.where(row8 < 4, five, turn(five_shift, 4, 0))

    for q in range(16):
        out[q, 0:64] = both
        out[q, W_SHIFT:W_FOUR] = shift
        out[q, W_FOUR:W_FIVE] = four
        out[q, W_FIVE:W_SEC] = five
        out[q, W_SEC:W_ROWS] = jnp.zeros((16, LANES), F32)
    lane32 = lanes_of((32, LANES))
    for side, (dx, dy) in enumerate(((1, 0), (3, 0), (0, 1), (0, 3))):
        q = 4 * lax.rem(gx + dx, 4) + lax.rem(gy + dy, 4)
        face = sides[side]
        low = lane32 < 64
        out[q, W_SHIFT : W_SHIFT + 32] = jnp.where(low, shift[0:32], turn(face, 64, 1))
        out[q, W_SHIFT + 32 : W_FOUR] = jnp.where(low, shift[32:64], face)
        out[q, W_SEC:W_ROWS] = sides2[side]
    cf[...] = jnp.where(
        lane32 % 4 < 2, lines[before, Z_FINE:Z_SEC], lines[after, Z_FINE:Z_SEC]
    )
    cf2[...] = jnp.where(lane4 % 4 < 2, lines[before, Z_SEC:Z_ROWS], lines[after, Z_SEC:Z_ROWS])


def wrapped(value):
    last = value.shape[0] - 1
    return [
        jnp.concatenate([value[1:], value[:1]], 0),
        jnp.concatenate([value[last:], value[:last]], 0),
        turn(value, -1, 1),
        turn(value, 1, 1),
        turn(value, -1, 2),
        turn(value, 1, 2),
    ]


def periodic_setup(r, k, s, coefs):
    near = wrapped(k)
    diagonal = s + 3.0 * k + 0.5 * sum(near)
    h = WEIGHT / diagonal
    half = 0.5 * h
    for n in range(6):
        coefs[n] = half * (k + near[n])
    start = h * r
    coefs[6] = start
    return start


def periodic_sweep(e, coefs):
    total = 0.2 * e + coefs[6]
    for n, other in enumerate(wrapped(e)):
        total = total + coefs[n] * other
    return total


def cycle_kernel(
    place, columns, initial, kp, ck, scale, first, cf, kp2, ck2, scale2, first2, cf2,
    out,
    fp, fp2, rk3, s3, k3, c3, ea, eb, l4, l5, s5, l6, c4, c5, c6, c7, w4, w3, w2, up,
):
    gx, gy, gz = place[0], place[1], place[2]

    def slot(dx, dy):
        return 4 * lax.rem(gx + dx, 4) + lax.rem(gy + dy, 4)

    for ix, dx in enumerate((3, 0, 1)):
        for iy, dy in enumerate((3, 0, 1)):
            q = slot(dx, dy)
            for i in range(8):
                piece = columns[q, 8 * i : 8 * i + 8]
                rk3[8 * ix + i, 8 * iy : 8 * iy + 8] = piece
                s3[8 * ix + i, 8 * iy : 8 * iy + 8] = columns[
                    q, W_SHIFT + 8 * i : W_SHIFT + 8 * i + 8
                ]
                k3[8 * ix + i, 8 + 8 * iy : 16 + 8 * iy] = turn(piece, 64, 1)
    rim = jnp.zeros((24, 8, LANES), F32)
    for ref in (k3, ea, eb):
        ref[:, 0:8] = rim
        ref[:, 32:40] = rim
    mid = pl.ds(8, 24)

    def setup3(x, carry):
        k = k3[x, mid]
        near = [
            k3[x + 1, mid], k3[x - 1, mid], k3[x, pl.ds(9, 24)], k3[x, pl.ds(7, 24)],
            turn(k, -1, 1), turn(k, 1, 1),
        ]
        h = WEIGHT / (s3[x] + 3.0 * k + 0.5 * sum(near))
        half = 0.5 * h
        for n in range(6):
            c3[n, x] = half * (k + near[n])
        g = h * rk3[x]
        c3[6, x] = g
        ea[x, mid] = g
        return carry

    lax.fori_loop(1, 23, setup3, 0)

    for qx in range(4):
        for qy in range(4):
            q = 4 * qx + qy
            for i in range(4):
                l4[4 * qx + i, 4 * qy : 4 * qy + 4] = columns[
                    q, W_FOUR + 4 * i : W_FOUR + 4 * i + 4
                ]
            for i in range(2):
                base = W_FIVE + 2 * i
                l5[2 * qx + i, 2 * qy : 2 * qy + 2] = columns[q, base : base + 2]
                s5[2 * qx + i, 2 * qy : 2 * qy + 2] = columns[q, base + 4 : base + 6]
    r4 = l4[...]
    e4 = periodic_setup(r4, turn(r4, 96, 2), turn(r4, 64, 2), c4)
    lane5 = lanes_of((8, 8, LANES))
    both5 = l5[...]
    swapped = turn(both5, 64, 2)
    shift5 = s5[...]
    r5 = jnp.where(lane5 < 64, both5, swapped)
    k5 = jnp.where(lane5 < 64, swapped, both5)
    sh5 = jnp.where(lane5 < 64, shift5, turn(shift5, 64, 2))
    e5 = periodic_setup(r5, k5, sh5, c5)
    to_six = square(lambda row, col: (row < 64) & (row // 2 == col % 32))

    def level_six(field, weight):
        halves = field.reshape(4, 2, 8, LANES)
        l6[...] = halves[:, 0] + halves[:, 1]
        summed = l6[:, pl.ds(0, 4, stride=2), :] + l6[:, pl.ds(1, 4, stride=2), :]
        l6[:, 0:4] = summed
        l6[:, 4:8] = summed
        return spread(flat(l6[...]), to_six) * weight

    r6, k6, sh6 = level_six(r5, 0.5), level_six(k5, 0.125), level_six(sh5, 0.5)
    mean = square(lambda row, col: row < 32)

    def cube(value):
        return value.reshape(4, 8, LANES)

    r7, k7, sh7 = [cube(spread(f, mean) * (1.0 / 32.0)) for f in (r6, k6, sh6)]
    e6 = periodic_setup(cube(r6), cube(k6), cube(sh6), c6)
    e7 = periodic_setup(r7, k7, sh7, c7)

    def sweep(_, carry):
        a, b, c, d = carry
        return (
            periodic_sweep(a, c4), periodic_sweep(b, c5), periodic_sweep(c, c6),
            periodic_sweep(d, c7),
        )

    e4, e5, e6, e7 = lax.fori_loop(0, COARSE_SWEEPS - 1, sweep, (e4, e5, e6, e7))

    source, target = ea, eb
    for step in range(2, COARSE_SWEEPS + 1):

        def sweep3(x, carry, source=source, target=target):
            e = source[x, mid]
            near = [
                source[x + 1, mid], source[x - 1, mid],
                source[x, pl.ds(9, 24)], source[x, pl.ds(7, 24)],
                turn(e, -1, 1), turn(e, 1, 1),
            ]
            total = 0.2 * e + c3[6, x]
            for n in range(6):
                total = total + c3[n, x] * near[n]
            target[x, mid] = total
            return carry

        lax.fori_loop(step, 24 - step, sweep3, 0)
        source, target = target, source

    lane16 = lanes_of((16, LANES))
    lane8 = lanes_of((8, LANES))
    l6[...] = e6 + e7
    six = turn(l6[gx, pl.ds(gy, 1)] + jnp.zeros((8, LANES), F32), 128 - 4 * gz, 1)
    six = spread(six, square(lambda row, col: row == col // 32))
    l5[...] = e5
    w4[...] = jnp.zeros((16, LANES), F32)
    w4[0:2] = l5[2 * gx, pl.ds(2 * gy, 2)]
    w4[2:4] = l5[2 * gx + 1, pl.ds(2 * gy, 2)]
    five = spread(turn(w4[0:8], 128 - 8 * gz, 1), square(lambda row, col: row == col // 16))
    five = five + six
    l4[...] = e4
    for i in range(4):
        w4[4 * i : 4 * i + 4] = l4[4 * gx + i, pl.ds(4 * gy, 4)]
    four = jnp.where((lane16 >= 8) & (lane16 < 24), w4[...], 0.0)
    four = spread(four, square(lambda row, col: row == 8 + col // 8))
    for i in range(4):
        for j in range(2):
            row = 2 * (i // 2) + j
            w4[4 * i + 2 * j : 4 * i + 2 * j + 2] = jnp.broadcast_to(
                five[row : row + 1], (2, LANES)
            )
    four = four + w4[...]
    own = source[8:16, 16:24]
    lane3 = lanes_of((8, 8, LANES))
    three = flat(jnp.where((lane3 >= 16) & (lane3 < 48), own, 0.0))
    three = spread(three, square(lambda row, col: row == 16 + col // 4))
    for i in range(8):
        block = four[4 * (i // 2) : 4 * (i // 2) + 4]
        w3[i, pl.ds(0, 4, stride=2), :] = block
        w3[i, pl.ds(1, 4, stride=2), :] = block
    three = three + flat(w3[...])

    inner2 = pl.ds(8, 16)
    lane2 = lanes_of((16, LANES))
    lane32 = lanes_of((32, LANES))
    sides = [slot(3, 0), slot(1, 0), slot(0, 3), slot(0, 1)]
    fp2[1:17, inner2] = first2[...]
    fp2[0, inner2] = columns[sides[0], W_SEC:W_ROWS]
    fp2[17, inner2] = columns[sides[1], W_SEC:W_ROWS]
    for x in range(16):
        fp2[x + 1, 7:8] = columns[sides[2], W_SEC + x : W_SEC + x + 1]
        fp2[x + 1, 24:25] = columns[sides[3], W_SEC + x : W_SEC + x + 1]
    rim_k2 = ck2[...]
    rim_f2 = cf2[...]
    for x in range(16):
        k = kp2[x + 1, inner2]
        e = fp2[x + 1, inner2]
        k_up, k_down = z_sides(k, rim_k2, x, lane2, 64)
        e_up, e_down = z_sides(e, rim_f2, x, lane2, 64)
        around = [
            (kp2[x, inner2], fp2[x, inner2]),
            (kp2[x + 2, inner2], fp2[x + 2, inner2]),
            (kp2[x + 1, pl.ds(7, 16)], fp2[x + 1, pl.ds(7, 16)]),
            (kp2[x + 1, pl.ds(9, 16)], fp2[x + 1, pl.ds(9, 16)]),
            (k_up, e_up),
            (k_down, e_down),
        ]
        total = k * sum(en for _, en in around) + sum(kn * en for kn, en in around)
        w2[x] = 1.2 * e + 0.5 * scale2[x] * total
    two = spread(flat(w2[...]), square(lambda row, col: row == col // 2))
    even8, odd8 = pl.ds(0, 8, stride=2), pl.ds(1, 8, stride=2)
    for i in range(16):
        block = three[8 * (i // 2) : 8 * (i // 2) + 8]
        w2[i, even8, :] = block
        w2[i, odd8, :] = block
    two = two.reshape(16, 16, LANES) + w2[...]
    up[:, pl.ds(0, 16, stride=2), :] = two
    up[:, pl.ds(1, 16, stride=2), :] = two

    inner = pl.ds(8, 32)

    def face_of(q):
        low = columns[q, W_SHIFT : W_SHIFT + 32]
        return jnp.where(lane32 < 64, turn(low, 64, 1), columns[q, W_SHIFT + 32 : W_FOUR])

    fp[0, inner] = face_of(sides[0])
    fp[33, inner] = face_of(sides[1])
    w2[0:2] = face_of(sides[2]).reshape(2, 16, LANES)
    w2[2:4] = face_of(sides[3]).reshape(2, 16, LANES)

    def fill(x, carry):
        fp[x + 1, inner] = first[x]
        row = pl.ds(lax.rem(x, 16), 1)
        fp[x + 1, 7:8] = w2[x // 16, row]
        fp[x + 1, 40:41] = w2[2 + x // 16, row]
        return carry

    lax.fori_loop(0, 32, fill, 0, unroll=4)
    rim_k = ck[...]
    rim_f = cf[...]

    def slab(x, carry):
        k = kp[x + 1, inner]
        e = fp[x + 1, inner]
        k_up, k_down = z_sides(k, rim_k, x, lane32, LANES)
        e_up, e_down = z_sides(e, rim_f, x, lane32, LANES)
        around = [
            (kp[x, inner], fp[x, inner]),
            (kp[x + 2, inner], fp[x + 2, inner]),
            (kp[x + 1, pl.ds(7, 32)], fp[x + 1, pl.ds(7, 32)]),
            (kp[x + 1, pl.ds(9, 32)], fp[x + 1, pl.ds(9, 32)]),
            (k_up, e_up),
            (k_down, e_down),
        ]
        total = k * sum(en for _, en in around) + sum(kn * en for kn, en in around)
        out[x] = initial[x] + (1.2 * e + 0.5 * scale[x] * total + up[x // 2])
        return carry

    lax.fori_loop(0, 32, slab, 0)


VM = pl.BlockSpec(memory_space=pltpu.VMEM)
SM = pl.BlockSpec(memory_space=pltpu.SMEM)


def shape(*dims):
    return jax.ShapeDtypeStruct(dims, F32)


def local(kernel, outs, ins, scratch, name):
    return pl.pallas_call(
        kernel,
        out_shape=outs,
        in_specs=ins,
        out_specs=[VM] * len(outs),
        scratch_shapes=[pltpu.VMEM(dims, F32) for dims in scratch],
        compiler_params=pltpu.CompilerParams(vmem_limit_bytes=40 * 1024 * 1024),
        name=name,
    )


def on_device(initial, rhs, kappa, sigma):
    place = jnp.stack([lax.axis_index(axis) for axis in ("gx", "gy", "gz")]).astype(jnp.int32)

    def passed(value, axis, step):
        count = lax.axis_size(axis)
        return lax.ppermute(value, axis, [(i, (i + step) % count) for i in range(count)])

    edge = shape(3, 32, LANES)
    xp, xm, yp, ym, zs = local(
        faces_kernel, [edge, edge, edge, edge, shape(2, 32, LANES)], [VM] * 2, [], "faces"
    )(kappa, initial)
    xlo, xhi = passed(xp, "gx", 1), passed(xm, "gx", -1)
    ylo, yhi = passed(yp, "gy", 1), passed(ym, "gy", -1)
    zlo, zhi = passed(zs, "gz", 1), passed(zs, "gz", -1)
    block = (32, 32, LANES)
    block2 = (16, 16, LANES)
    kp, ck, scale, first, message, sides, kp2, ck2, scale2, first2, sides2 = local(
        residual_kernel,
        [
            shape(34, 48, LANES), shape(32, LANES), shape(*block), shape(*block),
            shape(8, Z_ROWS, LANES), shape(4, 32, LANES), shape(18, 32, LANES),
            shape(16, LANES), shape(*block2), shape(*block2), shape(4, 16, LANES),
        ],
        [VM] * 10,
        [
            (34, 48, LANES), (16, 32, LANES), (16, 32, LANES), (16, 32, LANES),
            (4, 32, LANES), (8, 16, LANES),
        ],
        "residual",
    )(kappa, initial, rhs, sigma, xlo, xhi, ylo, yhi, zlo, zhi)
    lines = lax.all_to_all(message, "gz", 0, 0)
    windows, cf, cf2 = local(
        window_kernel,
        [shape(16, W_ROWS, LANES), shape(32, LANES), shape(16, LANES)],
        [SM] + [VM] * 3,
        [(8, 8, LANES)],
        "window",
    )(place, lines, sides, sides2)
    columns = lax.all_to_all(windows, ("gx", "gy"), 0, 0)
    padded3 = (24, 40, LANES)
    block3 = (24, 24, LANES)
    return local(
        cycle_kernel,
        [shape(*block)],
        [SM] + [VM] * 12,
        [
            (34, 48, LANES), (18, 32, LANES), block3, block3, padded3, (7,) + block3,
            padded3, padded3, block2, (8, 8, LANES), (8, 8, LANES), (4, 8, LANES),
            (7,) + block2, (7, 8, 8, LANES), (7, 4, 8, LANES), (7, 4, 8, LANES),
            (16, LANES), (8, 8, LANES), block2, (16, 32, LANES),
        ],
        "cycle",
    )(
        place, columns, initial, kp, ck, scale, first, cf, kp2, ck2, scale2, first2, cf2
    )[0]


def solution(mesh):
    spec = P("gx", "gy", "gz")
    return jax.shard_map(
        on_device, mesh=mesh, in_specs=(spec,) * 4, out_specs=spec, check_vma=False
    )
```

time: 804 us -> 81.1 us (0.10); the launches traced: 794 us -> 80.1 us
  starting transfers between devices: 262 us -> 17.2 us
  local copies, waits for them, and re-layouts: 199 us -> 2.1 us
  waiting for transfers between devices: 156 us -> 10.8 us
  other arithmetic: 101 us -> 0.08 us
  Pallas kernels: 0 us -> 26.1 us
  blocking collectives: 49.6 us -> 23.8 us
  between operations: 25.3 us -> 0.06 us
    ppermute x184 -> x6, starting transfers between devices: 262 us -> 9.97 us  [passed(): lax.ppermute(value, axis, [(i, (i + step) % count) for i in range(count)])]
    ppermute x184 -> x6, waiting for transfers between devices: 156 us -> 1.73 us  [passed(): lax.ppermute(value, axis, [(i, (i + step) % count) for i in range(count)])]
    reshape x13 -> x0, local copies, waits for them, and re-layouts: 134 us -> none  [the longest x6 123 us: coarsen(): blocks = field.reshape(sizes[0] // 2, 2, sizes[1] // 2, 2, sizes[2] // 2, 2)]
    reduce_sum x21 -> x0, other arithmetic: 55.6 us -> none  [the longest x18 53.8 us: coarsen(): return blocks.mean(axis=(1, 3, 5))]
    all_gather x3 -> x0, blocking collectives: 49.6 us -> none  [the longest x1 17.6 us: on_device(): lax.all_gather(rest_three, 'gz', axis=2, tiled=True)]
    pallas_call x0 -> x4, Pallas kernels: none -> 26.1 us  [the longest x1 18.7 us: on_device(): local(cycle_kernel, [shape(*block)], [SM] + [VM] * 12, [(34, 48, LANES),...]
    slice x91 -> x0, local copies, waits for them, and re-layouts: 26.1 us -> none  [the longest x40 8.39 us: extended(): lax.slice_in_dim(block, block.shape[dim] - width, None, axis=dim)]
    all_to_all x0 -> x1, blocking collectives: none -> 23.8 us  [on_device(): columns = lax.all_to_all(windows, ('gx', 'gy'), 0, 0)]
  transfers between devices with their start and end apart: 184 -> 7, of which waited for: 105 -> 2; matrix products, arithmetic and copies ran while one was open for 27% -> 0% of each run, Pallas kernels for 0% -> 0%
where the time goes in v1:
time: 81.1 us; the launch traced here: 80.1 us
  Pallas kernels  26.1 us (32%)
  blocking collectives  23.8 us (29%)
  starting transfers between devices  17.2 us (21%)
  waiting for transfers between devices  10.8 us (13%)
  local copies, waits for them, and re-layouts  2.1 us (3%)
    all_to_all x1, blocking collectives, on_device(): columns = lax.all_to_all(windows, ('gx', 'gy'), 0, 0)  23.8 us
    pallas_call x1, Pallas kernels, on_device(): local(cycle_kernel, [shape(*block)], [SM] + [VM] * 12, [(34, 48, LANES),...  18.7 us
    ppermute x6, starting transfers between devices, passed(): lax.ppermute(value, axis, [(i, (i + step) % count) for i in range(count)])  9.97 us
    all_to_all x1, waiting for transfers between devices, on_device(): lines = lax.all_to_all(message, 'gz', 0, 0)  9.07 us
    all_to_all x1, starting transfers between devices, on_device(): lines = lax.all_to_all(message, 'gz', 0, 0)  7.24 us
    pallas_call x1, Pallas kernels, on_device(): local(residual_kernel, [shape(34, 48, LANES), shape(32, LANES), shape(*bl...  5.61 us
    unnamed x10, local copies, waits for them, and re-layouts  2.1 us
    ppermute x6, waiting for transfers between devices, passed(): lax.ppermute(value, axis, [(i, (i + step) % count) for i in range(count)])  1.73 us
  transfers between devices with their start and end apart: 7, of which 2 were waited for; matrix products, arithmetic and copies ran while one was open for 0% of the time, Pallas kernels for 0%

profile of v1, /device:TPU:1, one launch (start us, length us, event | category | flops | bytes accessed | tf_op | source)
XLA Modules:
  0.0 80.1 jit_solution(9533190632947829846)
XLA Ops:
  0.0 1.0 %copy-done = f32[32,32,128]{2,1,0:T(8,128)S(1)} copy-done((f32[32,32,128]{2,1,0:T(8,128)S(1)}, f32[32,32,128]{2,1,0:T(8,128)}, u32[]{:S(2)}) %copy-start) | copy-done | bytes 524312
  1.0 1.0 %copy-done.2 = f32[32,32,128]{2,1,0:T(8,128)S(1)} copy-done((f32[32,32,128]{2,1,0:T(8,128)S(1)}, f32[32,32,128]{2,1,0:T(8,128)}, u32[]{:S(2)}) %copy-start.2) | copy-done | bytes 524312
  2.1 0.9 %faces.1 = (f32[3,32,128]{2,1,0:T(8,128)S(1)}, f32[3,32,128]{2,1,0:T(8,128)S(1)}, f32[3,32,128]{2,1,0:T(8,128)S(1)}, f32[3,32,128]{2,1,0:T(8,128)S(1)}, f32[2,32,128]{2,1,0:T(8,128)S(1)}) custom-call(f32[32,32,128]{2,1,0:T(8,128)S(1)} %copy-done.2, f32[32,32,128]{2,1,0:T(8,128)S(1)} %copy-done), custom_call_target="tpu_custom_call" | custom-call | tf_op jit(solution)/shard_map/faces/pallas_call | solution.py:591
  3.0 1.4 %collective-permute-start.5 = (f32[2,32,128]{2,1,0:T(8,128)S(1)}, f32[2,32,128]{2,1,0:T(8,128)S(1)}, u32[]{:S(2)}, u32[]{:S(2)}) collective-permute-start(f32[2,32,128]{2,1,0:T(8,128)S(1)} %get-tuple-element.28), channel_id=1, source_target_pairs={{0,7},{1,0},{2,1},{3,2},{4,3},{5,4},{6,5},{7,6},{8,15},{9,8},{10,9... | collective-permute-start | bytes 98312 | tf_op jit(solution)/shard_map/ppermute | solution.py:588
  4.4 1.4 %collective-permute-start = (f32[3,32,128]{2,1,0:T(8,128)S(1)}, f32[3,32,128]{2,1,0:T(8,128)S(1)}, u32[]{:S(2)}, u32[]{:S(2)}) collective-permute-start(f32[3,32,128]{2,1,0:T(8,128)S(1)} %get-tuple-element.24), channel_id=1, source_target_pairs={{0,32},{32,64},{64,96},{96,0},{1,33},{33,65},{65,97},{97,1},{2,34}... | collective-permute-start | bytes 147464 | tf_op jit(solution)/shard_map/ppermute | solution.py:588
  5.8 1.4 %collective-permute-start.1 = (f32[3,32,128]{2,1,0:T(8,128)S(1)}, f32[3,32,128]{2,1,0:T(8,128)S(1)}, u32[]{:S(2)}, u32[]{:S(2)}) collective-permute-start(f32[3,32,128]{2,1,0:T(8,128)S(1)} %get-tuple-element.25), channel_id=1, source_target_pairs={{0,96},{32,0},{64,32},{96,64},{1,97},{33,1},{65,33},{97,65},{2,98}... | collective-permute-start | bytes 147464 | tf_op jit(solution)/shard_map/ppermute | solution.py:588
  7.2 1.6 %collective-permute-start.2 = (f32[3,32,128]{2,1,0:T(8,128)S(1)}, f32[3,32,128]{2,1,0:T(8,128)S(1)}, u32[]{:S(2)}, u32[]{:S(2)}) collective-permute-start(f32[3,32,128]{2,1,0:T(8,128)S(1)} %get-tuple-element.26), channel_id=1, source_target_pairs={{0,8},{8,16},{16,24},{24,0},{1,9},{9,17},{17,25},{25,1},{2,10},{10... | collective-permute-start | bytes 147464 | tf_op jit(solution)/shard_map/ppermute | solution.py:588
  8.9 2.1 %collective-permute-start.3 = (f32[3,32,128]{2,1,0:T(8,128)S(1)}, f32[3,32,128]{2,1,0:T(8,128)S(1)}, u32[]{:S(2)}, u32[]{:S(2)}) collective-permute-start(f32[3,32,128]{2,1,0:T(8,128)S(1)} %get-tuple-element.27), channel_id=1, source_target_pairs={{0,24},{8,0},{16,8},{24,16},{1,25},{9,1},{17,9},{25,17},{2,26},{10... | collective-permute-start | bytes 147464 | tf_op jit(solution)/shard_map/ppermute | solution.py:588
  11.0 0.0 collective-permute-done.5.zhi
  11.0 2.0 %collective-permute-start.4 = (f32[2,32,128]{2,1,0:T(8,128)S(1)}, f32[2,32,128]{2,1,0:T(8,128)S(1)}, u32[]{:S(2)}, u32[]{:S(2)}) collective-permute-start(f32[2,32,128]{2,1,0:T(8,128)S(1)} %get-tuple-element.28), channel_id=1, source_target_pairs={{0,1},{1,2},{2,3},{3,4},{4,5},{5,6},{6,7},{7,0},{8,9},{9,10},{10,1... | collective-permute-start | bytes 98312 | tf_op jit(solution)/shard_map/ppermute | solution.py:588
  12.9 1.7 %collective-permute-done.4.zlo = f32[2,32,128]{2,1,0:T(8,128)S(1)} collective-permute-done((f32[2,32,128]{2,1,0:T(8,128)S(1)}, f32[2,32,128]{2,1,0:T(8,128)S(1)}, u32[]{:S(2)}, u32[]{:S(2)}) %collective-permute-start.4) | collective-permute-done | bytes 32800 | tf_op jit(solution)/shard_map/ppermute | solution.py:588
  14.7 0.0 collective-permute-done.xlo
  14.7 0.0 collective-permute-done.1.xhi
  14.7 0.0 collective-permute-done.2.ylo
  14.7 0.0 collective-permute-done.3.yhi
  14.7 0.0 copy-done.3
  14.7 5.6 %residual.1 = (f32[34,48,128]{2,1,0:T(8,128)S(1)}, f32[32,128]{1,0:T(8,128)S(1)}, f32[32,32,128]{2,1,0:T(8,128)S(1)}, f32[32,32,128]{2,1,0:T(8,128)S(1)}, f32[8,...) custom-call(f32[32,32,128]{2,1,0:T(8,128)S(1)} %copy-done.2, ...), custom_call_target="tpu_custom_call" | custom-call | tf_op jit(solution)/shard_map/residual/pallas_call | solution.py:599
  20.3 7.2 %all-to-all-start = ((f32[8,120,128]{2,1,0:T(8,128)}), f32[8,120,128]{2,1,0:T(8,128)S(1)}, u32[]{:S(2)}, u32[]{:S(2)}) async-start(f32[8,120,128]{2,1,0:T(8,128)} %get-tuple-element.29), calls=%async_computation | async-start | bytes 983040 | tf_op jit(solution)/shard_map/all_to_all | solution.py:613
  27.6 0.1 pad_add_fusion.place
  27.6 9.1 %all-to-all-done.lines = f32[8,120,128]{2,1,0:T(8,128)S(1)} async-done(((f32[8,120,128]{2,1,0:T(8,128)}), f32[8,120,128]{2,1,0:T(8,128)S(1)}, u32[]{:S(2)}, u32[]{:S(2)}) %all-to-all-start) | async-done | bytes 491552 | tf_op jit(solution)/shard_map/all_to_all | solution.py:613
  36.7 0.9 %window.1 = (f32[16,168,128]{2,1,0:T(8,128)S(1)}, f32[32,128]{1,0:T(8,128)S(1)}, f32[16,128]{1,0:T(8,128)S(1)}) custom-call(s32[3]{0:T(128)S(1)} %pad_add_fusion.place, f32[8,120,128]{2,1,0:T(8,128)S(1)} %all-to-all-done.lines, f32[4,32,128]{2,1,0:T(8,128)S(1)} %get-tuple-element.30.sides, f32[4,16,128]{2,1,0:T(8,128)S(1)} %get-tuple-element.31.sides2), custom_call_target="tpu_custom_call" | custom-call | tf_op jit(solution)/shard_map/window/pallas_call | solution.py:614
  37.6 0.0 copy-start.1
  37.7 23.8 %all_to_all.10.columns = f32[16,168,128]{2,1,0:T(8,128)S(1)} all-to-all(f32[16,168,128]{2,1,0:T(8,128)S(1)} %get-tuple-element.32), channel_id=1, replica_groups=mesh['gx'=4,'gy'=4,'gz'=8] {'gx','gy'}, dimensions={0} | all-to-all | bytes 2752512 | tf_op jit(solution)/shard_map/all_to_all | solution.py:621
  61.4 18.7 %cycle.1 = f32[32,32,128]{2,1,0:T(8,128)} custom-call(s32[3]{0:T(128)S(1)} %pad_add_fusion.place, f32[16,168,128]{2,1,0:T(8,128)S(1)} %all_to_all.10.columns, f32[32,32,128]{2,1,0:T(8,128)S(1)} %copy-done.1, f32[34,48,128]{2,1,0:T(8,128)S(1)} %get-tuple-element.33.kp, f32[32,128]{1,0:T(8,128)S(1)} %get-tuple-element.34.ck, ...), custom_call_target="tpu_custom_call" | custom-call | tf_op jit(solution)/shard_map/cycle/pallas_call | solution.py:624
  (6 shorter events, 0.0 us)
Async XLA Ops:
  0.0 1.0 %copy-start = (f32[32,32,128]{2,1,0:T(8,128)S(1)}, f32[32,32,128]{2,1,0:T(8,128)}, u32[]{:S(2)}) copy-start(f32[32,32,128]{2,1,0:T(8,128)} %initial.5) | copy-start | bytes 1572868
  1.0 1.0 %copy-start.2 = (f32[32,32,128]{2,1,0:T(8,128)S(1)}, f32[32,32,128]{2,1,0:T(8,128)}, u32[]{:S(2)}) copy-start(f32[32,32,128]{2,1,0:T(8,128)} %kappa.3) | copy-start | bytes 1572868
  2.1 12.6 %copy-start.3 = (f32[32,32,128]{2,1,0:T(8,128)S(1)}, f32[32,32,128]{2,1,0:T(8,128)}, u32[]{:S(2)}) copy-start(f32[32,32,128]{2,1,0:T(8,128)} %rhs.1) | copy-start | bytes 1572868
  2.1 12.6 %copy-start.4 = (f32[32,32,128]{2,1,0:T(8,128)S(1)}, f32[32,32,128]{2,1,0:T(8,128)}, u32[]{:S(2)}) copy-start(f32[32,32,128]{2,1,0:T(8,128)} %sigma.1) | copy-start | bytes 1572868
  3.0 8.0 %collective-permute-start.5 = (f32[2,32,128]{2,1,0:T(8,128)S(1)}, f32[2,32,128]{2,1,0:T(8,128)S(1)}, u32[]{:S(2)}, u32[]{:S(2)}) collective-permute-start(f32[2,32,128]{2,1,0:T(8,128)S(1)} %get-tuple-element.28), channel_id=1, source_target_pairs={{0,7},{1,0},{2,1},{3,2},{4,3},{5,4},{6,5},{7,6},{8,15},{9,8},{10,9... | collective-permute-start | bytes 98312 | tf_op jit(solution)/shard_map/ppermute | solution.py:588
  4.4 10.3 %collective-permute-start = (f32[3,32,128]{2,1,0:T(8,128)S(1)}, f32[3,32,128]{2,1,0:T(8,128)S(1)}, u32[]{:S(2)}, u32[]{:S(2)}) collective-permute-start(f32[3,32,128]{2,1,0:T(8,128)S(1)} %get-tuple-element.24), channel_id=1, source_target_pairs={{0,32},{32,64},{64,96},{96,0},{1,33},{33,65},{65,97},{97,1},{2,34}... | collective-permute-start | bytes 147464 | tf_op jit(solution)/shard_map/ppermute | solution.py:588
  5.8 8.9 %collective-permute-start.1 = (f32[3,32,128]{2,1,0:T(8,128)S(1)}, f32[3,32,128]{2,1,0:T(8,128)S(1)}, u32[]{:S(2)}, u32[]{:S(2)}) collective-permute-start(f32[3,32,128]{2,1,0:T(8,128)S(1)} %get-tuple-element.25), channel_id=1, source_target_pairs={{0,96},{32,0},{64,32},{96,64},{1,97},{33,1},{65,33},{97,65},{2,98}... | collective-permute-start | bytes 147464 | tf_op jit(solution)/shard_map/ppermute | solution.py:588
  7.2 7.5 %collective-permute-start.2 = (f32[3,32,128]{2,1,0:T(8,128)S(1)}, f32[3,32,128]{2,1,0:T(8,128)S(1)}, u32[]{:S(2)}, u32[]{:S(2)}) collective-permute-start(f32[3,32,128]{2,1,0:T(8,128)S(1)} %get-tuple-element.26), channel_id=1, source_target_pairs={{0,8},{8,16},{16,24},{24,0},{1,9},{9,17},{17,25},{25,1},{2,10},{10... | collective-permute-start | bytes 147464 | tf_op jit(solution)/shard_map/ppermute | solution.py:588
  8.9 5.8 %collective-permute-start.3 = (f32[3,32,128]{2,1,0:T(8,128)S(1)}, f32[3,32,128]{2,1,0:T(8,128)S(1)}, u32[]{:S(2)}, u32[]{:S(2)}) collective-permute-start(f32[3,32,128]{2,1,0:T(8,128)S(1)} %get-tuple-element.27), channel_id=1, source_target_pairs={{0,24},{8,0},{16,8},{24,16},{1,25},{9,1},{17,9},{25,17},{2,26},{10... | collective-permute-start | bytes 147464 | tf_op jit(solution)/shard_map/ppermute | solution.py:588
  11.0 3.7 %collective-permute-start.4 = (f32[2,32,128]{2,1,0:T(8,128)S(1)}, f32[2,32,128]{2,1,0:T(8,128)S(1)}, u32[]{:S(2)}, u32[]{:S(2)}) collective-permute-start(f32[2,32,128]{2,1,0:T(8,128)S(1)} %get-tuple-element.28), channel_id=1, source_target_pairs={{0,1},{1,2},{2,3},{3,4},{4,5},{5,6},{6,7},{7,0},{8,9},{9,10},{10,1... | collective-permute-start | bytes 98312 | tf_op jit(solution)/shard_map/ppermute | solution.py:588
  20.3 16.4 %all-to-all-start = ((f32[8,120,128]{2,1,0:T(8,128)}), f32[8,120,128]{2,1,0:T(8,128)S(1)}, u32[]{:S(2)}, u32[]{:S(2)}) async-start(f32[8,120,128]{2,1,0:T(8,128)} %get-tuple-element.29), calls=%async_computation | async-start | bytes 983040 | tf_op jit(solution)/shard_map/all_to_all | solution.py:613
  37.6 23.8 %copy-start.1 = (f32[32,32,128]{2,1,0:T(8,128)S(1)}, f32[32,32,128]{2,1,0:T(8,128)}, u32[]{:S(2)}) copy-start(f32[32,32,128]{2,1,0:T(8,128)} %initial.5) | copy-start | bytes 1572868

commit v2 on v1

--- a/solution.py
+++ b/solution.py
@@ -150,7 +150,7 @@
         pair_s[i] = s0 + s1
         return packed
 
-    packed = lax.fori_loop(0, 16, two, jnp.zeros((32, LANES), F32))
+    packed = lax.fori_loop(0, 16, two, jnp.zeros((32, LANES), F32), unroll=2)
     sides[0] = first[31]
     sides[1] = first[0]
     sides[2] = first[:, 31, :]
@@ -377,7 +377,7 @@
         ea[x, mid] = g
         return carry
 
-    lax.fori_loop(1, 23, setup3, 0)
+    lax.fori_loop(1, 23, setup3, 0, unroll=True)
 
     for qx in range(4):
         for qy in range(4):
@@ -445,7 +445,7 @@
             target[x, mid] = total
             return carry
 
-        lax.fori_loop(step, 24 - step, sweep3, 0)
+        lax.fori_loop(step, 24 - step, sweep3, 0, unroll=True)
         source, target = target, source
 
     lane16 = lanes_of((16, LANES))
@@ -557,7 +557,7 @@
         out[x] = initial[x] + (1.2 * e + 0.5 * scale[x] * total + up[x // 2])
         return carry
 
-    lax.fori_loop(0, 32, slab, 0)
+    lax.fori_loop(0, 32, slab, 0, unroll=4)
 
 
 VM = pl.BlockSpec(memory_space=pltpu.VMEM)

time: 81.1 us -> 67.4 us (0.83)
  Pallas kernels: 26.1 us -> 12.4 us
    pallas_call x1, Pallas kernels: 18.7 us -> 6.63 us  [on_device(): local(cycle_kernel, [shape(*block)], [SM] + [VM] * 12, [(34, 48, LANES),...]
    pallas_call x1, Pallas kernels: 5.61 us -> 4.02 us  [on_device(): local(residual_kernel, [shape(34, 48, LANES), shape(32, LANES), shape(*bl...]
where the time goes in v2:
time: 67.4 us; the launch traced here: 66.5 us
  blocking collectives  23.8 us (35%)
  starting transfers between devices  17.2 us (26%)
  Pallas kernels  12.4 us (18%)
  waiting for transfers between devices  10.8 us (16%)
  local copies, waits for them, and re-layouts  2.1 us (3%)
    all_to_all x1, blocking collectives, on_device(): columns = lax.all_to_all(windows, ('gx', 'gy'), 0, 0)  23.8 us
    ppermute x6, starting transfers between devices, passed(): lax.ppermute(value, axis, [(i, (i + step) % count) for i in range(count)])  9.97 us
    all_to_all x1, waiting for transfers between devices, on_device(): lines = lax.all_to_all(message, 'gz', 0, 0)  9.07 us
    all_to_all x1, starting transfers between devices, on_device(): lines = lax.all_to_all(message, 'gz', 0, 0)  7.23 us
    pallas_call x1, Pallas kernels, on_device(): local(cycle_kernel, [shape(*block)], [SM] + [VM] * 12, [(34, 48, LANES),...  6.63 us
    pallas_call x1, Pallas kernels, on_device(): local(residual_kernel, [shape(34, 48, LANES), shape(32, LANES), shape(*bl...  4.02 us
    unnamed x10, local copies, waits for them, and re-layouts  2.1 us
    ppermute x6, waiting for transfers between devices, passed(): lax.ppermute(value, axis, [(i, (i + step) % count) for i in range(count)])  1.73 us
  transfers between devices with their start and end apart: 7, of which 2 were waited for; matrix products, arithmetic and copies ran while one was open for 0% of the time, Pallas kernels for 0%

profile of v2, /device:TPU:1, one launch (start us, length us, event | category | flops | bytes accessed | tf_op | source)
XLA Modules:
  0.0 66.5 jit_solution(10767296904071548390)
XLA Ops:
  0.0 1.0 %copy-done = f32[32,32,128]{2,1,0:T(8,128)S(1)} copy-done((f32[32,32,128]{2,1,0:T(8,128)S(1)}, f32[32,32,128]{2,1,0:T(8,128)}, u32[]{:S(2)}) %copy-start) | copy-done | bytes 524312
  1.0 1.0 %copy-done.2 = f32[32,32,128]{2,1,0:T(8,128)S(1)} copy-done((f32[32,32,128]{2,1,0:T(8,128)S(1)}, f32[32,32,128]{2,1,0:T(8,128)}, u32[]{:S(2)}) %copy-start.2) | copy-done | bytes 524312
  2.1 0.9 %faces.1 = (f32[3,32,128]{2,1,0:T(8,128)S(1)}, f32[3,32,128]{2,1,0:T(8,128)S(1)}, f32[3,32,128]{2,1,0:T(8,128)S(1)}, f32[3,32,128]{2,1,0:T(8,128)S(1)}, f32[2,32,128]{2,1,0:T(8,128)S(1)}) custom-call(f32[32,32,128]{2,1,0:T(8,128)S(1)} %copy-done.2, f32[32,32,128]{2,1,0:T(8,128)S(1)} %copy-done), custom_call_target="tpu_custom_call" | custom-call | tf_op jit(solution)/shard_map/faces/pallas_call | solution.py:591
  3.0 1.4 %collective-permute-start.5 = (f32[2,32,128]{2,1,0:T(8,128)S(1)}, f32[2,32,128]{2,1,0:T(8,128)S(1)}, u32[]{:S(2)}, u32[]{:S(2)}) collective-permute-start(f32[2,32,128]{2,1,0:T(8,128)S(1)} %get-tuple-element.28), channel_id=1, source_target_pairs={{0,7},{1,0},{2,1},{3,2},{4,3},{5,4},{6,5},{7,6},{8,15},{9,8},{10,9... | collective-permute-start | bytes 98312 | tf_op jit(solution)/shard_map/ppermute | solution.py:588
  4.4 1.4 %collective-permute-start = (f32[3,32,128]{2,1,0:T(8,128)S(1)}, f32[3,32,128]{2,1,0:T(8,128)S(1)}, u32[]{:S(2)}, u32[]{:S(2)}) collective-permute-start(f32[3,32,128]{2,1,0:T(8,128)S(1)} %get-tuple-element.24), channel_id=1, source_target_pairs={{0,32},{32,64},{64,96},{96,0},{1,33},{33,65},{65,97},{97,1},{2,34}... | collective-permute-start | bytes 147464 | tf_op jit(solution)/shard_map/ppermute | solution.py:588
  5.8 1.4 %collective-permute-start.1 = (f32[3,32,128]{2,1,0:T(8,128)S(1)}, f32[3,32,128]{2,1,0:T(8,128)S(1)}, u32[]{:S(2)}, u32[]{:S(2)}) collective-permute-start(f32[3,32,128]{2,1,0:T(8,128)S(1)} %get-tuple-element.25), channel_id=1, source_target_pairs={{0,96},{32,0},{64,32},{96,64},{1,97},{33,1},{65,33},{97,65},{2,98}... | collective-permute-start | bytes 147464 | tf_op jit(solution)/shard_map/ppermute | solution.py:588
  7.2 1.6 %collective-permute-start.2 = (f32[3,32,128]{2,1,0:T(8,128)S(1)}, f32[3,32,128]{2,1,0:T(8,128)S(1)}, u32[]{:S(2)}, u32[]{:S(2)}) collective-permute-start(f32[3,32,128]{2,1,0:T(8,128)S(1)} %get-tuple-element.26), channel_id=1, source_target_pairs={{0,8},{8,16},{16,24},{24,0},{1,9},{9,17},{17,25},{25,1},{2,10},{10... | collective-permute-start | bytes 147464 | tf_op jit(solution)/shard_map/ppermute | solution.py:588
  8.9 2.1 %collective-permute-start.3 = (f32[3,32,128]{2,1,0:T(8,128)S(1)}, f32[3,32,128]{2,1,0:T(8,128)S(1)}, u32[]{:S(2)}, u32[]{:S(2)}) collective-permute-start(f32[3,32,128]{2,1,0:T(8,128)S(1)} %get-tuple-element.27), channel_id=1, source_target_pairs={{0,24},{8,0},{16,8},{24,16},{1,25},{9,1},{17,9},{25,17},{2,26},{10... | collective-permute-start | bytes 147464 | tf_op jit(solution)/shard_map/ppermute | solution.py:588
  11.0 0.0 collective-permute-done.5.zhi
  11.0 2.0 %collective-permute-start.4 = (f32[2,32,128]{2,1,0:T(8,128)S(1)}, f32[2,32,128]{2,1,0:T(8,128)S(1)}, u32[]{:S(2)}, u32[]{:S(2)}) collective-permute-start(f32[2,32,128]{2,1,0:T(8,128)S(1)} %get-tuple-element.28), channel_id=1, source_target_pairs={{0,1},{1,2},{2,3},{3,4},{4,5},{5,6},{6,7},{7,0},{8,9},{9,10},{10,1... | collective-permute-start | bytes 98312 | tf_op jit(solution)/shard_map/ppermute | solution.py:588
  12.9 1.7 %collective-permute-done.4.zlo = f32[2,32,128]{2,1,0:T(8,128)S(1)} collective-permute-done((f32[2,32,128]{2,1,0:T(8,128)S(1)}, f32[2,32,128]{2,1,0:T(8,128)S(1)}, u32[]{:S(2)}, u32[]{:S(2)}) %collective-permute-start.4) | collective-permute-done | bytes 32800 | tf_op jit(solution)/shard_map/ppermute | solution.py:588
  14.7 0.0 collective-permute-done.xlo
  14.7 0.0 collective-permute-done.1.xhi
  14.7 0.0 collective-permute-done.2.ylo
  14.7 0.0 collective-permute-done.3.yhi
  14.7 0.0 copy-done.3
  14.7 4.0 %residual.1 = (f32[34,48,128]{2,1,0:T(8,128)S(1)}, f32[32,128]{1,0:T(8,128)S(1)}, f32[32,32,128]{2,1,0:T(8,128)S(1)}, f32[32,32,128]{2,1,0:T(8,128)S(1)}, f32[8,...) custom-call(f32[32,32,128]{2,1,0:T(8,128)S(1)} %copy-done.2, ...), custom_call_target="tpu_custom_call" | custom-call | tf_op jit(solution)/shard_map/residual/pallas_call | solution.py:599
  18.7 7.2 %all-to-all-start = ((f32[8,120,128]{2,1,0:T(8,128)}), f32[8,120,128]{2,1,0:T(8,128)S(1)}, u32[]{:S(2)}, u32[]{:S(2)}) async-start(f32[8,120,128]{2,1,0:T(8,128)} %get-tuple-element.29), calls=%async_computation | async-start | bytes 983040 | tf_op jit(solution)/shard_map/all_to_all | solution.py:613
  26.0 0.1 pad_add_fusion.place
  26.0 9.1 %all-to-all-done.lines = f32[8,120,128]{2,1,0:T(8,128)S(1)} async-done(((f32[8,120,128]{2,1,0:T(8,128)}), f32[8,120,128]{2,1,0:T(8,128)S(1)}, u32[]{:S(2)}, u32[]{:S(2)}) %all-to-all-start) | async-done | bytes 491552 | tf_op jit(solution)/shard_map/all_to_all | solution.py:613
  35.1 0.9 %window.1 = (f32[16,168,128]{2,1,0:T(8,128)S(1)}, f32[32,128]{1,0:T(8,128)S(1)}, f32[16,128]{1,0:T(8,128)S(1)}) custom-call(s32[3]{0:T(128)S(1)} %pad_add_fusion.place, f32[8,120,128]{2,1,0:T(8,128)S(1)} %all-to-all-done.lines, f32[4,32,128]{2,1,0:T(8,128)S(1)} %get-tuple-element.30.sides, f32[4,16,128]{2,1,0:T(8,128)S(1)} %get-tuple-element.31.sides2), custom_call_target="tpu_custom_call" | custom-call | tf_op jit(solution)/shard_map/window/pallas_call | solution.py:614
  36.1 0.0 copy-start.1
  36.1 23.8 %all_to_all.10.columns = f32[16,168,128]{2,1,0:T(8,128)S(1)} all-to-all(f32[16,168,128]{2,1,0:T(8,128)S(1)} %get-tuple-element.32), channel_id=1, replica_groups=mesh['gx'=4,'gy'=4,'gz'=8] {'gx','gy'}, dimensions={0} | all-to-all | bytes 2752512 | tf_op jit(solution)/shard_map/all_to_all | solution.py:621
  59.8 6.6 %cycle.1 = f32[32,32,128]{2,1,0:T(8,128)} custom-call(s32[3]{0:T(128)S(1)} %pad_add_fusion.place, f32[16,168,128]{2,1,0:T(8,128)S(1)} %all_to_all.10.columns, f32[32,32,128]{2,1,0:T(8,128)S(1)} %copy-done.1, f32[34,48,128]{2,1,0:T(8,128)S(1)} %get-tuple-element.33.kp, f32[32,128]{1,0:T(8,128)S(1)} %get-tuple-element.34.ck, ...), custom_call_target="tpu_custom_call" | custom-call | tf_op jit(solution)/shard_map/cycle/pallas_call | solution.py:624
  (6 shorter events, 0.0 us)
Async XLA Ops:
  0.0 1.0 %copy-start = (f32[32,32,128]{2,1,0:T(8,128)S(1)}, f32[32,32,128]{2,1,0:T(8,128)}, u32[]{:S(2)}) copy-start(f32[32,32,128]{2,1,0:T(8,128)} %initial.5) | copy-start | bytes 1572868
  1.0 1.0 %copy-start.2 = (f32[32,32,128]{2,1,0:T(8,128)S(1)}, f32[32,32,128]{2,1,0:T(8,128)}, u32[]{:S(2)}) copy-start(f32[32,32,128]{2,1,0:T(8,128)} %kappa.3) | copy-start | bytes 1572868
  2.1 12.6 %copy-start.3 = (f32[32,32,128]{2,1,0:T(8,128)S(1)}, f32[32,32,128]{2,1,0:T(8,128)}, u32[]{:S(2)}) copy-start(f32[32,32,128]{2,1,0:T(8,128)} %rhs.1) | copy-start | bytes 1572868
  2.1 12.6 %copy-start.4 = (f32[32,32,128]{2,1,0:T(8,128)S(1)}, f32[32,32,128]{2,1,0:T(8,128)}, u32[]{:S(2)}) copy-start(f32[32,32,128]{2,1,0:T(8,128)} %sigma.1) | copy-start | bytes 1572868
  3.0 8.0 %collective-permute-start.5 = (f32[2,32,128]{2,1,0:T(8,128)S(1)}, f32[2,32,128]{2,1,0:T(8,128)S(1)}, u32[]{:S(2)}, u32[]{:S(2)}) collective-permute-start(f32[2,32,128]{2,1,0:T(8,128)S(1)} %get-tuple-element.28), channel_id=1, source_target_pairs={{0,7},{1,0},{2,1},{3,2},{4,3},{5,4},{6,5},{7,6},{8,15},{9,8},{10,9... | collective-permute-start | bytes 98312 | tf_op jit(solution)/shard_map/ppermute | solution.py:588
  4.4 10.3 %collective-permute-start = (f32[3,32,128]{2,1,0:T(8,128)S(1)}, f32[3,32,128]{2,1,0:T(8,128)S(1)}, u32[]{:S(2)}, u32[]{:S(2)}) collective-permute-start(f32[3,32,128]{2,1,0:T(8,128)S(1)} %get-tuple-element.24), channel_id=1, source_target_pairs={{0,32},{32,64},{64,96},{96,0},{1,33},{33,65},{65,97},{97,1},{2,34}... | collective-permute-start | bytes 147464 | tf_op jit(solution)/shard_map/ppermute | solution.py:588
  5.8 8.9 %collective-permute-start.1 = (f32[3,32,128]{2,1,0:T(8,128)S(1)}, f32[3,32,128]{2,1,0:T(8,128)S(1)}, u32[]{:S(2)}, u32[]{:S(2)}) collective-permute-start(f32[3,32,128]{2,1,0:T(8,128)S(1)} %get-tuple-element.25), channel_id=1, source_target_pairs={{0,96},{32,0},{64,32},{96,64},{1,97},{33,1},{65,33},{97,65},{2,98}... | collective-permute-start | bytes 147464 | tf_op jit(solution)/shard_map/ppermute | solution.py:588
  7.2 7.5 %collective-permute-start.2 = (f32[3,32,128]{2,1,0:T(8,128)S(1)}, f32[3,32,128]{2,1,0:T(8,128)S(1)}, u32[]{:S(2)}, u32[]{:S(2)}) collective-permute-start(f32[3,32,128]{2,1,0:T(8,128)S(1)} %get-tuple-element.26), channel_id=1, source_target_pairs={{0,8},{8,16},{16,24},{24,0},{1,9},{9,17},{17,25},{25,1},{2,10},{10... | collective-permute-start | bytes 147464 | tf_op jit(solution)/shard_map/ppermute | solution.py:588
  8.9 5.8 %collective-permute-start.3 = (f32[3,32,128]{2,1,0:T(8,128)S(1)}, f32[3,32,128]{2,1,0:T(8,128)S(1)}, u32[]{:S(2)}, u32[]{:S(2)}) collective-permute-start(f32[3,32,128]{2,1,0:T(8,128)S(1)} %get-tuple-element.27), channel_id=1, source_target_pairs={{0,24},{8,0},{16,8},{24,16},{1,25},{9,1},{17,9},{25,17},{2,26},{10... | collective-permute-start | bytes 147464 | tf_op jit(solution)/shard_map/ppermute | solution.py:588
  11.0 3.7 %collective-permute-start.4 = (f32[2,32,128]{2,1,0:T(8,128)S(1)}, f32[2,32,128]{2,1,0:T(8,128)S(1)}, u32[]{:S(2)}, u32[]{:S(2)}) collective-permute-start(f32[2,32,128]{2,1,0:T(8,128)S(1)} %get-tuple-element.28), channel_id=1, source_target_pairs={{0,1},{1,2},{2,3},{3,4},{4,5},{5,6},{6,7},{7,0},{8,9},{9,10},{10,1... | collective-permute-start | bytes 98312 | tf_op jit(solution)/shard_map/ppermute | solution.py:588
  18.7 16.4 %all-to-all-start = ((f32[8,120,128]{2,1,0:T(8,128)}), f32[8,120,128]{2,1,0:T(8,128)S(1)}, u32[]{:S(2)}, u32[]{:S(2)}) async-start(f32[8,120,128]{2,1,0:T(8,128)} %get-tuple-element.29), calls=%async_computation | async-start | bytes 983040 | tf_op jit(solution)/shard_map/all_to_all | solution.py:613
  36.1 23.8 %copy-start.1 = (f32[32,32,128]{2,1,0:T(8,128)S(1)}, f32[32,32,128]{2,1,0:T(8,128)}, u32[]{:S(2)}) copy-start(f32[32,32,128]{2,1,0:T(8,128)} %initial.5) | copy-start | bytes 1572868

commit v3 on v2

--- a/solution.py
+++ b/solution.py
@@ -11,8 +11,9 @@
 F32 = jnp.float32
 BF16 = jnp.bfloat16
 
-Z_FINE, Z_SEC, Z_ROWS = 72, 104, 120
-W_SHIFT, W_FOUR, W_FIVE, W_SEC, W_ROWS = 64, 128, 144, 152, 168
+Z_SMALL, Z_ROWS = 32, 40
+W_FACE, W_FOUR, W_SEC, W_FIVE, W_ROWS = 64, 96, 112, 120, 128
+BASE = 5
 
 
 def turn(value, shift, axis):
@@ -90,8 +91,8 @@
 
 
 def residual_kernel(
-    kappa, initial, rhs, sigma, xlo, xhi, ylo, yhi, zlo, zhi,
-    kp, ck, scale, first, message, sides, kp2, ck2, scale2, first2, sides2,
+    place, kappa, initial, rhs, sigma, xlo, xhi, ylo, yhi, zlo, zhi,
+    kp, ck, scale, first, message, whole, sides, kp2, ck2, scale2, first2, sides2,
     vp, pair_r, pair_k, pair_s, rims, small,
 ):
     lane = lanes_of((32, LANES))
@@ -229,80 +230,117 @@
     five = spread(small[2, 0:8], square(lambda row, col: (row < 96) & (row // 4 == col)))
     lane8 = lanes_of((8, LANES))
     five = five * jnp.where((lane8 >= 8) & (lane8 < 16), 1.0 / 64.0, 0.25)
+    whole[...] = three
+    five = turn(jnp.where(lane8 < 24, five, 0.0), 64, 1)
+    blank = jnp.zeros((32, LANES), F32)
     for p in range(8):
-        message[p, 0:64] = three
-        message[p, 64:72] = five
-        message[p, Z_FINE:Z_SEC] = packed
-        message[p, Z_SEC:Z_ROWS] = packed2
-
-
-def window_kernel(place, lines, sides, sides2, out, cf, cf2, small):
+        message[p, 0:Z_SMALL] = blank
+        message[p, Z_SMALL:Z_ROWS] = five
+    gz = place[2]
+    for step, start, tag in ((1, 16, 1), (7, 0, 2)):
+        p = lax.rem(gz + step, 8)
+        half = spread(
+            three,
+            square(
+                lambda row, col, start=start: (col < 48)
+                & (row == 32 * (col // 16) + start + col % 16)
+            ),
+        )
+        face = spread(packed, square(lambda row, col, tag=tag: row == 4 * (col - 96) + tag))
+        message[p, 0:Z_SMALL] = half[0:32] + turn(half[32:64], 48, 1) + face
+        face2 = spread(
+            packed2, square(lambda row, col, tag=tag: (col < 16) & (row == 4 * col + tag))
+        )
+        message[p, Z_SMALL:Z_ROWS] = face2[0:8] + turn(face2[8:16], 16, 1) + five
+
+
+def window_kernel(place, lines, whole, sides, sides2, out, own, cf, cf2, small):
     gx, gy, gz = place[0], place[1], place[2]
     before, after = lax.rem(gz + 7, 8), lax.rem(gz + 1, 8)
-    a, b, c = lines[before, 0:64], lines[gz, 0:64], lines[after, 0:64]
     lane = lanes_of((64, LANES))
-
-    def join(pieces):
-        total = pieces[-1][1]
-        for stop, piece in reversed(pieces[:-1]):
-            total = jnp.where(lane < stop, piece, total)
-        return total
-
-    both = join([
-        (16, turn(a, -16, 1)), (48, turn(b, 16, 1)), (64, turn(c, 48, 1)),
-        (80, turn(a, 16, 1)), (112, turn(b, 48, 1)), (128, turn(c, 80, 1)),
-    ])
-    shift = join([
-        (16, turn(a, -80, 1)), (48, turn(b, -48, 1)), (64, turn(c, -16, 1)),
-        (128, jnp.zeros((64, LANES), F32)),
-    ])
+    a_half, c_half = lines[before, 0:Z_SMALL], lines[after, 0:Z_SMALL]
+    a = jnp.concatenate([a_half, turn(a_half, -48, 1)], 0)
+    b = whole[...]
+    c = jnp.concatenate([c_half, turn(c_half, -48, 1)], 0)
+
+    def window(part):
+        low = turn(a, BASE - 16 - 16 * part, 1)
+        mid = turn(b, BASE - 32 * part, 1)
+        high = turn(c, BASE + 32 - 16 * part, 1)
+        value = jnp.where((lane < BASE) | (lane >= 112 + BASE), low, mid)
+        value = jnp.where((lane >= BASE + 32) & (lane < BASE + 48), high, value)
+        return jnp.where((lane >= BASE + 48) & (lane < 112 + BASE), 0.0, value)
+
+    r, k, s = window(0), window(1), window(2)
+    own[0], own[1], own[2] = r, k, s
+    main = jnp.where(lane < 42, r, jnp.where(lane < 86, turn(k, 43, 1), turn(s, 86, 1)))
+    low = jnp.where(lane == 127, r, jnp.where(lane == 126, k, turn(s, -2, 1)))
+    high = jnp.where(lane == 42, r, jnp.where(lane == 43, k, turn(s, 2, 1)))
+    ends = jnp.where(lane >= 64, low, turn(high, 86, 1))
 
     even, odd = pl.ds(0, 4, stride=2), pl.ds(1, 4, stride=2)
 
-    def shrink(field):
+    def shrink(field, part, weight):
         halves = field.reshape(4, 2, 8, LANES)
         small[0:4] = halves[:, 0] + halves[:, 1]
         summed = small[0:4, even, :] + small[0:4, odd, :]
         for i in range(4):
             small[4 + i // 2, 4 * (i % 2) : 4 * (i % 2) + 4] = summed[i]
-        return flat(small[4:6])
-
-    lane4 = lanes_of((16, LANES))
-    four = spread(shrink(both), square(lambda row, col: row // 2 == col))
-    four = four * jnp.where(lane4 < 32, 0.5, 0.125)
-    four = four + 0.5 * spread(
-        shrink(shift), square(lambda row, col: (row < 64) & (row // 2 + 64 == col))
-    )
-
+
+        def rule(row, col):
+            cell = (row + 16 - BASE) % LANES
+            return (cell < 64) & (cell // 2 == col - 32 * part)
+
+        return spread(flat(small[4:6]), square(rule)) * weight
+
+    four = shrink(r, 0, 0.5) + shrink(k, 1, 0.125) + shrink(s, 2, 0.5)
     lane8 = lanes_of((8, LANES))
+    for i in range(8):
+        start = 96 + 6 * (i % 4)
+        moved = turn(ends[8 * i : 8 * i + 8], start - 125, 1)
+        kept = jnp.where((lane8 >= start) & (lane8 < start + 6), moved, 0.0)
+        extra = kept if i % 4 == 0 else extra + kept
+        if i % 4 == 3:
+            small[i // 4] = extra
+    four = four + flat(small[0:2])
+
     row8 = lax.broadcasted_iota(jnp.int32, (8, LANES), 0)
     five = jnp.zeros((8, LANES), F32)
     five_shift = jnp.zeros((8, LANES), F32)
     for p in range(8):
-        piece = lines[p, 64:72]
-        five = jnp.where(lane8 // 8 == p, turn(piece, 8 * p, 1), five)
-        five = jnp.where(lane8 // 8 == p + 8, turn(piece, 56 + 8 * p, 1), five)
-        five_shift = jnp.where(lane8 // 8 == p, turn(piece, 8 * p - 16, 1), five_shift)
+        piece = lines[p, Z_SMALL:Z_ROWS]
+        five = jnp.where(lane8 // 8 == p, turn(piece, 8 * p - 64, 1), five)
+        five = jnp.where(lane8 // 8 == p + 8, turn(piece, 8 * p - 8, 1), five)
+        five_shift = jnp.where(lane8 // 8 == p, turn(piece, 8 * p - 80, 1), five_shift)
     five = jnp.where(row8 < 4, five, turn(five_shift, 4, 0))
 
     for q in range(16):
-        out[q, 0:64] = both
-        out[q, W_SHIFT:W_FOUR] = shift
-        out[q, W_FOUR:W_FIVE] = four
-        out[q, W_FIVE:W_SEC] = five
-        out[q, W_SEC:W_ROWS] = jnp.zeros((16, LANES), F32)
-    lane32 = lanes_of((32, LANES))
+        out[q, 0:W_FACE] = main
+        out[q, W_FACE:W_FOUR] = jnp.zeros((32, LANES), F32)
+        out[q, W_FOUR:W_SEC] = four
+        out[q, W_SEC:W_FIVE] = jnp.zeros((8, LANES), F32)
+        out[q, W_FIVE:W_ROWS] = five
     for side, (dx, dy) in enumerate(((1, 0), (3, 0), (0, 1), (0, 3))):
         q = 4 * lax.rem(gx + dx, 4) + lax.rem(gy + dy, 4)
-        face = sides[side]
-        low = lane32 < 64
-        out[q, W_SHIFT : W_SHIFT + 32] = jnp.where(low, shift[0:32], turn(face, 64, 1))
-        out[q, W_SHIFT + 32 : W_FOUR] = jnp.where(low, shift[32:64], face)
-        out[q, W_SEC:W_ROWS] = sides2[side]
-    cf[...] = jnp.where(
-        lane32 % 4 < 2, lines[before, Z_FINE:Z_SEC], lines[after, Z_FINE:Z_SEC]
+        out[q, W_FACE:W_FOUR] = sides[side]
+        face2 = sides2[side]
+        out[q, W_SEC:W_FIVE] = jnp.where(lane8 < 64, face2[0:8], face2[8:16])
+
+    def rim(low, high, ready):
+        below = spread(low, square(lambda row, col: ready(row) & (col == 4 * (row % 32) + 1)))
+        above = spread(high, square(lambda row, col: ready(row) & (col == 4 * (row % 32) + 2)))
+        return below + above
+
+    cf[...] = rim(a_half, c_half, lambda row: row >= 96)
+
+    def unfold(half):
+        return jnp.concatenate([half, turn(half, -16, 1)], 0)
+
+    cf2[...] = rim(
+        unfold(lines[before, Z_SMALL:Z_ROWS]),
+        unfold(lines[after, Z_SMALL:Z_ROWS]),
+        lambda row: row < 16,
     )
-    cf2[...] = jnp.where(lane4 % 4 < 2, lines[before, Z_SEC:Z_ROWS], lines[after, Z_SEC:Z_ROWS])
 
 
 def wrapped(value):
@@ -337,25 +375,39 @@
 
 
 def cycle_kernel(
-    place, columns, initial, kp, ck, scale, first, cf, kp2, ck2, scale2, first2, cf2,
+    place, columns, own, initial, kp, ck, scale, first, cf, kp2, ck2, scale2, first2, cf2,
     out,
-    fp, fp2, rk3, s3, k3, c3, ea, eb, l4, l5, s5, l6, c4, c5, c6, c7, w4, w3, w2, up,
+    fp, fp2, r3, s3, k3, c3, ea, eb, l4, l5, s5, l6, c4, c5, c6, c7, w4, w3, w2, up,
 ):
     gx, gy, gz = place[0], place[1], place[2]
 
     def slot(dx, dy):
         return 4 * lax.rem(gx + dx, 4) + lax.rem(gy + dy, 4)
 
+    lane8 = lanes_of((8, LANES))
     for ix, dx in enumerate((3, 0, 1)):
         for iy, dy in enumerate((3, 0, 1)):
             q = slot(dx, dy)
             for i in range(8):
-                piece = columns[q, 8 * i : 8 * i + 8]
-                rk3[8 * ix + i, 8 * iy : 8 * iy + 8] = piece
-                s3[8 * ix + i, 8 * iy : 8 * iy + 8] = columns[
-                    q, W_SHIFT + 8 * i : W_SHIFT + 8 * i + 8
-                ]
-                k3[8 * ix + i, 8 + 8 * iy : 16 + 8 * iy] = turn(piece, 64, 1)
+                if dx == 0 and dy == 0:
+                    r, k, s = [own[f, 8 * i : 8 * i + 8] for f in range(3)]
+                else:
+                    r = columns[q, 8 * i : 8 * i + 8]
+                    k = turn(r, -43, 1)
+                    s = turn(r, -86, 1)
+                    beside = (dx == 3 and i == 7) or (dx == 1 and i == 0) or dx == 0
+                    if beside and (dx == 0 or dy == 0):
+                        base = W_FOUR + 8 * (i // 4)
+                        low = turn(columns[q, base : base + 8], 29 - 6 * (i % 4), 1)
+                        high = turn(low, 42, 1)
+                        r = jnp.where(lane8 == 127, low, jnp.where(lane8 == 42, high, r))
+                        k = jnp.where(lane8 == 126, low, jnp.where(lane8 == 43, high, k))
+                        low, high = turn(low, 2, 1), turn(high, -2, 1)
+                        s = jnp.where(lane8 == 127, low, jnp.where(lane8 == 42, high, s))
+                x, y = 8 * ix + i, 8 * iy
+                r3[x, y : y + 8] = r
+                k3[x, y + 8 : y + 16] = k
+                s3[x, y : y + 8] = s
     rim = jnp.zeros((24, 8, LANES), F32)
     for ref in (k3, ea, eb):
         ref[:, 0:8] = rim
@@ -372,7 +424,7 @@
         half = 0.5 * h
         for n in range(6):
             c3[n, x] = half * (k + near[n])
-        g = h * rk3[x]
+        g = h * r3[x]
         c3[6, x] = g
         ea[x, mid] = g
         return carry
@@ -449,7 +501,6 @@
         source, target = target, source
 
     lane16 = lanes_of((16, LANES))
-    lane8 = lanes_of((8, LANES))
     l6[...] = e6 + e7
     six = turn(l6[gx, pl.ds(gy, 1)] + jnp.zeros((8, LANES), F32), 128 - 4 * gz, 1)
     six = spread(six, square(lambda row, col: row == col // 32))
@@ -471,10 +522,10 @@
                 five[row : row + 1], (2, LANES)
             )
     four = four + w4[...]
-    own = source[8:16, 16:24]
+    mine = source[8:16, 16:24]
     lane3 = lanes_of((8, 8, LANES))
-    three = flat(jnp.where((lane3 >= 16) & (lane3 < 48), own, 0.0))
-    three = spread(three, square(lambda row, col: row == 16 + col // 4))
+    three = flat(jnp.where((lane3 >= BASE) & (lane3 < BASE + 32), mine, 0.0))
+    three = spread(three, square(lambda row, col: row == BASE + col // 4))
     for i in range(8):
         block = four[4 * (i // 2) : 4 * (i // 2) + 4]
         w3[i, pl.ds(0, 4, stride=2), :] = block
@@ -486,11 +537,19 @@
     lane32 = lanes_of((32, LANES))
     sides = [slot(3, 0), slot(1, 0), slot(0, 3), slot(0, 1)]
     fp2[1:17, inner2] = first2[...]
-    fp2[0, inner2] = columns[sides[0], W_SEC:W_ROWS]
-    fp2[17, inner2] = columns[sides[1], W_SEC:W_ROWS]
+
+    def face2_of(q):
+        half = columns[q, W_SEC:W_FIVE]
+        other = turn(half, 64, 1)
+        return [jnp.where(lane8 < 64, half, other), jnp.where(lane8 < 64, other, half)]
+
+    fp2[0, pl.ds(8, 8)], fp2[0, pl.ds(16, 8)] = face2_of(sides[0])
+    fp2[17, pl.ds(8, 8)], fp2[17, pl.ds(16, 8)] = face2_of(sides[1])
+    low2, high2 = face2_of(sides[2]), face2_of(sides[3])
     for x in range(16):
-        fp2[x + 1, 7:8] = columns[sides[2], W_SEC + x : W_SEC + x + 1]
-        fp2[x + 1, 24:25] = columns[sides[3], W_SEC + x : W_SEC + x + 1]
+        row = slice(x % 8, x % 8 + 1)
+        fp2[x + 1, 7:8] = low2[x // 8][row]
+        fp2[x + 1, 24:25] = high2[x // 8][row]
     rim_k2 = ck2[...]
     rim_f2 = cf2[...]
     for x in range(16):
@@ -520,20 +579,14 @@
 
     inner = pl.ds(8, 32)
 
-    def face_of(q):
-        low = columns[q, W_SHIFT : W_SHIFT + 32]
-        return jnp.where(lane32 < 64, turn(low, 64, 1), columns[q, W_SHIFT + 32 : W_FOUR])
-
-    fp[0, inner] = face_of(sides[0])
-    fp[33, inner] = face_of(sides[1])
-    w2[0:2] = face_of(sides[2]).reshape(2, 16, LANES)
-    w2[2:4] = face_of(sides[3]).reshape(2, 16, LANES)
+    fp[0, inner] = columns[sides[0], W_FACE:W_FOUR]
+    fp[33, inner] = columns[sides[1], W_FACE:W_FOUR]
 
     def fill(x, carry):
         fp[x + 1, inner] = first[x]
-        row = pl.ds(lax.rem(x, 16), 1)
-        fp[x + 1, 7:8] = w2[x // 16, row]
-        fp[x + 1, 40:41] = w2[2 + x // 16, row]
+        row = pl.ds(W_FACE + x, 1)
+        fp[x + 1, 7:8] = columns[sides[2], row]
+        fp[x + 1, 40:41] = columns[sides[3], row]
         return carry
 
     lax.fori_loop(0, 32, fill, 0, unroll=4)
@@ -596,35 +649,35 @@
     zlo, zhi = passed(zs, "gz", 1), passed(zs, "gz", -1)
     block = (32, 32, LANES)
     block2 = (16, 16, LANES)
-    kp, ck, scale, first, message, sides, kp2, ck2, scale2, first2, sides2 = local(
+    kp, ck, scale, first, message, whole, sides, kp2, ck2, scale2, first2, sides2 = local(
         residual_kernel,
         [
             shape(34, 48, LANES), shape(32, LANES), shape(*block), shape(*block),
-            shape(8, Z_ROWS, LANES), shape(4, 32, LANES), shape(18, 32, LANES),
+            shape(8, Z_ROWS, LANES), shape(64, LANES), shape(4, 32, LANES), shape(18, 32, LANES),
             shape(16, LANES), shape(*block2), shape(*block2), shape(4, 16, LANES),
         ],
-        [VM] * 10,
+        [SM] + [VM] * 10,
         [
             (34, 48, LANES), (16, 32, LANES), (16, 32, LANES), (16, 32, LANES),
             (4, 32, LANES), (8, 16, LANES),
         ],
         "residual",
-    )(kappa, initial, rhs, sigma, xlo, xhi, ylo, yhi, zlo, zhi)
+    )(place, kappa, initial, rhs, sigma, xlo, xhi, ylo, yhi, zlo, zhi)
     lines = lax.all_to_all(message, "gz", 0, 0)
-    windows, cf, cf2 = local(
+    windows, own, cf, cf2 = local(
         window_kernel,
-        [shape(16, W_ROWS, LANES), shape(32, LANES), shape(16, LANES)],
-        [SM] + [VM] * 3,
+        [shape(16, W_ROWS, LANES), shape(3, 64, LANES), shape(32, LANES), shape(16, LANES)],
+        [SM] + [VM] * 4,
         [(8, 8, LANES)],
         "window",
-    )(place, lines, sides, sides2)
+    )(place, lines, whole, sides, sides2)
     columns = lax.all_to_all(windows, ("gx", "gy"), 0, 0)
     padded3 = (24, 40, LANES)
     block3 = (24, 24, LANES)
     return local(
         cycle_kernel,
         [shape(*block)],
-        [SM] + [VM] * 12,
+        [SM] + [VM] * 13,
         [
             (34, 48, LANES), (18, 32, LANES), block3, block3, padded3, (7,) + block3,
             padded3, padded3, block2, (8, 8, LANES), (8, 8, LANES), (4, 8, LANES),
@@ -633,7 +686,7 @@
         ],
         "cycle",
     )(
-        place, columns, initial, kp, ck, scale, first, cf, kp2, ck2, scale2, first2, cf2
+        place, columns, own, initial, kp, ck, scale, first, cf, kp2, ck2, scale2, first2, cf2
     )[0]
 
 

time: 67.4 us -> 61.8 us (0.917)
  the two profiles are of different devices: /device:TPU:1 before, /device:TPU:0 now
where the time goes in v3:
time: 61.8 us; the launch traced here: 61.4 us
  blocking collectives  32.1 us (52%)
  Pallas kernels  13.5 us (22%)
  starting transfers between devices  9.57 us (15%)
  local copies, waits for them, and re-layouts  4.17 us (7%)
  waiting for transfers between devices  1.98 us (3%)
    all_to_all x1, blocking collectives, on_device(): columns = lax.all_to_all(windows, ('gx', 'gy'), 0, 0)  22.8 us
    ppermute x6, starting transfers between devices, passed(): lax.ppermute(value, axis, [(i, (i + step) % count) for i in range(count)])  9.57 us
    all_to_all x1, blocking collectives, on_device(): lines = lax.all_to_all(message, 'gz', 0, 0)  9.33 us
    pallas_call x1, Pallas kernels, on_device(): local(cycle_kernel, [shape(*block)], [SM] + [VM] * 13, [(34, 48, LANES),...  7.51 us
    unnamed x12, local copies, waits for them, and re-layouts  4.17 us
    pallas_call x1, Pallas kernels, on_device(): local(residual_kernel, [shape(34, 48, LANES), shape(32, LANES), shape(*bl...  4.07 us
    ppermute x6, waiting for transfers between devices, passed(): lax.ppermute(value, axis, [(i, (i + step) % count) for i in range(count)])  1.98 us
  transfers between devices with their start and end apart: 6, of which 1 were waited for; matrix products, arithmetic and copies ran while one was open for 0% of the time, Pallas kernels for 0%

profile of v3, /device:TPU:0, one launch (start us, length us, event | category | flops | bytes accessed | tf_op | source)
XLA Modules:
  0.0 61.4 jit_solution(9437861380935839759)
XLA Ops:
  0.0 1.0 %copy-done = f32[32,32,128]{2,1,0:T(8,128)S(1)} copy-done((f32[32,32,128]{2,1,0:T(8,128)S(1)}, f32[32,32,128]{2,1,0:T(8,128)}, u32[]{:S(2)}) %copy-start) | copy-done | bytes 524312
  1.0 1.0 %copy-done.2 = f32[32,32,128]{2,1,0:T(8,128)S(1)} copy-done((f32[32,32,128]{2,1,0:T(8,128)S(1)}, f32[32,32,128]{2,1,0:T(8,128)}, u32[]{:S(2)}) %copy-start.2) | copy-done | bytes 524312
  2.1 0.9 %faces.1 = (f32[3,32,128]{2,1,0:T(8,128)S(1)}, f32[3,32,128]{2,1,0:T(8,128)S(1)}, f32[3,32,128]{2,1,0:T(8,128)S(1)}, f32[3,32,128]{2,1,0:T(8,128)S(1)}, f32[2,32,128]{2,1,0:T(8,128)S(1)}) custom-call(f32[32,32,128]{2,1,0:T(8,128)S(1)} %copy-done.2, f32[32,32,128]{2,1,0:T(8,128)S(1)} %copy-done), custom_call_target="tpu_custom_call" | custom-call | tf_op jit(solution)/shard_map/faces/pallas_call | solution.py:644
  3.0 2.3 %collective-permute-start.5 = (f32[2,32,128]{2,1,0:T(8,128)S(1)}, f32[2,32,128]{2,1,0:T(8,128)S(1)}, u32[]{:S(2)}, u32[]{:S(2)}) collective-permute-start(f32[2,32,128]{2,1,0:T(8,128)S(1)} %get-tuple-element.30), channel_id=1, source_target_pairs={{0,7},{1,0},{2,1},{3,2},{4,3},{5,4},{6,5},{7,6},{8,15},{9,8},{10,9... | collective-permute-start | bytes 98312 | tf_op jit(solution)/shard_map/ppermute | solution.py:641
  5.3 0.0 collective-permute-start.4
  5.3 1.6 %collective-permute-start = (f32[3,32,128]{2,1,0:T(8,128)S(1)}, f32[3,32,128]{2,1,0:T(8,128)S(1)}, u32[]{:S(2)}, u32[]{:S(2)}) collective-permute-start(f32[3,32,128]{2,1,0:T(8,128)S(1)} %get-tuple-element.26), channel_id=1, source_target_pairs={{0,32},{32,64},{64,96},{96,0},{1,33},{33,65},{65,97},{97,1},{2,34}... | collective-permute-start | bytes 147464 | tf_op jit(solution)/shard_map/ppermute | solution.py:641
  6.8 1.7 %collective-permute-start.1 = (f32[3,32,128]{2,1,0:T(8,128)S(1)}, f32[3,32,128]{2,1,0:T(8,128)S(1)}, u32[]{:S(2)}, u32[]{:S(2)}) collective-permute-start(f32[3,32,128]{2,1,0:T(8,128)S(1)} %get-tuple-element.27), channel_id=1, source_target_pairs={{0,96},{32,0},{64,32},{96,64},{1,97},{33,1},{65,33},{97,65},{2,98}... | collective-permute-start | bytes 147464 | tf_op jit(solution)/shard_map/ppermute | solution.py:641
  8.5 1.9 %collective-permute-start.2 = (f32[3,32,128]{2,1,0:T(8,128)S(1)}, f32[3,32,128]{2,1,0:T(8,128)S(1)}, u32[]{:S(2)}, u32[]{:S(2)}) collective-permute-start(f32[3,32,128]{2,1,0:T(8,128)S(1)} %get-tuple-element.28), channel_id=1, source_target_pairs={{0,8},{8,16},{16,24},{24,0},{1,9},{9,17},{17,25},{25,1},{2,10},{10... | collective-permute-start | bytes 147464 | tf_op jit(solution)/shard_map/ppermute | solution.py:641
  10.4 0.0 collective-permute-done.5.zhi
  10.4 2.1 %collective-permute-start.3 = (f32[3,32,128]{2,1,0:T(8,128)S(1)}, f32[3,32,128]{2,1,0:T(8,128)S(1)}, u32[]{:S(2)}, u32[]{:S(2)}) collective-permute-start(f32[3,32,128]{2,1,0:T(8,128)S(1)} %get-tuple-element.29), channel_id=1, source_target_pairs={{0,24},{8,0},{16,8},{24,16},{1,25},{9,1},{17,9},{25,17},{2,26},{10... | collective-permute-start | bytes 147464 | tf_op jit(solution)/shard_map/ppermute | solution.py:641
  12.5 0.1 pad_add_fusion.place
  12.6 0.0 collective-permute-done.4.zlo
  12.6 0.0 collective-permute-done.xlo
  12.6 0.0 collective-permute-done.1.xhi
  12.6 2.0 %collective-permute-done.2.ylo = f32[3,32,128]{2,1,0:T(8,128)S(1)} collective-permute-done((f32[3,32,128]{2,1,0:T(8,128)S(1)}, f32[3,32,128]{2,1,0:T(8,128)S(1)}, u32[]{:S(2)}, u32[]{:S(2)}) %collective-permute-start.2) | collective-permute-done | bytes 49184 | tf_op jit(solution)/shard_map/ppermute | solution.py:641
  14.6 0.0 collective-permute-done.3.yhi
  14.6 0.0 copy-start.4
  14.6 1.0 %copy-done.4 = f32[32,32,128]{2,1,0:T(8,128)S(1)} copy-done((f32[32,32,128]{2,1,0:T(8,128)S(1)}, f32[32,32,128]{2,1,0:T(8,128)}, u32[]{:S(2)}) %copy-start.4) | copy-done | bytes 524312
  15.7 1.0 %copy-done.5 = f32[32,32,128]{2,1,0:T(8,128)S(1)} copy-done((f32[32,32,128]{2,1,0:T(8,128)S(1)}, f32[32,32,128]{2,1,0:T(8,128)}, u32[]{:S(2)}) %copy-start.5) | copy-done | bytes 524312
  16.7 4.1 %residual.1 = (f32[34,48,128]{2,1,0:T(8,128)S(1)}, f32[32,128]{1,0:T(8,128)S(1)}, f32[32,32,128]{2,1,0:T(8,128)S(1)}, f32[32,32,128]{2,1,0:T(8,128)S(1)}, f32[8,...) custom-call(s32[3]{0:T(128)S(1)} %pad_add_fusion.place, ...), custom_call_target="tpu_custom_call" | custom-call | tf_op jit(solution)/shard_map/residual/pallas_call | solution.py:652
  20.8 9.3 %all_to_all.10.lines = f32[8,40,128]{2,1,0:T(8,128)S(1)} all-to-all(f32[8,40,128]{2,1,0:T(8,128)S(1)} %get-tuple-element.31), channel_id=1, replica_groups=mesh['gx'=4,'gy'=4,'gz'=8] {'gz'}, dimensions={0} | all-to-all | bytes 327680 | tf_op jit(solution)/shard_map/all_to_all | solution.py:666
  30.1 1.0 %window.1 = (f32[16,128,128]{2,1,0:T(8,128)S(1)}, f32[3,64,128]{2,1,0:T(8,128)S(1)}, f32[32,128]{1,0:T(8,128)S(1)}, f32[16,128]{1,0:T(8,128)S(1)}) custom-call(s32[3]{0:T(128)S(1)} %pad_add_fusion.place, f32[8,40,128]{2,1,0:T(8,128)S(1)} %all_to_all.10.lines, f32[64,128]{1,0:T(8,128)S(1)} %get-tuple-element.32.whole, ...), custom_call_target="tpu_custom_call" | custom-call | tf_op jit(solution)/shard_map/window/pallas_call | solution.py:667
  31.1 22.8 %all_to_all.11.columns = f32[16,128,128]{2,1,0:T(8,128)S(1)} all-to-all(f32[16,128,128]{2,1,0:T(8,128)S(1)} %get-tuple-element.35), channel_id=1, replica_groups=mesh['gx'=4,'gy'=4,'gz'=8] {'gx','gy'}, dimensions={0} | all-to-all | bytes 2097152 | tf_op jit(solution)/shard_map/all_to_all | solution.py:674
  53.9 7.5 %cycle.1 = f32[32,32,128]{2,1,0:T(8,128)} custom-call(s32[3]{0:T(128)S(1)} %pad_add_fusion.place, f32[16,128,128]{2,1,0:T(8,128)S(1)} %all_to_all.11.columns, f32[3,64,128]{2,1,0:T(8,128)S(1)} %get-tuple-element.36.own, f32[32,32,128]{2,1,0:T(8,128)S(1)} %copy-done.1, f32[34,48,128]{2,1,0:T(8,128)S(1)} %get-tuple-element.37.kp, ...), custom_call_target="tpu_custom_call" | custom-call | tf_op jit(solution)/shard_map/cycle/pallas_call | solution.py:677
  (7 shorter events, 0.0 us)
Async XLA Ops:
  0.0 1.0 %copy-start = (f32[32,32,128]{2,1,0:T(8,128)S(1)}, f32[32,32,128]{2,1,0:T(8,128)}, u32[]{:S(2)}) copy-start(f32[32,32,128]{2,1,0:T(8,128)} %initial.5) | copy-start | bytes 1572868
  1.0 1.0 %copy-start.2 = (f32[32,32,128]{2,1,0:T(8,128)S(1)}, f32[32,32,128]{2,1,0:T(8,128)}, u32[]{:S(2)}) copy-start(f32[32,32,128]{2,1,0:T(8,128)} %kappa.3) | copy-start | bytes 1572868
  2.1 12.5 %copy-start.1 = (f32[32,32,128]{2,1,0:T(8,128)S(1)}, f32[32,32,128]{2,1,0:T(8,128)}, u32[]{:S(2)}) copy-start(f32[32,32,128]{2,1,0:T(8,128)} %initial.5) | copy-start | bytes 1572868
  2.1 12.5 %copy-start.3 = (f32[32,32,128]{2,1,0:T(8,128)S(1)}, f32[32,32,128]{2,1,0:T(8,128)}, u32[]{:S(2)}) copy-start(f32[32,32,128]{2,1,0:T(8,128)} %kappa.3) | copy-start | bytes 1572868
  3.0 7.5 %collective-permute-start.5 = (f32[2,32,128]{2,1,0:T(8,128)S(1)}, f32[2,32,128]{2,1,0:T(8,128)S(1)}, u32[]{:S(2)}, u32[]{:S(2)}) collective-permute-start(f32[2,32,128]{2,1,0:T(8,128)S(1)} %get-tuple-element.30), channel_id=1, source_target_pairs={{0,7},{1,0},{2,1},{3,2},{4,3},{5,4},{6,5},{7,6},{8,15},{9,8},{10,9... | collective-permute-start | bytes 98312 | tf_op jit(solution)/shard_map/ppermute | solution.py:641
  5.3 7.4 %collective-permute-start.4 = (f32[2,32,128]{2,1,0:T(8,128)S(1)}, f32[2,32,128]{2,1,0:T(8,128)S(1)}, u32[]{:S(2)}, u32[]{:S(2)}) collective-permute-start(f32[2,32,128]{2,1,0:T(8,128)S(1)} %get-tuple-element.30), channel_id=1, source_target_pairs={{0,1},{1,2},{2,3},{3,4},{4,5},{5,6},{6,7},{7,0},{8,9},{9,10},{10,1... | collective-permute-start | bytes 98312 | tf_op jit(solution)/shard_map/ppermute | solution.py:641
  5.3 7.4 %collective-permute-start = (f32[3,32,128]{2,1,0:T(8,128)S(1)}, f32[3,32,128]{2,1,0:T(8,128)S(1)}, u32[]{:S(2)}, u32[]{:S(2)}) collective-permute-start(f32[3,32,128]{2,1,0:T(8,128)S(1)} %get-tuple-element.26), channel_id=1, source_target_pairs={{0,32},{32,64},{64,96},{96,0},{1,33},{33,65},{65,97},{97,1},{2,34}... | collective-permute-start | bytes 147464 | tf_op jit(solution)/shard_map/ppermute | solution.py:641
  6.8 5.8 %collective-permute-start.1 = (f32[3,32,128]{2,1,0:T(8,128)S(1)}, f32[3,32,128]{2,1,0:T(8,128)S(1)}, u32[]{:S(2)}, u32[]{:S(2)}) collective-permute-start(f32[3,32,128]{2,1,0:T(8,128)S(1)} %get-tuple-element.27), channel_id=1, source_target_pairs={{0,96},{32,0},{64,32},{96,64},{1,97},{33,1},{65,33},{97,65},{2,98}... | collective-permute-start | bytes 147464 | tf_op jit(solution)/shard_map/ppermute | solution.py:641
  8.5 6.1 %collective-permute-start.2 = (f32[3,32,128]{2,1,0:T(8,128)S(1)}, f32[3,32,128]{2,1,0:T(8,128)S(1)}, u32[]{:S(2)}, u32[]{:S(2)}) collective-permute-start(f32[3,32,128]{2,1,0:T(8,128)S(1)} %get-tuple-element.28), channel_id=1, source_target_pairs={{0,8},{8,16},{16,24},{24,0},{1,9},{9,17},{17,25},{25,1},{2,10},{10... | collective-permute-start | bytes 147464 | tf_op jit(solution)/shard_map/ppermute | solution.py:641
  10.4 4.2 %collective-permute-start.3 = (f32[3,32,128]{2,1,0:T(8,128)S(1)}, f32[3,32,128]{2,1,0:T(8,128)S(1)}, u32[]{:S(2)}, u32[]{:S(2)}) collective-permute-start(f32[3,32,128]{2,1,0:T(8,128)S(1)} %get-tuple-element.29), channel_id=1, source_target_pairs={{0,24},{8,0},{16,8},{24,16},{1,25},{9,1},{17,9},{25,17},{2,26},{10... | collective-permute-start | bytes 147464 | tf_op jit(solution)/shard_map/ppermute | solution.py:641
  14.6 1.0 %copy-start.4 = (f32[32,32,128]{2,1,0:T(8,128)S(1)}, f32[32,32,128]{2,1,0:T(8,128)}, u32[]{:S(2)}) copy-start(f32[32,32,128]{2,1,0:T(8,128)} %rhs.1) | copy-start | bytes 1572868
  15.7 1.0 %copy-start.5 = (f32[32,32,128]{2,1,0:T(8,128)S(1)}, f32[32,32,128]{2,1,0:T(8,128)}, u32[]{:S(2)}) copy-start(f32[32,32,128]{2,1,0:T(8,128)} %sigma.1) | copy-start | bytes 1572868

commit v4 on v3

v4 whole, which is shorter than its diff:
```python
import jax
import jax.numpy as jnp
from jax import lax
from jax.experimental import pallas as pl
from jax.experimental.pallas import tpu as pltpu
from jax.sharding import PartitionSpec as P

COARSE_SWEEPS = 8
WEIGHT = 0.8
LANES = 128
F32 = jnp.float32
BF16 = jnp.bfloat16

Z_SMALL, Z_ROWS = 32, 40
X_FACE, X_SEC, X_ENDS, X_ROWS = 64, 96, 104, 112
Y_FACE, Y_SEC, Y_ENDS, Y_ROWS = 192, 224, 232, 240
CHUNKS = 4
BASE = 5


def turn(value, shift, axis):
    size = value.shape[axis]
    if isinstance(shift, int):
        shift = shift % size
        if shift == 0:
            return value
    return pltpu.roll(value, shift, axis)


def lanes_of(shape):
    return lax.broadcasted_iota(jnp.int32, shape, len(shape) - 1)


def square(rule):
    row = lax.broadcasted_iota(jnp.int32, (LANES, LANES), 0)
    col = lax.broadcasted_iota(jnp.int32, (LANES, LANES), 1)
    return jnp.where(rule(row, col), 1.0, 0.0).astype(BF16)


def spread(value, chosen):
    total = None
    for part in range(3):
        piece = value.astype(BF16)
        term = jnp.dot(piece, chosen, preferred_element_type=F32)
        total = term if total is None else total + term
        if part < 2:
            value = value - piece.astype(F32)
    return total


def rows_of(x, shift, pitch, count):
    start = pitch * x + 8
    return pl.ds(start + shift if shift else pl.multiple_of(start, 8), count)


def flat(value):
    return value.reshape(-1, LANES)


def fetch(pairs, sems):
    depth = pairs[0][0].shape[0] // CHUNKS
    copies = []
    for c in range(CHUNKS):
        part = pl.ds(c * depth, depth)
        for n, (far, near) in enumerate(pairs):
            copy = pltpu.make_async_copy(far.at[part], near.at[part], sems.at[n, c])
            copy.start()
            copies.append(copy)
    return copies


def load_kernel(rhs_far, sigma_far, edge, rhs, sigma, sems):
    for copy in fetch(((rhs_far, rhs), (sigma_far, sigma)), sems):
        copy.wait()


def faces_kernel(kappa_far, initial_far, xp, xm, yp, ym, zs, kappa, initial, sems):
    depth = 32 // CHUNKS
    copies = fetch(((kappa_far, kappa), (initial_far, initial)), sems)
    lane = lanes_of((32, LANES))
    first = second = jnp.zeros((32, LANES), F32)

    def body(x, carry):
        first, second = carry
        mine = lane // 4 == x
        shift = 4 * x + 2
        first = jnp.where(mine, turn(kappa[x], shift, 1), first)
        second = jnp.where(mine, turn(initial[x], shift, 1), second)
        return first, second

    for c in range(CHUNKS):
        copies[2 * c].wait()
        copies[2 * c + 1].wait()
        first, second = lax.fori_loop(
            c * depth, (c + 1) * depth, body, (first, second), unroll=True
        )
    zs[0] = first
    zs[1] = second
    xp[0] = kappa[31]
    xp[1] = kappa[30]
    xp[2] = initial[31]
    xm[0] = kappa[0]
    xm[1] = kappa[1]
    xm[2] = initial[0]
    yp[0] = kappa[:, 31, :]
    yp[1] = kappa[:, 30, :]
    yp[2] = initial[:, 31, :]
    ym[0] = kappa[:, 0, :]
    ym[1] = kappa[:, 1, :]
    ym[2] = initial[:, 0, :]


def z_sides(value, rim, x, lane, period):
    near = turn(rim, 126 - 4 * x, 1)
    if period < LANES:
        other = turn(rim, lax.rem(190 - 4 * x, 128), 1)
        near = jnp.where((lane >= 32) & (lane < 96), other, near)
    inside = lane % period
    above = turn(jnp.where(inside == 0, near, value), LANES - 1, 1)
    below = turn(jnp.where(inside == period - 1, near, value), 1, 1)
    return above, below


def residual_kernel(
    kappa, initial, rhs, sigma, xlo, xhi, ylo, yhi, zlo, zhi,
    kp, ck, scale, first, zp, zm, whole, sides, kp2, ck2, scale2, first2, sides2,
    vp, pair_r, pair_k, pair_s, rims, small,
):
    lane = lanes_of((32, LANES))
    inner = pl.ds(8, 32)
    kp[rows_of(0, 0, 40, 32)] = xlo[0]
    kp[rows_of(33, 0, 40, 32)] = xhi[0]
    vp[0, inner] = xlo[2]
    vp[33, inner] = xhi[2]

    def fill(x, carry):
        one = pl.ds(x, 1)
        kp[rows_of(x + 1, 0, 40, 32)] = kappa[x]
        vp[x + 1, inner] = initial[x]
        kp[rows_of(x + 1, -1, 40, 1)] = ylo[0, one]
        kp[rows_of(x + 1, 32, 40, 1)] = yhi[0, one]
        vp[x + 1, 7:8] = ylo[2, one]
        vp[x + 1, 40:41] = yhi[2, one]
        return carry

    lax.fori_loop(0, 32, fill, 0, unroll=4)
    low_half = lane % 4 < 2
    rim_k = jnp.where(low_half, zlo[0], zhi[0])
    rim_v = jnp.where(low_half, zlo[1], zhi[1])
    ck[...] = rim_k

    def slab(x, packed):
        k = kappa[x]
        v = vp[x + 1, inner]
        around = [
            (kp[rows_of(x, 0, 40, 32)], vp[x, inner]),
            (kp[rows_of(x + 2, 0, 40, 32)], vp[x + 2, inner]),
            (kp[rows_of(x + 1, -1, 40, 32)], vp[x + 1, pl.ds(7, 32)]),
            (kp[rows_of(x + 1, 1, 40, 32)], vp[x + 1, pl.ds(9, 32)]),
        ]
        k_up, k_down = z_sides(k, rim_k, x, lane, LANES)
        v_up, v_down = z_sides(v, rim_v, x, lane, LANES)
        around += [(k_up, v_up), (k_down, v_down)]
        k_sum = sum(kn for kn, _ in around)
        v_sum = sum(vn for _, vn in around)
        both = sum(kn * vn for kn, vn in around)
        s = sigma[x]
        diagonal = s + 3.0 * k + 0.5 * k_sum
        r = rhs[x] - diagonal * v + 0.5 * (k * v_sum + both)
        h = WEIGHT / diagonal
        e = h * r
        scale[x] = h
        first[x] = e
        packed = jnp.where(lane // 4 == x, turn(e, 4 * x + 2, 1), packed)
        return r, k, s, packed

    def two(i, packed):
        r0, k0, s0, packed = slab(2 * i, packed)
        r1, k1, s1, packed = slab(2 * i + 1, packed)
        pair_r[i] = r0 + r1
        pair_k[i] = k0 + k1
        pair_s[i] = s0 + s1
        return packed

    packed = lax.fori_loop(0, 16, two, jnp.zeros((32, LANES), F32), unroll=2)
    sides[0] = first[31]
    sides[1] = first[0]
    sides[2] = first[:, 31, :]
    sides[3] = first[:, 0, :]

    even, odd = pl.ds(0, 16, stride=2), pl.ds(1, 16, stride=2)
    to_two = square(lambda row, col: row // 2 == col % 64)

    def level_two(ref, weight):
        summed = ref[:, even, :] + ref[:, odd, :]
        return (spread(flat(summed), to_two) * weight).reshape(16, 16, LANES)

    r2 = level_two(pair_r, 0.5)
    k2 = level_two(pair_k, 0.125)
    s2 = level_two(pair_s, 0.5)
    rims[0] = xlo[0] + xlo[1]
    rims[1] = xhi[0] + xhi[1]
    rims[2] = ylo[0] + ylo[1]
    rims[3] = yhi[0] + yhi[1]
    halo = rims[:, even, :] + rims[:, odd, :]
    halo = (spread(flat(halo), to_two) * 0.125).reshape(4, 16, LANES)
    kp2[rows_of(0, 0, 24, 16)] = halo[0]
    kp2[rows_of(17, 0, 24, 16)] = halo[1]
    for x in range(16):
        kp2[rows_of(x + 1, 0, 24, 16)] = k2[x]
        kp2[rows_of(x + 1, -1, 24, 1)] = halo[2, x : x + 1]
        kp2[rows_of(x + 1, 16, 24, 1)] = halo[3, x : x + 1]
    rims[0] = rim_k
    rim_pair = rims[0, even, :] + rims[0, odd, :]

    def rim_rule(row, col):
        low = (col % 4 == 1) & (row % 4 < 2)
        high = (col % 4 == 2) & (row % 4 >= 2)
        return (row // 8 == col // 4) & (low | high)

    rim_k2 = spread(rim_pair, square(rim_rule)) * 0.125
    ck2[...] = rim_k2
    lane2 = lanes_of((16, LANES))
    packed2 = jnp.zeros((16, LANES), F32)
    for x in range(16):
        k = k2[x]
        up, down = z_sides(k, rim_k2, x, lane2, 64)
        k_sum = (
            kp2[rows_of(x, 0, 24, 16)] + kp2[rows_of(x + 2, 0, 24, 16)]
            + kp2[rows_of(x + 1, -1, 24, 16)] + kp2[rows_of(x + 1, 1, 24, 16)] + up + down
        )
        h = WEIGHT / (s2[x] + 3.0 * k + 0.5 * k_sum)
        e = h * r2[x]
        scale2[x] = h
        first2[x] = e
        packed2 = jnp.where(lane2 // 4 == x, turn(e, 4 * x + 2, 1), packed2)
    sides2[0] = first2[15]
    sides2[1] = first2[0]
    sides2[2] = first2[:, 15, :]
    sides2[3] = first2[:, 0, :]

    even8, odd8 = pl.ds(0, 8, stride=2), pl.ds(1, 8, stride=2)

    def level_three(field, part, weight):
        halves = field.reshape(8, 2, 16, LANES)
        small[...] = halves[:, 0] + halves[:, 1]
        summed = small[:, even8, :] + small[:, odd8, :]
        rule = square(lambda row, col: (row < 64) & (row // 2 == col - 32 * part))
        return spread(flat(summed), rule) * weight

    three = level_three(r2, 0, 0.5) + level_three(k2, 1, 0.125) + level_three(s2, 2, 0.5)
    whole[...] = three
    for out, start, tag in ((zp, 16, 1), (zm, 0, 2)):
        half = spread(
            three,
            square(
                lambda row, col, start=start: (col < 48)
                & (row == 32 * (col // 16) + start + col % 16)
            ),
        )
        face = spread(packed, square(lambda row, col, tag=tag: row == 4 * (col - 96) + tag))
        out[0:Z_SMALL] = half[0:32] + turn(half[32:64], 48, 1) + face
        face2 = spread(
            packed2, square(lambda row, col, tag=tag: (col < 16) & (row == 4 * col + tag))
        )
        out[Z_SMALL:Z_ROWS] = face2[0:8] + turn(face2[8:16], 16, 1)


def block_kernel(whole, block, small):
    three = whole[...]
    halves = three.reshape(4, 2, 8, LANES)
    small[0:4, 0:8] = halves[:, 0] + halves[:, 1]
    summed = small[0:4, pl.ds(0, 4, stride=2), :] + small[0:4, pl.ds(1, 4, stride=2), :]
    for i in range(4):
        small[4, 4 * i : 4 * i + 4] = summed[i]
    four = small[4]

    def pick(part, start):
        rule = square(
            lambda row, col: (row // 32 == part)
            & (col >= start) & (col < start + 16) & (row % 32 // 2 == col - start)
        )
        return spread(four, rule)

    both = 0.5 * pick(0, 0) + 0.125 * pick(1, 64)
    below = 0.5 * pick(2, 0)
    for i in range(4):
        rows = slice(4 * i, 4 * i + 4)
        upper = turn(both[rows], 16 * i, 1) if i == 0 else upper + turn(both[rows], 16 * i, 1)
        lower = turn(below[rows], 16 * i, 1) if i == 0 else lower + turn(below[rows], 16 * i, 1)
    small[5, 0:4] = upper
    small[5, 4:8] = lower
    block[...] = small[5, 0:8]


def window_kernel(
    zlo, zhi, whole, sides, sides2, block, own, xp, xm, ye, cf, cf2, blocks, small
):
    value = block[...]
    for p in range(128):
        blocks[p] = value
    lane = lanes_of((64, LANES))
    a_half, c_half = zlo[0:Z_SMALL], zhi[0:Z_SMALL]
    a = jnp.concatenate([a_half, turn(a_half, -48, 1)], 0)
    b = whole[...]
    c = jnp.concatenate([c_half, turn(c_half, -48, 1)], 0)

    def window(part):
        low = turn(a, BASE - 16 - 16 * part, 1)
        mid = turn(b, BASE - 32 * part, 1)
        high = turn(c, BASE + 32 - 16 * part, 1)
        value = jnp.where((lane < BASE) | (lane >= 112 + BASE), low, mid)
        value = jnp.where((lane >= BASE + 32) & (lane < BASE + 48), high, value)
        return jnp.where((lane >= BASE + 48) & (lane < 112 + BASE), 0.0, value)

    r, k, s = window(0), window(1), window(2)
    own[0], own[1], own[2] = r, k, s
    main = jnp.where(lane < 42, r, jnp.where(lane < 86, turn(k, 43, 1), turn(s, 86, 1)))
    low = jnp.where(lane == 127, r, jnp.where(lane == 126, k, turn(s, -2, 1)))
    high = jnp.where(lane == 42, r, jnp.where(lane == 43, k, turn(s, 2, 1)))
    ends = jnp.where(lane >= 64, low, turn(high, 86, 1))
    small[...] = ends.reshape(8, 8, LANES)
    ye[0] = small[:, 7, :]
    ye[1] = small[:, 0, :]
    lane8 = lanes_of((8, LANES))
    for side, out, i in ((0, xp, 7), (1, xm, 0)):
        out[0:X_FACE] = main
        out[X_FACE:X_SEC] = sides[side]
        out[X_SEC:X_ENDS] = jnp.where(lane8 < 64, sides2[side, 0:8], sides2[side, 8:16])
        out[X_ENDS:X_ROWS] = ends[8 * i : 8 * i + 8]

    def rim(low, high, ready):
        below = spread(low, square(lambda row, col: ready(row) & (col == 4 * (row % 32) + 1)))
        above = spread(high, square(lambda row, col: ready(row) & (col == 4 * (row % 32) + 2)))
        return below + above

    cf[...] = rim(a_half, c_half, lambda row: row >= 96)

    def unfold(half):
        return jnp.concatenate([half, turn(half, -16, 1)], 0)

    cf2[...] = rim(
        unfold(zlo[Z_SMALL:Z_ROWS]), unfold(zhi[Z_SMALL:Z_ROWS]), lambda row: row < 16
    )


def columns_kernel(xlo, xhi, xp, sides, sides2, ye, after, yp, ym):
    lane8 = lanes_of((8, LANES))
    for side, out in ((0, yp), (1, ym)):
        out[0:64] = xlo[0:64]
        out[64:128] = xp[0:64]
        out[128:192] = xhi[0:64]
        out[Y_FACE:Y_SEC] = sides[2 + side]
        face = sides2.at[2 + side]
        out[Y_SEC:Y_ENDS] = jnp.where(lane8 < 64, face[0:8], face[8:16])
        out[Y_ENDS:Y_ROWS] = ye[side]


def wrapped(value):
    last = value.shape[0] - 1
    return [
        jnp.concatenate([value[1:], value[:1]], 0),
        jnp.concatenate([value[last:], value[:last]], 0),
        turn(value, -1, 1),
        turn(value, 1, 1),
        turn(value, -1, 2),
        turn(value, 1, 2),
    ]


def periodic_setup(r, k, s, coefs):
    near = wrapped(k)
    diagonal = s + 3.0 * k + 0.5 * sum(near)
    h = WEIGHT / diagonal
    half = 0.5 * h
    for n in range(6):
        coefs[n] = half * (k + near[n])
    start = h * r
    coefs[6] = start
    return start


def periodic_sweep(e, coefs):
    total = 0.2 * e + coefs[6]
    for n, other in enumerate(wrapped(e)):
        total = total + coefs[n] * other
    return total


def planes_kernel(
    place, blocks_far, four_out,
    r4, k4, s4, half, l5, l6, c4, c5, c6, c7, w4, blocks, sems,
):
    copies = fetch(((blocks_far, blocks),), sems)
    gx, gy, gz = place[0], place[1], place[2]
    lane8 = lanes_of((8, LANES))
    group = lane8 // 16

    def assemble(q, carry):
        pieces = [blocks[8 * q + g] for g in range(8)]
        for i in range(4):
            straight = crossed = jnp.zeros((8, LANES), F32)
            for g in range(8):
                moved = turn(pieces[g], 16 * (g - i), 1)
                straight = jnp.where(group == g, moved, straight)
                crossed = jnp.where(group == (g + 4) % 8, moved, crossed)
            x = 4 * (q // 4) + i
            rows = pl.ds(pl.multiple_of(4 * (q % 4), 4), 4)
            r4[x, rows] = straight[0:4]
            s4[x, rows] = straight[4:8]
            k4[x, rows] = turn(crossed, 64, 1)[0:4]
        return carry

    for c in range(CHUNKS):
        copies[c].wait()
        lax.fori_loop(4 * c, 4 * c + 4, assemble, 0, unroll=True)
    fields4 = r4[...], k4[...], s4[...]
    e4 = periodic_setup(*fields4, c4)
    to_five = square(lambda row, col: row // 2 == col % 64)
    to_six = square(lambda row, col: (row < 64) & (row // 2 == col % 32))
    mean = square(lambda row, col: row < 32)

    def level_five(field, weight):
        pairs = field.reshape(8, 2, 16, LANES)
        half[...] = pairs[:, 0] + pairs[:, 1]
        summed = half[:, pl.ds(0, 8, stride=2), :] + half[:, pl.ds(1, 8, stride=2), :]
        return (spread(flat(summed), to_five) * weight).reshape(8, 8, LANES)

    def level_six(field, weight):
        pairs = field.reshape(4, 2, 8, LANES)
        l6[...] = pairs[:, 0] + pairs[:, 1]
        summed = l6[:, pl.ds(0, 4, stride=2), :] + l6[:, pl.ds(1, 4, stride=2), :]
        l6[:, 0:4] = summed
        l6[:, 4:8] = summed
        return (spread(flat(l6[...]), to_six) * weight).reshape(4, 8, LANES)

    def level_seven(field):
        return (spread(flat(field), mean) * (1.0 / 32.0)).reshape(4, 8, LANES)

    weights = (0.5, 0.125, 0.5)
    fields5 = [level_five(f, w) for f, w in zip(fields4, weights)]
    e5 = periodic_setup(*fields5, c5)
    fields6 = [level_six(f, w) for f, w in zip(fields5, weights)]
    e6 = periodic_setup(*fields6, c6)
    e7 = periodic_setup(*[level_seven(f) for f in fields6], c7)

    def sweep(_, carry):
        a, b, c, d = carry
        return (
            periodic_sweep(a, c4), periodic_sweep(b, c5), periodic_sweep(c, c6),
            periodic_sweep(d, c7),
        )

    e4, e5, e6, e7 = lax.fori_loop(0, COARSE_SWEEPS - 1, sweep, (e4, e5, e6, e7))

    l6[...] = e6 + e7
    six = turn(l6[gx, pl.ds(gy, 1)] + jnp.zeros((8, LANES), F32), 128 - 4 * gz, 1)
    six = spread(six, square(lambda row, col: row == col // 32))
    l5[...] = e5
    w4[...] = jnp.zeros((16, LANES), F32)
    w4[0:2] = l5[2 * gx, pl.ds(2 * gy, 2)]
    w4[2:4] = l5[2 * gx + 1, pl.ds(2 * gy, 2)]
    five = spread(turn(w4[0:8], 128 - 8 * gz, 1), square(lambda row, col: row == col // 16))
    five = five + six
    r4[...] = e4
    for i in range(4):
        w4[4 * i : 4 * i + 4] = r4[4 * gx + i, pl.ds(4 * gy, 4)]
    four = turn(w4[...], lax.rem(128 - 16 * gz, 128), 1)
    four = spread(four, square(lambda row, col: row == col // 8))
    for i in range(4):
        for j in range(2):
            row = 2 * (i // 2) + j
            w4[4 * i + 2 * j : 4 * i + 2 * j + 2] = jnp.broadcast_to(
                five[row : row + 1], (2, LANES)
            )
    four_out[...] = four + w4[...]


def fine_kernel(
    kp, ck, scale, first, cf, kp2, ck2, scale2, first2, cf2,
    base, base2, edge, edge2, fp, fp2,
):
    inner, inner2 = pl.ds(8, 32), pl.ds(8, 16)
    lane2, lane32 = [lanes_of((rows, LANES)) for rows in (16, 32)]
    fp2[1:17, inner2] = first2[...]
    for x in (0, 17):
        fp2[x, inner2] = jnp.zeros((16, LANES), F32)
    fp2[:, 0:8] = jnp.zeros((18, 8, LANES), F32)
    fp2[:, 24:32] = jnp.zeros((18, 8, LANES), F32)

    def second(k_ref, f_ref, x, rows, k_rim, f_rim, lane, period, h):
        inside, pitch = pl.ds(8, rows), rows + 8
        k, e = k_ref[rows_of(x + 1, 0, pitch, rows)], f_ref[x + 1, inside]
        k_up, k_down = z_sides(k, k_rim, x, lane, period)
        e_up, e_down = z_sides(e, f_rim, x, lane, period)
        around = [
            (k_ref[rows_of(x, 0, pitch, rows)], f_ref[x, inside]),
            (k_ref[rows_of(x + 2, 0, pitch, rows)], f_ref[x + 2, inside]),
            (k_ref[rows_of(x + 1, -1, pitch, rows)], f_ref[x + 1, pl.ds(7, rows)]),
            (k_ref[rows_of(x + 1, 1, pitch, rows)], f_ref[x + 1, pl.ds(9, rows)]),
            (k_up, e_up),
            (k_down, e_down),
        ]
        total = k * sum(en for _, en in around) + sum(kn * en for kn, en in around)
        return 1.2 * e + 0.5 * h * total

    rim_k2, rim_f2 = ck2[...], cf2[...]
    for x in range(16):
        base2[x] = second(kp2, fp2, x, 16, rim_k2, rim_f2, lane2, 64, scale2[x])

    for x in (0, 33):
        fp[x, inner] = jnp.zeros((32, LANES), F32)
    blank = jnp.zeros((8, LANES), F32)

    def fill(x, carry):
        fp[x + 1, inner] = first[x]
        fp[x + 1, 0:8] = blank
        fp[x + 1, 40:48] = blank
        return carry

    lax.fori_loop(0, 32, fill, 0, unroll=4)
    rim_k, rim_f = ck[...], cf[...]

    def slab(x, carry):
        base[x] = second(kp, fp, x, 32, rim_k, rim_f, lane32, LANES, scale[x])
        return carry

    lax.fori_loop(0, 32, slab, 0, unroll=4)
    for n, (x, step) in enumerate(((0, -1), (31, 1))):
        k = kp[rows_of(x + 1, 0, 40, 32)] + kp[rows_of(x + 1 + step, 0, 40, 32)]
        edge[n] = 0.5 * scale[x] * k
    for n, (x, step) in enumerate(((0, -1), (15, 1))):
        k = kp2[rows_of(x + 1, 0, 24, 16)] + kp2[rows_of(x + 1 + step, 0, 24, 16)]
        edge2[n] = 0.5 * scale2[x] * k
    for n, (y, step) in enumerate(((0, -1), (31, 1))):
        k = kp[pl.ds(48 + y, 32, stride=40), :] + kp[pl.ds(48 + y + step, 32, stride=40), :]
        edge[2 + n] = 0.5 * scale[:, y, :] * k
    for n, (y, step) in enumerate(((0, -1), (15, 1))):
        k = kp2[pl.ds(32 + y, 16, stride=24), :] + kp2[pl.ds(32 + y + step, 16, stride=24), :]
        edge2[2 + n] = 0.5 * scale2[:, y, :] * k


def finish_kernel(
    initial_far, own, xlo, xhi, ylo, yhi, four_in, base, base2, edge, edge2,
    out_far,
    r3, s3, k3, c3, ea, eb, w3, w2, w32, up, out, initial, sems,
):
    inputs = fetch(((initial_far, initial),), sems)
    lane8 = lanes_of((8, LANES))
    for ix in range(3):
        for iy, y_ref in enumerate((ylo, None, yhi)):
            for i in range(8):
                if ix == 1 and iy == 1:
                    r, k, s = [own[f, 8 * i : 8 * i + 8] for f in range(3)]
                else:
                    if iy == 1:
                        r = (xlo if ix == 0 else xhi)[8 * i : 8 * i + 8]
                    else:
                        r = y_ref[64 * ix + 8 * i : 64 * ix + 8 * i + 8]
                    k = turn(r, -43, 1)
                    s = turn(r, -86, 1)
                    if iy == 1 and ((ix == 0 and i == 7) or (ix == 2 and i == 0)):
                        low = (xlo if ix == 0 else xhi)[X_ENDS:X_ROWS]
                        high = turn(low, 42, 1)
                        r = jnp.where(lane8 == 127, low, jnp.where(lane8 == 42, high, r))
                        k = jnp.where(lane8 == 126, low, jnp.where(lane8 == 43, high, k))
                        low, high = turn(low, 2, 1), turn(high, -2, 1)
                        s = jnp.where(lane8 == 127, low, jnp.where(lane8 == 42, high, s))
                x, y = 8 * ix + i, 8 * iy
                r3[x, y : y + 8] = r
                k3[x, y + 8 : y + 16] = k
                s3[x, y : y + 8] = s
    lane1 = lanes_of((1, LANES))
    for y, y_ref in ((7, ylo), (16, yhi)):
        low = y_ref[Y_ENDS:Y_ROWS]
        high = turn(low, 42, 1)
        low_s, high_s = turn(low, 2, 1), turn(high, -2, 1)
        for i in range(8):
            row = slice(i, i + 1)

            def patch(ref, at, below, above, low_lane, high_lane):
                kept = jnp.where(lane1 == high_lane, above[row], ref[8 + i, at : at + 1])
                ref[8 + i, at : at + 1] = jnp.where(lane1 == low_lane, below[row], kept)

            patch(r3, y, low, high, 127, 42)
            patch(k3, y + 8, low, high, 126, 43)
            patch(s3, y, low_s, high_s, 127, 42)
    rim = jnp.zeros((24, 8, LANES), F32)
    for ref in (k3, ea, eb):
        ref[:, 0:8] = rim
        ref[:, 32:40] = rim
    mid = pl.ds(8, 24)

    def setup3(x, carry):
        k = k3[x, mid]
        near = [
            k3[x + 1, mid], k3[x - 1, mid], k3[x, pl.ds(9, 24)], k3[x, pl.ds(7, 24)],
            turn(k, -1, 1), turn(k, 1, 1),
        ]
        h = WEIGHT / (s3[x] + 3.0 * k + 0.5 * sum(near))
        half = 0.5 * h
        for n in range(6):
            c3[n, x] = half * (k + near[n])
        g = h * r3[x]
        c3[6, x] = g
        ea[x, mid] = g
        return carry

    lax.fori_loop(1, 23, setup3, 0, unroll=True)
    source, target = ea, eb
    for step in range(2, COARSE_SWEEPS + 1):

        def sweep3(x, carry, source=source, target=target):
            e = source[x, mid]
            near = [
                source[x + 1, mid], source[x - 1, mid],
                source[x, pl.ds(9, 24)], source[x, pl.ds(7, 24)],
                turn(e, -1, 1), turn(e, 1, 1),
            ]
            total = 0.2 * e + c3[6, x]
            for n in range(6):
                total = total + c3[n, x] * near[n]
            target[x, mid] = total
            return carry

        lax.fori_loop(step, 24 - step, sweep3, 0, unroll=True)
        source, target = target, source

    mine = source[8:16, 16:24]
    lane3 = lanes_of((8, 8, LANES))
    three = flat(jnp.where((lane3 >= BASE) & (lane3 < BASE + 32), mine, 0.0))
    three = spread(three, square(lambda row, col: row == BASE + col // 4))
    four = four_in[...]
    for i in range(8):
        block = four[4 * (i // 2) : 4 * (i // 2) + 4]
        w3[i, pl.ds(0, 4, stride=2), :] = block
        w3[i, pl.ds(1, 4, stride=2), :] = block
    three = three + flat(w3[...])

    def beyond(ref, start):
        half = ref[start : start + 8]
        other = turn(half, 64, 1)
        return jnp.concatenate(
            [jnp.where(lane8 < 64, half, other), jnp.where(lane8 < 64, other, half)], 0
        )

    w2[...] = base2[...]
    for n, (x, ref) in enumerate(((0, xlo), (15, xhi))):
        w2[x] = w2[x] + edge2[n] * beyond(ref, X_SEC)
    for n, (y, ref) in enumerate(((0, ylo), (15, yhi))):
        w2[:, y, :] = w2[:, y, :] + edge2[2 + n] * beyond(ref, Y_SEC)
    two = spread(flat(w2[...]), square(lambda row, col: row == col // 2))
    even8, odd8 = pl.ds(0, 8, stride=2), pl.ds(1, 8, stride=2)
    for i in range(16):
        block = three[8 * (i // 2) : 8 * (i // 2) + 8]
        w32[i, even8, :] = block
        w32[i, odd8, :] = block
    two = two.reshape(16, 16, LANES) + w32[...]
    up[:, pl.ds(0, 16, stride=2), :] = two
    up[:, pl.ds(1, 16, stride=2), :] = two

    depth = 32 // CHUNKS
    copies = []
    for c in range(CHUNKS):
        part = pl.ds(c * depth, depth)
        inputs[c].wait()
        for x in range(c * depth, (c + 1) * depth):
            total = initial[x] + (base[x] + up[x // 2])
            if x in (0, 31):
                face = (xhi if x else xlo)[X_FACE:X_SEC]
                total = total + edge[1 if x else 0] * face
            out[x] = total
        for n, (y, ref) in enumerate(((0, ylo), (31, yhi))):
            face = ref[pl.ds(Y_FACE + c * depth, depth)]
            out[part, y, :] = out[part, y, :] + edge[2 + n, part] * face
        copy = pltpu.make_async_copy(out.at[part], out_far.at[part], sems.at[1, c])
        copy.start()
        copies.append(copy)
    for copy in copies:
        copy.wait()


VM = pl.BlockSpec(memory_space=pltpu.VMEM)
SM = pl.BlockSpec(memory_space=pltpu.SMEM)
FAR = pl.BlockSpec(memory_space=pltpu.HBM)


def shape(*dims):
    return pltpu.VMEM(dims, F32)


def local(kernel, outs, ins, scratch, name, sems=None, out_spec=VM):
    scratch = [pltpu.VMEM(dims, F32) for dims in scratch]
    if sems is not None:
        scratch.append(pltpu.SemaphoreType.DMA(sems))
    return pl.pallas_call(
        kernel,
        out_shape=outs,
        in_specs=ins,
        out_specs=[out_spec] * len(outs),
        scratch_shapes=scratch,
        compiler_params=pltpu.CompilerParams(vmem_limit_bytes=24 * 1024 * 1024),
        name=name,
    )


def on_device(initial, rhs, kappa, sigma):
    place = jnp.stack([lax.axis_index(axis) for axis in ("gx", "gy", "gz")]).astype(jnp.int32)

    def passed(value, axis, step):
        count = lax.axis_size(axis)
        return lax.ppermute(value, axis, [(i, (i + step) % count) for i in range(count)])

    block = (32, 32, LANES)
    block2 = (16, 16, LANES)
    edge = shape(3, 32, LANES)
    far = [
        pltpu.with_memory_space_constraint(value, pltpu.HBM)
        for value in (kappa, initial, rhs, sigma)
    ]
    xp, xm, yp, ym, zs, kappa, initial = local(
        faces_kernel,
        [edge, edge, edge, edge, shape(2, 32, LANES)] + [shape(*block)] * 2,
        [FAR] * 2, [], "faces", sems=(2, CHUNKS),
    )(*far[:2])
    rhs, sigma = local(
        load_kernel, [shape(*block)] * 2, [FAR, FAR, VM], [], "load", sems=(2, CHUNKS)
    )(*far[2:], zs)
    zlo, zhi = passed(zs, "gz", 1), passed(zs, "gz", -1)
    xlo, xhi = passed(xp, "gx", 1), passed(xm, "gx", -1)
    ylo, yhi = passed(yp, "gy", 1), passed(ym, "gy", -1)
    kp, ck, scale, first, zp, zm, whole, sides, kp2, ck2, scale2, first2, sides2 = local(
        residual_kernel,
        [
            shape(1368, LANES), shape(32, LANES), shape(*block), shape(*block),
            shape(Z_ROWS, LANES), shape(Z_ROWS, LANES),
            shape(64, LANES), shape(4, 32, LANES), shape(440, LANES),
            shape(16, LANES), shape(*block2), shape(*block2), shape(4, 16, LANES),
        ],
        [VM] * 10,
        [
            (34, 48, LANES), (16, 32, LANES), (16, 32, LANES), (16, 32, LANES),
            (4, 32, LANES), (8, 16, LANES),
        ],
        "residual",
    )(kappa, initial, rhs, sigma, xlo, xhi, ylo, yhi, zlo, zhi)

    (level4,) = local(block_kernel, [shape(8, LANES)], [VM], [(8, 16, LANES)], "block")(whole)
    zlo, zhi = passed(zp, "gz", 1), passed(zm, "gz", -1)
    own, xp, xm, ye, cf, cf2, blocks = local(
        window_kernel,
        [
            shape(3, 64, LANES), shape(X_ROWS, LANES), shape(X_ROWS, LANES),
            shape(2, 8, LANES), shape(32, LANES), shape(16, LANES),
            pltpu.HBM((128, 8, LANES), F32),
        ],
        [VM] * 6, [(8, 8, LANES)], "window",
    )(zlo, zhi, whole, sides, sides2, level4)
    xlo, xhi = passed(xp, "gx", 1), passed(xm, "gx", -1)
    planes = lax.all_to_all(blocks, ("gx", "gy", "gz"), 0, 0)
    base, base2, edge, edge2 = local(
        fine_kernel,
        [shape(*block), shape(*block2), shape(4, 32, LANES), shape(4, 16, LANES)],
        [VM] * 10, [(34, 48, LANES), (18, 32, LANES)], "fine",
    )(kp, ck, scale, first, cf, kp2, ck2, scale2, first2, cf2)
    yp, ym = local(
        columns_kernel, [shape(Y_ROWS, LANES)] * 2, [VM] * 7, [], "columns"
    )(xlo, xhi, xp, sides, sides2, ye, edge2)
    ylo, yhi = passed(yp, "gy", 1), passed(ym, "gy", -1)
    (four,) = local(
        planes_kernel, [shape(16, LANES)], [SM, FAR],
        [
            block2, block2, block2, (8, 16, LANES), (8, 8, LANES), (4, 8, LANES),
            (7,) + block2, (7, 8, 8, LANES), (7, 4, 8, LANES), (7, 4, 8, LANES), (16, LANES),
            (128, 8, LANES),
        ],
        "planes", sems=(1, CHUNKS),
    )(place, pltpu.with_memory_space_constraint(planes, pltpu.HBM))
    padded3 = (24, 40, LANES)
    block3 = (24, 24, LANES)
    return local(
        finish_kernel, [pltpu.HBM(block, F32)], [FAR] + [VM] * 10,
        [
            block3, block3, padded3, (7,) + block3, padded3, padded3,
            (8, 8, LANES), block2, block2, (16, 32, LANES), block, block,
        ],
        "finish", sems=(2, CHUNKS), out_spec=FAR,
    )(far[1], own, xlo, xhi, ylo, yhi, four, base, base2, edge, edge2)[0]


def solution(mesh):
    spec = P("gx", "gy", "gz")
    return jax.shard_map(
        on_device, mesh=mesh, in_specs=(spec,) * 4, out_specs=spec, check_vma=False
    )
```

time: 61.8 us -> 52.1 us (0.84)
  the two profiles are of different devices: /device:TPU:0 before, /device:TPU:1 now
where the time goes in v4:
time: 52.1 us; the launch traced here: 51.9 us
  starting transfers between devices  24.6 us (47%)
  Pallas kernels  19 us (36%)
  waiting for transfers between devices  8.17 us (16%)
    ppermute x12, starting transfers between devices, passed(): lax.ppermute(value, axis, [(i, (i + step) % count) for i in range(count)])  16 us
    all_to_all x1, starting transfers between devices, on_device(): planes = lax.all_to_all(blocks, ('gx', 'gy', 'gz'), 0, 0)  8.55 us
    ppermute x12, waiting for transfers between devices, passed(): lax.ppermute(value, axis, [(i, (i + step) % count) for i in range(count)])  6.44 us
    pallas_call x1, Pallas kernels, on_device(): local(planes_kernel, [shape(16, LANES)], [SM, FAR], [block2, block2, bloc...  4.76 us
    pallas_call x1, Pallas kernels, on_device(): local(residual_kernel, [shape(1368, LANES), shape(32, LANES), shape(*bloc...  3.47 us
    pallas_call x1, Pallas kernels, on_device(): local(finish_kernel, [pltpu.HBM(block, F32)], [FAR] + [VM] * 10, [block3,...  3.29 us
    pallas_call x1, Pallas kernels, on_device(): local(fine_kernel, [shape(*block), shape(*block2), shape(4, 32, LANES), s...  3.17 us
    all_to_all x1, waiting for transfers between devices, on_device(): planes = lax.all_to_all(blocks, ('gx', 'gy', 'gz'), 0, 0)  1.73 us
  transfers between devices with their start and end apart: 13, of which 6 were waited for; matrix products, arithmetic and copies ran while one was open for 0% of the time, Pallas kernels for 18%

profile of v4, /device:TPU:1, one launch (start us, length us, event | category | flops | bytes accessed | tf_op | source)
XLA Modules:
  0.0 51.9 jit_solution(14880745002517352530)
XLA Ops:
  0.0 1.6 %faces.1 = (f32[3,32,128]{2,1,0:T(8,128)S(1)}, f32[3,32,128]{2,1,0:T(8,128)S(1)}, f32[3,32,128]{2,1,0:T(8,128)S(1)}, f32[3,32,128]{2,1,0:T(8,128)S(1)}, f32[2,32...) custom-call(f32[32,32,128]{2,1,0:T(8,128)} %kappa_far.1, f32[32,32,128]{2,1,0:T(8,128)} %initial_far.3), custom_call_target="tpu_custom_call" | custom-call | tf_op jit(solution)/shard_map/faces/pallas_call | solution.py:721
  1.6 2.6 %collective-permute-start.4 = (f32[2,32,128]{2,1,0:T(8,128)S(1)}, f32[2,32,128]{2,1,0:T(8,128)S(1)}, u32[]{:S(2)}, u32[]{:S(2)}) collective-permute-start(f32[2,32,128]{2,1,0:T(8,128)S(1)} %get-tuple-element.42.edge), channel_id=1, source_target_pairs={{0,1},{1,2},{2,3},{3,4},{4,5},{5,6},{6,7},{7,0},{8,9},{9,10},{10,1... | collective-permute-start | bytes 98312 | tf_op jit(solution)/shard_map/ppermute | solution.py:712
  4.2 1.3 %collective-permute-start = (f32[3,32,128]{2,1,0:T(8,128)S(1)}, f32[3,32,128]{2,1,0:T(8,128)S(1)}, u32[]{:S(2)}, u32[]{:S(2)}) collective-permute-start(f32[3,32,128]{2,1,0:T(8,128)S(1)} %get-tuple-element.45), channel_id=1, source_target_pairs={{0,32},{32,64},{64,96},{96,0},{1,33},{33,65},{65,97},{97,1},{2,34}... | collective-permute-start | bytes 147464 | tf_op jit(solution)/shard_map/ppermute | solution.py:712
  5.5 1.4 %collective-permute-start.1 = (f32[3,32,128]{2,1,0:T(8,128)S(1)}, f32[3,32,128]{2,1,0:T(8,128)S(1)}, u32[]{:S(2)}, u32[]{:S(2)}) collective-permute-start(f32[3,32,128]{2,1,0:T(8,128)S(1)} %get-tuple-element.46), channel_id=1, source_target_pairs={{0,96},{32,0},{64,32},{96,64},{1,97},{33,1},{65,33},{97,65},{2,98}... | collective-permute-start | bytes 147464 | tf_op jit(solution)/shard_map/ppermute | solution.py:712
  7.0 1.6 %collective-permute-start.2 = (f32[3,32,128]{2,1,0:T(8,128)S(1)}, f32[3,32,128]{2,1,0:T(8,128)S(1)}, u32[]{:S(2)}, u32[]{:S(2)}) collective-permute-start(f32[3,32,128]{2,1,0:T(8,128)S(1)} %get-tuple-element.47), channel_id=1, source_target_pairs={{0,8},{8,16},{16,24},{24,0},{1,9},{9,17},{17,25},{25,1},{2,10},{10... | collective-permute-start | bytes 147464 | tf_op jit(solution)/shard_map/ppermute | solution.py:712
  8.6 2.1 %collective-permute-start.3 = (f32[3,32,128]{2,1,0:T(8,128)S(1)}, f32[3,32,128]{2,1,0:T(8,128)S(1)}, u32[]{:S(2)}, u32[]{:S(2)}) collective-permute-start(f32[3,32,128]{2,1,0:T(8,128)S(1)} %get-tuple-element.48), channel_id=1, source_target_pairs={{0,24},{8,0},{16,8},{24,16},{1,25},{9,1},{17,9},{25,17},{2,26},{10... | collective-permute-start | bytes 147464 | tf_op jit(solution)/shard_map/ppermute | solution.py:712
  10.7 1.4 %load.1 = (f32[32,32,128]{2,1,0:T(8,128)S(1)}, f32[32,32,128]{2,1,0:T(8,128)S(1)}) custom-call(f32[32,32,128]{2,1,0:T(8,128)} %rhs_far.1, f32[32,32,128]{2,1,0:T(8,128)} %sigma_far.1, f32[2,32,128]{2,1,0:T(8,128)S(1)} %get-tuple-element.42.edge), custom_call_target="tpu_custom_call" | custom-call | tf_op jit(solution)/shard_map/load/pallas_call | solution.py:726
  12.1 2.0 %collective-permute-done.5.zhi = f32[2,32,128]{2,1,0:T(8,128)S(1)} collective-permute-done((f32[2,32,128]{2,1,0:T(8,128)S(1)}, f32[2,32,128]{2,1,0:T(8,128)S(1)}, u32[]{:S(2)}, u32[]{:S(2)}) %collective-permute-start.5) | collective-permute-done | bytes 32800 | tf_op jit(solution)/shard_map/ppermute | solution.py:712
  14.1 3.5 %residual.1 = (f32[1368,128]{1,0:T(8,128)S(1)}, f32[32,128]{1,0:T(8,128)S(1)}, f32[32,32,128]{2,1,0:T(8,128)S(1)}, f32[32,32,128]{2,1,0:T(8,128)S(1)}, f32[40,12...) custom-call(f32[32,32,128]{2,1,0:T(8,128)S(1)} %get-tuple-element.40, ...), custom_call_target="tpu_custom_call" | custom-call | tf_op jit(solution)/shard_map/residual/pallas_call | solution.py:732
  17.6 0.5 collective-permute-start.7
  18.4 0.4 collective-permute-done.6.zlo
  18.8 2.0 %collective-permute-done.7.zhi = f32[40,128]{1,0:T(8,128)S(1)} collective-permute-done((f32[40,128]{1,0:T(8,128)S(1)}, f32[40,128]{1,0:T(8,128)S(1)}, u32[]{:S(2)}, u32[]{:S(2)}) %collective-permute-start.7) | collective-permute-done | bytes 20512 | tf_op jit(solution)/shard_map/ppermute | solution.py:712
  20.8 1.0 %window.1 = (f32[3,64,128]{2,1,0:T(8,128)S(1)}, f32[112,128]{1,0:T(8,128)S(1)}, f32[112,128]{1,0:T(8,128)S(1)}, f32[2,8,128]{2,1,0:T(8,128)S(1)}, f32[32,128]{1,...) custom-call(f32[40,128]{1,0:T(8,128)S(1)} %collective-permute-done.6.zlo, ...), custom_call_target="tpu_custom_call" | custom-call | tf_op jit(solution)/shard_map/window/pallas_call | solution.py:750
  21.9 8.5 %all-to-all-start = ((f32[128,8,128]{2,1,0:T(8,128)}), f32[128,8,128]{2,1,0:T(8,128)}, u32[]{:S(2)}, u32[]{:S(2)}) async-start(f32[128,8,128]{2,1,0:T(8,128)} %get-tuple-element.71), calls=%async_computation | async-start | bytes 1048576 | tf_op jit(solution)/shard_map/all_to_all | solution.py:760
  30.4 1.5 %collective-permute-start.8 = (f32[112,128]{1,0:T(8,128)S(1)}, f32[112,128]{1,0:T(8,128)S(1)}, u32[]{:S(2)}, u32[]{:S(2)}) collective-permute-start(f32[112,128]{1,0:T(8,128)S(1)} %get-tuple-element.55.xp), channel_id=1, source_target_pairs={{0,32},{32,64},{64,96},{96,0},{1,33},{33,65},{65,97},{97,1},{2,34}... | collective-permute-start | bytes 172040 | tf_op jit(solution)/shard_map/ppermute | solution.py:712
  31.9 1.3 %collective-permute-start.9 = (f32[112,128]{1,0:T(8,128)S(1)}, f32[112,128]{1,0:T(8,128)S(1)}, u32[]{:S(2)}, u32[]{:S(2)}) collective-permute-start(f32[112,128]{1,0:T(8,128)S(1)} %get-tuple-element.56), channel_id=1, source_target_pairs={{0,96},{32,0},{64,32},{96,64},{1,97},{33,1},{65,33},{97,65},{2,98}... | collective-permute-start | bytes 172040 | tf_op jit(solution)/shard_map/ppermute | solution.py:712
  33.2 3.2 %fine.1 = (f32[32,32,128]{2,1,0:T(8,128)S(1)}, f32[16,16,128]{2,1,0:T(8,128)S(1)}, f32[4,32,128]{2,1,0:T(8,128)S(1)}, f32[4,16,128]{2,1,0:T(8,128)S(1)}) custom-call(f32[1368,128]{1,0:T(8,128)S(1)} %get-tuple-element.58.kp, f32[32,128]{1,0:T(8,128)S(1)} %get-tuple-element.59.ck, f32[32,32,128]{2,1,0:T(8,128)S(1)} %get-tuple-element.60.scale, ...), custom_call_target="tpu_custom_call" | custom-call | tf_op jit(solution)/shard_map/fine/pallas_call | solution.py:761
  36.4 0.6 %collective-permute-done.8.xlo = f32[112,128]{1,0:T(8,128)S(1)} collective-permute-done((f32[112,128]{1,0:T(8,128)S(1)}, f32[112,128]{1,0:T(8,128)S(1)}, u32[]{:S(2)}, u32[]{:S(2)}) %collective-permute-start.8) | collective-permute-done | bytes 57376 | tf_op jit(solution)/shard_map/ppermute | solution.py:712
  37.0 1.4 %collective-permute-done.9.xhi = f32[112,128]{1,0:T(8,128)S(1)} collective-permute-done((f32[112,128]{1,0:T(8,128)S(1)}, f32[112,128]{1,0:T(8,128)S(1)}, u32[]{:S(2)}, u32[]{:S(2)}) %collective-permute-start.9) | collective-permute-done | bytes 57376 | tf_op jit(solution)/shard_map/ppermute | solution.py:712
  38.4 1.6 %collective-permute-start.10 = (f32[240,128]{1,0:T(8,128)S(1)}, f32[240,128]{1,0:T(8,128)S(1)}, u32[]{:S(2)}, u32[]{:S(2)}) collective-permute-start(f32[240,128]{1,0:T(8,128)S(1)} %get-tuple-element.69), channel_id=1, source_target_pairs={{0,8},{8,16},{16,24},{24,0},{1,9},{9,17},{17,25},{25,1},{2,10},{10... | collective-permute-start | bytes 368648 | tf_op jit(solution)/shard_map/ppermute | solution.py:712
  40.1 1.9 %collective-permute-start.11 = (f32[240,128]{1,0:T(8,128)S(1)}, f32[240,128]{1,0:T(8,128)S(1)}, u32[]{:S(2)}, u32[]{:S(2)}) collective-permute-start(f32[240,128]{1,0:T(8,128)S(1)} %get-tuple-element.70), channel_id=1, source_target_pairs={{0,24},{8,0},{16,8},{24,16},{1,25},{9,1},{17,9},{25,17},{2,26},{10... | collective-permute-start | bytes 368648 | tf_op jit(solution)/shard_map/ppermute | solution.py:712
  42.1 1.7 %all-to-all-done.blocks_far = f32[128,8,128]{2,1,0:T(8,128)} async-done(((f32[128,8,128]{2,1,0:T(8,128)}), f32[128,8,128]{2,1,0:T(8,128)}, u32[]{:S(2)}, u32[]{:S(2)}) %all-to-all-start) | async-done | bytes 524320 | tf_op jit(solution)/shard_map/all_to_all | solution.py:760
  43.8 4.8 %planes.1.four_in = f32[16,128]{1,0:T(8,128)S(1)} custom-call(s32[3]{0:T(128)S(1)} %pad_add_fusion.place, f32[128,8,128]{2,1,0:T(8,128)} %all-to-all-done.blocks_far), custom_call_target="tpu_custom_call" | custom-call | tf_op jit(solution)/shard_map/planes/pallas_call | solution.py:770
  48.6 3.3 %finish.1 = f32[32,32,128]{2,1,0:T(8,128)} custom-call(f32[32,32,128]{2,1,0:T(8,128)} %initial_far.3, f32[3,64,128]{2,1,0:T(8,128)S(1)} %get-tuple-element.54.own, f32[112,128]{1,0:T(8,128)S(1)} %collective-permute-done.8.xlo, f32[112,128]{1,0:T(8,128)S(1)} %collective-permute-done.9.xhi, f32[240,128]{1,0:T(8,128)S(1)} %collective-permute-done.10.ylo, ...), custom_call_target="tpu_custom_call" | custom-call | tf_op jit(solution)/shard_map/finish/pallas_call | solution.py:781
  (12 shorter events, 0.4 us)
Async XLA Ops:
  1.6 9.1 %collective-permute-start.4 = (f32[2,32,128]{2,1,0:T(8,128)S(1)}, f32[2,32,128]{2,1,0:T(8,128)S(1)}, u32[]{:S(2)}, u32[]{:S(2)}) collective-permute-start(f32[2,32,128]{2,1,0:T(8,128)S(1)} %get-tuple-element.42.edge), channel_id=1, source_target_pairs={{0,1},{1,2},{2,3},{3,4},{4,5},{5,6},{6,7},{7,0},{8,9},{9,10},{10,1... | collective-permute-start | bytes 98312 | tf_op jit(solution)/shard_map/ppermute | solution.py:712
  4.2 9.8 %collective-permute-start = (f32[3,32,128]{2,1,0:T(8,128)S(1)}, f32[3,32,128]{2,1,0:T(8,128)S(1)}, u32[]{:S(2)}, u32[]{:S(2)}) collective-permute-start(f32[3,32,128]{2,1,0:T(8,128)S(1)} %get-tuple-element.45), channel_id=1, source_target_pairs={{0,32},{32,64},{64,96},{96,0},{1,33},{33,65},{65,97},{97,1},{2,34}... | collective-permute-start | bytes 147464 | tf_op jit(solution)/shard_map/ppermute | solution.py:712
  5.5 8.6 %collective-permute-start.1 = (f32[3,32,128]{2,1,0:T(8,128)S(1)}, f32[3,32,128]{2,1,0:T(8,128)S(1)}, u32[]{:S(2)}, u32[]{:S(2)}) collective-permute-start(f32[3,32,128]{2,1,0:T(8,128)S(1)} %get-tuple-element.46), channel_id=1, source_target_pairs={{0,96},{32,0},{64,32},{96,64},{1,97},{33,1},{65,33},{97,65},{2,98}... | collective-permute-start | bytes 147464 | tf_op jit(solution)/shard_map/ppermute | solution.py:712
  7.0 7.1 %collective-permute-start.2 = (f32[3,32,128]{2,1,0:T(8,128)S(1)}, f32[3,32,128]{2,1,0:T(8,128)S(1)}, u32[]{:S(2)}, u32[]{:S(2)}) collective-permute-start(f32[3,32,128]{2,1,0:T(8,128)S(1)} %get-tuple-element.47), channel_id=1, source_target_pairs={{0,8},{8,16},{16,24},{24,0},{1,9},{9,17},{17,25},{25,1},{2,10},{10... | collective-permute-start | bytes 147464 | tf_op jit(solution)/shard_map/ppermute | solution.py:712
  8.6 5.5 %collective-permute-start.3 = (f32[3,32,128]{2,1,0:T(8,128)S(1)}, f32[3,32,128]{2,1,0:T(8,128)S(1)}, u32[]{:S(2)}, u32[]{:S(2)}) collective-permute-start(f32[3,32,128]{2,1,0:T(8,128)S(1)} %get-tuple-element.48), channel_id=1, source_target_pairs={{0,24},{8,0},{16,8},{24,16},{1,25},{9,1},{17,9},{25,17},{2,26},{10... | collective-permute-start | bytes 147464 | tf_op jit(solution)/shard_map/ppermute | solution.py:712
  10.7 3.3 %collective-permute-start.5 = (f32[2,32,128]{2,1,0:T(8,128)S(1)}, f32[2,32,128]{2,1,0:T(8,128)S(1)}, u32[]{:S(2)}, u32[]{:S(2)}) collective-permute-start(f32[2,32,128]{2,1,0:T(8,128)S(1)} %get-tuple-element.42.edge), channel_id=1, source_target_pairs={{0,7},{1,0},{2,1},{3,2},{4,3},{5,4},{6,5},{7,6},{8,15},{9,8},{10,9... | collective-permute-start | bytes 98312 | tf_op jit(solution)/shard_map/ppermute | solution.py:712
  17.6 1.2 %collective-permute-start.6 = (f32[40,128]{1,0:T(8,128)S(1)}, f32[40,128]{1,0:T(8,128)S(1)}, u32[]{:S(2)}, u32[]{:S(2)}) collective-permute-start(f32[40,128]{1,0:T(8,128)S(1)} %get-tuple-element.49), channel_id=1, source_target_pairs={{0,1},{1,2},{2,3},{3,4},{4,5},{5,6},{6,7},{7,0},{8,9},{9,10},{10,1... | collective-permute-start | bytes 61448 | tf_op jit(solution)/shard_map/ppermute | solution.py:712
  17.6 3.2 %collective-permute-start.7 = (f32[40,128]{1,0:T(8,128)S(1)}, f32[40,128]{1,0:T(8,128)S(1)}, u32[]{:S(2)}, u32[]{:S(2)}) collective-permute-start(f32[40,128]{1,0:T(8,128)S(1)} %get-tuple-element.50), channel_id=1, source_target_pairs={{0,7},{1,0},{2,1},{3,2},{4,3},{5,4},{6,5},{7,6},{8,15},{9,8},{10,9... | collective-permute-start | bytes 61448 | tf_op jit(solution)/shard_map/ppermute | solution.py:712
  21.9 21.9 %all-to-all-start = ((f32[128,8,128]{2,1,0:T(8,128)}), f32[128,8,128]{2,1,0:T(8,128)}, u32[]{:S(2)}, u32[]{:S(2)}) async-start(f32[128,8,128]{2,1,0:T(8,128)} %get-tuple-element.71), calls=%async_computation | async-start | bytes 1048576 | tf_op jit(solution)/shard_map/all_to_all | solution.py:760
  30.4 6.6 %collective-permute-start.8 = (f32[112,128]{1,0:T(8,128)S(1)}, f32[112,128]{1,0:T(8,128)S(1)}, u32[]{:S(2)}, u32[]{:S(2)}) collective-permute-start(f32[112,128]{1,0:T(8,128)S(1)} %get-tuple-element.55.xp), channel_id=1, source_target_pairs={{0,32},{32,64},{64,96},{96,0},{1,33},{33,65},{65,97},{97,1},{2,34}... | collective-permute-start | bytes 172040 | tf_op jit(solution)/shard_map/ppermute | solution.py:712
  31.9 6.5 %collective-permute-start.9 = (f32[112,128]{1,0:T(8,128)S(1)}, f32[112,128]{1,0:T(8,128)S(1)}, u32[]{:S(2)}, u32[]{:S(2)}) collective-permute-start(f32[112,128]{1,0:T(8,128)S(1)} %get-tuple-element.56), channel_id=1, source_target_pairs={{0,96},{32,0},{64,32},{96,64},{1,97},{33,1},{65,33},{97,65},{2,98}... | collective-permute-start | bytes 172040 | tf_op jit(solution)/shard_map/ppermute | solution.py:712
  38.4 10.2 %collective-permute-start.10 = (f32[240,128]{1,0:T(8,128)S(1)}, f32[240,128]{1,0:T(8,128)S(1)}, u32[]{:S(2)}, u32[]{:S(2)}) collective-permute-start(f32[240,128]{1,0:T(8,128)S(1)} %get-tuple-element.69), channel_id=1, source_target_pairs={{0,8},{8,16},{16,24},{24,0},{1,9},{9,17},{17,25},{25,1},{2,10},{10... | collective-permute-start | bytes 368648 | tf_op jit(solution)/shard_map/ppermute | solution.py:712
  40.1 8.5 %collective-permute-start.11 = (f32[240,128]{1,0:T(8,128)S(1)}, f32[240,128]{1,0:T(8,128)S(1)}, u32[]{:S(2)}, u32[]{:S(2)}) collective-permute-start(f32[240,128]{1,0:T(8,128)S(1)} %get-tuple-element.70), channel_id=1, source_target_pairs={{0,24},{8,0},{16,8},{24,16},{1,25},{9,1},{17,9},{25,17},{2,26},{10... | collective-permute-start | bytes 368648 | tf_op jit(solution)/shard_map/ppermute | solution.py:712

commit v5 on v4

--- a/solution.py
+++ b/solution.py
@@ -250,6 +250,16 @@
 
     three = level_three(r2, 0, 0.5) + level_three(k2, 1, 0.125) + level_three(s2, 2, 0.5)
     whole[...] = three
+    cubes = three.reshape(2, 4, 8, LANES)
+    small[0:2, 0:8] = cubes[:, 0] + cubes[:, 1] + cubes[:, 2] + cubes[:, 3]
+    quads = [small[0:2, pl.ds(j, 2, stride=4), :] for j in range(4)]
+    quad = quads[0] + quads[1] + quads[2] + quads[3]
+    small[2, 0:8] = jnp.zeros((8, LANES), F32)
+    small[2, 0:2] = quad[0]
+    small[2, 2:4] = quad[1]
+    five = spread(small[2, 0:8], square(lambda row, col: (row < 96) & (row // 4 == col - 64)))
+    lane8 = lanes_of((8, LANES))
+    five = five * jnp.where((lane8 >= 72) & (lane8 < 80), 1.0 / 64.0, 0.25)
     for out, start, tag in ((zp, 16, 1), (zm, 0, 2)):
         half = spread(
             three,
@@ -263,42 +273,30 @@
         face2 = spread(
             packed2, square(lambda row, col, tag=tag: (col < 16) & (row == 4 * col + tag))
         )
-        out[Z_SMALL:Z_ROWS] = face2[0:8] + turn(face2[8:16], 16, 1)
-
-
-def block_kernel(whole, block, small):
-    three = whole[...]
-    halves = three.reshape(4, 2, 8, LANES)
-    small[0:4, 0:8] = halves[:, 0] + halves[:, 1]
-    summed = small[0:4, pl.ds(0, 4, stride=2), :] + small[0:4, pl.ds(1, 4, stride=2), :]
-    for i in range(4):
-        small[4, 4 * i : 4 * i + 4] = summed[i]
-    four = small[4]
-
-    def pick(part, start):
-        rule = square(
-            lambda row, col: (row // 32 == part)
-            & (col >= start) & (col < start + 16) & (row % 32 // 2 == col - start)
-        )
-        return spread(four, rule)
-
-    both = 0.5 * pick(0, 0) + 0.125 * pick(1, 64)
-    below = 0.5 * pick(2, 0)
-    for i in range(4):
-        rows = slice(4 * i, 4 * i + 4)
-        upper = turn(both[rows], 16 * i, 1) if i == 0 else upper + turn(both[rows], 16 * i, 1)
-        lower = turn(below[rows], 16 * i, 1) if i == 0 else lower + turn(below[rows], 16 * i, 1)
-    small[5, 0:4] = upper
-    small[5, 4:8] = lower
-    block[...] = small[5, 0:8]
+        out[Z_SMALL:Z_ROWS] = face2[0:8] + turn(face2[8:16], 16, 1) + five
+
+
+def second(k_ref, f_ref, x, rows, k_rim, f_rim, lane, period, h):
+    inside, pitch = pl.ds(8, rows), rows + 8
+    k, e = k_ref[rows_of(x + 1, 0, pitch, rows)], f_ref[x + 1, inside]
+    k_up, k_down = z_sides(k, k_rim, x, lane, period)
+    e_up, e_down = z_sides(e, f_rim, x, lane, period)
+    around = [
+        (k_ref[rows_of(x, 0, pitch, rows)], f_ref[x, inside]),
+        (k_ref[rows_of(x + 2, 0, pitch, rows)], f_ref[x + 2, inside]),
+        (k_ref[rows_of(x + 1, -1, pitch, rows)], f_ref[x + 1, pl.ds(7, rows)]),
+        (k_ref[rows_of(x + 1, 1, pitch, rows)], f_ref[x + 1, pl.ds(9, rows)]),
+        (k_up, e_up),
+        (k_down, e_down),
+    ]
+    total = k * sum(en for _, en in around) + sum(kn * en for kn, en in around)
+    return 1.2 * e + 0.5 * h * total
 
 
 def window_kernel(
-    zlo, zhi, whole, sides, sides2, block, own, xp, xm, ye, cf, cf2, blocks, small
+    zlo, zhi, zp, whole, sides, sides2, kp2, ck2, scale2, first2,
+    own, xp, xm, ye, cf, base2, edge2, blocks, small, fp2,
 ):
-    value = block[...]
-    for p in range(128):
-        blocks[p] = value
     lane = lanes_of((64, LANES))
     a_half, c_half = zlo[0:Z_SMALL], zhi[0:Z_SMALL]
     a = jnp.concatenate([a_half, turn(a_half, -48, 1)], 0)
@@ -315,6 +313,33 @@
 
     r, k, s = window(0), window(1), window(2)
     own[0], own[1], own[2] = r, k, s
+
+    even, odd = pl.ds(0, 4, stride=2), pl.ds(1, 4, stride=2)
+
+    def shrink(field, part, weight):
+        halves = field.reshape(4, 2, 8, LANES)
+        small[0:4] = halves[:, 0] + halves[:, 1]
+        summed = small[0:4, even, :] + small[0:4, odd, :]
+        for i in range(4):
+            small[4 + i // 2, 4 * (i % 2) : 4 * (i % 2) + 4] = summed[i]
+
+        def rule(row, col):
+            cell = (row + 16 - BASE) % LANES
+            return (cell < 64) & (cell // 2 == col - 32 * part)
+
+        return spread(flat(small[4:6]), square(rule)) * weight
+
+    four = shrink(r, 0, 0.5) + shrink(k, 1, 0.125) + shrink(s, 2, 0.5)
+    lane8 = lanes_of((8, LANES))
+    triple = jnp.zeros((8, LANES), F32)
+    for n, ref in enumerate((zlo, zp, zhi)):
+        for f in range(3):
+            start = 24 * f + 8 * n
+            moved = turn(ref[Z_SMALL:Z_ROWS], start - 64 - 8 * f, 1)
+            triple = jnp.where((lane8 >= start) & (lane8 < start + 8), moved, triple)
+    for q in range(16):
+        blocks[q, 0:16] = four
+        blocks[q, 16:24] = triple
     main = jnp.where(lane < 42, r, jnp.where(lane < 86, turn(k, 43, 1), turn(s, 86, 1)))
     low = jnp.where(lane == 127, r, jnp.where(lane == 126, k, turn(s, -2, 1)))
     high = jnp.where(lane == 42, r, jnp.where(lane == 43, k, turn(s, 2, 1)))
@@ -322,7 +347,6 @@
     small[...] = ends.reshape(8, 8, LANES)
     ye[0] = small[:, 7, :]
     ye[1] = small[:, 0, :]
-    lane8 = lanes_of((8, LANES))
     for side, out, i in ((0, xp, 7), (1, xm, 0)):
         out[0:X_FACE] = main
         out[X_FACE:X_SEC] = sides[side]
@@ -339,9 +363,23 @@
     def unfold(half):
         return jnp.concatenate([half, turn(half, -16, 1)], 0)
 
-    cf2[...] = rim(
-        unfold(zlo[Z_SMALL:Z_ROWS]), unfold(zhi[Z_SMALL:Z_ROWS]), lambda row: row < 16
-    )
+    rim_f2 = rim(unfold(zlo[Z_SMALL:Z_ROWS]), unfold(zhi[Z_SMALL:Z_ROWS]), lambda row: row < 16)
+    rim_k2 = ck2[...]
+    lane2 = lanes_of((16, LANES))
+    inner2 = pl.ds(8, 16)
+    fp2[1:17, inner2] = first2[...]
+    for x in (0, 17):
+        fp2[x, inner2] = jnp.zeros((16, LANES), F32)
+    fp2[:, 0:8] = jnp.zeros((18, 8, LANES), F32)
+    fp2[:, 24:32] = jnp.zeros((18, 8, LANES), F32)
+    for x in range(16):
+        base2[x] = second(kp2, fp2, x, 16, rim_k2, rim_f2, lane2, 64, scale2[x])
+    for n, (x, step) in enumerate(((0, -1), (15, 1))):
+        k = kp2[rows_of(x + 1, 0, 24, 16)] + kp2[rows_of(x + 1 + step, 0, 24, 16)]
+        edge2[n] = 0.5 * scale2[x] * k
+    for n, (y, step) in enumerate(((0, -1), (15, 1))):
+        k = kp2[pl.ds(32 + y, 16, stride=24), :] + kp2[pl.ds(32 + y + step, 16, stride=24), :]
+        edge2[2 + n] = 0.5 * scale2[:, y, :] * k
 
 
 def columns_kernel(xlo, xhi, xp, sides, sides2, ye, after, yp, ym):
@@ -387,127 +425,88 @@
     return total
 
 
-def planes_kernel(
-    place, blocks_far, four_out,
-    r4, k4, s4, half, l5, l6, c4, c5, c6, c7, w4, blocks, sems,
-):
-    copies = fetch(((blocks_far, blocks),), sems)
-    gx, gy, gz = place[0], place[1], place[2]
-    lane8 = lanes_of((8, LANES))
-    group = lane8 // 16
-
-    def assemble(q, carry):
-        pieces = [blocks[8 * q + g] for g in range(8)]
+def ring_kernel(blocks, ring):
+    for q in range(16):
+        for i in range(2):
+            row = 8 * (2 * (q // 4) + i) + 2 * (q % 4)
+            ring[row : row + 2] = blocks[q, 16 + 2 * i : 18 + 2 * i]
+
+
+def four_kernel(place, blocks, four_out, l4, c4, w4):
+    gx, gy = place[0], place[1]
+    for q in range(16):
         for i in range(4):
-            straight = crossed = jnp.zeros((8, LANES), F32)
-            for g in range(8):
-                moved = turn(pieces[g], 16 * (g - i), 1)
-                straight = jnp.where(group == g, moved, straight)
-                crossed = jnp.where(group == (g + 4) % 8, moved, crossed)
-            x = 4 * (q // 4) + i
-            rows = pl.ds(pl.multiple_of(4 * (q % 4), 4), 4)
-            r4[x, rows] = straight[0:4]
-            s4[x, rows] = straight[4:8]
-            k4[x, rows] = turn(crossed, 64, 1)[0:4]
-        return carry
-
-    for c in range(CHUNKS):
-        copies[c].wait()
-        lax.fori_loop(4 * c, 4 * c + 4, assemble, 0, unroll=True)
-    fields4 = r4[...], k4[...], s4[...]
-    e4 = periodic_setup(*fields4, c4)
-    to_five = square(lambda row, col: row // 2 == col % 64)
+            l4[4 * (q // 4) + i, 4 * (q % 4) : 4 * (q % 4) + 4] = blocks[q, 4 * i : 4 * i + 4]
+    r4 = l4[...]
+    e4 = periodic_setup(r4, turn(r4, 96, 2), turn(r4, 64, 2), c4)
+    e4 = lax.fori_loop(0, COARSE_SWEEPS - 1, lambda _, e: periodic_sweep(e, c4), e4)
+    l4[...] = e4
+    for i in range(4):
+        w4[4 * i : 4 * i + 4] = l4[4 * gx + i, pl.ds(4 * gy, 4)]
+    lane16 = lanes_of((16, LANES))
+    four = jnp.where((lane16 >= 8) & (lane16 < 24), w4[...], 0.0)
+    four_out[...] = spread(four, square(lambda row, col: row == 8 + col // 8))
+
+
+def five_kernel(place, ring, low, high, five_out, l5, l6, c5, c6, c7, w4):
+    gx, gy = place[0], place[1]
+    lane = lanes_of((64, LANES))
+
+    def field(f):
+        mid = turn(ring[...], -8 - 24 * f, 1)
+        up = turn(high[...], 16 - 24 * f, 1)
+        down = turn(low[...], 32 - 24 * f, 1)
+        value = jnp.where(lane < 16, mid, jnp.where(lane < 40, up, down))
+        value = jnp.where((lane >= 56) & (lane < 64), turn(mid, 64, 1), value)
+        value = jnp.where(lane < 64, value, turn(value, 64, 1))
+        return value.reshape(8, 8, LANES)
+
     to_six = square(lambda row, col: (row < 64) & (row // 2 == col % 32))
     mean = square(lambda row, col: row < 32)
 
-    def level_five(field, weight):
-        pairs = field.reshape(8, 2, 16, LANES)
-        half[...] = pairs[:, 0] + pairs[:, 1]
-        summed = half[:, pl.ds(0, 8, stride=2), :] + half[:, pl.ds(1, 8, stride=2), :]
-        return (spread(flat(summed), to_five) * weight).reshape(8, 8, LANES)
-
-    def level_six(field, weight):
-        pairs = field.reshape(4, 2, 8, LANES)
+    def level_six(values, weight):
+        pairs = values.reshape(4, 2, 8, LANES)
         l6[...] = pairs[:, 0] + pairs[:, 1]
         summed = l6[:, pl.ds(0, 4, stride=2), :] + l6[:, pl.ds(1, 4, stride=2), :]
         l6[:, 0:4] = summed
         l6[:, 4:8] = summed
         return (spread(flat(l6[...]), to_six) * weight).reshape(4, 8, LANES)
 
-    def level_seven(field):
-        return (spread(flat(field), mean) * (1.0 / 32.0)).reshape(4, 8, LANES)
-
-    weights = (0.5, 0.125, 0.5)
-    fields5 = [level_five(f, w) for f, w in zip(fields4, weights)]
+    def level_seven(values):
+        return (spread(flat(values), mean) * (1.0 / 32.0)).reshape(4, 8, LANES)
+
+    fields5 = [field(f) for f in range(3)]
+    fields6 = [level_six(v, w) for v, w in zip(fields5, (0.5, 0.125, 0.5))]
     e5 = periodic_setup(*fields5, c5)
-    fields6 = [level_six(f, w) for f, w in zip(fields5, weights)]
     e6 = periodic_setup(*fields6, c6)
-    e7 = periodic_setup(*[level_seven(f) for f in fields6], c7)
+    e7 = periodic_setup(*[level_seven(v) for v in fields6], c7)
 
     def sweep(_, carry):
-        a, b, c, d = carry
-        return (
-            periodic_sweep(a, c4), periodic_sweep(b, c5), periodic_sweep(c, c6),
-            periodic_sweep(d, c7),
-        )
-
-    e4, e5, e6, e7 = lax.fori_loop(0, COARSE_SWEEPS - 1, sweep, (e4, e5, e6, e7))
-
+        b, c, d = carry
+        return periodic_sweep(b, c5), periodic_sweep(c, c6), periodic_sweep(d, c7)
+
+    e5, e6, e7 = lax.fori_loop(0, COARSE_SWEEPS - 1, sweep, (e5, e6, e7))
     l6[...] = e6 + e7
-    six = turn(l6[gx, pl.ds(gy, 1)] + jnp.zeros((8, LANES), F32), 128 - 4 * gz, 1)
+    six = l6[gx, pl.ds(gy, 1)] + jnp.zeros((8, LANES), F32)
     six = spread(six, square(lambda row, col: row == col // 32))
     l5[...] = e5
     w4[...] = jnp.zeros((16, LANES), F32)
     w4[0:2] = l5[2 * gx, pl.ds(2 * gy, 2)]
     w4[2:4] = l5[2 * gx + 1, pl.ds(2 * gy, 2)]
-    five = spread(turn(w4[0:8], 128 - 8 * gz, 1), square(lambda row, col: row == col // 16))
-    five = five + six
-    r4[...] = e4
-    for i in range(4):
-        w4[4 * i : 4 * i + 4] = r4[4 * gx + i, pl.ds(4 * gy, 4)]
-    four = turn(w4[...], lax.rem(128 - 16 * gz, 128), 1)
-    four = spread(four, square(lambda row, col: row == col // 8))
+    five = six + spread(w4[0:8], square(lambda row, col: row == col // 16))
     for i in range(4):
         for j in range(2):
             row = 2 * (i // 2) + j
-            w4[4 * i + 2 * j : 4 * i + 2 * j + 2] = jnp.broadcast_to(
+            five_out[4 * i + 2 * j : 4 * i + 2 * j + 2] = jnp.broadcast_to(
                 five[row : row + 1], (2, LANES)
             )
-    four_out[...] = four + w4[...]
 
 
 def fine_kernel(
-    kp, ck, scale, first, cf, kp2, ck2, scale2, first2, cf2,
-    base, base2, edge, edge2, fp, fp2,
+    kp, ck, scale, first, cf, base, edge, fp
 ):
-    inner, inner2 = pl.ds(8, 32), pl.ds(8, 16)
-    lane2, lane32 = [lanes_of((rows, LANES)) for rows in (16, 32)]
-    fp2[1:17, inner2] = first2[...]
-    for x in (0, 17):
-        fp2[x, inner2] = jnp.zeros((16, LANES), F32)
-    fp2[:, 0:8] = jnp.zeros((18, 8, LANES), F32)
-    fp2[:, 24:32] = jnp.zeros((18, 8, LANES), F32)
-
-    def second(k_ref, f_ref, x, rows, k_rim, f_rim, lane, period, h):
-        inside, pitch = pl.ds(8, rows), rows + 8
-        k, e = k_ref[rows_of(x + 1, 0, pitch, rows)], f_ref[x + 1, inside]
-        k_up, k_down = z_sides(k, k_rim, x, lane, period)
-        e_up, e_down = z_sides(e, f_rim, x, lane, period)
-        around = [
-            (k_ref[rows_of(x, 0, pitch, rows)], f_ref[x, inside]),
-            (k_ref[rows_of(x + 2, 0, pitch, rows)], f_ref[x + 2, inside]),
-            (k_ref[rows_of(x + 1, -1, pitch, rows)], f_ref[x + 1, pl.ds(7, rows)]),
-            (k_ref[rows_of(x + 1, 1, pitch, rows)], f_ref[x + 1, pl.ds(9, rows)]),
-            (k_up, e_up),
-            (k_down, e_down),
-        ]
-        total = k * sum(en for _, en in around) + sum(kn * en for kn, en in around)
-        return 1.2 * e + 0.5 * h * total
-
-    rim_k2, rim_f2 = ck2[...], cf2[...]
-    for x in range(16):
-        base2[x] = second(kp2, fp2, x, 16, rim_k2, rim_f2, lane2, 64, scale2[x])
-
+    inner = pl.ds(8, 32)
+    lane32 = lanes_of((32, LANES))
     for x in (0, 33):
         fp[x, inner] = jnp.zeros((32, LANES), F32)
     blank = jnp.zeros((8, LANES), F32)
@@ -529,23 +528,12 @@
     for n, (x, step) in enumerate(((0, -1), (31, 1))):
         k = kp[rows_of(x + 1, 0, 40, 32)] + kp[rows_of(x + 1 + step, 0, 40, 32)]
         edge[n] = 0.5 * scale[x] * k
-    for n, (x, step) in enumerate(((0, -1), (15, 1))):
-        k = kp2[rows_of(x + 1, 0, 24, 16)] + kp2[rows_of(x + 1 + step, 0, 24, 16)]
-        edge2[n] = 0.5 * scale2[x] * k
     for n, (y, step) in enumerate(((0, -1), (31, 1))):
         k = kp[pl.ds(48 + y, 32, stride=40), :] + kp[pl.ds(48 + y + step, 32, stride=40), :]
         edge[2 + n] = 0.5 * scale[:, y, :] * k
-    for n, (y, step) in enumerate(((0, -1), (15, 1))):
-        k = kp2[pl.ds(32 + y, 16, stride=24), :] + kp2[pl.ds(32 + y + step, 16, stride=24), :]
-        edge2[2 + n] = 0.5 * scale2[:, y, :] * k
-
-
-def finish_kernel(
-    initial_far, own, xlo, xhi, ylo, yhi, four_in, base, base2, edge, edge2,
-    out_far,
-    r3, s3, k3, c3, ea, eb, w3, w2, w32, up, out, initial, sems,
-):
-    inputs = fetch(((initial_far, initial),), sems)
+
+
+def three_kernel(own, xlo, xhi, ylo, yhi, three_out, r3, s3, k3, c3, ea, eb):
     lane8 = lanes_of((8, LANES))
     for ix in range(3):
         for iy, y_ref in enumerate((ylo, None, yhi)):
@@ -629,13 +617,22 @@
     mine = source[8:16, 16:24]
     lane3 = lanes_of((8, 8, LANES))
     three = flat(jnp.where((lane3 >= BASE) & (lane3 < BASE + 32), mine, 0.0))
-    three = spread(three, square(lambda row, col: row == BASE + col // 4))
-    four = four_in[...]
+    three_out[...] = spread(three, square(lambda row, col: row == BASE + col // 4))
+
+
+def finish_kernel(
+    initial_far, three_in, four_in, five_in, xlo, xhi, ylo, yhi, base, base2, edge, edge2,
+    out_far,
+    w3, w2, w32, up, out, initial, sems,
+):
+    inputs = fetch(((initial_far, initial),), sems)
+    lane8 = lanes_of((8, LANES))
+    four = four_in[...] + five_in[...]
     for i in range(8):
         block = four[4 * (i // 2) : 4 * (i // 2) + 4]
         w3[i, pl.ds(0, 4, stride=2), :] = block
         w3[i, pl.ds(1, 4, stride=2), :] = block
-    three = three + flat(w3[...])
+    three = three_in[...] + flat(w3[...])
 
     def beyond(ref, start):
         half = ref[start : start + 8]
@@ -745,47 +742,51 @@
         "residual",
     )(kappa, initial, rhs, sigma, xlo, xhi, ylo, yhi, zlo, zhi)
 
-    (level4,) = local(block_kernel, [shape(8, LANES)], [VM], [(8, 16, LANES)], "block")(whole)
     zlo, zhi = passed(zp, "gz", 1), passed(zm, "gz", -1)
-    own, xp, xm, ye, cf, cf2, blocks = local(
+    own, xp, xm, ye, cf, base2, edge2, blocks = local(
         window_kernel,
         [
             shape(3, 64, LANES), shape(X_ROWS, LANES), shape(X_ROWS, LANES),
-            shape(2, 8, LANES), shape(32, LANES), shape(16, LANES),
-            pltpu.HBM((128, 8, LANES), F32),
+            shape(2, 8, LANES), shape(32, LANES), shape(*block2), shape(4, 16, LANES),
+            shape(16, 24, LANES),
         ],
-        [VM] * 6, [(8, 8, LANES)], "window",
-    )(zlo, zhi, whole, sides, sides2, level4)
+        [VM] * 10, [(8, 8, LANES), (18, 32, LANES)], "window",
+    )(zlo, zhi, zp, whole, sides, sides2, kp2, ck2, scale2, first2)
     xlo, xhi = passed(xp, "gx", 1), passed(xm, "gx", -1)
-    planes = lax.all_to_all(blocks, ("gx", "gy", "gz"), 0, 0)
-    base, base2, edge, edge2 = local(
+    planes = lax.all_to_all(blocks, ("gx", "gy"), 0, 0)
+    base, edge = local(
         fine_kernel,
-        [shape(*block), shape(*block2), shape(4, 32, LANES), shape(4, 16, LANES)],
-        [VM] * 10, [(34, 48, LANES), (18, 32, LANES)], "fine",
-    )(kp, ck, scale, first, cf, kp2, ck2, scale2, first2, cf2)
+        [shape(*block), shape(4, 32, LANES)], [VM] * 5, [(34, 48, LANES)], "fine",
+    )(kp, ck, scale, first, cf)
     yp, ym = local(
         columns_kernel, [shape(Y_ROWS, LANES)] * 2, [VM] * 7, [], "columns"
-    )(xlo, xhi, xp, sides, sides2, ye, edge2)
+    )(xlo, xhi, xp, sides, sides2, ye, edge)
     ylo, yhi = passed(yp, "gy", 1), passed(ym, "gy", -1)
+    (ring,) = local(ring_kernel, [shape(64, LANES)], [VM], [], "ring")(planes)
+    ring_low, ring_high = passed(ring, "gz", 3), passed(ring, "gz", -3)
+    small = shape(16, LANES)
     (four,) = local(
-        planes_kernel, [shape(16, LANES)], [SM, FAR],
-        [
-            block2, block2, block2, (8, 16, LANES), (8, 8, LANES), (4, 8, LANES),
-            (7,) + block2, (7, 8, 8, LANES), (7, 4, 8, LANES), (7, 4, 8, LANES), (16, LANES),
-            (128, 8, LANES),
-        ],
-        "planes", sems=(1, CHUNKS),
-    )(place, pltpu.with_memory_space_constraint(planes, pltpu.HBM))
+        four_kernel, [small], [SM, VM], [block2, (7,) + block2, (16, LANES)], "four"
+    )(place, planes)
     padded3 = (24, 40, LANES)
     block3 = (24, 24, LANES)
+    (three,) = local(
+        three_kernel, [shape(64, LANES)], [VM] * 5,
+        [block3, block3, padded3, (7,) + block3, padded3, padded3], "three",
+    )(own, xlo, xhi, ylo, yhi)
+    (five,) = local(
+        five_kernel, [small], [SM] + [VM] * 3,
+        [
+            (8, 8, LANES), (4, 8, LANES), (7, 8, 8, LANES), (7, 4, 8, LANES), (7, 4, 8, LANES),
+            (16, LANES),
+        ],
+        "five",
+    )(place, ring, ring_low, ring_high)
     return local(
-        finish_kernel, [pltpu.HBM(block, F32)], [FAR] + [VM] * 10,
-        [
-            block3, block3, padded3, (7,) + block3, padded3, padded3,
-            (8, 8, LANES), block2, block2, (16, 32, LANES), block, block,
-        ],
+        finish_kernel, [pltpu.HBM(block, F32)], [FAR] + [VM] * 11,
+        [(8, 8, LANES), block2, block2, (16, 32, LANES), block, block],
         "finish", sems=(2, CHUNKS), out_spec=FAR,
-    )(far[1], own, xlo, xhi, ylo, yhi, four, base, base2, edge, edge2)[0]
+    )(far[1], three, four, five, xlo, xhi, ylo, yhi, base, base2, edge, edge2)[0]
 
 
 def solution(mesh):

time: 52.1 us -> 51 us (0.979)
  Pallas kernels: 19 us -> 17.6 us
    ppermute x12 -> x14, starting transfers between devices: 16 us -> 19.1 us  [passed(): lax.ppermute(value, axis, [(i, (i + step) % count) for i in range(count)])]
    all_to_all x1, starting transfers between devices: 8.55 us -> 5.82 us  [on_device(): planes = lax.all_to_all(blocks, ('gx', 'gy'), 0, 0)]
    pallas_call x4 -> x6, Pallas kernels: 11.5 us -> 9.16 us  [the longest x1 2.02 us: on_device(): local(finish_kernel, [pltpu.HBM(block, F32)], [FAR] + [VM] * 11, [(8, 8,...]
    all_to_all x1, waiting for transfers between devices: 1.73 us -> 0.01 us  [on_device(): planes = lax.all_to_all(blocks, ('gx', 'gy'), 0, 0)]
    ppermute x12 -> x14, waiting for transfers between devices: 6.44 us -> 8.04 us  [passed(): lax.ppermute(value, axis, [(i, (i + step) % count) for i in range(count)])]
    pallas_call x1, Pallas kernels: 1.05 us -> 1.95 us  [on_device(): local(window_kernel, [shape(3, 64, LANES), shape(X_ROWS, LANES), shape(X_...]
  transfers between devices with their start and end apart: 13 -> 15, of which waited for: 6 -> 5; matrix products, arithmetic and copies ran while one was open for 0% -> 0% of each run, Pallas kernels for 18% -> 13%
where the time goes in v5:
time: 51 us; the launch traced here: 50.7 us
  starting transfers between devices  24.9 us (49%)
  Pallas kernels  17.6 us (35%)
  waiting for transfers between devices  8.04 us (16%)
    ppermute x14, starting transfers between devices, passed(): lax.ppermute(value, axis, [(i, (i + step) % count) for i in range(count)])  19.1 us
    ppermute x14, waiting for transfers between devices, passed(): lax.ppermute(value, axis, [(i, (i + step) % count) for i in range(count)])  8.04 us
    all_to_all x1, starting transfers between devices, on_device(): planes = lax.all_to_all(blocks, ('gx', 'gy'), 0, 0)  5.82 us
    pallas_call x1, Pallas kernels, on_device(): local(residual_kernel, [shape(1368, LANES), shape(32, LANES), shape(*bloc...  3.49 us
    pallas_call x1, Pallas kernels, on_device(): local(finish_kernel, [pltpu.HBM(block, F32)], [FAR] + [VM] * 11, [(8, 8,...  2.02 us
    pallas_call x1, Pallas kernels, on_device(): local(five_kernel, [small], [SM] + [VM] * 3, [(8, 8, LANES), (4, 8, LANES...  2.01 us
    pallas_call x1, Pallas kernels, on_device(): local(window_kernel, [shape(3, 64, LANES), shape(X_ROWS, LANES), shape(X_...  1.95 us
    pallas_call x1, Pallas kernels, on_device(): local(four_kernel, [small], [SM, VM], [block2, (7,) + block2, (16, LANES)...  1.89 us
  transfers between devices with their start and end apart: 15, of which 5 were waited for; matrix products, arithmetic and copies ran while one was open for 0% of the time, Pallas kernels for 13%

profile of v5, /device:TPU:1, one launch (start us, length us, event | category | flops | bytes accessed | tf_op | source)
XLA Modules:
  0.0 50.7 jit_solution(4987135150734586384)
XLA Ops:
  0.0 1.6 %faces.1 = (f32[3,32,128]{2,1,0:T(8,128)S(1)}, f32[3,32,128]{2,1,0:T(8,128)S(1)}, f32[3,32,128]{2,1,0:T(8,128)S(1)}, f32[3,32,128]{2,1,0:T(8,128)S(1)}, f32[2,32...) custom-call(f32[32,32,128]{2,1,0:T(8,128)} %kappa_far.1, f32[32,32,128]{2,1,0:T(8,128)} %initial_far.3), custom_call_target="tpu_custom_call" | custom-call | tf_op jit(solution)/shard_map/faces/pallas_call | solution.py:718
  1.6 2.6 %collective-permute-start.4 = (f32[2,32,128]{2,1,0:T(8,128)S(1)}, f32[2,32,128]{2,1,0:T(8,128)S(1)}, u32[]{:S(2)}, u32[]{:S(2)}) collective-permute-start(f32[2,32,128]{2,1,0:T(8,128)S(1)} %get-tuple-element.41.edge), channel_id=1, source_target_pairs={{0,1},{1,2},{2,3},{3,4},{4,5},{5,6},{6,7},{7,0},{8,9},{9,10},{10,1... | collective-permute-start | bytes 98312 | tf_op jit(solution)/shard_map/ppermute | solution.py:709
  4.2 1.3 %collective-permute-start = (f32[3,32,128]{2,1,0:T(8,128)S(1)}, f32[3,32,128]{2,1,0:T(8,128)S(1)}, u32[]{:S(2)}, u32[]{:S(2)}) collective-permute-start(f32[3,32,128]{2,1,0:T(8,128)S(1)} %get-tuple-element.44), channel_id=1, source_target_pairs={{0,32},{32,64},{64,96},{96,0},{1,33},{33,65},{65,97},{97,1},{2,34}... | collective-permute-start | bytes 147464 | tf_op jit(solution)/shard_map/ppermute | solution.py:709
  5.5 1.4 %collective-permute-start.1 = (f32[3,32,128]{2,1,0:T(8,128)S(1)}, f32[3,32,128]{2,1,0:T(8,128)S(1)}, u32[]{:S(2)}, u32[]{:S(2)}) collective-permute-start(f32[3,32,128]{2,1,0:T(8,128)S(1)} %get-tuple-element.45), channel_id=1, source_target_pairs={{0,96},{32,0},{64,32},{96,64},{1,97},{33,1},{65,33},{97,65},{2,98}... | collective-permute-start | bytes 147464 | tf_op jit(solution)/shard_map/ppermute | solution.py:709
  7.0 1.6 %collective-permute-start.2 = (f32[3,32,128]{2,1,0:T(8,128)S(1)}, f32[3,32,128]{2,1,0:T(8,128)S(1)}, u32[]{:S(2)}, u32[]{:S(2)}) collective-permute-start(f32[3,32,128]{2,1,0:T(8,128)S(1)} %get-tuple-element.46), channel_id=1, source_target_pairs={{0,8},{8,16},{16,24},{24,0},{1,9},{9,17},{17,25},{25,1},{2,10},{10... | collective-permute-start | bytes 147464 | tf_op jit(solution)/shard_map/ppermute | solution.py:709
  8.6 2.1 %collective-permute-start.3 = (f32[3,32,128]{2,1,0:T(8,128)S(1)}, f32[3,32,128]{2,1,0:T(8,128)S(1)}, u32[]{:S(2)}, u32[]{:S(2)}) collective-permute-start(f32[3,32,128]{2,1,0:T(8,128)S(1)} %get-tuple-element.47), channel_id=1, source_target_pairs={{0,24},{8,0},{16,8},{24,16},{1,25},{9,1},{17,9},{25,17},{2,26},{10... | collective-permute-start | bytes 147464 | tf_op jit(solution)/shard_map/ppermute | solution.py:709
  10.7 1.4 %load.1 = (f32[32,32,128]{2,1,0:T(8,128)S(1)}, f32[32,32,128]{2,1,0:T(8,128)S(1)}) custom-call(f32[32,32,128]{2,1,0:T(8,128)} %rhs_far.1, f32[32,32,128]{2,1,0:T(8,128)} %sigma_far.1, f32[2,32,128]{2,1,0:T(8,128)S(1)} %get-tuple-element.41.edge), custom_call_target="tpu_custom_call" | custom-call | tf_op jit(solution)/shard_map/load/pallas_call | solution.py:723
  12.1 2.0 %collective-permute-done.5.zhi = f32[2,32,128]{2,1,0:T(8,128)S(1)} collective-permute-done((f32[2,32,128]{2,1,0:T(8,128)S(1)}, f32[2,32,128]{2,1,0:T(8,128)S(1)}, u32[]{:S(2)}, u32[]{:S(2)}) %collective-permute-start.5) | collective-permute-done | bytes 32800 | tf_op jit(solution)/shard_map/ppermute | solution.py:709
  14.1 3.5 %residual.1 = (f32[1368,128]{1,0:T(8,128)S(1)}, f32[32,128]{1,0:T(8,128)S(1)}, f32[32,32,128]{2,1,0:T(8,128)S(1)}, f32[32,32,128]{2,1,0:T(8,128)S(1)}, f32[40,12...) custom-call(f32[32,32,128]{2,1,0:T(8,128)S(1)} %get-tuple-element.39, ...), custom_call_target="tpu_custom_call" | custom-call | tf_op jit(solution)/shard_map/residual/pallas_call | solution.py:729
  18.8 2.0 %collective-permute-done.7.zhi = f32[40,128]{1,0:T(8,128)S(1)} collective-permute-done((f32[40,128]{1,0:T(8,128)S(1)}, f32[40,128]{1,0:T(8,128)S(1)}, u32[]{:S(2)}, u32[]{:S(2)}) %collective-permute-start.7) | collective-permute-done | bytes 20512 | tf_op jit(solution)/shard_map/ppermute | solution.py:709
  20.9 2.0 %window.1 = (f32[3,64,128]{2,1,0:T(8,128)S(1)}, f32[112,128]{1,0:T(8,128)S(1)}, f32[112,128]{1,0:T(8,128)S(1)}, f32[2,8,128]{2,1,0:T(8,128)S(1)}, f32[32,128]{1,...) custom-call(f32[40,128]{1,0:T(8,128)S(1)} %collective-permute-done.6.zlo, ...), custom_call_target="tpu_custom_call" | custom-call | tf_op jit(solution)/shard_map/window/pallas_call | solution.py:746
  22.8 5.8 %all-to-all-start = ((f32[16,24,128]{2,1,0:T(8,128)}), f32[16,24,128]{2,1,0:T(8,128)S(1)}, u32[]{:S(2)}, u32[]{:S(2)}) async-start(f32[16,24,128]{2,1,0:T(8,128)} %get-tuple-element.69), calls=%async_computation | async-start | bytes 393216 | tf_op jit(solution)/shard_map/all_to_all | solution.py:756
  28.6 1.4 %collective-permute-start.8 = (f32[112,128]{1,0:T(8,128)S(1)}, f32[112,128]{1,0:T(8,128)S(1)}, u32[]{:S(2)}, u32[]{:S(2)}) collective-permute-start(f32[112,128]{1,0:T(8,128)S(1)} %get-tuple-element.58.xp), channel_id=1, source_target_pairs={{0,32},{32,64},{64,96},{96,0},{1,33},{33,65},{65,97},{97,1},{2,34}... | collective-permute-start | bytes 172040 | tf_op jit(solution)/shard_map/ppermute | solution.py:709
  30.0 1.4 %collective-permute-start.9 = (f32[112,128]{1,0:T(8,128)S(1)}, f32[112,128]{1,0:T(8,128)S(1)}, u32[]{:S(2)}, u32[]{:S(2)}) collective-permute-start(f32[112,128]{1,0:T(8,128)S(1)} %get-tuple-element.59), channel_id=1, source_target_pairs={{0,96},{32,0},{64,32},{96,64},{1,97},{33,1},{65,33},{97,65},{2,98}... | collective-permute-start | bytes 172040 | tf_op jit(solution)/shard_map/ppermute | solution.py:709
  31.4 1.8 %fine.1 = (f32[32,32,128]{2,1,0:T(8,128)S(1)}, f32[4,32,128]{2,1,0:T(8,128)S(1)}) custom-call(f32[1368,128]{1,0:T(8,128)S(1)} %get-tuple-element.61.kp, f32[32,128]{1,0:T(8,128)S(1)} %get-tuple-element.62.ck, f32[32,32,128]{2,1,0:T(8,128)S(1)} %get-tuple-element.63.scale, f32[32,32,128]{2,1,0:T(8,128)S(1)} %get-tuple-element.64.first, ...), custom_call_target="tpu_custom_call" | custom-call | tf_op jit(solution)/shard_map/fine/pallas_call | solution.py:757
  33.2 1.9 %collective-permute-done.8.xlo = f32[112,128]{1,0:T(8,128)S(1)} collective-permute-done((f32[112,128]{1,0:T(8,128)S(1)}, f32[112,128]{1,0:T(8,128)S(1)}, u32[]{:S(2)}, u32[]{:S(2)}) %collective-permute-start.8) | collective-permute-done | bytes 57376 | tf_op jit(solution)/shard_map/ppermute | solution.py:709
  35.1 1.3 %collective-permute-start.10 = (f32[240,128]{1,0:T(8,128)S(1)}, f32[240,128]{1,0:T(8,128)S(1)}, u32[]{:S(2)}, u32[]{:S(2)}) collective-permute-start(f32[240,128]{1,0:T(8,128)S(1)} %get-tuple-element.67), channel_id=1, source_target_pairs={{0,8},{8,16},{16,24},{24,0},{1,9},{9,17},{17,25},{25,1},{2,10},{10... | collective-permute-start | bytes 368648 | tf_op jit(solution)/shard_map/ppermute | solution.py:709
  36.4 1.5 %collective-permute-start.11 = (f32[240,128]{1,0:T(8,128)S(1)}, f32[240,128]{1,0:T(8,128)S(1)}, u32[]{:S(2)}, u32[]{:S(2)}) collective-permute-start(f32[240,128]{1,0:T(8,128)S(1)} %get-tuple-element.68), channel_id=1, source_target_pairs={{0,24},{8,0},{16,8},{24,16},{1,25},{9,1},{17,9},{25,17},{2,26},{10... | collective-permute-start | bytes 368648 | tf_op jit(solution)/shard_map/ppermute | solution.py:709
  37.9 4.0 %collective-permute-start.12 = (f32[64,128]{1,0:T(8,128)S(1)}, f32[64,128]{1,0:T(8,128)S(1)}, u32[]{:S(2)}, u32[]{:S(2)}) collective-permute-start(f32[64,128]{1,0:T(8,128)S(1)} %ring.1), channel_id=1, source_target_pairs={{0,3},{1,4},{2,5},{3,6},{4,7},{5,0},{6,1},{7,2},{8,11},{9,12},{10,... | collective-permute-start | bytes 98312 | tf_op jit(solution)/shard_map/ppermute | solution.py:709
  41.9 1.4 %three.1.three_in = f32[64,128]{1,0:T(8,128)S(1)} custom-call(f32[3,64,128]{2,1,0:T(8,128)S(1)} %get-tuple-element.57.own, f32[112,128]{1,0:T(8,128)S(1)} %collective-permute-done.8.xlo, f32[112,128]{1,0:T(8,128)S(1)} %collective-permute-done.9.xhi, f32[240,128]{1,0:T(8,128)S(1)} %collective-permute-done.10.ylo, f32[240,128]{1,0:T(8,128)S(1)} %collective-permute-done.11.yhi), custom_call_target="tpu_custom_call" | custom-call | tf_op jit(solution)/shard_map/three/pallas_call | solution.py:773
  43.4 1.9 %four.1.four_in = f32[16,128]{1,0:T(8,128)S(1)} custom-call(s32[3]{0:T(128)S(1)} %pad_add_fusion.place, f32[16,24,128]{2,1,0:T(8,128)S(1)} %all-to-all-done.blocks), custom_call_target="tpu_custom_call" | custom-call | tf_op jit(solution)/shard_map/four/pallas_call | solution.py:768
  45.3 1.4 %collective-permute-done.13.high = f32[64,128]{1,0:T(8,128)S(1)} collective-permute-done((f32[64,128]{1,0:T(8,128)S(1)}, f32[64,128]{1,0:T(8,128)S(1)}, u32[]{:S(2)}, u32[]{:S(2)}) %collective-permute-start.13) | collective-permute-done | bytes 32800 | tf_op jit(solution)/shard_map/ppermute | solution.py:709
  46.7 2.0 %five.1.five_in = f32[16,128]{1,0:T(8,128)S(1)} custom-call(s32[3]{0:T(128)S(1)} %pad_add_fusion.place, f32[64,128]{1,0:T(8,128)S(1)} %ring.1, f32[64,128]{1,0:T(8,128)S(1)} %collective-permute-done.12.low, f32[64,128]{1,0:T(8,128)S(1)} %collective-permute-done.13.high), custom_call_target="tpu_custom_call" | custom-call | tf_op jit(solution)/shard_map/five/pallas_call | solution.py:777
  48.7 2.0 %finish.1 = f32[32,32,128]{2,1,0:T(8,128)} custom-call(f32[32,32,128]{2,1,0:T(8,128)} %initial_far.3, f32[64,128]{1,0:T(8,128)S(1)} %three.1.three_in, f32[16,128]{1,0:T(8,128)S(1)} %four.1.four_in, f32[16,128]{1,0:T(8,128)S(1)} %five.1.five_in, f32[112,128]{1,0:T(8,128)S(1)} %collective-permute-done.8.xlo, f32[112,128]{1,0:T(8,128)S(1)} %collective-permute-done.9.xhi, ...), custom_call_target="tpu_custom_call" | custom-call | tf_op jit(solution)/shard_map/finish/pallas_call | solution.py:785
  (18 shorter events, 1.4 us)
Async XLA Ops:
  1.6 9.1 %collective-permute-start.4 = (f32[2,32,128]{2,1,0:T(8,128)S(1)}, f32[2,32,128]{2,1,0:T(8,128)S(1)}, u32[]{:S(2)}, u32[]{:S(2)}) collective-permute-start(f32[2,32,128]{2,1,0:T(8,128)S(1)} %get-tuple-element.41.edge), channel_id=1, source_target_pairs={{0,1},{1,2},{2,3},{3,4},{4,5},{5,6},{6,7},{7,0},{8,9},{9,10},{10,1... | collective-permute-start | bytes 98312 | tf_op jit(solution)/shard_map/ppermute | solution.py:709
  4.2 9.8 %collective-permute-start = (f32[3,32,128]{2,1,0:T(8,128)S(1)}, f32[3,32,128]{2,1,0:T(8,128)S(1)}, u32[]{:S(2)}, u32[]{:S(2)}) collective-permute-start(f32[3,32,128]{2,1,0:T(8,128)S(1)} %get-tuple-element.44), channel_id=1, source_target_pairs={{0,32},{32,64},{64,96},{96,0},{1,33},{33,65},{65,97},{97,1},{2,34}... | collective-permute-start | bytes 147464 | tf_op jit(solution)/shard_map/ppermute | solution.py:709
  5.5 8.6 %collective-permute-start.1 = (f32[3,32,128]{2,1,0:T(8,128)S(1)}, f32[3,32,128]{2,1,0:T(8,128)S(1)}, u32[]{:S(2)}, u32[]{:S(2)}) collective-permute-start(f32[3,32,128]{2,1,0:T(8,128)S(1)} %get-tuple-element.45), channel_id=1, source_target_pairs={{0,96},{32,0},{64,32},{96,64},{1,97},{33,1},{65,33},{97,65},{2,98}... | collective-permute-start | bytes 147464 | tf_op jit(solution)/shard_map/ppermute | solution.py:709
  7.0 7.1 %collective-permute-start.2 = (f32[3,32,128]{2,1,0:T(8,128)S(1)}, f32[3,32,128]{2,1,0:T(8,128)S(1)}, u32[]{:S(2)}, u32[]{:S(2)}) collective-permute-start(f32[3,32,128]{2,1,0:T(8,128)S(1)} %get-tuple-element.46), channel_id=1, source_target_pairs={{0,8},{8,16},{16,24},{24,0},{1,9},{9,17},{17,25},{25,1},{2,10},{10... | collective-permute-start | bytes 147464 | tf_op jit(solution)/shard_map/ppermute | solution.py:709
  8.6 5.5 %collective-permute-start.3 = (f32[3,32,128]{2,1,0:T(8,128)S(1)}, f32[3,32,128]{2,1,0:T(8,128)S(1)}, u32[]{:S(2)}, u32[]{:S(2)}) collective-permute-start(f32[3,32,128]{2,1,0:T(8,128)S(1)} %get-tuple-element.47), channel_id=1, source_target_pairs={{0,24},{8,0},{16,8},{24,16},{1,25},{9,1},{17,9},{25,17},{2,26},{10... | collective-permute-start | bytes 147464 | tf_op jit(solution)/shard_map/ppermute | solution.py:709
  10.7 3.3 %collective-permute-start.5 = (f32[2,32,128]{2,1,0:T(8,128)S(1)}, f32[2,32,128]{2,1,0:T(8,128)S(1)}, u32[]{:S(2)}, u32[]{:S(2)}) collective-permute-start(f32[2,32,128]{2,1,0:T(8,128)S(1)} %get-tuple-element.41.edge), channel_id=1, source_target_pairs={{0,7},{1,0},{2,1},{3,2},{4,3},{5,4},{6,5},{7,6},{8,15},{9,8},{10,9... | collective-permute-start | bytes 98312 | tf_op jit(solution)/shard_map/ppermute | solution.py:709
  17.6 1.2 %collective-permute-start.6 = (f32[40,128]{1,0:T(8,128)S(1)}, f32[40,128]{1,0:T(8,128)S(1)}, u32[]{:S(2)}, u32[]{:S(2)}) collective-permute-start(f32[40,128]{1,0:T(8,128)S(1)} %get-tuple-element.48.zp), channel_id=1, source_target_pairs={{0,1},{1,2},{2,3},{3,4},{4,5},{5,6},{6,7},{7,0},{8,9},{9,10},{10,1... | collective-permute-start | bytes 61448 | tf_op jit(solution)/shard_map/ppermute | solution.py:709
  17.6 3.2 %collective-permute-start.7 = (f32[40,128]{1,0:T(8,128)S(1)}, f32[40,128]{1,0:T(8,128)S(1)}, u32[]{:S(2)}, u32[]{:S(2)}) collective-permute-start(f32[40,128]{1,0:T(8,128)S(1)} %get-tuple-element.49), channel_id=1, source_target_pairs={{0,7},{1,0},{2,1},{3,2},{4,3},{5,4},{6,5},{7,6},{8,15},{9,8},{10,9... | collective-permute-start | bytes 61448 | tf_op jit(solution)/shard_map/ppermute | solution.py:709
  22.8 15.1 %all-to-all-start = ((f32[16,24,128]{2,1,0:T(8,128)}), f32[16,24,128]{2,1,0:T(8,128)S(1)}, u32[]{:S(2)}, u32[]{:S(2)}) async-start(f32[16,24,128]{2,1,0:T(8,128)} %get-tuple-element.69), calls=%async_computation | async-start | bytes 393216 | tf_op jit(solution)/shard_map/all_to_all | solution.py:756
  28.6 6.5 %collective-permute-start.8 = (f32[112,128]{1,0:T(8,128)S(1)}, f32[112,128]{1,0:T(8,128)S(1)}, u32[]{:S(2)}, u32[]{:S(2)}) collective-permute-start(f32[112,128]{1,0:T(8,128)S(1)} %get-tuple-element.58.xp), channel_id=1, source_target_pairs={{0,32},{32,64},{64,96},{96,0},{1,33},{33,65},{65,97},{97,1},{2,34}... | collective-permute-start | bytes 172040 | tf_op jit(solution)/shard_map/ppermute | solution.py:709
  30.0 5.1 %collective-permute-start.9 = (f32[112,128]{1,0:T(8,128)S(1)}, f32[112,128]{1,0:T(8,128)S(1)}, u32[]{:S(2)}, u32[]{:S(2)}) collective-permute-start(f32[112,128]{1,0:T(8,128)S(1)} %get-tuple-element.59), channel_id=1, source_target_pairs={{0,96},{32,0},{64,32},{96,64},{1,97},{33,1},{65,33},{97,65},{2,98}... | collective-permute-start | bytes 172040 | tf_op jit(solution)/shard_map/ppermute | solution.py:709
  35.1 6.8 %collective-permute-start.10 = (f32[240,128]{1,0:T(8,128)S(1)}, f32[240,128]{1,0:T(8,128)S(1)}, u32[]{:S(2)}, u32[]{:S(2)}) collective-permute-start(f32[240,128]{1,0:T(8,128)S(1)} %get-tuple-element.67), channel_id=1, source_target_pairs={{0,8},{8,16},{16,24},{24,0},{1,9},{9,17},{17,25},{25,1},{2,10},{10... | collective-permute-start | bytes 368648 | tf_op jit(solution)/shard_map/ppermute | solution.py:709
  36.4 5.6 %collective-permute-start.11 = (f32[240,128]{1,0:T(8,128)S(1)}, f32[240,128]{1,0:T(8,128)S(1)}, u32[]{:S(2)}, u32[]{:S(2)}) collective-permute-start(f32[240,128]{1,0:T(8,128)S(1)} %get-tuple-element.68), channel_id=1, source_target_pairs={{0,24},{8,0},{16,8},{24,16},{1,25},{9,1},{17,9},{25,17},{2,26},{10... | collective-permute-start | bytes 368648 | tf_op jit(solution)/shard_map/ppermute | solution.py:709
  37.9 7.4 %collective-permute-start.12 = (f32[64,128]{1,0:T(8,128)S(1)}, f32[64,128]{1,0:T(8,128)S(1)}, u32[]{:S(2)}, u32[]{:S(2)}) collective-permute-start(f32[64,128]{1,0:T(8,128)S(1)} %ring.1), channel_id=1, source_target_pairs={{0,3},{1,4},{2,5},{3,6},{4,7},{5,0},{6,1},{7,2},{8,11},{9,12},{10,... | collective-permute-start | bytes 98312 | tf_op jit(solution)/shard_map/ppermute | solution.py:709
  41.8 4.8 %collective-permute-start.13 = (f32[64,128]{1,0:T(8,128)S(1)}, f32[64,128]{1,0:T(8,128)S(1)}, u32[]{:S(2)}, u32[]{:S(2)}) collective-permute-start(f32[64,128]{1,0:T(8,128)S(1)} %ring.1), channel_id=1, source_target_pairs={{0,5},{1,6},{2,7},{3,0},{4,1},{5,2},{6,3},{7,4},{8,13},{9,14},{10,... | collective-permute-start | bytes 98312 | tf_op jit(solution)/shard_map/ppermute | solution.py:709

commit v6 on v5

--- a/solution.py
+++ b/solution.py
@@ -14,7 +14,7 @@
 Z_SMALL, Z_ROWS = 32, 40
 X_FACE, X_SEC, X_ENDS, X_ROWS = 64, 96, 104, 112
 Y_FACE, Y_SEC, Y_ENDS, Y_ROWS = 192, 224, 232, 240
-CHUNKS = 4
+CHUNKS = 2
 BASE = 5
 
 
@@ -123,8 +123,8 @@
 
 def residual_kernel(
     kappa, initial, rhs, sigma, xlo, xhi, ylo, yhi, zlo, zhi,
-    kp, ck, scale, first, zp, zm, whole, sides, kp2, ck2, scale2, first2, sides2,
-    vp, pair_r, pair_k, pair_s, rims, small,
+    kp, ck, scale, first, zp, zm, fives, whole, sides_x, sides_y, kp2, ck2, scale2, first2,
+    sides2_x, sides2_y, vp, pair_r, pair_k, pair_s, rims, small,
 ):
     lane = lanes_of((32, LANES))
     inner = pl.ds(8, 32)
@@ -182,11 +182,11 @@
         pair_s[i] = s0 + s1
         return packed
 
-    packed = lax.fori_loop(0, 16, two, jnp.zeros((32, LANES), F32), unroll=2)
-    sides[0] = first[31]
-    sides[1] = first[0]
-    sides[2] = first[:, 31, :]
-    sides[3] = first[:, 0, :]
+    packed = lax.fori_loop(0, 16, two, jnp.zeros((32, LANES), F32), unroll=3)
+    sides_x[0] = first[31]
+    sides_x[1] = first[0]
+    sides_y[0] = first[:, 31, :]
+    sides_y[1] = first[:, 0, :]
 
     even, odd = pl.ds(0, 16, stride=2), pl.ds(1, 16, stride=2)
     to_two = square(lambda row, col: row // 2 == col % 64)
@@ -234,10 +234,10 @@
         scale2[x] = h
         first2[x] = e
         packed2 = jnp.where(lane2 // 4 == x, turn(e, 4 * x + 2, 1), packed2)
-    sides2[0] = first2[15]
-    sides2[1] = first2[0]
-    sides2[2] = first2[:, 15, :]
-    sides2[3] = first2[:, 0, :]
+    sides2_x[0] = first2[15]
+    sides2_x[1] = first2[0]
+    sides2_y[0] = first2[:, 15, :]
+    sides2_y[1] = first2[:, 0, :]
 
     even8, odd8 = pl.ds(0, 8, stride=2), pl.ds(1, 8, stride=2)
 
@@ -260,6 +260,7 @@
     five = spread(small[2, 0:8], square(lambda row, col: (row < 96) & (row // 4 == col - 64)))
     lane8 = lanes_of((8, LANES))
     five = five * jnp.where((lane8 >= 72) & (lane8 < 80), 1.0 / 64.0, 0.25)
+    fives[...] = five
     for out, start, tag in ((zp, 16, 1), (zm, 0, 2)):
         half = spread(
             three,
@@ -294,8 +295,8 @@
 
 
 def window_kernel(
-    zlo, zhi, zp, whole, sides, sides2, kp2, ck2, scale2, first2,
-    own, xp, xm, ye, cf, base2, edge2, blocks, small, fp2,
+    zlo, zhi, fives, whole, sides, sides2,
+    own, xp, xm, ye, cf, cf2, blocks, small,
 ):
     lane = lanes_of((64, LANES))
     a_half, c_half = zlo[0:Z_SMALL], zhi[0:Z_SMALL]
@@ -331,15 +332,13 @@
 
     four = shrink(r, 0, 0.5) + shrink(k, 1, 0.125) + shrink(s, 2, 0.5)
     lane8 = lanes_of((8, LANES))
-    triple = jnp.zeros((8, LANES), F32)
-    for n, ref in enumerate((zlo, zp, zhi)):
-        for f in range(3):
-            start = 24 * f + 8 * n
-            moved = turn(ref[Z_SMALL:Z_ROWS], start - 64 - 8 * f, 1)
-            triple = jnp.where((lane8 >= start) & (lane8 < start + 8), moved, triple)
+    for n, ref in enumerate((zlo[Z_SMALL:Z_ROWS], fives[...], zhi[Z_SMALL:Z_ROWS])):
+        small[4 + n // 2, 4 * (n % 2) : 4 * (n % 2) + 4] = turn(ref, 32, 1)[0:4]
+    small[5, 4:8] = jnp.zeros((4, LANES), F32)
+    lane4 = lanes_of((16, LANES))
+    four = jnp.where((lane4 < 96) | (lane4 >= 120), four, flat(small[4:6]))
     for q in range(16):
-        blocks[q, 0:16] = four
-        blocks[q, 16:24] = triple
+        blocks[q] = four
     main = jnp.where(lane < 42, r, jnp.where(lane < 86, turn(k, 43, 1), turn(s, 86, 1)))
     low = jnp.where(lane == 127, r, jnp.where(lane == 126, k, turn(s, -2, 1)))
     high = jnp.where(lane == 42, r, jnp.where(lane == 43, k, turn(s, 2, 1)))
@@ -363,7 +362,11 @@
     def unfold(half):
         return jnp.concatenate([half, turn(half, -16, 1)], 0)
 
-    rim_f2 = rim(unfold(zlo[Z_SMALL:Z_ROWS]), unfold(zhi[Z_SMALL:Z_ROWS]), lambda row: row < 16)
+    cf2[...] = rim(unfold(zlo[Z_SMALL:Z_ROWS]), unfold(zhi[Z_SMALL:Z_ROWS]), lambda row: row < 16)
+
+
+def second_kernel(kp2, ck2, scale2, first2, cf2, base2, edge2, fp2):
+    rim_f2 = cf2[...]
     rim_k2 = ck2[...]
     lane2 = lanes_of((16, LANES))
     inner2 = pl.ds(8, 16)
@@ -372,8 +375,11 @@
         fp2[x, inner2] = jnp.zeros((16, LANES), F32)
     fp2[:, 0:8] = jnp.zeros((18, 8, LANES), F32)
     fp2[:, 24:32] = jnp.zeros((18, 8, LANES), F32)
-    for x in range(16):
+    def slab(x, carry):
         base2[x] = second(kp2, fp2, x, 16, rim_k2, rim_f2, lane2, 64, scale2[x])
+        return carry
+
+    lax.fori_loop(0, 16, slab, 0, unroll=8)
     for n, (x, step) in enumerate(((0, -1), (15, 1))):
         k = kp2[rows_of(x + 1, 0, 24, 16)] + kp2[rows_of(x + 1 + step, 0, 24, 16)]
         edge2[n] = 0.5 * scale2[x] * k
@@ -382,14 +388,14 @@
         edge2[2 + n] = 0.5 * scale2[:, y, :] * k
 
 
-def columns_kernel(xlo, xhi, xp, sides, sides2, ye, after, yp, ym):
+def columns_kernel(xlo, xhi, xp, sides, sides2, ye, after, after2, yp, ym):
     lane8 = lanes_of((8, LANES))
     for side, out in ((0, yp), (1, ym)):
         out[0:64] = xlo[0:64]
         out[64:128] = xp[0:64]
         out[128:192] = xhi[0:64]
-        out[Y_FACE:Y_SEC] = sides[2 + side]
-        face = sides2.at[2 + side]
+        out[Y_FACE:Y_SEC] = sides[side]
+        face = sides2.at[side]
         out[Y_SEC:Y_ENDS] = jnp.where(lane8 < 64, face[0:8], face[8:16])
         out[Y_ENDS:Y_ROWS] = ye[side]
 
@@ -429,77 +435,81 @@
     for q in range(16):
         for i in range(2):
             row = 8 * (2 * (q // 4) + i) + 2 * (q % 4)
-            ring[row : row + 2] = blocks[q, 16 + 2 * i : 18 + 2 * i]
-
-
-def four_kernel(place, blocks, four_out, l4, c4, w4):
+            for n in range(3):
+                source = blocks[q, 4 * n + 2 * i : 4 * n + 2 * i + 2]
+                ring[n, row : row + 2] = source
+
+
+def planes_kernel(
+    place, blocks, ring, low, high, four_out, l4, l5, l6, c4, c5, c6, c7, w4
+):
     gx, gy = place[0], place[1]
     for q in range(16):
         for i in range(4):
             l4[4 * (q // 4) + i, 4 * (q % 4) : 4 * (q % 4) + 4] = blocks[q, 4 * i : 4 * i + 4]
+    lane = lanes_of((8, 8, LANES))
+
+    def field(f):
+        value = jnp.zeros((8, 8, LANES), F32)
+        for ref, first in ((high, 2), (low, -4), (ring, -1)):
+            for n in range(3):
+                start = 8 * (first + n) % 64
+                moved = turn(ref[n].reshape(8, 8, LANES), start - 96 - 8 * f, 2)
+                value = jnp.where(lane // 8 == start // 8, moved, value)
+        return jnp.where(lane < 64, value, turn(value, 64, 2))
+
+    to_six = square(lambda row, col: (row < 64) & (row // 2 == col % 32))
+    mean = square(lambda row, col: row < 32)
+
+    def level_six(values, weight, n):
+        pairs = values.reshape(4, 2, 8, LANES)
+        l6[n] = pairs[:, 0] + pairs[:, 1]
+        summed = l6[n, :, pl.ds(0, 4, stride=2), :] + l6[n, :, pl.ds(1, 4, stride=2), :]
+        l6[n, :, 0:4] = summed
+        l6[n, :, 4:8] = summed
+        return (spread(flat(l6[n]), to_six) * weight).reshape(4, 8, LANES)
+
+    def level_seven(values):
+        return (spread(flat(values), mean) * (1.0 / 32.0)).reshape(4, 8, LANES)
+
+    fields5 = [field(f) for f in range(3)]
+    fields6 = [level_six(v, w, n) for n, (v, w) in enumerate(zip(fields5, (0.5, 0.125, 0.5)))]
+    fields7 = [level_seven(v) for v in fields6]
     r4 = l4[...]
     e4 = periodic_setup(r4, turn(r4, 96, 2), turn(r4, 64, 2), c4)
-    e4 = lax.fori_loop(0, COARSE_SWEEPS - 1, lambda _, e: periodic_sweep(e, c4), e4)
-    l4[...] = e4
-    for i in range(4):
-        w4[4 * i : 4 * i + 4] = l4[4 * gx + i, pl.ds(4 * gy, 4)]
-    lane16 = lanes_of((16, LANES))
-    four = jnp.where((lane16 >= 8) & (lane16 < 24), w4[...], 0.0)
-    four_out[...] = spread(four, square(lambda row, col: row == 8 + col // 8))
-
-
-def five_kernel(place, ring, low, high, five_out, l5, l6, c5, c6, c7, w4):
-    gx, gy = place[0], place[1]
-    lane = lanes_of((64, LANES))
-
-    def field(f):
-        mid = turn(ring[...], -8 - 24 * f, 1)
-        up = turn(high[...], 16 - 24 * f, 1)
-        down = turn(low[...], 32 - 24 * f, 1)
-        value = jnp.where(lane < 16, mid, jnp.where(lane < 40, up, down))
-        value = jnp.where((lane >= 56) & (lane < 64), turn(mid, 64, 1), value)
-        value = jnp.where(lane < 64, value, turn(value, 64, 1))
-        return value.reshape(8, 8, LANES)
-
-    to_six = square(lambda row, col: (row < 64) & (row // 2 == col % 32))
-    mean = square(lambda row, col: row < 32)
-
-    def level_six(values, weight):
-        pairs = values.reshape(4, 2, 8, LANES)
-        l6[...] = pairs[:, 0] + pairs[:, 1]
-        summed = l6[:, pl.ds(0, 4, stride=2), :] + l6[:, pl.ds(1, 4, stride=2), :]
-        l6[:, 0:4] = summed
-        l6[:, 4:8] = summed
-        return (spread(flat(l6[...]), to_six) * weight).reshape(4, 8, LANES)
-
-    def level_seven(values):
-        return (spread(flat(values), mean) * (1.0 / 32.0)).reshape(4, 8, LANES)
-
-    fields5 = [field(f) for f in range(3)]
-    fields6 = [level_six(v, w) for v, w in zip(fields5, (0.5, 0.125, 0.5))]
     e5 = periodic_setup(*fields5, c5)
     e6 = periodic_setup(*fields6, c6)
-    e7 = periodic_setup(*[level_seven(v) for v in fields6], c7)
+    e7 = periodic_setup(*fields7, c7)
 
     def sweep(_, carry):
-        b, c, d = carry
-        return periodic_sweep(b, c5), periodic_sweep(c, c6), periodic_sweep(d, c7)
-
-    e5, e6, e7 = lax.fori_loop(0, COARSE_SWEEPS - 1, sweep, (e5, e6, e7))
-    l6[...] = e6 + e7
-    six = l6[gx, pl.ds(gy, 1)] + jnp.zeros((8, LANES), F32)
+        a, b, c, d = carry
+        return (
+            periodic_sweep(a, c4), periodic_sweep(b, c5), periodic_sweep(c, c6),
+            periodic_sweep(d, c7),
+        )
+
+    e4, e5, e6, e7 = lax.fori_loop(0, COARSE_SWEEPS - 1, sweep, (e4, e5, e6, e7))
+    l6[0] = e6 + e7
+    six = l6[0, gx, pl.ds(gy, 1)] + jnp.zeros((8, LANES), F32)
     six = spread(six, square(lambda row, col: row == col // 32))
     l5[...] = e5
     w4[...] = jnp.zeros((16, LANES), F32)
     w4[0:2] = l5[2 * gx, pl.ds(2 * gy, 2)]
     w4[2:4] = l5[2 * gx + 1, pl.ds(2 * gy, 2)]
     five = six + spread(w4[0:8], square(lambda row, col: row == col // 16))
+    l4[...] = e4
+    for i in range(4):
+        w4[4 * i : 4 * i + 4] = l4[4 * gx + i, pl.ds(4 * gy, 4)]
+    lane16 = lanes_of((16, LANES))
+    four = jnp.where((lane16 >= 8) & (lane16 < 24), w4[...], 0.0)
+    four = spread(four, square(lambda row, col: row == 8 + col // 8))
     for i in range(4):
         for j in range(2):
             row = 2 * (i // 2) + j
-            five_out[4 * i + 2 * j : 4 * i + 2 * j + 2] = jnp.broadcast_to(
+            w4[4 * i + 2 * j : 4 * i + 2 * j + 2] = jnp.broadcast_to(
                 five[row : row + 1], (2, LANES)
             )
+    four_out[...] = four + w4[...]
 
 
 def fine_kernel(
@@ -533,7 +543,12 @@
         edge[2 + n] = 0.5 * scale[:, y, :] * k
 
 
-def three_kernel(own, xlo, xhi, ylo, yhi, three_out, r3, s3, k3, c3, ea, eb):
+def three_kernel(
+    initial_far, own, xlo, xhi, ylo, yhi, base, base2, edge, edge2,
+    three_out, two_out, fine_out,
+    r3, s3, k3, c3, ea, eb, w2, sems,
+):
+    inputs = fetch(((initial_far, fine_out),), sems)
     lane8 = lanes_of((8, LANES))
     for ix in range(3):
         for iy, y_ref in enumerate((ylo, None, yhi)):
@@ -619,21 +634,6 @@
     three = flat(jnp.where((lane3 >= BASE) & (lane3 < BASE + 32), mine, 0.0))
     three_out[...] = spread(three, square(lambda row, col: row == BASE + col // 4))
 
-
-def finish_kernel(
-    initial_far, three_in, four_in, five_in, xlo, xhi, ylo, yhi, base, base2, edge, edge2,
-    out_far,
-    w3, w2, w32, up, out, initial, sems,
-):
-    inputs = fetch(((initial_far, initial),), sems)
-    lane8 = lanes_of((8, LANES))
-    four = four_in[...] + five_in[...]
-    for i in range(8):
-        block = four[4 * (i // 2) : 4 * (i // 2) + 4]
-        w3[i, pl.ds(0, 4, stride=2), :] = block
-        w3[i, pl.ds(1, 4, stride=2), :] = block
-    three = three_in[...] + flat(w3[...])
-
     def beyond(ref, start):
         half = ref[start : start + 8]
         other = turn(half, 64, 1)
@@ -646,13 +646,38 @@
         w2[x] = w2[x] + edge2[n] * beyond(ref, X_SEC)
     for n, (y, ref) in enumerate(((0, ylo), (15, yhi))):
         w2[:, y, :] = w2[:, y, :] + edge2[2 + n] * beyond(ref, Y_SEC)
-    two = spread(flat(w2[...]), square(lambda row, col: row == col // 2))
+    two_out[...] = spread(flat(w2[...]), square(lambda row, col: row == col // 2))
+
+    for copy in inputs:
+        copy.wait()
+
+    def add(x, carry):
+        fine_out[x] = fine_out[x] + base[x]
+        return carry
+
+    lax.fori_loop(0, 32, add, 0, unroll=8)
+    for n, (x, ref) in enumerate(((0, xlo), (31, xhi))):
+        fine_out[x] = fine_out[x] + edge[n] * ref[X_FACE:X_SEC]
+    for n, (y, ref) in enumerate(((0, ylo), (31, yhi))):
+        fine_out[:, y, :] = fine_out[:, y, :] + edge[2 + n] * ref[Y_FACE:Y_SEC]
+
+
+def finish_kernel(
+    three_in, two_in, four_in, fine_in, out_far, w3, w32, up, out, sems
+):
+    four = four_in[...]
+    for i in range(8):
+        block = four[4 * (i // 2) : 4 * (i // 2) + 4]
+        w3[i, pl.ds(0, 4, stride=2), :] = block
+        w3[i, pl.ds(1, 4, stride=2), :] = block
+    three = three_in[...] + flat(w3[...])
+
     even8, odd8 = pl.ds(0, 8, stride=2), pl.ds(1, 8, stride=2)
     for i in range(16):
         block = three[8 * (i // 2) : 8 * (i // 2) + 8]
         w32[i, even8, :] = block
         w32[i, odd8, :] = block
-    two = two.reshape(16, 16, LANES) + w32[...]
+    two = two_in[...].reshape(16, 16, LANES) + w32[...]
     up[:, pl.ds(0, 16, stride=2), :] = two
     up[:, pl.ds(1, 16, stride=2), :] = two
 
@@ -660,17 +685,9 @@
     copies = []
     for c in range(CHUNKS):
         part = pl.ds(c * depth, depth)
-        inputs[c].wait()
         for x in range(c * depth, (c + 1) * depth):
-            total = initial[x] + (base[x] + up[x // 2])
-            if x in (0, 31):
-                face = (xhi if x else xlo)[X_FACE:X_SEC]
-                total = total + edge[1 if x else 0] * face
-            out[x] = total
-        for n, (y, ref) in enumerate(((0, ylo), (31, yhi))):
-            face = ref[pl.ds(Y_FACE + c * depth, depth)]
-            out[part, y, :] = out[part, y, :] + edge[2 + n, part] * face
-        copy = pltpu.make_async_copy(out.at[part], out_far.at[part], sems.at[1, c])
+            out[x] = fine_in[x] + up[x // 2]
+        copy = pltpu.make_async_copy(out.at[part], out_far.at[part], sems.at[c])
         copy.start()
         copies.append(copy)
     for copy in copies:
@@ -726,13 +743,17 @@
     zlo, zhi = passed(zs, "gz", 1), passed(zs, "gz", -1)
     xlo, xhi = passed(xp, "gx", 1), passed(xm, "gx", -1)
     ylo, yhi = passed(yp, "gy", 1), passed(ym, "gy", -1)
-    kp, ck, scale, first, zp, zm, whole, sides, kp2, ck2, scale2, first2, sides2 = local(
+    (
+        kp, ck, scale, first, zp, zm, fives, whole, sides_x, sides_y, kp2, ck2, scale2, first2,
+        sides2_x, sides2_y,
+    ) = local(
         residual_kernel,
         [
             shape(1368, LANES), shape(32, LANES), shape(*block), shape(*block),
-            shape(Z_ROWS, LANES), shape(Z_ROWS, LANES),
-            shape(64, LANES), shape(4, 32, LANES), shape(440, LANES),
-            shape(16, LANES), shape(*block2), shape(*block2), shape(4, 16, LANES),
+            shape(Z_ROWS, LANES), shape(Z_ROWS, LANES), shape(8, LANES),
+            shape(64, LANES), shape(2, 32, LANES), shape(2, 32, LANES), shape(440, LANES),
+            shape(16, LANES), shape(*block2), shape(*block2), shape(2, 16, LANES),
+            shape(2, 16, LANES),
         ],
         [VM] * 10,
         [
@@ -743,50 +764,51 @@
     )(kappa, initial, rhs, sigma, xlo, xhi, ylo, yhi, zlo, zhi)
 
     zlo, zhi = passed(zp, "gz", 1), passed(zm, "gz", -1)
-    own, xp, xm, ye, cf, base2, edge2, blocks = local(
+    own, xp, xm, ye, cf, cf2, blocks = local(
         window_kernel,
         [
             shape(3, 64, LANES), shape(X_ROWS, LANES), shape(X_ROWS, LANES),
-            shape(2, 8, LANES), shape(32, LANES), shape(*block2), shape(4, 16, LANES),
-            shape(16, 24, LANES),
+            shape(2, 8, LANES), shape(32, LANES), shape(16, LANES),
+            shape(16, 16, LANES),
         ],
-        [VM] * 10, [(8, 8, LANES), (18, 32, LANES)], "window",
-    )(zlo, zhi, zp, whole, sides, sides2, kp2, ck2, scale2, first2)
+        [VM] * 6, [(8, 8, LANES)], "window",
+    )(zlo, zhi, fives, whole, sides_x, sides2_x)
     xlo, xhi = passed(xp, "gx", 1), passed(xm, "gx", -1)
     planes = lax.all_to_all(blocks, ("gx", "gy"), 0, 0)
     base, edge = local(
         fine_kernel,
         [shape(*block), shape(4, 32, LANES)], [VM] * 5, [(34, 48, LANES)], "fine",
     )(kp, ck, scale, first, cf)
+    base2, edge2 = local(
+        second_kernel, [shape(*block2), shape(4, 16, LANES)], [VM] * 5, [(18, 32, LANES)],
+        "second",
+    )(kp2, ck2, scale2, first2, cf2)
     yp, ym = local(
-        columns_kernel, [shape(Y_ROWS, LANES)] * 2, [VM] * 7, [], "columns"
-    )(xlo, xhi, xp, sides, sides2, ye, edge)
+        columns_kernel, [shape(Y_ROWS, LANES)] * 2, [VM] * 8, [], "columns"
+    )(xlo, xhi, xp, sides_y, sides2_y, ye, edge, edge2)
     ylo, yhi = passed(yp, "gy", 1), passed(ym, "gy", -1)
-    (ring,) = local(ring_kernel, [shape(64, LANES)], [VM], [], "ring")(planes)
+    (ring,) = local(ring_kernel, [shape(3, 64, LANES)], [VM], [], "ring")(planes)
     ring_low, ring_high = passed(ring, "gz", 3), passed(ring, "gz", -3)
-    small = shape(16, LANES)
-    (four,) = local(
-        four_kernel, [small], [SM, VM], [block2, (7,) + block2, (16, LANES)], "four"
-    )(place, planes)
     padded3 = (24, 40, LANES)
     block3 = (24, 24, LANES)
-    (three,) = local(
-        three_kernel, [shape(64, LANES)], [VM] * 5,
-        [block3, block3, padded3, (7,) + block3, padded3, padded3], "three",
-    )(own, xlo, xhi, ylo, yhi)
-    (five,) = local(
-        five_kernel, [small], [SM] + [VM] * 3,
+    three, two, fine = local(
+        three_kernel, [shape(64, LANES), shape(256, LANES), shape(*block)], [FAR] + [VM] * 9,
+        [block3, block3, padded3, (7,) + block3, padded3, padded3, block2], "three",
+        sems=(1, CHUNKS),
+    )(far[1], own, xlo, xhi, ylo, yhi, base, base2, edge, edge2)
+    (four,) = local(
+        planes_kernel, [shape(16, LANES)], [SM] + [VM] * 4,
         [
-            (8, 8, LANES), (4, 8, LANES), (7, 8, 8, LANES), (7, 4, 8, LANES), (7, 4, 8, LANES),
-            (16, LANES),
+            block2, (8, 8, LANES), (3, 4, 8, LANES), (7,) + block2,
+            (7, 8, 8, LANES), (7, 4, 8, LANES), (7, 4, 8, LANES), (16, LANES),
         ],
-        "five",
-    )(place, ring, ring_low, ring_high)
+        "planes",
+    )(place, planes, ring, ring_low, ring_high)
     return local(
-        finish_kernel, [pltpu.HBM(block, F32)], [FAR] + [VM] * 11,
-        [(8, 8, LANES), block2, block2, (16, 32, LANES), block, block],
-        "finish", sems=(2, CHUNKS), out_spec=FAR,
-    )(far[1], three, four, five, xlo, xhi, ylo, yhi, base, base2, edge, edge2)[0]
+        finish_kernel, [pltpu.HBM(block, F32)], [VM] * 4,
+        [(8, 8, LANES), block2, (16, 32, LANES), block],
+        "finish", sems=(CHUNKS,), out_spec=FAR,
+    )(three, two, four, fine)[0]
 
 
 def solution(mesh):

time: 51 us -> 49 us (0.961)
  Pallas kernels: 17.6 us -> 15.3 us
    pallas_call x1, Pallas kernels: 1.95 us -> 1.06 us  [on_device(): local(window_kernel, [shape(3, 64, LANES), shape(X_ROWS, LANES), shape(X_...]
    pallas_call x6, Pallas kernels: 7.37 us -> 6.78 us  [the longest x1 2.68 us: on_device(): local(planes_kernel, [shape(16, LANES)], [SM] + [VM] * 4, [block2, (8, 8,...]
    pallas_call x1, Pallas kernels: 3.49 us -> 2.96 us  [on_device(): local(residual_kernel, [shape(1368, LANES), shape(32, LANES), shape(*bloc...]
where the time goes in v6:
time: 49 us; the launch traced here: 48.8 us
  starting transfers between devices  24.9 us (51%)
  Pallas kernels  15.3 us (31%)
  waiting for transfers between devices  8.34 us (17%)
    ppermute x14, starting transfers between devices, passed(): lax.ppermute(value, axis, [(i, (i + step) % count) for i in range(count)])  19.1 us
    ppermute x14, waiting for transfers between devices, passed(): lax.ppermute(value, axis, [(i, (i + step) % count) for i in range(count)])  8.34 us
    all_to_all x1, starting transfers between devices, on_device(): planes = lax.all_to_all(blocks, ('gx', 'gy'), 0, 0)  5.81 us
    pallas_call x1, Pallas kernels, on_device(): local(residual_kernel, [shape(1368, LANES), shape(32, LANES), shape(*bloc...  2.96 us
    pallas_call x1, Pallas kernels, on_device(): local(planes_kernel, [shape(16, LANES)], [SM] + [VM] * 4, [block2, (8, 8,...  2.68 us
    pallas_call x1, Pallas kernels, on_device(): local(three_kernel, [shape(64, LANES), shape(256, LANES), shape(*block)],...  2.55 us
    pallas_call x1, Pallas kernels, on_device(): local(fine_kernel, [shape(*block), shape(4, 32, LANES)], [VM] * 5, [(34,...  1.81 us
    pallas_call x1, Pallas kernels, on_device(): local(faces_kernel, [edge, edge, edge, edge, shape(2, 32, LANES)] + [shap...  1.51 us
  transfers between devices with their start and end apart: 15, of which 5 were waited for; matrix products, arithmetic and copies ran while one was open for 0% of the time, Pallas kernels for 13%

profile of v6, /device:TPU:1, one launch (start us, length us, event | category | flops | bytes accessed | tf_op | source)
XLA Modules:
  0.0 48.8 jit_solution(7957070809917830642)
XLA Ops:
  0.0 1.5 %faces.1 = (f32[3,32,128]{2,1,0:T(8,128)S(1)}, f32[3,32,128]{2,1,0:T(8,128)S(1)}, f32[3,32,128]{2,1,0:T(8,128)S(1)}, f32[3,32,128]{2,1,0:T(8,128)S(1)}, f32[2,32...) custom-call(f32[32,32,128]{2,1,0:T(8,128)} %kappa_far.1, f32[32,32,128]{2,1,0:T(8,128)} %initial_far.3), custom_call_target="tpu_custom_call" | custom-call | tf_op jit(solution)/shard_map/faces/pallas_call | solution.py:735
  1.5 2.6 %collective-permute-start.4 = (f32[2,32,128]{2,1,0:T(8,128)S(1)}, f32[2,32,128]{2,1,0:T(8,128)S(1)}, u32[]{:S(2)}, u32[]{:S(2)}) collective-permute-start(f32[2,32,128]{2,1,0:T(8,128)S(1)} %get-tuple-element.48.edge), channel_id=1, source_target_pairs={{0,1},{1,2},{2,3},{3,4},{4,5},{5,6},{6,7},{7,0},{8,9},{9,10},{10,1... | collective-permute-start | bytes 98312 | tf_op jit(solution)/shard_map/ppermute | solution.py:726
  4.1 1.3 %collective-permute-start = (f32[3,32,128]{2,1,0:T(8,128)S(1)}, f32[3,32,128]{2,1,0:T(8,128)S(1)}, u32[]{:S(2)}, u32[]{:S(2)}) collective-permute-start(f32[3,32,128]{2,1,0:T(8,128)S(1)} %get-tuple-element.51), channel_id=1, source_target_pairs={{0,32},{32,64},{64,96},{96,0},{1,33},{33,65},{65,97},{97,1},{2,34}... | collective-permute-start | bytes 147464 | tf_op jit(solution)/shard_map/ppermute | solution.py:726
  5.4 1.4 %collective-permute-start.1 = (f32[3,32,128]{2,1,0:T(8,128)S(1)}, f32[3,32,128]{2,1,0:T(8,128)S(1)}, u32[]{:S(2)}, u32[]{:S(2)}) collective-permute-start(f32[3,32,128]{2,1,0:T(8,128)S(1)} %get-tuple-element.52), channel_id=1, source_target_pairs={{0,96},{32,0},{64,32},{96,64},{1,97},{33,1},{65,33},{97,65},{2,98}... | collective-permute-start | bytes 147464 | tf_op jit(solution)/shard_map/ppermute | solution.py:726
  6.9 1.6 %collective-permute-start.2 = (f32[3,32,128]{2,1,0:T(8,128)S(1)}, f32[3,32,128]{2,1,0:T(8,128)S(1)}, u32[]{:S(2)}, u32[]{:S(2)}) collective-permute-start(f32[3,32,128]{2,1,0:T(8,128)S(1)} %get-tuple-element.53), channel_id=1, source_target_pairs={{0,8},{8,16},{16,24},{24,0},{1,9},{9,17},{17,25},{25,1},{2,10},{10... | collective-permute-start | bytes 147464 | tf_op jit(solution)/shard_map/ppermute | solution.py:726
  8.5 2.1 %collective-permute-start.3 = (f32[3,32,128]{2,1,0:T(8,128)S(1)}, f32[3,32,128]{2,1,0:T(8,128)S(1)}, u32[]{:S(2)}, u32[]{:S(2)}) collective-permute-start(f32[3,32,128]{2,1,0:T(8,128)S(1)} %get-tuple-element.54), channel_id=1, source_target_pairs={{0,24},{8,0},{16,8},{24,16},{1,25},{9,1},{17,9},{25,17},{2,26},{10... | collective-permute-start | bytes 147464 | tf_op jit(solution)/shard_map/ppermute | solution.py:726
  10.6 1.2 %load.1 = (f32[32,32,128]{2,1,0:T(8,128)S(1)}, f32[32,32,128]{2,1,0:T(8,128)S(1)}) custom-call(f32[32,32,128]{2,1,0:T(8,128)} %rhs_far.1, f32[32,32,128]{2,1,0:T(8,128)} %sigma_far.1, f32[2,32,128]{2,1,0:T(8,128)S(1)} %get-tuple-element.48.edge), custom_call_target="tpu_custom_call" | custom-call | tf_op jit(solution)/shard_map/load/pallas_call | solution.py:740
  11.9 2.1 %collective-permute-done.5.zhi = f32[2,32,128]{2,1,0:T(8,128)S(1)} collective-permute-done((f32[2,32,128]{2,1,0:T(8,128)S(1)}, f32[2,32,128]{2,1,0:T(8,128)S(1)}, u32[]{:S(2)}, u32[]{:S(2)}) %collective-permute-start.5) | collective-permute-done | bytes 32800 | tf_op jit(solution)/shard_map/ppermute | solution.py:726
  14.0 3.0 %residual.1 = (f32[1368,128]{1,0:T(8,128)S(1)}, f32[32,128]{1,0:T(8,128)S(1)}, f32[32,32,128]{2,1,0:T(8,128)S(1)}, f32[32,32,128]{2,1,0:T(8,128)S(1)}, f32[40,12...) custom-call(f32[32,32,128]{2,1,0:T(8,128)S(1)} %get-tuple-element.46, ...), custom_call_target="tpu_custom_call" | custom-call | tf_op jit(solution)/shard_map/residual/pallas_call | solution.py:749
  17.5 0.7 %collective-permute-done.6.zlo = f32[40,128]{1,0:T(8,128)S(1)} collective-permute-done((f32[40,128]{1,0:T(8,128)S(1)}, f32[40,128]{1,0:T(8,128)S(1)}, u32[]{:S(2)}, u32[]{:S(2)}) %collective-permute-start.6) | collective-permute-done | bytes 20512 | tf_op jit(solution)/shard_map/ppermute | solution.py:726
  18.2 2.0 %collective-permute-done.7.zhi = f32[40,128]{1,0:T(8,128)S(1)} collective-permute-done((f32[40,128]{1,0:T(8,128)S(1)}, f32[40,128]{1,0:T(8,128)S(1)}, u32[]{:S(2)}, u32[]{:S(2)}) %collective-permute-start.7) | collective-permute-done | bytes 20512 | tf_op jit(solution)/shard_map/ppermute | solution.py:726
  20.2 1.1 %window.1 = (f32[3,64,128]{2,1,0:T(8,128)S(1)}, f32[112,128]{1,0:T(8,128)S(1)}, f32[112,128]{1,0:T(8,128)S(1)}, f32[2,8,128]{2,1,0:T(8,128)S(1)}, f32[32,128]{1,...) custom-call(f32[40,128]{1,0:T(8,128)S(1)} %collective-permute-done.6.zlo, ...), custom_call_target="tpu_custom_call" | custom-call | tf_op jit(solution)/shard_map/window/pallas_call | solution.py:767
  21.3 5.8 %all-to-all-start = ((f32[16,16,128]{2,1,0:T(8,128)}), f32[16,16,128]{2,1,0:T(8,128)S(1)}, u32[]{:S(2)}, u32[]{:S(2)}) async-start(f32[16,16,128]{2,1,0:T(8,128)} %get-tuple-element.85), calls=%async_computation | async-start | bytes 262144 | tf_op jit(solution)/shard_map/all_to_all | solution.py:777
  27.1 1.4 %collective-permute-start.8 = (f32[112,128]{1,0:T(8,128)S(1)}, f32[112,128]{1,0:T(8,128)S(1)}, u32[]{:S(2)}, u32[]{:S(2)}) collective-permute-start(f32[112,128]{1,0:T(8,128)S(1)} %get-tuple-element.62.xp), channel_id=1, source_target_pairs={{0,32},{32,64},{64,96},{96,0},{1,33},{33,65},{65,97},{97,1},{2,34}... | collective-permute-start | bytes 172040 | tf_op jit(solution)/shard_map/ppermute | solution.py:726
  28.5 1.4 %collective-permute-start.9 = (f32[112,128]{1,0:T(8,128)S(1)}, f32[112,128]{1,0:T(8,128)S(1)}, u32[]{:S(2)}, u32[]{:S(2)}) collective-permute-start(f32[112,128]{1,0:T(8,128)S(1)} %get-tuple-element.63), channel_id=1, source_target_pairs={{0,96},{32,0},{64,32},{96,64},{1,97},{33,1},{65,33},{97,65},{2,98}... | collective-permute-start | bytes 172040 | tf_op jit(solution)/shard_map/ppermute | solution.py:726
  29.8 0.6 %second.1 = (f32[16,16,128]{2,1,0:T(8,128)S(1)}, f32[4,16,128]{2,1,0:T(8,128)S(1)}) custom-call(f32[440,128]{1,0:T(8,128)S(1)} %get-tuple-element.73.kp2, f32[16,128]{1,0:T(8,128)S(1)} %get-tuple-element.74.ck2, f32[16,16,128]{2,1,0:T(8,128)S(1)} %get-tuple-element.75.scale2, f32[16,16,128]{2,1,0:T(8,128)S(1)} %get-tuple-element.76.first2, ...), custom_call_target="tpu_custom_call" | custom-call | tf_op jit(solution)/shard_map/second/pallas_call | solution.py:782
  30.5 1.8 %fine.1 = (f32[32,32,128]{2,1,0:T(8,128)S(1)}, f32[4,32,128]{2,1,0:T(8,128)S(1)}) custom-call(f32[1368,128]{1,0:T(8,128)S(1)} %get-tuple-element.67.kp, f32[32,128]{1,0:T(8,128)S(1)} %get-tuple-element.68.ck, f32[32,32,128]{2,1,0:T(8,128)S(1)} %get-tuple-element.69.scale, f32[32,32,128]{2,1,0:T(8,128)S(1)} %get-tuple-element.70.first, ...), custom_call_target="tpu_custom_call" | custom-call | tf_op jit(solution)/shard_map/fine/pallas_call | solution.py:778
  32.9 1.3 %collective-permute-start.10 = (f32[240,128]{1,0:T(8,128)S(1)}, f32[240,128]{1,0:T(8,128)S(1)}, u32[]{:S(2)}, u32[]{:S(2)}) collective-permute-start(f32[240,128]{1,0:T(8,128)S(1)} %get-tuple-element.79), channel_id=1, source_target_pairs={{0,8},{8,16},{16,24},{24,0},{1,9},{9,17},{17,25},{25,1},{2,10},{10... | collective-permute-start | bytes 368648 | tf_op jit(solution)/shard_map/ppermute | solution.py:726
  34.2 1.5 %collective-permute-start.11 = (f32[240,128]{1,0:T(8,128)S(1)}, f32[240,128]{1,0:T(8,128)S(1)}, u32[]{:S(2)}, u32[]{:S(2)}) collective-permute-start(f32[240,128]{1,0:T(8,128)S(1)} %get-tuple-element.80), channel_id=1, source_target_pairs={{0,24},{8,0},{16,8},{24,16},{1,25},{9,1},{17,9},{25,17},{2,26},{10... | collective-permute-start | bytes 368648 | tf_op jit(solution)/shard_map/ppermute | solution.py:726
  35.7 3.9 %collective-permute-start.12 = (f32[3,64,128]{2,1,0:T(8,128)S(1)}, f32[3,64,128]{2,1,0:T(8,128)S(1)}, u32[]{:S(2)}, u32[]{:S(2)}) collective-permute-start(f32[3,64,128]{2,1,0:T(8,128)S(1)} %ring.1), channel_id=1, source_target_pairs={{0,3},{1,4},{2,5},{3,6},{4,7},{5,0},{6,1},{7,2},{8,11},{9,12},{10,... | collective-permute-start | bytes 294920 | tf_op jit(solution)/shard_map/ppermute | solution.py:726
  39.7 2.5 %three.1 = (f32[64,128]{1,0:T(8,128)S(1)}, f32[256,128]{1,0:T(8,128)S(1)}, f32[32,32,128]{2,1,0:T(8,128)S(1)}) custom-call(f32[32,32,128]{2,1,0:T(8,128)} %initial_far.3, f32[3,64,128]{2,1,0:T(8,128)S(1)} %get-tuple-element.61.own, f32[112,128]{1,0:T(8,128)S(1)} %collective-permute-done.8.xlo, f32[112,128]{1,0:T(8,128)S(1)} %collective-permute-done.9.xhi, ...), custom_call_target="tpu_custom_call" | custom-call | tf_op jit(solution)/shard_map/three/pallas_call | solution.py:794
  42.3 2.9 %collective-permute-done.13.high = f32[3,64,128]{2,1,0:T(8,128)S(1)} collective-permute-done((f32[3,64,128]{2,1,0:T(8,128)S(1)}, f32[3,64,128]{2,1,0:T(8,128)S(1)}, u32[]{:S(2)}, u32[]{:S(2)}) %collective-permute-start.13) | collective-permute-done | bytes 98336 | tf_op jit(solution)/shard_map/ppermute | solution.py:726
  45.2 2.7 %planes.1.four_in = f32[16,128]{1,0:T(8,128)S(1)} custom-call(s32[3]{0:T(128)S(1)} %pad_add_fusion.place, f32[16,16,128]{2,1,0:T(8,128)S(1)} %all-to-all-done.blocks, f32[3,64,128]{2,1,0:T(8,128)S(1)} %ring.1, f32[3,64,128]{2,1,0:T(8,128)S(1)} %collective-permute-done.12.low, f32[3,64,128]{2,1,0:T(8,128)S(1)} %collective-permute-done.13.high), custom_call_target="tpu_custom_call" | custom-call | tf_op jit(solution)/shard_map/planes/pallas_call | solution.py:799
  47.9 0.9 %finish.1 = f32[32,32,128]{2,1,0:T(8,128)} custom-call(f32[64,128]{1,0:T(8,128)S(1)} %get-tuple-element.83.three_in, f32[256,128]{1,0:T(8,128)S(1)} %get-tuple-element.84.two_in, f32[16,128]{1,0:T(8,128)S(1)} %planes.1.four_in, f32[32,32,128]{2,1,0:T(8,128)S(1)} %get-tuple-element.86.fine_in), custom_call_target="tpu_custom_call" | custom-call | tf_op jit(solution)/shard_map/finish/pallas_call | solution.py:807
  (18 shorter events, 1.3 us)
Async XLA Ops:
  1.5 9.1 %collective-permute-start.4 = (f32[2,32,128]{2,1,0:T(8,128)S(1)}, f32[2,32,128]{2,1,0:T(8,128)S(1)}, u32[]{:S(2)}, u32[]{:S(2)}) collective-permute-start(f32[2,32,128]{2,1,0:T(8,128)S(1)} %get-tuple-element.48.edge), channel_id=1, source_target_pairs={{0,1},{1,2},{2,3},{3,4},{4,5},{5,6},{6,7},{7,0},{8,9},{9,10},{10,1... | collective-permute-start | bytes 98312 | tf_op jit(solution)/shard_map/ppermute | solution.py:726
  4.1 9.8 %collective-permute-start = (f32[3,32,128]{2,1,0:T(8,128)S(1)}, f32[3,32,128]{2,1,0:T(8,128)S(1)}, u32[]{:S(2)}, u32[]{:S(2)}) collective-permute-start(f32[3,32,128]{2,1,0:T(8,128)S(1)} %get-tuple-element.51), channel_id=1, source_target_pairs={{0,32},{32,64},{64,96},{96,0},{1,33},{33,65},{65,97},{97,1},{2,34}... | collective-permute-start | bytes 147464 | tf_op jit(solution)/shard_map/ppermute | solution.py:726
  5.4 8.6 %collective-permute-start.1 = (f32[3,32,128]{2,1,0:T(8,128)S(1)}, f32[3,32,128]{2,1,0:T(8,128)S(1)}, u32[]{:S(2)}, u32[]{:S(2)}) collective-permute-start(f32[3,32,128]{2,1,0:T(8,128)S(1)} %get-tuple-element.52), channel_id=1, source_target_pairs={{0,96},{32,0},{64,32},{96,64},{1,97},{33,1},{65,33},{97,65},{2,98}... | collective-permute-start | bytes 147464 | tf_op jit(solution)/shard_map/ppermute | solution.py:726
  6.9 7.1 %collective-permute-start.2 = (f32[3,32,128]{2,1,0:T(8,128)S(1)}, f32[3,32,128]{2,1,0:T(8,128)S(1)}, u32[]{:S(2)}, u32[]{:S(2)}) collective-permute-start(f32[3,32,128]{2,1,0:T(8,128)S(1)} %get-tuple-element.53), channel_id=1, source_target_pairs={{0,8},{8,16},{16,24},{24,0},{1,9},{9,17},{17,25},{25,1},{2,10},{10... | collective-permute-start | bytes 147464 | tf_op jit(solution)/shard_map/ppermute | solution.py:726
  8.5 5.5 %collective-permute-start.3 = (f32[3,32,128]{2,1,0:T(8,128)S(1)}, f32[3,32,128]{2,1,0:T(8,128)S(1)}, u32[]{:S(2)}, u32[]{:S(2)}) collective-permute-start(f32[3,32,128]{2,1,0:T(8,128)S(1)} %get-tuple-element.54), channel_id=1, source_target_pairs={{0,24},{8,0},{16,8},{24,16},{1,25},{9,1},{17,9},{25,17},{2,26},{10... | collective-permute-start | bytes 147464 | tf_op jit(solution)/shard_map/ppermute | solution.py:726
  10.6 3.3 %collective-permute-start.5 = (f32[2,32,128]{2,1,0:T(8,128)S(1)}, f32[2,32,128]{2,1,0:T(8,128)S(1)}, u32[]{:S(2)}, u32[]{:S(2)}) collective-permute-start(f32[2,32,128]{2,1,0:T(8,128)S(1)} %get-tuple-element.48.edge), channel_id=1, source_target_pairs={{0,7},{1,0},{2,1},{3,2},{4,3},{5,4},{6,5},{7,6},{8,15},{9,8},{10,9... | collective-permute-start | bytes 98312 | tf_op jit(solution)/shard_map/ppermute | solution.py:726
  17.0 1.2 %collective-permute-start.6 = (f32[40,128]{1,0:T(8,128)S(1)}, f32[40,128]{1,0:T(8,128)S(1)}, u32[]{:S(2)}, u32[]{:S(2)}) collective-permute-start(f32[40,128]{1,0:T(8,128)S(1)} %get-tuple-element.55), channel_id=1, source_target_pairs={{0,1},{1,2},{2,3},{3,4},{4,5},{5,6},{6,7},{7,0},{8,9},{9,10},{10,1... | collective-permute-start | bytes 61448 | tf_op jit(solution)/shard_map/ppermute | solution.py:726
  17.0 3.2 %collective-permute-start.7 = (f32[40,128]{1,0:T(8,128)S(1)}, f32[40,128]{1,0:T(8,128)S(1)}, u32[]{:S(2)}, u32[]{:S(2)}) collective-permute-start(f32[40,128]{1,0:T(8,128)S(1)} %get-tuple-element.56), channel_id=1, source_target_pairs={{0,7},{1,0},{2,1},{3,2},{4,3},{5,4},{6,5},{7,6},{8,15},{9,8},{10,9... | collective-permute-start | bytes 61448 | tf_op jit(solution)/shard_map/ppermute | solution.py:726
  21.3 14.4 %all-to-all-start = ((f32[16,16,128]{2,1,0:T(8,128)}), f32[16,16,128]{2,1,0:T(8,128)S(1)}, u32[]{:S(2)}, u32[]{:S(2)}) async-start(f32[16,16,128]{2,1,0:T(8,128)} %get-tuple-element.85), calls=%async_computation | async-start | bytes 262144 | tf_op jit(solution)/shard_map/all_to_all | solution.py:777
  27.1 5.8 %collective-permute-start.8 = (f32[112,128]{1,0:T(8,128)S(1)}, f32[112,128]{1,0:T(8,128)S(1)}, u32[]{:S(2)}, u32[]{:S(2)}) collective-permute-start(f32[112,128]{1,0:T(8,128)S(1)} %get-tuple-element.62.xp), channel_id=1, source_target_pairs={{0,32},{32,64},{64,96},{96,0},{1,33},{33,65},{65,97},{97,1},{2,34}... | collective-permute-start | bytes 172040 | tf_op jit(solution)/shard_map/ppermute | solution.py:726
  28.5 4.4 %collective-permute-start.9 = (f32[112,128]{1,0:T(8,128)S(1)}, f32[112,128]{1,0:T(8,128)S(1)}, u32[]{:S(2)}, u32[]{:S(2)}) collective-permute-start(f32[112,128]{1,0:T(8,128)S(1)} %get-tuple-element.63), channel_id=1, source_target_pairs={{0,96},{32,0},{64,32},{96,64},{1,97},{33,1},{65,33},{97,65},{2,98}... | collective-permute-start | bytes 172040 | tf_op jit(solution)/shard_map/ppermute | solution.py:726
  32.9 6.8 %collective-permute-start.10 = (f32[240,128]{1,0:T(8,128)S(1)}, f32[240,128]{1,0:T(8,128)S(1)}, u32[]{:S(2)}, u32[]{:S(2)}) collective-permute-start(f32[240,128]{1,0:T(8,128)S(1)} %get-tuple-element.79), channel_id=1, source_target_pairs={{0,8},{8,16},{16,24},{24,0},{1,9},{9,17},{17,25},{25,1},{2,10},{10... | collective-permute-start | bytes 368648 | tf_op jit(solution)/shard_map/ppermute | solution.py:726
  34.2 5.5 %collective-permute-start.11 = (f32[240,128]{1,0:T(8,128)S(1)}, f32[240,128]{1,0:T(8,128)S(1)}, u32[]{:S(2)}, u32[]{:S(2)}) collective-permute-start(f32[240,128]{1,0:T(8,128)S(1)} %get-tuple-element.80), channel_id=1, source_target_pairs={{0,24},{8,0},{16,8},{24,16},{1,25},{9,1},{17,9},{25,17},{2,26},{10... | collective-permute-start | bytes 368648 | tf_op jit(solution)/shard_map/ppermute | solution.py:726
  35.7 6.6 %collective-permute-start.12 = (f32[3,64,128]{2,1,0:T(8,128)S(1)}, f32[3,64,128]{2,1,0:T(8,128)S(1)}, u32[]{:S(2)}, u32[]{:S(2)}) collective-permute-start(f32[3,64,128]{2,1,0:T(8,128)S(1)} %ring.1), channel_id=1, source_target_pairs={{0,3},{1,4},{2,5},{3,6},{4,7},{5,0},{6,1},{7,2},{8,11},{9,12},{10,... | collective-permute-start | bytes 294920 | tf_op jit(solution)/shard_map/ppermute | solution.py:726
  39.6 5.5 %collective-permute-start.13 = (f32[3,64,128]{2,1,0:T(8,128)S(1)}, f32[3,64,128]{2,1,0:T(8,128)S(1)}, u32[]{:S(2)}, u32[]{:S(2)}) collective-permute-start(f32[3,64,128]{2,1,0:T(8,128)S(1)} %ring.1), channel_id=1, source_target_pairs={{0,5},{1,6},{2,7},{3,0},{4,1},{5,2},{6,3},{7,4},{8,13},{9,14},{10,... | collective-permute-start | bytes 294920 | tf_op jit(solution)/shard_map/ppermute | solution.py:726

commit v7 on v6

--- a/solution.py
+++ b/solution.py
@@ -67,11 +67,6 @@
             copy.start()
             copies.append(copy)
     return copies
-
-
-def load_kernel(rhs_far, sigma_far, edge, rhs, sigma, sems):
-    for copy in fetch(((rhs_far, rhs), (sigma_far, sigma)), sems):
-        copy.wait()
 
 
 def faces_kernel(kappa_far, initial_far, xp, xm, yp, ym, zs, kappa, initial, sems):
@@ -121,26 +116,23 @@
     return above, below
 
 
-def residual_kernel(
-    kappa, initial, rhs, sigma, xlo, xhi, ylo, yhi, zlo, zhi,
-    kp, ck, scale, first, zp, zm, fives, whole, sides_x, sides_y, kp2, ck2, scale2, first2,
-    sides2_x, sides2_y, vp, pair_r, pair_k, pair_s, rims, small,
+def inside_kernel(
+    kappa, initial, rhs, sigma, zlo, zhi, kp, ck, diagonal, rest, pair_k, pair_s, vp
 ):
     lane = lanes_of((32, LANES))
     inner = pl.ds(8, 32)
-    kp[rows_of(0, 0, 40, 32)] = xlo[0]
-    kp[rows_of(33, 0, 40, 32)] = xhi[0]
-    vp[0, inner] = xlo[2]
-    vp[33, inner] = xhi[2]
+    blank, blank8 = jnp.zeros((32, LANES), F32), jnp.zeros((8, LANES), F32)
+    for x in (0, 33):
+        kp[rows_of(x, 0, 40, 32)] = blank
+        vp[x, inner] = blank
+    kp[40 * 33 : 40 * 33 + 8] = blank8
 
     def fill(x, carry):
-        one = pl.ds(x, 1)
+        kp[rows_of(x + 1, -8, 40, 8)] = blank8
         kp[rows_of(x + 1, 0, 40, 32)] = kappa[x]
         vp[x + 1, inner] = initial[x]
-        kp[rows_of(x + 1, -1, 40, 1)] = ylo[0, one]
-        kp[rows_of(x + 1, 32, 40, 1)] = yhi[0, one]
-        vp[x + 1, 7:8] = ylo[2, one]
-        vp[x + 1, 40:41] = yhi[2, one]
+        vp[x + 1, 0:8] = blank8
+        vp[x + 1, 40:48] = blank8
         return carry
 
     lax.fori_loop(0, 32, fill, 0, unroll=4)
@@ -149,9 +141,9 @@
     rim_v = jnp.where(low_half, zlo[1], zhi[1])
     ck[...] = rim_k
 
-    def slab(x, packed):
+    def slab(x):
         k = kappa[x]
-        v = vp[x + 1, inner]
+        v = initial[x]
         around = [
             (kp[rows_of(x, 0, 40, 32)], vp[x, inner]),
             (kp[rows_of(x + 2, 0, 40, 32)], vp[x + 2, inner]),
@@ -165,24 +157,61 @@
         v_sum = sum(vn for _, vn in around)
         both = sum(kn * vn for kn, vn in around)
         s = sigma[x]
-        diagonal = s + 3.0 * k + 0.5 * k_sum
-        r = rhs[x] - diagonal * v + 0.5 * (k * v_sum + both)
-        h = WEIGHT / diagonal
+        d = s + 3.0 * k + 0.5 * k_sum
+        diagonal[x] = d
+        rest[x] = rhs[x] - d * v + 0.5 * (k * v_sum + both)
+        return k, s
+
+    def two(i, carry):
+        k0, s0 = slab(2 * i)
+        k1, s1 = slab(2 * i + 1)
+        pair_k[i] = k0 + k1
+        pair_s[i] = s0 + s1
+        return carry
+
+    lax.fori_loop(0, 16, two, 0, unroll=3)
+
+
+def residual_kernel(
+    kappa, initial, kp_in, diagonal_in, rest_in, rim, pair_k, pair_s, xlo, xhi, ylo, yhi,
+    kp, scale, first, zp, zm, fives, whole, sides_x, sides_y, kp2, ck2, scale2, first2,
+    sides2_x, sides2_y, pair_r, rims, small,
+):
+    lane = lanes_of((32, LANES))
+    rim_k = rim[...]
+    kp[rows_of(0, 0, 40, 32)] = xlo[0]
+    kp[rows_of(33, 0, 40, 32)] = xhi[0]
+    kp[pl.ds(47, 32, stride=40), :] = ylo[0]
+    kp[pl.ds(80, 32, stride=40), :] = yhi[0]
+
+    def beyond(at, message):
+        kn, vn = message[0], message[2]
+        scale[at] = scale[at] + 0.5 * kn
+        k, v = kappa[at], initial[at]
+        first[at] = first[at] + 0.5 * ((k + kn) * vn - kn * v)
+
+    every = slice(None)
+    beyond(0, xlo)
+    beyond(31, xhi)
+    beyond((every, 0, every), ylo)
+    beyond((every, 31, every), yhi)
+
+    def slab(x, packed):
+        r = first[x]
+        h = WEIGHT / scale[x]
         e = h * r
         scale[x] = h
         first[x] = e
         packed = jnp.where(lane // 4 == x, turn(e, 4 * x + 2, 1), packed)
-        return r, k, s, packed
+        return r, packed
 
     def two(i, packed):
-        r0, k0, s0, packed = slab(2 * i, packed)
-        r1, k1, s1, packed = slab(2 * i + 1, packed)
+        r0, packed = slab(2 * i, packed)
+        r1, packed = slab(2 * i + 1, packed)
         pair_r[i] = r0 + r1
-        pair_k[i] = k0 + k1
-        pair_s[i] = s0 + s1
         return packed
 
-    packed = lax.fori_loop(0, 16, two, jnp.zeros((32, LANES), F32), unroll=3)
+    packed = lax.fori_loop(0, 16, two, jnp.zeros((32, LANES), F32), unroll=8)
     sides_x[0] = first[31]
     sides_x[1] = first[0]
     sides_y[0] = first[:, 31, :]
@@ -703,7 +732,7 @@
     return pltpu.VMEM(dims, F32)
 
 
-def local(kernel, outs, ins, scratch, name, sems=None, out_spec=VM):
+def local(kernel, outs, ins, scratch, name, sems=None, out_spec=VM, aliases=None):
     scratch = [pltpu.VMEM(dims, F32) for dims in scratch]
     if sems is not None:
         scratch.append(pltpu.SemaphoreType.DMA(sems))
@@ -713,6 +742,7 @@
         in_specs=ins,
         out_specs=[out_spec] * len(outs),
         scratch_shapes=scratch,
+        input_output_aliases=aliases or {},
         compiler_params=pltpu.CompilerParams(vmem_limit_bytes=24 * 1024 * 1024),
         name=name,
     )
@@ -730,38 +760,41 @@
     edge = shape(3, 32, LANES)
     far = [
         pltpu.with_memory_space_constraint(value, pltpu.HBM)
-        for value in (kappa, initial, rhs, sigma)
+        for value in (kappa, initial)
     ]
     xp, xm, yp, ym, zs, kappa, initial = local(
         faces_kernel,
         [edge, edge, edge, edge, shape(2, 32, LANES)] + [shape(*block)] * 2,
         [FAR] * 2, [], "faces", sems=(2, CHUNKS),
-    )(*far[:2])
-    rhs, sigma = local(
-        load_kernel, [shape(*block)] * 2, [FAR, FAR, VM], [], "load", sems=(2, CHUNKS)
-    )(*far[2:], zs)
+    )(*far)
     zlo, zhi = passed(zs, "gz", 1), passed(zs, "gz", -1)
     xlo, xhi = passed(xp, "gx", 1), passed(xm, "gx", -1)
     ylo, yhi = passed(yp, "gy", 1), passed(ym, "gy", -1)
+    kp, ck, diagonal, rest, pair_k, pair_s = local(
+        inside_kernel,
+        [
+            shape(1368, LANES), shape(32, LANES), shape(*block), shape(*block),
+            shape(16, 32, LANES), shape(16, 32, LANES),
+        ],
+        [VM] * 6, [(34, 48, LANES)], "inside",
+    )(kappa, initial, rhs, sigma, zlo, zhi)
     (
-        kp, ck, scale, first, zp, zm, fives, whole, sides_x, sides_y, kp2, ck2, scale2, first2,
+        kp, scale, first, zp, zm, fives, whole, sides_x, sides_y, kp2, ck2, scale2, first2,
         sides2_x, sides2_y,
     ) = local(
         residual_kernel,
         [
-            shape(1368, LANES), shape(32, LANES), shape(*block), shape(*block),
+            shape(1368, LANES), shape(*block), shape(*block),
             shape(Z_ROWS, LANES), shape(Z_ROWS, LANES), shape(8, LANES),
             shape(64, LANES), shape(2, 32, LANES), shape(2, 32, LANES), shape(440, LANES),
             shape(16, LANES), shape(*block2), shape(*block2), shape(2, 16, LANES),
             shape(2, 16, LANES),
         ],
-        [VM] * 10,
-        [
-            (34, 48, LANES), (16, 32, LANES), (16, 32, LANES), (16, 32, LANES),
-            (4, 32, LANES), (8, 16, LANES),
-        ],
-        "residual",
-    )(kappa, initial, rhs, sigma, xlo, xhi, ylo, yhi, zlo, zhi)
+        [VM] * 12, [(16, 32, LANES), (4, 32, LANES), (8, 16, LANES)],
+        "residual", aliases={2: 0, 3: 1, 4: 2},
+    )(
+        kappa, initial, kp, diagonal, rest, ck, pair_k, pair_s, xlo, xhi, ylo, yhi
+    )
 
     zlo, zhi = passed(zp, "gz", 1), passed(zm, "gz", -1)
     own, xp, xm, ye, cf, cf2, blocks = local(

time: 49 us -> 48.3 us (0.986)
  starting transfers between devices: 24.9 us -> 24.2 us
  waiting for transfers between devices: 8.34 us -> 8.97 us
  Pallas kernels: 15.3 us -> 14.7 us
    all_to_all x1, starting transfers between devices: 5.81 us -> 4.67 us  [on_device(): planes = lax.all_to_all(blocks, ('gx', 'gy'), 0, 0)]
    pallas_call x2, Pallas kernels: 4.18 us -> 3.44 us  [the longest x1 1.92 us: on_device(): local(inside_kernel, [shape(1368, LANES), shape(32, LANES), shape(*block)...]
    ppermute x14, waiting for transfers between devices: 8.34 us -> 8.96 us  [passed(): lax.ppermute(value, axis, [(i, (i + step) % count) for i in range(count)])]
  transfers between devices with their start and end apart: 15 -> 15, of which waited for: 5 -> 4; matrix products, arithmetic and copies ran while one was open for 0% -> 0% of each run, Pallas kernels for 13% -> 14%
where the time goes in v7:
time: 48.3 us; the launch traced here: 48.1 us
  starting transfers between devices  24.2 us (50%)
  Pallas kernels  14.7 us (30%)
  waiting for transfers between devices  8.97 us (19%)
    ppermute x14, starting transfers between devices, passed(): lax.ppermute(value, axis, [(i, (i + step) % count) for i in range(count)])  19.6 us
    ppermute x14, waiting for transfers between devices, passed(): lax.ppermute(value, axis, [(i, (i + step) % count) for i in range(count)])  8.96 us
    all_to_all x1, starting transfers between devices, on_device(): planes = lax.all_to_all(blocks, ('gx', 'gy'), 0, 0)  4.67 us
    pallas_call x1, Pallas kernels, on_device(): local(planes_kernel, [shape(16, LANES)], [SM] + [VM] * 4, [block2, (8, 8,...  2.68 us
    pallas_call x1, Pallas kernels, on_device(): local(three_kernel, [shape(64, LANES), shape(256, LANES), shape(*block)],...  2.54 us
    pallas_call x1, Pallas kernels, on_device(): local(inside_kernel, [shape(1368, LANES), shape(32, LANES), shape(*block)...  1.92 us
    pallas_call x1, Pallas kernels, on_device(): local(fine_kernel, [shape(*block), shape(4, 32, LANES)], [VM] * 5, [(34,...  1.8 us
    pallas_call x1, Pallas kernels, on_device(): local(faces_kernel, [edge, edge, edge, edge, shape(2, 32, LANES)] + [shap...  1.6 us
  transfers between devices with their start and end apart: 15, of which 4 were waited for; matrix products, arithmetic and copies ran while one was open for 0% of the time, Pallas kernels for 14%

profile of v7, /device:TPU:1, one launch (start us, length us, event | category | flops | bytes accessed | tf_op | source)
XLA Modules:
  0.0 48.1 jit_solution(15242289149669232023)
XLA Ops:
  0.0 1.6 %faces.1 = (f32[3,32,128]{2,1,0:T(8,128)S(1)}, f32[3,32,128]{2,1,0:T(8,128)S(1)}, f32[3,32,128]{2,1,0:T(8,128)S(1)}, f32[3,32,128]{2,1,0:T(8,128)S(1)}, f32[2,32...) custom-call(f32[32,32,128]{2,1,0:T(8,128)} %kappa_far.1, f32[32,32,128]{2,1,0:T(8,128)} %initial_far.3), custom_call_target="tpu_custom_call" | custom-call | tf_op jit(solution)/shard_map/faces/pallas_call | solution.py:765
  1.6 2.6 %collective-permute-start = (f32[2,32,128]{2,1,0:T(8,128)S(1)}, f32[2,32,128]{2,1,0:T(8,128)S(1)}, u32[]{:S(2)}, u32[]{:S(2)}) collective-permute-start(f32[2,32,128]{2,1,0:T(8,128)S(1)} %get-tuple-element.51), channel_id=1, source_target_pairs={{0,1},{1,2},{2,3},{3,4},{4,5},{5,6},{6,7},{7,0},{8,9},{9,10},{10,1... | collective-permute-start | bytes 98312 | tf_op jit(solution)/shard_map/ppermute | solution.py:756
  4.2 1.3 %collective-permute-start.2 = (f32[3,32,128]{2,1,0:T(8,128)S(1)}, f32[3,32,128]{2,1,0:T(8,128)S(1)}, u32[]{:S(2)}, u32[]{:S(2)}) collective-permute-start(f32[3,32,128]{2,1,0:T(8,128)S(1)} %get-tuple-element.58), channel_id=1, source_target_pairs={{0,32},{32,64},{64,96},{96,0},{1,33},{33,65},{65,97},{97,1},{2,34}... | collective-permute-start | bytes 147464 | tf_op jit(solution)/shard_map/ppermute | solution.py:756
  5.5 1.4 %collective-permute-start.3 = (f32[3,32,128]{2,1,0:T(8,128)S(1)}, f32[3,32,128]{2,1,0:T(8,128)S(1)}, u32[]{:S(2)}, u32[]{:S(2)}) collective-permute-start(f32[3,32,128]{2,1,0:T(8,128)S(1)} %get-tuple-element.59), channel_id=1, source_target_pairs={{0,96},{32,0},{64,32},{96,64},{1,97},{33,1},{65,33},{97,65},{2,98}... | collective-permute-start | bytes 147464 | tf_op jit(solution)/shard_map/ppermute | solution.py:756
  7.0 1.6 %collective-permute-start.4 = (f32[3,32,128]{2,1,0:T(8,128)S(1)}, f32[3,32,128]{2,1,0:T(8,128)S(1)}, u32[]{:S(2)}, u32[]{:S(2)}) collective-permute-start(f32[3,32,128]{2,1,0:T(8,128)S(1)} %get-tuple-element.60), channel_id=1, source_target_pairs={{0,8},{8,16},{16,24},{24,0},{1,9},{9,17},{17,25},{25,1},{2,10},{10... | collective-permute-start | bytes 147464 | tf_op jit(solution)/shard_map/ppermute | solution.py:756
  8.6 2.1 %collective-permute-start.5 = (f32[3,32,128]{2,1,0:T(8,128)S(1)}, f32[3,32,128]{2,1,0:T(8,128)S(1)}, u32[]{:S(2)}, u32[]{:S(2)}) collective-permute-start(f32[3,32,128]{2,1,0:T(8,128)S(1)} %get-tuple-element.61), channel_id=1, source_target_pairs={{0,24},{8,0},{16,8},{24,16},{1,25},{9,1},{17,9},{25,17},{2,26},{10... | collective-permute-start | bytes 147464 | tf_op jit(solution)/shard_map/ppermute | solution.py:756
  10.7 3.3 %collective-permute-done.1.zhi = f32[2,32,128]{2,1,0:T(8,128)S(1)} collective-permute-done((f32[2,32,128]{2,1,0:T(8,128)S(1)}, f32[2,32,128]{2,1,0:T(8,128)S(1)}, u32[]{:S(2)}, u32[]{:S(2)}) %collective-permute-start.1) | collective-permute-done | bytes 32800 | tf_op jit(solution)/shard_map/ppermute | solution.py:756
  14.1 1.9 %inside.1 = (f32[1368,128]{1,0:T(8,128)S(1)}, f32[32,128]{1,0:T(8,128)S(1)}, f32[32,32,128]{2,1,0:T(8,128)S(1)}, f32[32,32,128]{2,1,0:T(8,128)S(1)}, f32[16,32,1...) custom-call(f32[32,32,128]{2,1,0:T(8,128)S(1)} %get-tuple-element.49.kappa, f32[32,32,128]{2,1,0:T(8,128)S(1)} %get-tuple-element.50.initial, ...), custom_call_target="tpu_custom_call" | custom-call | tf_op jit(solution)/shard_map/inside/pallas_call | solution.py:773
  16.0 1.5 %residual.1 = (f32[1368,128]{1,0:T(8,128)S(1)}, f32[32,32,128]{2,1,0:T(8,128)S(1)}, f32[32,32,128]{2,1,0:T(8,128)S(1)}, f32[40,128]{1,0:T(8,128)S(1)}, f32[40,12...) custom-call(f32[32,32,128]{2,1,0:T(8,128)S(1)} %get-tuple-element.49, ...), custom_call_target="tpu_custom_call", output_to_operand_aliasing={{0}: (2, {}), {1}: (3, {}), {2}: (4, {})} | custom-call | tf_op jit(solution)/shard_map/residual/pallas_call | solution.py:784
  18.1 0.7 %collective-permute-done.6.zlo = f32[40,128]{1,0:T(8,128)S(1)} collective-permute-done((f32[40,128]{1,0:T(8,128)S(1)}, f32[40,128]{1,0:T(8,128)S(1)}, u32[]{:S(2)}, u32[]{:S(2)}) %collective-permute-start.6) | collective-permute-done | bytes 20512 | tf_op jit(solution)/shard_map/ppermute | solution.py:756
  18.8 2.0 %collective-permute-done.7.zhi = f32[40,128]{1,0:T(8,128)S(1)} collective-permute-done((f32[40,128]{1,0:T(8,128)S(1)}, f32[40,128]{1,0:T(8,128)S(1)}, u32[]{:S(2)}, u32[]{:S(2)}) %collective-permute-start.7) | collective-permute-done | bytes 20512 | tf_op jit(solution)/shard_map/ppermute | solution.py:756
  20.8 1.1 %window.1 = (f32[3,64,128]{2,1,0:T(8,128)S(1)}, f32[112,128]{1,0:T(8,128)S(1)}, f32[112,128]{1,0:T(8,128)S(1)}, f32[2,8,128]{2,1,0:T(8,128)S(1)}, f32[32,128]{1,...) custom-call(f32[40,128]{1,0:T(8,128)S(1)} %collective-permute-done.6.zlo, ...), custom_call_target="tpu_custom_call" | custom-call | tf_op jit(solution)/shard_map/window/pallas_call | solution.py:800
  21.9 4.7 %all-to-all-start = ((f32[16,16,128]{2,1,0:T(8,128)}), f32[16,16,128]{2,1,0:T(8,128)S(1)}, u32[]{:S(2)}, u32[]{:S(2)}) async-start(f32[16,16,128]{2,1,0:T(8,128)} %get-tuple-element.91), calls=%async_computation | async-start | bytes 262144 | tf_op jit(solution)/shard_map/all_to_all | solution.py:810
  26.5 1.4 %collective-permute-start.8 = (f32[112,128]{1,0:T(8,128)S(1)}, f32[112,128]{1,0:T(8,128)S(1)}, u32[]{:S(2)}, u32[]{:S(2)}) collective-permute-start(f32[112,128]{1,0:T(8,128)S(1)} %get-tuple-element.69.xp), channel_id=1, source_target_pairs={{0,32},{32,64},{64,96},{96,0},{1,33},{33,65},{65,97},{97,1},{2,34}... | collective-permute-start | bytes 172040 | tf_op jit(solution)/shard_map/ppermute | solution.py:756
  27.9 1.4 %collective-permute-start.9 = (f32[112,128]{1,0:T(8,128)S(1)}, f32[112,128]{1,0:T(8,128)S(1)}, u32[]{:S(2)}, u32[]{:S(2)}) collective-permute-start(f32[112,128]{1,0:T(8,128)S(1)} %get-tuple-element.70), channel_id=1, source_target_pairs={{0,96},{32,0},{64,32},{96,64},{1,97},{33,1},{65,33},{97,65},{2,98}... | collective-permute-start | bytes 172040 | tf_op jit(solution)/shard_map/ppermute | solution.py:756
  29.3 1.8 %fine.1 = (f32[32,32,128]{2,1,0:T(8,128)S(1)}, f32[4,32,128]{2,1,0:T(8,128)S(1)}) custom-call(f32[1368,128]{1,0:T(8,128)S(1)} %get-tuple-element.74.kp, f32[32,128]{1,0:T(8,128)S(1)} %get-tuple-element.55.rim.ck, f32[32,32,128]{2,1,0:T(8,128)S(1)} %get-tuple-element.75.scale, f32[32,32,128]{2,1,0:T(8,128)S(1)} %get-tuple-element.76.first, ...), custom_call_target="tpu_custom_call" | custom-call | tf_op jit(solution)/shard_map/fine/pallas_call | solution.py:811
  31.1 0.6 %second.1 = (f32[16,16,128]{2,1,0:T(8,128)S(1)}, f32[4,16,128]{2,1,0:T(8,128)S(1)}) custom-call(f32[440,128]{1,0:T(8,128)S(1)} %get-tuple-element.79.kp2, f32[16,128]{1,0:T(8,128)S(1)} %get-tuple-element.80.ck2, f32[16,16,128]{2,1,0:T(8,128)S(1)} %get-tuple-element.81.scale2, f32[16,16,128]{2,1,0:T(8,128)S(1)} %get-tuple-element.82.first2, ...), custom_call_target="tpu_custom_call" | custom-call | tf_op jit(solution)/shard_map/second/pallas_call | solution.py:815
  31.8 1.4 %collective-permute-start.10 = (f32[240,128]{1,0:T(8,128)S(1)}, f32[240,128]{1,0:T(8,128)S(1)}, u32[]{:S(2)}, u32[]{:S(2)}) collective-permute-start(f32[240,128]{1,0:T(8,128)S(1)} %get-tuple-element.85), channel_id=1, source_target_pairs={{0,8},{8,16},{16,24},{24,0},{1,9},{9,17},{17,25},{25,1},{2,10},{10... | collective-permute-start | bytes 368648 | tf_op jit(solution)/shard_map/ppermute | solution.py:756
  33.1 1.4 %collective-permute-start.11 = (f32[240,128]{1,0:T(8,128)S(1)}, f32[240,128]{1,0:T(8,128)S(1)}, u32[]{:S(2)}, u32[]{:S(2)}) collective-permute-start(f32[240,128]{1,0:T(8,128)S(1)} %get-tuple-element.86), channel_id=1, source_target_pairs={{0,24},{8,0},{16,8},{24,16},{1,25},{9,1},{17,9},{25,17},{2,26},{10... | collective-permute-start | bytes 368648 | tf_op jit(solution)/shard_map/ppermute | solution.py:756
  34.6 4.4 %collective-permute-start.12 = (f32[3,64,128]{2,1,0:T(8,128)S(1)}, f32[3,64,128]{2,1,0:T(8,128)S(1)}, u32[]{:S(2)}, u32[]{:S(2)}) collective-permute-start(f32[3,64,128]{2,1,0:T(8,128)S(1)} %ring.1), channel_id=1, source_target_pairs={{0,3},{1,4},{2,5},{3,6},{4,7},{5,0},{6,1},{7,2},{8,11},{9,12},{10,... | collective-permute-start | bytes 294920 | tf_op jit(solution)/shard_map/ppermute | solution.py:756
  39.1 2.5 %three.1 = (f32[64,128]{1,0:T(8,128)S(1)}, f32[256,128]{1,0:T(8,128)S(1)}, f32[32,32,128]{2,1,0:T(8,128)S(1)}) custom-call(f32[32,32,128]{2,1,0:T(8,128)} %initial_far.3, f32[3,64,128]{2,1,0:T(8,128)S(1)} %get-tuple-element.68.own, f32[112,128]{1,0:T(8,128)S(1)} %collective-permute-done.8.xlo, f32[112,128]{1,0:T(8,128)S(1)} %collective-permute-done.9.xhi, ...), custom_call_target="tpu_custom_call" | custom-call | tf_op jit(solution)/shard_map/three/pallas_call | solution.py:827
  41.6 2.9 %collective-permute-done.13.high = f32[3,64,128]{2,1,0:T(8,128)S(1)} collective-permute-done((f32[3,64,128]{2,1,0:T(8,128)S(1)}, f32[3,64,128]{2,1,0:T(8,128)S(1)}, u32[]{:S(2)}, u32[]{:S(2)}) %collective-permute-start.13) | collective-permute-done | bytes 98336 | tf_op jit(solution)/shard_map/ppermute | solution.py:756
  44.5 2.7 %planes.1.four_in = f32[16,128]{1,0:T(8,128)S(1)} custom-call(s32[3]{0:T(128)S(1)} %pad_add_fusion.place, f32[16,16,128]{2,1,0:T(8,128)S(1)} %all-to-all-done.blocks, f32[3,64,128]{2,1,0:T(8,128)S(1)} %ring.1, f32[3,64,128]{2,1,0:T(8,128)S(1)} %collective-permute-done.12.low, f32[3,64,128]{2,1,0:T(8,128)S(1)} %collective-permute-done.13.high), custom_call_target="tpu_custom_call" | custom-call | tf_op jit(solution)/shard_map/planes/pallas_call | solution.py:832
  47.2 0.9 %finish.1 = f32[32,32,128]{2,1,0:T(8,128)} custom-call(f32[64,128]{1,0:T(8,128)S(1)} %get-tuple-element.89.three_in, f32[256,128]{1,0:T(8,128)S(1)} %get-tuple-element.90.two_in, f32[16,128]{1,0:T(8,128)S(1)} %planes.1.four_in, f32[32,32,128]{2,1,0:T(8,128)S(1)} %get-tuple-element.92.fine_in), custom_call_target="tpu_custom_call" | custom-call | tf_op jit(solution)/shard_map/finish/pallas_call | solution.py:840
  (22 shorter events, 0.7 us)
Async XLA Ops:
  0.0 14.1 %copy-start = (f32[32,32,128]{2,1,0:T(8,128)S(1)}, f32[32,32,128]{2,1,0:T(8,128)}, u32[]{:S(2)}) copy-start(f32[32,32,128]{2,1,0:T(8,128)} %rhs.1) | copy-start | bytes 1572868
  0.0 14.1 %copy-start.1 = (f32[32,32,128]{2,1,0:T(8,128)S(1)}, f32[32,32,128]{2,1,0:T(8,128)}, u32[]{:S(2)}) copy-start(f32[32,32,128]{2,1,0:T(8,128)} %sigma.1) | copy-start | bytes 1572868
  1.6 9.1 %collective-permute-start = (f32[2,32,128]{2,1,0:T(8,128)S(1)}, f32[2,32,128]{2,1,0:T(8,128)S(1)}, u32[]{:S(2)}, u32[]{:S(2)}) collective-permute-start(f32[2,32,128]{2,1,0:T(8,128)S(1)} %get-tuple-element.51), channel_id=1, source_target_pairs={{0,1},{1,2},{2,3},{3,4},{4,5},{5,6},{6,7},{7,0},{8,9},{9,10},{10,1... | collective-permute-start | bytes 98312 | tf_op jit(solution)/shard_map/ppermute | solution.py:756
  4.2 11.8 %collective-permute-start.2 = (f32[3,32,128]{2,1,0:T(8,128)S(1)}, f32[3,32,128]{2,1,0:T(8,128)S(1)}, u32[]{:S(2)}, u32[]{:S(2)}) collective-permute-start(f32[3,32,128]{2,1,0:T(8,128)S(1)} %get-tuple-element.58), channel_id=1, source_target_pairs={{0,32},{32,64},{64,96},{96,0},{1,33},{33,65},{65,97},{97,1},{2,34}... | collective-permute-start | bytes 147464 | tf_op jit(solution)/shard_map/ppermute | solution.py:756
  5.5 10.5 %collective-permute-start.3 = (f32[3,32,128]{2,1,0:T(8,128)S(1)}, f32[3,32,128]{2,1,0:T(8,128)S(1)}, u32[]{:S(2)}, u32[]{:S(2)}) collective-permute-start(f32[3,32,128]{2,1,0:T(8,128)S(1)} %get-tuple-element.59), channel_id=1, source_target_pairs={{0,96},{32,0},{64,32},{96,64},{1,97},{33,1},{65,33},{97,65},{2,98}... | collective-permute-start | bytes 147464 | tf_op jit(solution)/shard_map/ppermute | solution.py:756
  7.0 9.1 %collective-permute-start.4 = (f32[3,32,128]{2,1,0:T(8,128)S(1)}, f32[3,32,128]{2,1,0:T(8,128)S(1)}, u32[]{:S(2)}, u32[]{:S(2)}) collective-permute-start(f32[3,32,128]{2,1,0:T(8,128)S(1)} %get-tuple-element.60), channel_id=1, source_target_pairs={{0,8},{8,16},{16,24},{24,0},{1,9},{9,17},{17,25},{25,1},{2,10},{10... | collective-permute-start | bytes 147464 | tf_op jit(solution)/shard_map/ppermute | solution.py:756
  8.6 7.4 %collective-permute-start.5 = (f32[3,32,128]{2,1,0:T(8,128)S(1)}, f32[3,32,128]{2,1,0:T(8,128)S(1)}, u32[]{:S(2)}, u32[]{:S(2)}) collective-permute-start(f32[3,32,128]{2,1,0:T(8,128)S(1)} %get-tuple-element.61), channel_id=1, source_target_pairs={{0,24},{8,0},{16,8},{24,16},{1,25},{9,1},{17,9},{25,17},{2,26},{10... | collective-permute-start | bytes 147464 | tf_op jit(solution)/shard_map/ppermute | solution.py:756
  10.7 3.3 %collective-permute-start.1 = (f32[2,32,128]{2,1,0:T(8,128)S(1)}, f32[2,32,128]{2,1,0:T(8,128)S(1)}, u32[]{:S(2)}, u32[]{:S(2)}) collective-permute-start(f32[2,32,128]{2,1,0:T(8,128)S(1)} %get-tuple-element.51), channel_id=1, source_target_pairs={{0,7},{1,0},{2,1},{3,2},{4,3},{5,4},{6,5},{7,6},{8,15},{9,8},{10,9... | collective-permute-start | bytes 98312 | tf_op jit(solution)/shard_map/ppermute | solution.py:756
  17.6 1.2 %collective-permute-start.6 = (f32[40,128]{1,0:T(8,128)S(1)}, f32[40,128]{1,0:T(8,128)S(1)}, u32[]{:S(2)}, u32[]{:S(2)}) collective-permute-start(f32[40,128]{1,0:T(8,128)S(1)} %get-tuple-element.62), channel_id=1, source_target_pairs={{0,1},{1,2},{2,3},{3,4},{4,5},{5,6},{6,7},{7,0},{8,9},{9,10},{10,1... | collective-permute-start | bytes 61448 | tf_op jit(solution)/shard_map/ppermute | solution.py:756
  17.6 3.2 %collective-permute-start.7 = (f32[40,128]{1,0:T(8,128)S(1)}, f32[40,128]{1,0:T(8,128)S(1)}, u32[]{:S(2)}, u32[]{:S(2)}) collective-permute-start(f32[40,128]{1,0:T(8,128)S(1)} %get-tuple-element.63), channel_id=1, source_target_pairs={{0,7},{1,0},{2,1},{3,2},{4,3},{5,4},{6,5},{7,6},{8,15},{9,8},{10,9... | collective-permute-start | bytes 61448 | tf_op jit(solution)/shard_map/ppermute | solution.py:756
  21.9 12.7 %all-to-all-start = ((f32[16,16,128]{2,1,0:T(8,128)}), f32[16,16,128]{2,1,0:T(8,128)S(1)}, u32[]{:S(2)}, u32[]{:S(2)}) async-start(f32[16,16,128]{2,1,0:T(8,128)} %get-tuple-element.91), calls=%async_computation | async-start | bytes 262144 | tf_op jit(solution)/shard_map/all_to_all | solution.py:810
  26.5 5.2 %collective-permute-start.8 = (f32[112,128]{1,0:T(8,128)S(1)}, f32[112,128]{1,0:T(8,128)S(1)}, u32[]{:S(2)}, u32[]{:S(2)}) collective-permute-start(f32[112,128]{1,0:T(8,128)S(1)} %get-tuple-element.69.xp), channel_id=1, source_target_pairs={{0,32},{32,64},{64,96},{96,0},{1,33},{33,65},{65,97},{97,1},{2,34}... | collective-permute-start | bytes 172040 | tf_op jit(solution)/shard_map/ppermute | solution.py:756
  27.9 3.8 %collective-permute-start.9 = (f32[112,128]{1,0:T(8,128)S(1)}, f32[112,128]{1,0:T(8,128)S(1)}, u32[]{:S(2)}, u32[]{:S(2)}) collective-permute-start(f32[112,128]{1,0:T(8,128)S(1)} %get-tuple-element.70), channel_id=1, source_target_pairs={{0,96},{32,0},{64,32},{96,64},{1,97},{33,1},{65,33},{97,65},{2,98}... | collective-permute-start | bytes 172040 | tf_op jit(solution)/shard_map/ppermute | solution.py:756
  31.8 7.3 %collective-permute-start.10 = (f32[240,128]{1,0:T(8,128)S(1)}, f32[240,128]{1,0:T(8,128)S(1)}, u32[]{:S(2)}, u32[]{:S(2)}) collective-permute-start(f32[240,128]{1,0:T(8,128)S(1)} %get-tuple-element.85), channel_id=1, source_target_pairs={{0,8},{8,16},{16,24},{24,0},{1,9},{9,17},{17,25},{25,1},{2,10},{10... | collective-permute-start | bytes 368648 | tf_op jit(solution)/shard_map/ppermute | solution.py:756
  33.1 5.9 %collective-permute-start.11 = (f32[240,128]{1,0:T(8,128)S(1)}, f32[240,128]{1,0:T(8,128)S(1)}, u32[]{:S(2)}, u32[]{:S(2)}) collective-permute-start(f32[240,128]{1,0:T(8,128)S(1)} %get-tuple-element.86), channel_id=1, source_target_pairs={{0,24},{8,0},{16,8},{24,16},{1,25},{9,1},{17,9},{25,17},{2,26},{10... | collective-permute-start | bytes 368648 | tf_op jit(solution)/shard_map/ppermute | solution.py:756
  34.6 7.1 %collective-permute-start.12 = (f32[3,64,128]{2,1,0:T(8,128)S(1)}, f32[3,64,128]{2,1,0:T(8,128)S(1)}, u32[]{:S(2)}, u32[]{:S(2)}) collective-permute-start(f32[3,64,128]{2,1,0:T(8,128)S(1)} %ring.1), channel_id=1, source_target_pairs={{0,3},{1,4},{2,5},{3,6},{4,7},{5,0},{6,1},{7,2},{8,11},{9,12},{10,... | collective-permute-start | bytes 294920 | tf_op jit(solution)/shard_map/ppermute | solution.py:756
  39.0 5.5 %collective-permute-start.13 = (f32[3,64,128]{2,1,0:T(8,128)S(1)}, f32[3,64,128]{2,1,0:T(8,128)S(1)}, u32[]{:S(2)}, u32[]{:S(2)}) collective-permute-start(f32[3,64,128]{2,1,0:T(8,128)S(1)} %ring.1), channel_id=1, source_target_pairs={{0,5},{1,6},{2,7},{3,0},{4,1},{5,2},{6,3},{7,4},{8,13},{9,14},{10,... | collective-permute-start | bytes 294920 | tf_op jit(solution)/shard_map/ppermute | solution.py:756

commit v8 on v7

--- a/solution.py
+++ b/solution.py
@@ -125,7 +125,9 @@
     for x in (0, 33):
         kp[rows_of(x, 0, 40, 32)] = blank
         vp[x, inner] = blank
+    kp[0:8] = blank8
     kp[40 * 33 : 40 * 33 + 8] = blank8
+    kp[40 * 34 : 40 * 34 + 8] = blank8
 
     def fill(x, carry):
         kp[rows_of(x + 1, -8, 40, 8)] = blank8
@@ -173,45 +175,47 @@
 
 
 def residual_kernel(
-    kappa, initial, kp_in, diagonal_in, rest_in, rim, pair_k, pair_s, xlo, xhi, ylo, yhi,
-    kp, scale, first, zp, zm, fives, whole, sides_x, sides_y, kp2, ck2, scale2, first2,
-    sides2_x, sides2_y, pair_r, rims, small,
+    kappa, initial, diagonal, rest, rim, pair_k, pair_s, xlo, xhi, ylo, yhi,
+    scale, first, beside, zp, zm, fives, whole, sides_x, sides_y, kp2, ck2, scale2, first2,
+    sides2_x, sides2_y, pair_r, rims, small, fix,
 ):
     lane = lanes_of((32, LANES))
+    row = lax.broadcasted_iota(jnp.int32, (32, LANES), 0)
     rim_k = rim[...]
-    kp[rows_of(0, 0, 40, 32)] = xlo[0]
-    kp[rows_of(33, 0, 40, 32)] = xhi[0]
-    kp[pl.ds(47, 32, stride=40), :] = ylo[0]
-    kp[pl.ds(80, 32, stride=40), :] = yhi[0]
-
-    def beyond(at, message):
+    for n, message in enumerate((xlo, xhi, ylo, yhi)):
+        beside[n] = message[0]
+
+    def beyond(k, v, message):
         kn, vn = message[0], message[2]
-        scale[at] = scale[at] + 0.5 * kn
-        k, v = kappa[at], initial[at]
-        first[at] = first[at] + 0.5 * ((k + kn) * vn - kn * v)
-
-    every = slice(None)
-    beyond(0, xlo)
-    beyond(31, xhi)
-    beyond((every, 0, every), ylo)
-    beyond((every, 31, every), yhi)
-
-    def slab(x, packed):
-        r = first[x]
-        h = WEIGHT / scale[x]
+        return 0.5 * kn, 0.5 * ((k + kn) * vn - kn * v)
+
+    fix[0], fix[1] = beyond(kappa[:, 0, :], initial[:, 0, :], ylo)
+    fix[2], fix[3] = beyond(kappa[:, 31, :], initial[:, 31, :], yhi)
+
+    def slab(x, packed, message=None):
+        one = pl.ds(x, 1)
+        d, r = diagonal[x], rest[x]
+        if message is not None:
+            more_d, more_r = beyond(kappa[x], initial[x], message)
+            d, r = d + more_d, r + more_r
+        d = jnp.where(row == 0, d + fix[0, one], jnp.where(row == 31, d + fix[2, one], d))
+        r = jnp.where(row == 0, r + fix[1, one], jnp.where(row == 31, r + fix[3, one], r))
+        h = WEIGHT / d
         e = h * r
         scale[x] = h
         first[x] = e
         packed = jnp.where(lane // 4 == x, turn(e, 4 * x + 2, 1), packed)
         return r, packed
 
-    def two(i, packed):
-        r0, packed = slab(2 * i, packed)
-        r1, packed = slab(2 * i + 1, packed)
+    def two(i, packed, low=None, high=None):
+        r0, packed = slab(2 * i, packed, low)
+        r1, packed = slab(2 * i + 1, packed, high)
         pair_r[i] = r0 + r1
         return packed
 
-    packed = lax.fori_loop(0, 16, two, jnp.zeros((32, LANES), F32), unroll=8)
+    packed = two(0, jnp.zeros((32, LANES), F32), low=xlo)
+    packed = lax.fori_loop(1, 15, two, packed, unroll=14)
+    packed = two(15, packed, high=xhi)
     sides_x[0] = first[31]
     sides_x[1] = first[0]
     sides_y[0] = first[:, 31, :]
@@ -542,7 +546,7 @@
 
 
 def fine_kernel(
-    kp, ck, scale, first, cf, base, edge, fp
+    kp, ck, scale, first, cf, beside, base, edge, fp
 ):
     inner = pl.ds(8, 32)
     lane32 = lanes_of((32, LANES))
@@ -564,11 +568,10 @@
         return carry
 
     lax.fori_loop(0, 32, slab, 0, unroll=4)
-    for n, (x, step) in enumerate(((0, -1), (31, 1))):
-        k = kp[rows_of(x + 1, 0, 40, 32)] + kp[rows_of(x + 1 + step, 0, 40, 32)]
-        edge[n] = 0.5 * scale[x] * k
-    for n, (y, step) in enumerate(((0, -1), (31, 1))):
-        k = kp[pl.ds(48 + y, 32, stride=40), :] + kp[pl.ds(48 + y + step, 32, stride=40), :]
+    for n, x in enumerate((0, 31)):
+        edge[n] = 0.5 * scale[x] * (kp[rows_of(x + 1, 0, 40, 32)] + beside[n])
+    for n, y in enumerate((0, 31)):
+        k = kp[pl.ds(48 + y, 32, stride=40), :] + beside[2 + n]
         edge[2 + n] = 0.5 * scale[:, y, :] * k
 
 
@@ -732,7 +735,7 @@
     return pltpu.VMEM(dims, F32)
 
 
-def local(kernel, outs, ins, scratch, name, sems=None, out_spec=VM, aliases=None):
+def local(kernel, outs, ins, scratch, name, sems=None, out_spec=VM):
     scratch = [pltpu.VMEM(dims, F32) for dims in scratch]
     if sems is not None:
         scratch.append(pltpu.SemaphoreType.DMA(sems))
@@ -742,7 +745,6 @@
         in_specs=ins,
         out_specs=[out_spec] * len(outs),
         scratch_shapes=scratch,
-        input_output_aliases=aliases or {},
         compiler_params=pltpu.CompilerParams(vmem_limit_bytes=24 * 1024 * 1024),
         name=name,
     )
@@ -779,22 +781,20 @@
         [VM] * 6, [(34, 48, LANES)], "inside",
     )(kappa, initial, rhs, sigma, zlo, zhi)
     (
-        kp, scale, first, zp, zm, fives, whole, sides_x, sides_y, kp2, ck2, scale2, first2,
+        scale, first, beside, zp, zm, fives, whole, sides_x, sides_y, kp2, ck2, scale2, first2,
         sides2_x, sides2_y,
     ) = local(
         residual_kernel,
         [
-            shape(1368, LANES), shape(*block), shape(*block),
+            shape(*block), shape(*block), shape(4, 32, LANES),
             shape(Z_ROWS, LANES), shape(Z_ROWS, LANES), shape(8, LANES),
             shape(64, LANES), shape(2, 32, LANES), shape(2, 32, LANES), shape(440, LANES),
             shape(16, LANES), shape(*block2), shape(*block2), shape(2, 16, LANES),
             shape(2, 16, LANES),
         ],
-        [VM] * 12, [(16, 32, LANES), (4, 32, LANES), (8, 16, LANES)],
-        "residual", aliases={2: 0, 3: 1, 4: 2},
-    )(
-        kappa, initial, kp, diagonal, rest, ck, pair_k, pair_s, xlo, xhi, ylo, yhi
-    )
+        [VM] * 11, [(16, 32, LANES), (4, 32, LANES), (8, 16, LANES), (4, 32, LANES)],
+        "residual",
+    )(kappa, initial, diagonal, rest, ck, pair_k, pair_s, xlo, xhi, ylo, yhi)
 
     zlo, zhi = passed(zp, "gz", 1), passed(zm, "gz", -1)
     own, xp, xm, ye, cf, cf2, blocks = local(
@@ -810,8 +810,8 @@
     planes = lax.all_to_all(blocks, ("gx", "gy"), 0, 0)
     base, edge = local(
         fine_kernel,
-        [shape(*block), shape(4, 32, LANES)], [VM] * 5, [(34, 48, LANES)], "fine",
-    )(kp, ck, scale, first, cf)
+        [shape(*block), shape(4, 32, LANES)], [VM] * 6, [(34, 48, LANES)], "fine",
+    )(kp, ck, scale, first, cf, beside)
     base2, edge2 = local(
         second_kernel, [shape(*block2), shape(4, 16, LANES)], [VM] * 5, [(18, 32, LANES)],
         "second",

time: 48.3 us -> 47.9 us (level)
  no operation moved by 1% of the time
where the time goes in v8:
time: 47.9 us; the launch traced here: 47.7 us
  starting transfers between devices  24.2 us (51%)
  Pallas kernels  14.3 us (30%)
  waiting for transfers between devices  8.97 us (19%)
    ppermute x14, starting transfers between devices, passed(): lax.ppermute(value, axis, [(i, (i + step) % count) for i in range(count)])  19.6 us
    ppermute x14, waiting for transfers between devices, passed(): lax.ppermute(value, axis, [(i, (i + step) % count) for i in range(count)])  8.97 us
    all_to_all x1, starting transfers between devices, on_device(): planes = lax.all_to_all(blocks, ('gx', 'gy'), 0, 0)  4.66 us
    pallas_call x1, Pallas kernels, on_device(): local(planes_kernel, [shape(16, LANES)], [SM] + [VM] * 4, [block2, (8, 8,...  2.68 us
    pallas_call x1, Pallas kernels, on_device(): local(three_kernel, [shape(64, LANES), shape(256, LANES), shape(*block)],...  2.55 us
    pallas_call x1, Pallas kernels, on_device(): local(inside_kernel, [shape(1368, LANES), shape(32, LANES), shape(*block)...  1.88 us
    pallas_call x1, Pallas kernels, on_device(): local(fine_kernel, [shape(*block), shape(4, 32, LANES)], [VM] * 6, [(34,...  1.81 us
    pallas_call x1, Pallas kernels, on_device(): local(faces_kernel, [edge, edge, edge, edge, shape(2, 32, LANES)] + [shap...  1.59 us
  transfers between devices with their start and end apart: 15, of which 4 were waited for; matrix products, arithmetic and copies ran while one was open for 0% of the time, Pallas kernels for 14%

profile of v8, /device:TPU:1, one launch (start us, length us, event | category | flops | bytes accessed | tf_op | source)
XLA Modules:
  0.0 47.7 jit_solution(3263520645315022781)
XLA Ops:
  0.0 1.6 %faces.1 = (f32[3,32,128]{2,1,0:T(8,128)S(1)}, f32[3,32,128]{2,1,0:T(8,128)S(1)}, f32[3,32,128]{2,1,0:T(8,128)S(1)}, f32[3,32,128]{2,1,0:T(8,128)S(1)}, f32[2,32...) custom-call(f32[32,32,128]{2,1,0:T(8,128)} %kappa_far.1, f32[32,32,128]{2,1,0:T(8,128)} %initial_far.3), custom_call_target="tpu_custom_call" | custom-call | tf_op jit(solution)/shard_map/faces/pallas_call | solution.py:767
  1.6 2.6 %collective-permute-start = (f32[2,32,128]{2,1,0:T(8,128)S(1)}, f32[2,32,128]{2,1,0:T(8,128)S(1)}, u32[]{:S(2)}, u32[]{:S(2)}) collective-permute-start(f32[2,32,128]{2,1,0:T(8,128)S(1)} %get-tuple-element.51), channel_id=1, source_target_pairs={{0,1},{1,2},{2,3},{3,4},{4,5},{5,6},{6,7},{7,0},{8,9},{9,10},{10,1... | collective-permute-start | bytes 98312 | tf_op jit(solution)/shard_map/ppermute | solution.py:758
  4.2 1.3 %collective-permute-start.2 = (f32[3,32,128]{2,1,0:T(8,128)S(1)}, f32[3,32,128]{2,1,0:T(8,128)S(1)}, u32[]{:S(2)}, u32[]{:S(2)}) collective-permute-start(f32[3,32,128]{2,1,0:T(8,128)S(1)} %get-tuple-element.57), channel_id=1, source_target_pairs={{0,32},{32,64},{64,96},{96,0},{1,33},{33,65},{65,97},{97,1},{2,34}... | collective-permute-start | bytes 147464 | tf_op jit(solution)/shard_map/ppermute | solution.py:758
  5.5 1.4 %collective-permute-start.3 = (f32[3,32,128]{2,1,0:T(8,128)S(1)}, f32[3,32,128]{2,1,0:T(8,128)S(1)}, u32[]{:S(2)}, u32[]{:S(2)}) collective-permute-start(f32[3,32,128]{2,1,0:T(8,128)S(1)} %get-tuple-element.58), channel_id=1, source_target_pairs={{0,96},{32,0},{64,32},{96,64},{1,97},{33,1},{65,33},{97,65},{2,98}... | collective-permute-start | bytes 147464 | tf_op jit(solution)/shard_map/ppermute | solution.py:758
  7.0 1.6 %collective-permute-start.4 = (f32[3,32,128]{2,1,0:T(8,128)S(1)}, f32[3,32,128]{2,1,0:T(8,128)S(1)}, u32[]{:S(2)}, u32[]{:S(2)}) collective-permute-start(f32[3,32,128]{2,1,0:T(8,128)S(1)} %get-tuple-element.59), channel_id=1, source_target_pairs={{0,8},{8,16},{16,24},{24,0},{1,9},{9,17},{17,25},{25,1},{2,10},{10... | collective-permute-start | bytes 147464 | tf_op jit(solution)/shard_map/ppermute | solution.py:758
  8.6 2.1 %collective-permute-start.5 = (f32[3,32,128]{2,1,0:T(8,128)S(1)}, f32[3,32,128]{2,1,0:T(8,128)S(1)}, u32[]{:S(2)}, u32[]{:S(2)}) collective-permute-start(f32[3,32,128]{2,1,0:T(8,128)S(1)} %get-tuple-element.60), channel_id=1, source_target_pairs={{0,24},{8,0},{16,8},{24,16},{1,25},{9,1},{17,9},{25,17},{2,26},{10... | collective-permute-start | bytes 147464 | tf_op jit(solution)/shard_map/ppermute | solution.py:758
  10.7 3.3 %collective-permute-done.1.zhi = f32[2,32,128]{2,1,0:T(8,128)S(1)} collective-permute-done((f32[2,32,128]{2,1,0:T(8,128)S(1)}, f32[2,32,128]{2,1,0:T(8,128)S(1)}, u32[]{:S(2)}, u32[]{:S(2)}) %collective-permute-start.1) | collective-permute-done | bytes 32800 | tf_op jit(solution)/shard_map/ppermute | solution.py:758
  14.1 1.9 %inside.1 = (f32[1368,128]{1,0:T(8,128)S(1)}, f32[32,128]{1,0:T(8,128)S(1)}, f32[32,32,128]{2,1,0:T(8,128)S(1)}, f32[32,32,128]{2,1,0:T(8,128)S(1)}, f32[16,32,1...) custom-call(f32[32,32,128]{2,1,0:T(8,128)S(1)} %get-tuple-element.49.kappa, f32[32,32,128]{2,1,0:T(8,128)S(1)} %get-tuple-element.50.initial, ...), custom_call_target="tpu_custom_call" | custom-call | tf_op jit(solution)/shard_map/inside/pallas_call | solution.py:775
  16.0 1.2 %residual.1 = (f32[32,32,128]{2,1,0:T(8,128)S(1)}, f32[32,32,128]{2,1,0:T(8,128)S(1)}, f32[4,32,128]{2,1,0:T(8,128)S(1)}, f32[40,128]{1,0:T(8,128)S(1)}, f32[40,...) custom-call(f32[32,32,128]{2,1,0:T(8,128)S(1)} %get-tuple-element.49, ...), custom_call_target="tpu_custom_call" | custom-call | tf_op jit(solution)/shard_map/residual/pallas_call | solution.py:786
  17.7 0.7 %collective-permute-done.6.zlo = f32[40,128]{1,0:T(8,128)S(1)} collective-permute-done((f32[40,128]{1,0:T(8,128)S(1)}, f32[40,128]{1,0:T(8,128)S(1)}, u32[]{:S(2)}, u32[]{:S(2)}) %collective-permute-start.6) | collective-permute-done | bytes 20512 | tf_op jit(solution)/shard_map/ppermute | solution.py:758
  18.4 2.0 %collective-permute-done.7.zhi = f32[40,128]{1,0:T(8,128)S(1)} collective-permute-done((f32[40,128]{1,0:T(8,128)S(1)}, f32[40,128]{1,0:T(8,128)S(1)}, u32[]{:S(2)}, u32[]{:S(2)}) %collective-permute-start.7) | collective-permute-done | bytes 20512 | tf_op jit(solution)/shard_map/ppermute | solution.py:758
  20.4 1.1 %window.1 = (f32[3,64,128]{2,1,0:T(8,128)S(1)}, f32[112,128]{1,0:T(8,128)S(1)}, f32[112,128]{1,0:T(8,128)S(1)}, f32[2,8,128]{2,1,0:T(8,128)S(1)}, f32[32,128]{1,...) custom-call(f32[40,128]{1,0:T(8,128)S(1)} %collective-permute-done.6.zlo, ...), custom_call_target="tpu_custom_call" | custom-call | tf_op jit(solution)/shard_map/window/pallas_call | solution.py:800
  21.5 4.7 %all-to-all-start = ((f32[16,16,128]{2,1,0:T(8,128)}), f32[16,16,128]{2,1,0:T(8,128)S(1)}, u32[]{:S(2)}, u32[]{:S(2)}) async-start(f32[16,16,128]{2,1,0:T(8,128)} %get-tuple-element.91), calls=%async_computation | async-start | bytes 262144 | tf_op jit(solution)/shard_map/all_to_all | solution.py:810
  26.1 1.4 %collective-permute-start.8 = (f32[112,128]{1,0:T(8,128)S(1)}, f32[112,128]{1,0:T(8,128)S(1)}, u32[]{:S(2)}, u32[]{:S(2)}) collective-permute-start(f32[112,128]{1,0:T(8,128)S(1)} %get-tuple-element.68.xp), channel_id=1, source_target_pairs={{0,32},{32,64},{64,96},{96,0},{1,33},{33,65},{65,97},{97,1},{2,34}... | collective-permute-start | bytes 172040 | tf_op jit(solution)/shard_map/ppermute | solution.py:758
  27.5 1.4 %collective-permute-start.9 = (f32[112,128]{1,0:T(8,128)S(1)}, f32[112,128]{1,0:T(8,128)S(1)}, u32[]{:S(2)}, u32[]{:S(2)}) collective-permute-start(f32[112,128]{1,0:T(8,128)S(1)} %get-tuple-element.69), channel_id=1, source_target_pairs={{0,96},{32,0},{64,32},{96,64},{1,97},{33,1},{65,33},{97,65},{2,98}... | collective-permute-start | bytes 172040 | tf_op jit(solution)/shard_map/ppermute | solution.py:758
  28.9 0.6 %second.1 = (f32[16,16,128]{2,1,0:T(8,128)S(1)}, f32[4,16,128]{2,1,0:T(8,128)S(1)}) custom-call(f32[440,128]{1,0:T(8,128)S(1)} %get-tuple-element.79.kp2, f32[16,128]{1,0:T(8,128)S(1)} %get-tuple-element.80.ck2, f32[16,16,128]{2,1,0:T(8,128)S(1)} %get-tuple-element.81.scale2, f32[16,16,128]{2,1,0:T(8,128)S(1)} %get-tuple-element.82.first2, ...), custom_call_target="tpu_custom_call" | custom-call | tf_op jit(solution)/shard_map/second/pallas_call | solution.py:815
  29.5 1.8 %fine.1 = (f32[32,32,128]{2,1,0:T(8,128)S(1)}, f32[4,32,128]{2,1,0:T(8,128)S(1)}) custom-call(f32[1368,128]{1,0:T(8,128)S(1)} %get-tuple-element.73.kp, f32[32,128]{1,0:T(8,128)S(1)} %get-tuple-element.54.rim.ck, f32[32,32,128]{2,1,0:T(8,128)S(1)} %get-tuple-element.74.scale, f32[32,32,128]{2,1,0:T(8,128)S(1)} %get-tuple-element.75.first, ...), custom_call_target="tpu_custom_call" | custom-call | tf_op jit(solution)/shard_map/fine/pallas_call | solution.py:811
  31.4 1.4 %collective-permute-start.10 = (f32[240,128]{1,0:T(8,128)S(1)}, f32[240,128]{1,0:T(8,128)S(1)}, u32[]{:S(2)}, u32[]{:S(2)}) collective-permute-start(f32[240,128]{1,0:T(8,128)S(1)} %get-tuple-element.85), channel_id=1, source_target_pairs={{0,8},{8,16},{16,24},{24,0},{1,9},{9,17},{17,25},{25,1},{2,10},{10... | collective-permute-start | bytes 368648 | tf_op jit(solution)/shard_map/ppermute | solution.py:758
  32.7 1.4 %collective-permute-start.11 = (f32[240,128]{1,0:T(8,128)S(1)}, f32[240,128]{1,0:T(8,128)S(1)}, u32[]{:S(2)}, u32[]{:S(2)}) collective-permute-start(f32[240,128]{1,0:T(8,128)S(1)} %get-tuple-element.86), channel_id=1, source_target_pairs={{0,24},{8,0},{16,8},{24,16},{1,25},{9,1},{17,9},{25,17},{2,26},{10... | collective-permute-start | bytes 368648 | tf_op jit(solution)/shard_map/ppermute | solution.py:758
  34.2 4.4 %collective-permute-start.12 = (f32[3,64,128]{2,1,0:T(8,128)S(1)}, f32[3,64,128]{2,1,0:T(8,128)S(1)}, u32[]{:S(2)}, u32[]{:S(2)}) collective-permute-start(f32[3,64,128]{2,1,0:T(8,128)S(1)} %ring.1), channel_id=1, source_target_pairs={{0,3},{1,4},{2,5},{3,6},{4,7},{5,0},{6,1},{7,2},{8,11},{9,12},{10,... | collective-permute-start | bytes 294920 | tf_op jit(solution)/shard_map/ppermute | solution.py:758
  38.7 2.5 %three.1 = (f32[64,128]{1,0:T(8,128)S(1)}, f32[256,128]{1,0:T(8,128)S(1)}, f32[32,32,128]{2,1,0:T(8,128)S(1)}) custom-call(f32[32,32,128]{2,1,0:T(8,128)} %initial_far.3, f32[3,64,128]{2,1,0:T(8,128)S(1)} %get-tuple-element.67.own, f32[112,128]{1,0:T(8,128)S(1)} %collective-permute-done.8.xlo, f32[112,128]{1,0:T(8,128)S(1)} %collective-permute-done.9.xhi, ...), custom_call_target="tpu_custom_call" | custom-call | tf_op jit(solution)/shard_map/three/pallas_call | solution.py:827
  41.2 2.9 %collective-permute-done.13.high = f32[3,64,128]{2,1,0:T(8,128)S(1)} collective-permute-done((f32[3,64,128]{2,1,0:T(8,128)S(1)}, f32[3,64,128]{2,1,0:T(8,128)S(1)}, u32[]{:S(2)}, u32[]{:S(2)}) %collective-permute-start.13) | collective-permute-done | bytes 98336 | tf_op jit(solution)/shard_map/ppermute | solution.py:758
  44.1 2.7 %planes.1.four_in = f32[16,128]{1,0:T(8,128)S(1)} custom-call(s32[3]{0:T(128)S(1)} %pad_add_fusion.place, f32[16,16,128]{2,1,0:T(8,128)S(1)} %all-to-all-done.blocks, f32[3,64,128]{2,1,0:T(8,128)S(1)} %ring.1, f32[3,64,128]{2,1,0:T(8,128)S(1)} %collective-permute-done.12.low, f32[3,64,128]{2,1,0:T(8,128)S(1)} %collective-permute-done.13.high), custom_call_target="tpu_custom_call" | custom-call | tf_op jit(solution)/shard_map/planes/pallas_call | solution.py:832
  46.8 0.9 %finish.1 = f32[32,32,128]{2,1,0:T(8,128)} custom-call(f32[64,128]{1,0:T(8,128)S(1)} %get-tuple-element.89.three_in, f32[256,128]{1,0:T(8,128)S(1)} %get-tuple-element.90.two_in, f32[16,128]{1,0:T(8,128)S(1)} %planes.1.four_in, f32[32,32,128]{2,1,0:T(8,128)S(1)} %get-tuple-element.92.fine_in), custom_call_target="tpu_custom_call" | custom-call | tf_op jit(solution)/shard_map/finish/pallas_call | solution.py:840
  (22 shorter events, 0.7 us)
Async XLA Ops:
  0.0 14.1 %copy-start = (f32[32,32,128]{2,1,0:T(8,128)S(1)}, f32[32,32,128]{2,1,0:T(8,128)}, u32[]{:S(2)}) copy-start(f32[32,32,128]{2,1,0:T(8,128)} %rhs.1) | copy-start | bytes 1572868
  0.0 14.1 %copy-start.1 = (f32[32,32,128]{2,1,0:T(8,128)S(1)}, f32[32,32,128]{2,1,0:T(8,128)}, u32[]{:S(2)}) copy-start(f32[32,32,128]{2,1,0:T(8,128)} %sigma.1) | copy-start | bytes 1572868
  1.6 9.1 %collective-permute-start = (f32[2,32,128]{2,1,0:T(8,128)S(1)}, f32[2,32,128]{2,1,0:T(8,128)S(1)}, u32[]{:S(2)}, u32[]{:S(2)}) collective-permute-start(f32[2,32,128]{2,1,0:T(8,128)S(1)} %get-tuple-element.51), channel_id=1, source_target_pairs={{0,1},{1,2},{2,3},{3,4},{4,5},{5,6},{6,7},{7,0},{8,9},{9,10},{10,1... | collective-permute-start | bytes 98312 | tf_op jit(solution)/shard_map/ppermute | solution.py:758
  4.2 11.7 %collective-permute-start.2 = (f32[3,32,128]{2,1,0:T(8,128)S(1)}, f32[3,32,128]{2,1,0:T(8,128)S(1)}, u32[]{:S(2)}, u32[]{:S(2)}) collective-permute-start(f32[3,32,128]{2,1,0:T(8,128)S(1)} %get-tuple-element.57), channel_id=1, source_target_pairs={{0,32},{32,64},{64,96},{96,0},{1,33},{33,65},{65,97},{97,1},{2,34}... | collective-permute-start | bytes 147464 | tf_op jit(solution)/shard_map/ppermute | solution.py:758
  5.5 10.4 %collective-permute-start.3 = (f32[3,32,128]{2,1,0:T(8,128)S(1)}, f32[3,32,128]{2,1,0:T(8,128)S(1)}, u32[]{:S(2)}, u32[]{:S(2)}) collective-permute-start(f32[3,32,128]{2,1,0:T(8,128)S(1)} %get-tuple-element.58), channel_id=1, source_target_pairs={{0,96},{32,0},{64,32},{96,64},{1,97},{33,1},{65,33},{97,65},{2,98}... | collective-permute-start | bytes 147464 | tf_op jit(solution)/shard_map/ppermute | solution.py:758
  7.0 9.0 %collective-permute-start.4 = (f32[3,32,128]{2,1,0:T(8,128)S(1)}, f32[3,32,128]{2,1,0:T(8,128)S(1)}, u32[]{:S(2)}, u32[]{:S(2)}) collective-permute-start(f32[3,32,128]{2,1,0:T(8,128)S(1)} %get-tuple-element.59), channel_id=1, source_target_pairs={{0,8},{8,16},{16,24},{24,0},{1,9},{9,17},{17,25},{25,1},{2,10},{10... | collective-permute-start | bytes 147464 | tf_op jit(solution)/shard_map/ppermute | solution.py:758
  8.6 7.4 %collective-permute-start.5 = (f32[3,32,128]{2,1,0:T(8,128)S(1)}, f32[3,32,128]{2,1,0:T(8,128)S(1)}, u32[]{:S(2)}, u32[]{:S(2)}) collective-permute-start(f32[3,32,128]{2,1,0:T(8,128)S(1)} %get-tuple-element.60), channel_id=1, source_target_pairs={{0,24},{8,0},{16,8},{24,16},{1,25},{9,1},{17,9},{25,17},{2,26},{10... | collective-permute-start | bytes 147464 | tf_op jit(solution)/shard_map/ppermute | solution.py:758
  10.7 3.3 %collective-permute-start.1 = (f32[2,32,128]{2,1,0:T(8,128)S(1)}, f32[2,32,128]{2,1,0:T(8,128)S(1)}, u32[]{:S(2)}, u32[]{:S(2)}) collective-permute-start(f32[2,32,128]{2,1,0:T(8,128)S(1)} %get-tuple-element.51), channel_id=1, source_target_pairs={{0,7},{1,0},{2,1},{3,2},{4,3},{5,4},{6,5},{7,6},{8,15},{9,8},{10,9... | collective-permute-start | bytes 98312 | tf_op jit(solution)/shard_map/ppermute | solution.py:758
  17.2 1.2 %collective-permute-start.6 = (f32[40,128]{1,0:T(8,128)S(1)}, f32[40,128]{1,0:T(8,128)S(1)}, u32[]{:S(2)}, u32[]{:S(2)}) collective-permute-start(f32[40,128]{1,0:T(8,128)S(1)} %get-tuple-element.61), channel_id=1, source_target_pairs={{0,1},{1,2},{2,3},{3,4},{4,5},{5,6},{6,7},{7,0},{8,9},{9,10},{10,1... | collective-permute-start | bytes 61448 | tf_op jit(solution)/shard_map/ppermute | solution.py:758
  17.2 3.2 %collective-permute-start.7 = (f32[40,128]{1,0:T(8,128)S(1)}, f32[40,128]{1,0:T(8,128)S(1)}, u32[]{:S(2)}, u32[]{:S(2)}) collective-permute-start(f32[40,128]{1,0:T(8,128)S(1)} %get-tuple-element.62), channel_id=1, source_target_pairs={{0,7},{1,0},{2,1},{3,2},{4,3},{5,4},{6,5},{7,6},{8,15},{9,8},{10,9... | collective-permute-start | bytes 61448 | tf_op jit(solution)/shard_map/ppermute | solution.py:758
  21.5 12.6 %all-to-all-start = ((f32[16,16,128]{2,1,0:T(8,128)}), f32[16,16,128]{2,1,0:T(8,128)S(1)}, u32[]{:S(2)}, u32[]{:S(2)}) async-start(f32[16,16,128]{2,1,0:T(8,128)} %get-tuple-element.91), calls=%async_computation | async-start | bytes 262144 | tf_op jit(solution)/shard_map/all_to_all | solution.py:810
  26.1 5.2 %collective-permute-start.8 = (f32[112,128]{1,0:T(8,128)S(1)}, f32[112,128]{1,0:T(8,128)S(1)}, u32[]{:S(2)}, u32[]{:S(2)}) collective-permute-start(f32[112,128]{1,0:T(8,128)S(1)} %get-tuple-element.68.xp), channel_id=1, source_target_pairs={{0,32},{32,64},{64,96},{96,0},{1,33},{33,65},{65,97},{97,1},{2,34}... | collective-permute-start | bytes 172040 | tf_op jit(solution)/shard_map/ppermute | solution.py:758
  27.5 3.8 %collective-permute-start.9 = (f32[112,128]{1,0:T(8,128)S(1)}, f32[112,128]{1,0:T(8,128)S(1)}, u32[]{:S(2)}, u32[]{:S(2)}) collective-permute-start(f32[112,128]{1,0:T(8,128)S(1)} %get-tuple-element.69), channel_id=1, source_target_pairs={{0,96},{32,0},{64,32},{96,64},{1,97},{33,1},{65,33},{97,65},{2,98}... | collective-permute-start | bytes 172040 | tf_op jit(solution)/shard_map/ppermute | solution.py:758
  31.4 7.3 %collective-permute-start.10 = (f32[240,128]{1,0:T(8,128)S(1)}, f32[240,128]{1,0:T(8,128)S(1)}, u32[]{:S(2)}, u32[]{:S(2)}) collective-permute-start(f32[240,128]{1,0:T(8,128)S(1)} %get-tuple-element.85), channel_id=1, source_target_pairs={{0,8},{8,16},{16,24},{24,0},{1,9},{9,17},{17,25},{25,1},{2,10},{10... | collective-permute-start | bytes 368648 | tf_op jit(solution)/shard_map/ppermute | solution.py:758
  32.7 5.9 %collective-permute-start.11 = (f32[240,128]{1,0:T(8,128)S(1)}, f32[240,128]{1,0:T(8,128)S(1)}, u32[]{:S(2)}, u32[]{:S(2)}) collective-permute-start(f32[240,128]{1,0:T(8,128)S(1)} %get-tuple-element.86), channel_id=1, source_target_pairs={{0,24},{8,0},{16,8},{24,16},{1,25},{9,1},{17,9},{25,17},{2,26},{10... | collective-permute-start | bytes 368648 | tf_op jit(solution)/shard_map/ppermute | solution.py:758
  34.2 7.1 %collective-permute-start.12 = (f32[3,64,128]{2,1,0:T(8,128)S(1)}, f32[3,64,128]{2,1,0:T(8,128)S(1)}, u32[]{:S(2)}, u32[]{:S(2)}) collective-permute-start(f32[3,64,128]{2,1,0:T(8,128)S(1)} %ring.1), channel_id=1, source_target_pairs={{0,3},{1,4},{2,5},{3,6},{4,7},{5,0},{6,1},{7,2},{8,11},{9,12},{10,... | collective-permute-start | bytes 294920 | tf_op jit(solution)/shard_map/ppermute | solution.py:758
  38.6 5.5 %collective-permute-start.13 = (f32[3,64,128]{2,1,0:T(8,128)S(1)}, f32[3,64,128]{2,1,0:T(8,128)S(1)}, u32[]{:S(2)}, u32[]{:S(2)}) collective-permute-start(f32[3,64,128]{2,1,0:T(8,128)S(1)} %ring.1), channel_id=1, source_target_pairs={{0,5},{1,6},{2,7},{3,0},{4,1},{5,2},{6,3},{7,4},{8,13},{9,14},{10,... | collective-permute-start | bytes 294920 | tf_op jit(solution)/shard_map/ppermute | solution.py:758

commit v9 on v8

--- a/solution.py
+++ b/solution.py
@@ -576,11 +576,10 @@
 
 
 def three_kernel(
-    initial_far, own, xlo, xhi, ylo, yhi, base, base2, edge, edge2,
+    initial, own, xlo, xhi, ylo, yhi, base, base2, edge, edge2,
     three_out, two_out, fine_out,
-    r3, s3, k3, c3, ea, eb, w2, sems,
+    r3, s3, k3, c3, ea, eb, w2,
 ):
-    inputs = fetch(((initial_far, fine_out),), sems)
     lane8 = lanes_of((8, LANES))
     for ix in range(3):
         for iy, y_ref in enumerate((ylo, None, yhi)):
@@ -680,11 +679,8 @@
         w2[:, y, :] = w2[:, y, :] + edge2[2 + n] * beyond(ref, Y_SEC)
     two_out[...] = spread(flat(w2[...]), square(lambda row, col: row == col // 2))
 
-    for copy in inputs:
-        copy.wait()
-
     def add(x, carry):
-        fine_out[x] = fine_out[x] + base[x]
+        fine_out[x] = initial[x] + base[x]
         return carry
 
     lax.fori_loop(0, 32, add, 0, unroll=8)
@@ -751,6 +747,7 @@
 
 
 def on_device(initial, rhs, kappa, sigma):
+    start = initial
     place = jnp.stack([lax.axis_index(axis) for axis in ("gx", "gy", "gz")]).astype(jnp.int32)
 
     def passed(value, axis, step):
@@ -825,10 +822,9 @@
     padded3 = (24, 40, LANES)
     block3 = (24, 24, LANES)
     three, two, fine = local(
-        three_kernel, [shape(64, LANES), shape(256, LANES), shape(*block)], [FAR] + [VM] * 9,
+        three_kernel, [shape(64, LANES), shape(256, LANES), shape(*block)], [VM] * 10,
         [block3, block3, padded3, (7,) + block3, padded3, padded3, block2], "three",
-        sems=(1, CHUNKS),
-    )(far[1], own, xlo, xhi, ylo, yhi, base, base2, edge, edge2)
+    )(start, own, xlo, xhi, ylo, yhi, base, base2, edge, edge2)
     (four,) = local(
         planes_kernel, [shape(16, LANES)], [SM] + [VM] * 4,
         [

time: 47.9 us -> 47.9 us (level)
  Pallas kernels: 14.3 us -> 13.4 us
  waiting for transfers between devices: 8.97 us -> 9.81 us
    pallas_call x1, Pallas kernels: 2.55 us -> 1.69 us  [on_device(): local(three_kernel, [shape(64, LANES), shape(256, LANES), shape(*block)],...]
    ppermute x14, waiting for transfers between devices: 8.97 us -> 9.81 us  [passed(): lax.ppermute(value, axis, [(i, (i + step) % count) for i in range(count)])]
  transfers between devices with their start and end apart: 15 -> 15, of which waited for: 4 -> 4; matrix products, arithmetic and copies ran while one was open for 0% -> 0% of each run, Pallas kernels for 14% -> 13%
where the time goes in v9:
time: 47.9 us; the launch traced here: 47.7 us
  starting transfers between devices  24.2 us (51%)
  Pallas kernels  13.4 us (28%)
  waiting for transfers between devices  9.81 us (20%)
    ppermute x14, starting transfers between devices, passed(): lax.ppermute(value, axis, [(i, (i + step) % count) for i in range(count)])  19.6 us
    ppermute x14, waiting for transfers between devices, passed(): lax.ppermute(value, axis, [(i, (i + step) % count) for i in range(count)])  9.81 us
    all_to_all x1, starting transfers between devices, on_device(): planes = lax.all_to_all(blocks, ('gx', 'gy'), 0, 0)  4.66 us
    pallas_call x1, Pallas kernels, on_device(): local(planes_kernel, [shape(16, LANES)], [SM] + [VM] * 4, [block2, (8, 8,...  2.68 us
    pallas_call x1, Pallas kernels, on_device(): local(inside_kernel, [shape(1368, LANES), shape(32, LANES), shape(*block)...  1.88 us
    pallas_call x1, Pallas kernels, on_device(): local(fine_kernel, [shape(*block), shape(4, 32, LANES)], [VM] * 6, [(34,...  1.79 us
    pallas_call x1, Pallas kernels, on_device(): local(three_kernel, [shape(64, LANES), shape(256, LANES), shape(*block)],...  1.69 us
    pallas_call x1, Pallas kernels, on_device(): local(faces_kernel, [edge, edge, edge, edge, shape(2, 32, LANES)] + [shap...  1.59 us
  transfers between devices with their start and end apart: 15, of which 4 were waited for; matrix products, arithmetic and copies ran while one was open for 0% of the time, Pallas kernels for 13%

profile of v9, /device:TPU:1, one launch (start us, length us, event | category | flops | bytes accessed | tf_op | source)
XLA Modules:
  0.0 47.7 jit_solution(10225220729723360256)
XLA Ops:
  0.0 1.6 %faces.1 = (f32[3,32,128]{2,1,0:T(8,128)S(1)}, f32[3,32,128]{2,1,0:T(8,128)S(1)}, f32[3,32,128]{2,1,0:T(8,128)S(1)}, f32[3,32,128]{2,1,0:T(8,128)S(1)}, f32[2,32...) custom-call(f32[32,32,128]{2,1,0:T(8,128)} %kappa_far.1, f32[32,32,128]{2,1,0:T(8,128)} %initial.1), custom_call_target="tpu_custom_call" | custom-call | tf_op jit(solution)/shard_map/faces/pallas_call | solution.py:764
  1.6 2.6 %collective-permute-start = (f32[2,32,128]{2,1,0:T(8,128)S(1)}, f32[2,32,128]{2,1,0:T(8,128)S(1)}, u32[]{:S(2)}, u32[]{:S(2)}) collective-permute-start(f32[2,32,128]{2,1,0:T(8,128)S(1)} %get-tuple-element.51), channel_id=1, source_target_pairs={{0,1},{1,2},{2,3},{3,4},{4,5},{5,6},{6,7},{7,0},{8,9},{9,10},{10,1... | collective-permute-start | bytes 98312 | tf_op jit(solution)/shard_map/ppermute | solution.py:755
  4.2 1.3 %collective-permute-start.2 = (f32[3,32,128]{2,1,0:T(8,128)S(1)}, f32[3,32,128]{2,1,0:T(8,128)S(1)}, u32[]{:S(2)}, u32[]{:S(2)}) collective-permute-start(f32[3,32,128]{2,1,0:T(8,128)S(1)} %get-tuple-element.57), channel_id=1, source_target_pairs={{0,32},{32,64},{64,96},{96,0},{1,33},{33,65},{65,97},{97,1},{2,34}... | collective-permute-start | bytes 147464 | tf_op jit(solution)/shard_map/ppermute | solution.py:755
  5.5 1.4 %collective-permute-start.3 = (f32[3,32,128]{2,1,0:T(8,128)S(1)}, f32[3,32,128]{2,1,0:T(8,128)S(1)}, u32[]{:S(2)}, u32[]{:S(2)}) collective-permute-start(f32[3,32,128]{2,1,0:T(8,128)S(1)} %get-tuple-element.58), channel_id=1, source_target_pairs={{0,96},{32,0},{64,32},{96,64},{1,97},{33,1},{65,33},{97,65},{2,98}... | collective-permute-start | bytes 147464 | tf_op jit(solution)/shard_map/ppermute | solution.py:755
  7.0 1.6 %collective-permute-start.4 = (f32[3,32,128]{2,1,0:T(8,128)S(1)}, f32[3,32,128]{2,1,0:T(8,128)S(1)}, u32[]{:S(2)}, u32[]{:S(2)}) collective-permute-start(f32[3,32,128]{2,1,0:T(8,128)S(1)} %get-tuple-element.59), channel_id=1, source_target_pairs={{0,8},{8,16},{16,24},{24,0},{1,9},{9,17},{17,25},{25,1},{2,10},{10... | collective-permute-start | bytes 147464 | tf_op jit(solution)/shard_map/ppermute | solution.py:755
  8.6 2.1 %collective-permute-start.5 = (f32[3,32,128]{2,1,0:T(8,128)S(1)}, f32[3,32,128]{2,1,0:T(8,128)S(1)}, u32[]{:S(2)}, u32[]{:S(2)}) collective-permute-start(f32[3,32,128]{2,1,0:T(8,128)S(1)} %get-tuple-element.60), channel_id=1, source_target_pairs={{0,24},{8,0},{16,8},{24,16},{1,25},{9,1},{17,9},{25,17},{2,26},{10... | collective-permute-start | bytes 147464 | tf_op jit(solution)/shard_map/ppermute | solution.py:755
  10.7 3.3 %collective-permute-done.1.zhi = f32[2,32,128]{2,1,0:T(8,128)S(1)} collective-permute-done((f32[2,32,128]{2,1,0:T(8,128)S(1)}, f32[2,32,128]{2,1,0:T(8,128)S(1)}, u32[]{:S(2)}, u32[]{:S(2)}) %collective-permute-start.1) | collective-permute-done | bytes 32800 | tf_op jit(solution)/shard_map/ppermute | solution.py:755
  14.1 1.9 %inside.1 = (f32[1368,128]{1,0:T(8,128)S(1)}, f32[32,128]{1,0:T(8,128)S(1)}, f32[32,32,128]{2,1,0:T(8,128)S(1)}, f32[32,32,128]{2,1,0:T(8,128)S(1)}, f32[16,32,1...) custom-call(f32[32,32,128]{2,1,0:T(8,128)S(1)} %get-tuple-element.49.kappa, f32[32,32,128]{2,1,0:T(8,128)S(1)} %get-tuple-element.50.initial, ...), custom_call_target="tpu_custom_call" | custom-call | tf_op jit(solution)/shard_map/inside/pallas_call | solution.py:772
  16.0 1.2 %residual.1 = (f32[32,32,128]{2,1,0:T(8,128)S(1)}, f32[32,32,128]{2,1,0:T(8,128)S(1)}, f32[4,32,128]{2,1,0:T(8,128)S(1)}, f32[40,128]{1,0:T(8,128)S(1)}, f32[40,...) custom-call(f32[32,32,128]{2,1,0:T(8,128)S(1)} %get-tuple-element.49, ...), custom_call_target="tpu_custom_call" | custom-call | tf_op jit(solution)/shard_map/residual/pallas_call | solution.py:783
  17.7 0.7 %collective-permute-done.6.zlo = f32[40,128]{1,0:T(8,128)S(1)} collective-permute-done((f32[40,128]{1,0:T(8,128)S(1)}, f32[40,128]{1,0:T(8,128)S(1)}, u32[]{:S(2)}, u32[]{:S(2)}) %collective-permute-start.6) | collective-permute-done | bytes 20512 | tf_op jit(solution)/shard_map/ppermute | solution.py:755
  18.4 2.0 %collective-permute-done.7.zhi = f32[40,128]{1,0:T(8,128)S(1)} collective-permute-done((f32[40,128]{1,0:T(8,128)S(1)}, f32[40,128]{1,0:T(8,128)S(1)}, u32[]{:S(2)}, u32[]{:S(2)}) %collective-permute-start.7) | collective-permute-done | bytes 20512 | tf_op jit(solution)/shard_map/ppermute | solution.py:755
  20.4 1.1 %window.1 = (f32[3,64,128]{2,1,0:T(8,128)S(1)}, f32[112,128]{1,0:T(8,128)S(1)}, f32[112,128]{1,0:T(8,128)S(1)}, f32[2,8,128]{2,1,0:T(8,128)S(1)}, f32[32,128]{1,...) custom-call(f32[40,128]{1,0:T(8,128)S(1)} %collective-permute-done.6.zlo, ...), custom_call_target="tpu_custom_call" | custom-call | tf_op jit(solution)/shard_map/window/pallas_call | solution.py:797
  21.5 4.7 %all-to-all-start = ((f32[16,16,128]{2,1,0:T(8,128)}), f32[16,16,128]{2,1,0:T(8,128)S(1)}, u32[]{:S(2)}, u32[]{:S(2)}) async-start(f32[16,16,128]{2,1,0:T(8,128)} %get-tuple-element.91), calls=%async_computation | async-start | bytes 262144 | tf_op jit(solution)/shard_map/all_to_all | solution.py:807
  26.1 1.4 %collective-permute-start.8 = (f32[112,128]{1,0:T(8,128)S(1)}, f32[112,128]{1,0:T(8,128)S(1)}, u32[]{:S(2)}, u32[]{:S(2)}) collective-permute-start(f32[112,128]{1,0:T(8,128)S(1)} %get-tuple-element.68.xp), channel_id=1, source_target_pairs={{0,32},{32,64},{64,96},{96,0},{1,33},{33,65},{65,97},{97,1},{2,34}... | collective-permute-start | bytes 172040 | tf_op jit(solution)/shard_map/ppermute | solution.py:755
  27.5 1.4 %collective-permute-start.9 = (f32[112,128]{1,0:T(8,128)S(1)}, f32[112,128]{1,0:T(8,128)S(1)}, u32[]{:S(2)}, u32[]{:S(2)}) collective-permute-start(f32[112,128]{1,0:T(8,128)S(1)} %get-tuple-element.69), channel_id=1, source_target_pairs={{0,96},{32,0},{64,32},{96,64},{1,97},{33,1},{65,33},{97,65},{2,98}... | collective-permute-start | bytes 172040 | tf_op jit(solution)/shard_map/ppermute | solution.py:755
  28.9 0.6 %second.1 = (f32[16,16,128]{2,1,0:T(8,128)S(1)}, f32[4,16,128]{2,1,0:T(8,128)S(1)}) custom-call(f32[440,128]{1,0:T(8,128)S(1)} %get-tuple-element.79.kp2, f32[16,128]{1,0:T(8,128)S(1)} %get-tuple-element.80.ck2, f32[16,16,128]{2,1,0:T(8,128)S(1)} %get-tuple-element.81.scale2, f32[16,16,128]{2,1,0:T(8,128)S(1)} %get-tuple-element.82.first2, ...), custom_call_target="tpu_custom_call" | custom-call | tf_op jit(solution)/shard_map/second/pallas_call | solution.py:812
  29.5 1.8 %fine.1 = (f32[32,32,128]{2,1,0:T(8,128)S(1)}, f32[4,32,128]{2,1,0:T(8,128)S(1)}) custom-call(f32[1368,128]{1,0:T(8,128)S(1)} %get-tuple-element.73.kp, f32[32,128]{1,0:T(8,128)S(1)} %get-tuple-element.54.rim.ck, f32[32,32,128]{2,1,0:T(8,128)S(1)} %get-tuple-element.74.scale, f32[32,32,128]{2,1,0:T(8,128)S(1)} %get-tuple-element.75.first, ...), custom_call_target="tpu_custom_call" | custom-call | tf_op jit(solution)/shard_map/fine/pallas_call | solution.py:808
  31.4 1.4 %collective-permute-start.10 = (f32[240,128]{1,0:T(8,128)S(1)}, f32[240,128]{1,0:T(8,128)S(1)}, u32[]{:S(2)}, u32[]{:S(2)}) collective-permute-start(f32[240,128]{1,0:T(8,128)S(1)} %get-tuple-element.85), channel_id=1, source_target_pairs={{0,8},{8,16},{16,24},{24,0},{1,9},{9,17},{17,25},{25,1},{2,10},{10... | collective-permute-start | bytes 368648 | tf_op jit(solution)/shard_map/ppermute | solution.py:755
  32.7 1.4 %collective-permute-start.11 = (f32[240,128]{1,0:T(8,128)S(1)}, f32[240,128]{1,0:T(8,128)S(1)}, u32[]{:S(2)}, u32[]{:S(2)}) collective-permute-start(f32[240,128]{1,0:T(8,128)S(1)} %get-tuple-element.86), channel_id=1, source_target_pairs={{0,24},{8,0},{16,8},{24,16},{1,25},{9,1},{17,9},{25,17},{2,26},{10... | collective-permute-start | bytes 368648 | tf_op jit(solution)/shard_map/ppermute | solution.py:755
  34.2 4.4 %collective-permute-start.12 = (f32[3,64,128]{2,1,0:T(8,128)S(1)}, f32[3,64,128]{2,1,0:T(8,128)S(1)}, u32[]{:S(2)}, u32[]{:S(2)}) collective-permute-start(f32[3,64,128]{2,1,0:T(8,128)S(1)} %ring.1), channel_id=1, source_target_pairs={{0,3},{1,4},{2,5},{3,6},{4,7},{5,0},{6,1},{7,2},{8,11},{9,12},{10,... | collective-permute-start | bytes 294920 | tf_op jit(solution)/shard_map/ppermute | solution.py:755
  38.7 1.7 %three.1 = (f32[64,128]{1,0:T(8,128)S(1)}, f32[256,128]{1,0:T(8,128)S(1)}, f32[32,32,128]{2,1,0:T(8,128)S(1)}) custom-call(f32[32,32,128]{2,1,0:T(8,128)S(1)} %copy-done, f32[3,64,128]{2,1,0:T(8,128)S(1)} %get-tuple-element.67.own, f32[112,128]{1,0:T(8,128)S(1)} %collective-permute-done.8.xlo, f32[112,128]{1,0:T(8,128)S(1)} %collective-permute-done.9.xhi, ...), custom_call_target="tpu_custom_call" | custom-call | tf_op jit(solution)/shard_map/three/pallas_call | solution.py:824
  40.4 3.7 %collective-permute-done.13.high = f32[3,64,128]{2,1,0:T(8,128)S(1)} collective-permute-done((f32[3,64,128]{2,1,0:T(8,128)S(1)}, f32[3,64,128]{2,1,0:T(8,128)S(1)}, u32[]{:S(2)}, u32[]{:S(2)}) %collective-permute-start.13) | collective-permute-done | bytes 98336 | tf_op jit(solution)/shard_map/ppermute | solution.py:755
  44.1 2.7 %planes.1.four_in = f32[16,128]{1,0:T(8,128)S(1)} custom-call(s32[3]{0:T(128)S(1)} %pad_add_fusion.place, f32[16,16,128]{2,1,0:T(8,128)S(1)} %all-to-all-done.blocks, f32[3,64,128]{2,1,0:T(8,128)S(1)} %ring.1, f32[3,64,128]{2,1,0:T(8,128)S(1)} %collective-permute-done.12.low, f32[3,64,128]{2,1,0:T(8,128)S(1)} %collective-permute-done.13.high), custom_call_target="tpu_custom_call" | custom-call | tf_op jit(solution)/shard_map/planes/pallas_call | solution.py:828
  46.8 0.9 %finish.1 = f32[32,32,128]{2,1,0:T(8,128)} custom-call(f32[64,128]{1,0:T(8,128)S(1)} %get-tuple-element.89.three_in, f32[256,128]{1,0:T(8,128)S(1)} %get-tuple-element.90.two_in, f32[16,128]{1,0:T(8,128)S(1)} %planes.1.four_in, f32[32,32,128]{2,1,0:T(8,128)S(1)} %get-tuple-element.92.fine_in), custom_call_target="tpu_custom_call" | custom-call | tf_op jit(solution)/shard_map/finish/pallas_call | solution.py:836
  (24 shorter events, 0.7 us)
Async XLA Ops:
  0.0 14.1 %copy-start.1 = (f32[32,32,128]{2,1,0:T(8,128)S(1)}, f32[32,32,128]{2,1,0:T(8,128)}, u32[]{:S(2)}) copy-start(f32[32,32,128]{2,1,0:T(8,128)} %rhs.1) | copy-start | bytes 1572868
  0.0 14.1 %copy-start.2 = (f32[32,32,128]{2,1,0:T(8,128)S(1)}, f32[32,32,128]{2,1,0:T(8,128)}, u32[]{:S(2)}) copy-start(f32[32,32,128]{2,1,0:T(8,128)} %sigma.1) | copy-start | bytes 1572868
  1.6 9.1 %collective-permute-start = (f32[2,32,128]{2,1,0:T(8,128)S(1)}, f32[2,32,128]{2,1,0:T(8,128)S(1)}, u32[]{:S(2)}, u32[]{:S(2)}) collective-permute-start(f32[2,32,128]{2,1,0:T(8,128)S(1)} %get-tuple-element.51), channel_id=1, source_target_pairs={{0,1},{1,2},{2,3},{3,4},{4,5},{5,6},{6,7},{7,0},{8,9},{9,10},{10,1... | collective-permute-start | bytes 98312 | tf_op jit(solution)/shard_map/ppermute | solution.py:755
  4.2 11.7 %collective-permute-start.2 = (f32[3,32,128]{2,1,0:T(8,128)S(1)}, f32[3,32,128]{2,1,0:T(8,128)S(1)}, u32[]{:S(2)}, u32[]{:S(2)}) collective-permute-start(f32[3,32,128]{2,1,0:T(8,128)S(1)} %get-tuple-element.57), channel_id=1, source_target_pairs={{0,32},{32,64},{64,96},{96,0},{1,33},{33,65},{65,97},{97,1},{2,34}... | collective-permute-start | bytes 147464 | tf_op jit(solution)/shard_map/ppermute | solution.py:755
  5.5 10.4 %collective-permute-start.3 = (f32[3,32,128]{2,1,0:T(8,128)S(1)}, f32[3,32,128]{2,1,0:T(8,128)S(1)}, u32[]{:S(2)}, u32[]{:S(2)}) collective-permute-start(f32[3,32,128]{2,1,0:T(8,128)S(1)} %get-tuple-element.58), channel_id=1, source_target_pairs={{0,96},{32,0},{64,32},{96,64},{1,97},{33,1},{65,33},{97,65},{2,98}... | collective-permute-start | bytes 147464 | tf_op jit(solution)/shard_map/ppermute | solution.py:755
  7.0 9.0 %collective-permute-start.4 = (f32[3,32,128]{2,1,0:T(8,128)S(1)}, f32[3,32,128]{2,1,0:T(8,128)S(1)}, u32[]{:S(2)}, u32[]{:S(2)}) collective-permute-start(f32[3,32,128]{2,1,0:T(8,128)S(1)} %get-tuple-element.59), channel_id=1, source_target_pairs={{0,8},{8,16},{16,24},{24,0},{1,9},{9,17},{17,25},{25,1},{2,10},{10... | collective-permute-start | bytes 147464 | tf_op jit(solution)/shard_map/ppermute | solution.py:755
  8.6 7.4 %collective-permute-start.5 = (f32[3,32,128]{2,1,0:T(8,128)S(1)}, f32[3,32,128]{2,1,0:T(8,128)S(1)}, u32[]{:S(2)}, u32[]{:S(2)}) collective-permute-start(f32[3,32,128]{2,1,0:T(8,128)S(1)} %get-tuple-element.60), channel_id=1, source_target_pairs={{0,24},{8,0},{16,8},{24,16},{1,25},{9,1},{17,9},{25,17},{2,26},{10... | collective-permute-start | bytes 147464 | tf_op jit(solution)/shard_map/ppermute | solution.py:755
  10.7 3.3 %collective-permute-start.1 = (f32[2,32,128]{2,1,0:T(8,128)S(1)}, f32[2,32,128]{2,1,0:T(8,128)S(1)}, u32[]{:S(2)}, u32[]{:S(2)}) collective-permute-start(f32[2,32,128]{2,1,0:T(8,128)S(1)} %get-tuple-element.51), channel_id=1, source_target_pairs={{0,7},{1,0},{2,1},{3,2},{4,3},{5,4},{6,5},{7,6},{8,15},{9,8},{10,9... | collective-permute-start | bytes 98312 | tf_op jit(solution)/shard_map/ppermute | solution.py:755
  17.2 1.2 %collective-permute-start.6 = (f32[40,128]{1,0:T(8,128)S(1)}, f32[40,128]{1,0:T(8,128)S(1)}, u32[]{:S(2)}, u32[]{:S(2)}) collective-permute-start(f32[40,128]{1,0:T(8,128)S(1)} %get-tuple-element.61), channel_id=1, source_target_pairs={{0,1},{1,2},{2,3},{3,4},{4,5},{5,6},{6,7},{7,0},{8,9},{9,10},{10,1... | collective-permute-start | bytes 61448 | tf_op jit(solution)/shard_map/ppermute | solution.py:755
  17.2 3.2 %collective-permute-start.7 = (f32[40,128]{1,0:T(8,128)S(1)}, f32[40,128]{1,0:T(8,128)S(1)}, u32[]{:S(2)}, u32[]{:S(2)}) collective-permute-start(f32[40,128]{1,0:T(8,128)S(1)} %get-tuple-element.62), channel_id=1, source_target_pairs={{0,7},{1,0},{2,1},{3,2},{4,3},{5,4},{6,5},{7,6},{8,15},{9,8},{10,9... | collective-permute-start | bytes 61448 | tf_op jit(solution)/shard_map/ppermute | solution.py:755
  21.5 12.6 %all-to-all-start = ((f32[16,16,128]{2,1,0:T(8,128)}), f32[16,16,128]{2,1,0:T(8,128)S(1)}, u32[]{:S(2)}, u32[]{:S(2)}) async-start(f32[16,16,128]{2,1,0:T(8,128)} %get-tuple-element.91), calls=%async_computation | async-start | bytes 262144 | tf_op jit(solution)/shard_map/all_to_all | solution.py:807
  26.1 5.2 %collective-permute-start.8 = (f32[112,128]{1,0:T(8,128)S(1)}, f32[112,128]{1,0:T(8,128)S(1)}, u32[]{:S(2)}, u32[]{:S(2)}) collective-permute-start(f32[112,128]{1,0:T(8,128)S(1)} %get-tuple-element.68.xp), channel_id=1, source_target_pairs={{0,32},{32,64},{64,96},{96,0},{1,33},{33,65},{65,97},{97,1},{2,34}... | collective-permute-start | bytes 172040 | tf_op jit(solution)/shard_map/ppermute | solution.py:755
  27.5 3.8 %collective-permute-start.9 = (f32[112,128]{1,0:T(8,128)S(1)}, f32[112,128]{1,0:T(8,128)S(1)}, u32[]{:S(2)}, u32[]{:S(2)}) collective-permute-start(f32[112,128]{1,0:T(8,128)S(1)} %get-tuple-element.69), channel_id=1, source_target_pairs={{0,96},{32,0},{64,32},{96,64},{1,97},{33,1},{65,33},{97,65},{2,98}... | collective-permute-start | bytes 172040 | tf_op jit(solution)/shard_map/ppermute | solution.py:755
  31.3 7.4 %copy-start = (f32[32,32,128]{2,1,0:T(8,128)S(1)}, f32[32,32,128]{2,1,0:T(8,128)}, u32[]{:S(2)}) copy-start(f32[32,32,128]{2,1,0:T(8,128)} %initial.1) | copy-start | bytes 1572868
  31.4 7.3 %collective-permute-start.10 = (f32[240,128]{1,0:T(8,128)S(1)}, f32[240,128]{1,0:T(8,128)S(1)}, u32[]{:S(2)}, u32[]{:S(2)}) collective-permute-start(f32[240,128]{1,0:T(8,128)S(1)} %get-tuple-element.85), channel_id=1, source_target_pairs={{0,8},{8,16},{16,24},{24,0},{1,9},{9,17},{17,25},{25,1},{2,10},{10... | collective-permute-start | bytes 368648 | tf_op jit(solution)/shard_map/ppermute | solution.py:755
  32.7 5.9 %collective-permute-start.11 = (f32[240,128]{1,0:T(8,128)S(1)}, f32[240,128]{1,0:T(8,128)S(1)}, u32[]{:S(2)}, u32[]{:S(2)}) collective-permute-start(f32[240,128]{1,0:T(8,128)S(1)} %get-tuple-element.86), channel_id=1, source_target_pairs={{0,24},{8,0},{16,8},{24,16},{1,25},{9,1},{17,9},{25,17},{2,26},{10... | collective-permute-start | bytes 368648 | tf_op jit(solution)/shard_map/ppermute | solution.py:755
  34.2 6.2 %collective-permute-start.12 = (f32[3,64,128]{2,1,0:T(8,128)S(1)}, f32[3,64,128]{2,1,0:T(8,128)S(1)}, u32[]{:S(2)}, u32[]{:S(2)}) collective-permute-start(f32[3,64,128]{2,1,0:T(8,128)S(1)} %ring.1), channel_id=1, source_target_pairs={{0,3},{1,4},{2,5},{3,6},{4,7},{5,0},{6,1},{7,2},{8,11},{9,12},{10,... | collective-permute-start | bytes 294920 | tf_op jit(solution)/shard_map/ppermute | solution.py:755
  38.6 5.5 %collective-permute-start.13 = (f32[3,64,128]{2,1,0:T(8,128)S(1)}, f32[3,64,128]{2,1,0:T(8,128)S(1)}, u32[]{:S(2)}, u32[]{:S(2)}) collective-permute-start(f32[3,64,128]{2,1,0:T(8,128)S(1)} %ring.1), channel_id=1, source_target_pairs={{0,5},{1,6},{2,7},{3,0},{4,1},{5,2},{6,3},{7,4},{8,13},{9,14},{10,... | collective-permute-start | bytes 294920 | tf_op jit(solution)/shard_map/ppermute | solution.py:755

commit v10 on v9

--- a/solution.py
+++ b/solution.py
@@ -465,12 +465,11 @@
 
 
 def ring_kernel(blocks, ring):
-    for q in range(16):
-        for i in range(2):
-            row = 8 * (2 * (q // 4) + i) + 2 * (q % 4)
-            for n in range(3):
-                source = blocks[q, 4 * n + 2 * i : 4 * n + 2 * i + 2]
-                ring[n, row : row + 2] = source
+    for x in range(8):
+        for n in range(3):
+            start = 4 * n + 2 * (x % 2)
+            pieces = [blocks[4 * (x // 2) + y, start : start + 2] for y in range(4)]
+            ring[n, 8 * x : 8 * x + 8] = jnp.concatenate(pieces, 0)
 
 
 def planes_kernel(
@@ -508,7 +507,7 @@
     fields5 = [field(f) for f in range(3)]
     fields6 = [level_six(v, w, n) for n, (v, w) in enumerate(zip(fields5, (0.5, 0.125, 0.5)))]
     fields7 = [level_seven(v) for v in fields6]
-    r4 = l4[...]
+    r4 = l4[0:16]
     e4 = periodic_setup(r4, turn(r4, 96, 2), turn(r4, 64, 2), c4)
     e5 = periodic_setup(*fields5, c5)
     e6 = periodic_setup(*fields6, c6)
@@ -525,16 +524,16 @@
     l6[0] = e6 + e7
     six = l6[0, gx, pl.ds(gy, 1)] + jnp.zeros((8, LANES), F32)
     six = spread(six, square(lambda row, col: row == col // 32))
-    l5[...] = e5
-    w4[...] = jnp.zeros((16, LANES), F32)
+    l5[0:8] = e5
+    w4[0:16] = jnp.zeros((16, LANES), F32)
     w4[0:2] = l5[2 * gx, pl.ds(2 * gy, 2)]
     w4[2:4] = l5[2 * gx + 1, pl.ds(2 * gy, 2)]
     five = six + spread(w4[0:8], square(lambda row, col: row == col // 16))
-    l4[...] = e4
+    l4[0:16] = e4
     for i in range(4):
         w4[4 * i : 4 * i + 4] = l4[4 * gx + i, pl.ds(4 * gy, 4)]
     lane16 = lanes_of((16, LANES))
-    four = jnp.where((lane16 >= 8) & (lane16 < 24), w4[...], 0.0)
+    four = jnp.where((lane16 >= 8) & (lane16 < 24), w4[0:16], 0.0)
     four = spread(four, square(lambda row, col: row == 8 + col // 8))
     for i in range(4):
         for j in range(2):
@@ -542,7 +541,7 @@
             w4[4 * i + 2 * j : 4 * i + 2 * j + 2] = jnp.broadcast_to(
                 five[row : row + 1], (2, LANES)
             )
-    four_out[...] = four + w4[...]
+    four_out[...] = four + w4[0:16]
 
 
 def fine_kernel(
@@ -698,7 +697,7 @@
         block = four[4 * (i // 2) : 4 * (i // 2) + 4]
         w3[i, pl.ds(0, 4, stride=2), :] = block
         w3[i, pl.ds(1, 4, stride=2), :] = block
-    three = three_in[...] + flat(w3[...])
+    three = three_in[...] + flat(w3[0:8])
 
     even8, odd8 = pl.ds(0, 8, stride=2), pl.ds(1, 8, stride=2)
     for i in range(16):
@@ -789,7 +788,7 @@
             shape(16, LANES), shape(*block2), shape(*block2), shape(2, 16, LANES),
             shape(2, 16, LANES),
         ],
-        [VM] * 11, [(16, 32, LANES), (4, 32, LANES), (8, 16, LANES), (4, 32, LANES)],
+        [VM] * 11, [(16, 32, LANES), (4, 32, LANES), (8, 16, LANES), (5, 32, LANES)],
         "residual",
     )(kappa, initial, diagonal, rest, ck, pair_k, pair_s, xlo, xhi, ylo, yhi)
 
@@ -828,14 +827,14 @@
     (four,) = local(
         planes_kernel, [shape(16, LANES)], [SM] + [VM] * 4,
         [
-            block2, (8, 8, LANES), (3, 4, 8, LANES), (7,) + block2,
-            (7, 8, 8, LANES), (7, 4, 8, LANES), (7, 4, 8, LANES), (16, LANES),
+            (17, 16, LANES), (9, 8, LANES), (4, 4, 8, LANES), (7,) + block2,
+            (7, 8, 8, LANES), (7, 4, 8, LANES), (7, 4, 8, LANES), (24, LANES),
         ],
         "planes",
     )(place, planes, ring, ring_low, ring_high)
     return local(
         finish_kernel, [pltpu.HBM(block, F32)], [VM] * 4,
-        [(8, 8, LANES), block2, (16, 32, LANES), block],
+        [(9, 8, LANES), block2, (16, 32, LANES), block],
         "finish", sems=(CHUNKS,), out_spec=FAR,
     )(three, two, four, fine)[0]
 

time: 47.9 us -> 47.9 us (level)
  no operation moved by 1% of the time
where the time goes in v10:
time: 47.9 us; the launch traced here: 47.7 us
  starting transfers between devices  24.2 us (51%)
  Pallas kernels  13.4 us (28%)
  waiting for transfers between devices  9.81 us (20%)
    ppermute x14, starting transfers between devices, passed(): lax.ppermute(value, axis, [(i, (i + step) % count) for i in range(count)])  19.6 us
    ppermute x14, waiting for transfers between devices, passed(): lax.ppermute(value, axis, [(i, (i + step) % count) for i in range(count)])  9.81 us
    all_to_all x1, starting transfers between devices, on_device(): planes = lax.all_to_all(blocks, ('gx', 'gy'), 0, 0)  4.66 us
    pallas_call x1, Pallas kernels, on_device(): local(planes_kernel, [shape(16, LANES)], [SM] + [VM] * 4, [(17, 16, LANES...  2.68 us
    pallas_call x1, Pallas kernels, on_device(): local(inside_kernel, [shape(1368, LANES), shape(32, LANES), shape(*block)...  1.88 us
    pallas_call x1, Pallas kernels, on_device(): local(fine_kernel, [shape(*block), shape(4, 32, LANES)], [VM] * 6, [(34,...  1.79 us
    pallas_call x1, Pallas kernels, on_device(): local(three_kernel, [shape(64, LANES), shape(256, LANES), shape(*block)],...  1.69 us
    pallas_call x1, Pallas kernels, on_device(): local(faces_kernel, [edge, edge, edge, edge, shape(2, 32, LANES)] + [shap...  1.59 us
  transfers between devices with their start and end apart: 15, of which 4 were waited for; matrix products, arithmetic and copies ran while one was open for 0% of the time, Pallas kernels for 13%

profile of v10, /device:TPU:1, one launch (start us, length us, event | category | flops | bytes accessed | tf_op | source)
XLA Modules:
  0.0 47.7 jit_solution(12290670073113406022)
XLA Ops:
  0.0 1.6 %faces.1 = (f32[3,32,128]{2,1,0:T(8,128)S(1)}, f32[3,32,128]{2,1,0:T(8,128)S(1)}, f32[3,32,128]{2,1,0:T(8,128)S(1)}, f32[3,32,128]{2,1,0:T(8,128)S(1)}, f32[2,32...) custom-call(f32[32,32,128]{2,1,0:T(8,128)} %kappa_far.1, f32[32,32,128]{2,1,0:T(8,128)} %initial.1), custom_call_target="tpu_custom_call" | custom-call | tf_op jit(solution)/shard_map/faces/pallas_call | solution.py:763
  1.6 2.6 %collective-permute-start = (f32[2,32,128]{2,1,0:T(8,128)S(1)}, f32[2,32,128]{2,1,0:T(8,128)S(1)}, u32[]{:S(2)}, u32[]{:S(2)}) collective-permute-start(f32[2,32,128]{2,1,0:T(8,128)S(1)} %get-tuple-element.51), channel_id=1, source_target_pairs={{0,1},{1,2},{2,3},{3,4},{4,5},{5,6},{6,7},{7,0},{8,9},{9,10},{10,1... | collective-permute-start | bytes 98312 | tf_op jit(solution)/shard_map/ppermute | solution.py:754
  4.2 1.3 %collective-permute-start.2 = (f32[3,32,128]{2,1,0:T(8,128)S(1)}, f32[3,32,128]{2,1,0:T(8,128)S(1)}, u32[]{:S(2)}, u32[]{:S(2)}) collective-permute-start(f32[3,32,128]{2,1,0:T(8,128)S(1)} %get-tuple-element.57), channel_id=1, source_target_pairs={{0,32},{32,64},{64,96},{96,0},{1,33},{33,65},{65,97},{97,1},{2,34}... | collective-permute-start | bytes 147464 | tf_op jit(solution)/shard_map/ppermute | solution.py:754
  5.5 1.4 %collective-permute-start.3 = (f32[3,32,128]{2,1,0:T(8,128)S(1)}, f32[3,32,128]{2,1,0:T(8,128)S(1)}, u32[]{:S(2)}, u32[]{:S(2)}) collective-permute-start(f32[3,32,128]{2,1,0:T(8,128)S(1)} %get-tuple-element.58), channel_id=1, source_target_pairs={{0,96},{32,0},{64,32},{96,64},{1,97},{33,1},{65,33},{97,65},{2,98}... | collective-permute-start | bytes 147464 | tf_op jit(solution)/shard_map/ppermute | solution.py:754
  7.0 1.6 %collective-permute-start.4 = (f32[3,32,128]{2,1,0:T(8,128)S(1)}, f32[3,32,128]{2,1,0:T(8,128)S(1)}, u32[]{:S(2)}, u32[]{:S(2)}) collective-permute-start(f32[3,32,128]{2,1,0:T(8,128)S(1)} %get-tuple-element.59), channel_id=1, source_target_pairs={{0,8},{8,16},{16,24},{24,0},{1,9},{9,17},{17,25},{25,1},{2,10},{10... | collective-permute-start | bytes 147464 | tf_op jit(solution)/shard_map/ppermute | solution.py:754
  8.6 2.1 %collective-permute-start.5 = (f32[3,32,128]{2,1,0:T(8,128)S(1)}, f32[3,32,128]{2,1,0:T(8,128)S(1)}, u32[]{:S(2)}, u32[]{:S(2)}) collective-permute-start(f32[3,32,128]{2,1,0:T(8,128)S(1)} %get-tuple-element.60), channel_id=1, source_target_pairs={{0,24},{8,0},{16,8},{24,16},{1,25},{9,1},{17,9},{25,17},{2,26},{10... | collective-permute-start | bytes 147464 | tf_op jit(solution)/shard_map/ppermute | solution.py:754
  10.7 3.3 %collective-permute-done.1.zhi = f32[2,32,128]{2,1,0:T(8,128)S(1)} collective-permute-done((f32[2,32,128]{2,1,0:T(8,128)S(1)}, f32[2,32,128]{2,1,0:T(8,128)S(1)}, u32[]{:S(2)}, u32[]{:S(2)}) %collective-permute-start.1) | collective-permute-done | bytes 32800 | tf_op jit(solution)/shard_map/ppermute | solution.py:754
  14.1 1.9 %inside.1 = (f32[1368,128]{1,0:T(8,128)S(1)}, f32[32,128]{1,0:T(8,128)S(1)}, f32[32,32,128]{2,1,0:T(8,128)S(1)}, f32[32,32,128]{2,1,0:T(8,128)S(1)}, f32[16,32,1...) custom-call(f32[32,32,128]{2,1,0:T(8,128)S(1)} %get-tuple-element.49.kappa, f32[32,32,128]{2,1,0:T(8,128)S(1)} %get-tuple-element.50.initial, ...), custom_call_target="tpu_custom_call" | custom-call | tf_op jit(solution)/shard_map/inside/pallas_call | solution.py:771
  16.0 1.2 %residual.1 = (f32[32,32,128]{2,1,0:T(8,128)S(1)}, f32[32,32,128]{2,1,0:T(8,128)S(1)}, f32[4,32,128]{2,1,0:T(8,128)S(1)}, f32[40,128]{1,0:T(8,128)S(1)}, f32[40,...) custom-call(f32[32,32,128]{2,1,0:T(8,128)S(1)} %get-tuple-element.49, ...), custom_call_target="tpu_custom_call" | custom-call | tf_op jit(solution)/shard_map/residual/pallas_call | solution.py:782
  17.7 0.7 %collective-permute-done.6.zlo = f32[40,128]{1,0:T(8,128)S(1)} collective-permute-done((f32[40,128]{1,0:T(8,128)S(1)}, f32[40,128]{1,0:T(8,128)S(1)}, u32[]{:S(2)}, u32[]{:S(2)}) %collective-permute-start.6) | collective-permute-done | bytes 20512 | tf_op jit(solution)/shard_map/ppermute | solution.py:754
  18.4 2.0 %collective-permute-done.7.zhi = f32[40,128]{1,0:T(8,128)S(1)} collective-permute-done((f32[40,128]{1,0:T(8,128)S(1)}, f32[40,128]{1,0:T(8,128)S(1)}, u32[]{:S(2)}, u32[]{:S(2)}) %collective-permute-start.7) | collective-permute-done | bytes 20512 | tf_op jit(solution)/shard_map/ppermute | solution.py:754
  20.4 1.1 %window.1 = (f32[3,64,128]{2,1,0:T(8,128)S(1)}, f32[112,128]{1,0:T(8,128)S(1)}, f32[112,128]{1,0:T(8,128)S(1)}, f32[2,8,128]{2,1,0:T(8,128)S(1)}, f32[32,128]{1,...) custom-call(f32[40,128]{1,0:T(8,128)S(1)} %collective-permute-done.6.zlo, ...), custom_call_target="tpu_custom_call" | custom-call | tf_op jit(solution)/shard_map/window/pallas_call | solution.py:796
  21.5 4.7 %all-to-all-start = ((f32[16,16,128]{2,1,0:T(8,128)}), f32[16,16,128]{2,1,0:T(8,128)S(1)}, u32[]{:S(2)}, u32[]{:S(2)}) async-start(f32[16,16,128]{2,1,0:T(8,128)} %get-tuple-element.91), calls=%async_computation | async-start | bytes 262144 | tf_op jit(solution)/shard_map/all_to_all | solution.py:806
  26.1 1.4 %collective-permute-start.8 = (f32[112,128]{1,0:T(8,128)S(1)}, f32[112,128]{1,0:T(8,128)S(1)}, u32[]{:S(2)}, u32[]{:S(2)}) collective-permute-start(f32[112,128]{1,0:T(8,128)S(1)} %get-tuple-element.68.xp), channel_id=1, source_target_pairs={{0,32},{32,64},{64,96},{96,0},{1,33},{33,65},{65,97},{97,1},{2,34}... | collective-permute-start | bytes 172040 | tf_op jit(solution)/shard_map/ppermute | solution.py:754
  27.5 1.4 %collective-permute-start.9 = (f32[112,128]{1,0:T(8,128)S(1)}, f32[112,128]{1,0:T(8,128)S(1)}, u32[]{:S(2)}, u32[]{:S(2)}) collective-permute-start(f32[112,128]{1,0:T(8,128)S(1)} %get-tuple-element.69), channel_id=1, source_target_pairs={{0,96},{32,0},{64,32},{96,64},{1,97},{33,1},{65,33},{97,65},{2,98}... | collective-permute-start | bytes 172040 | tf_op jit(solution)/shard_map/ppermute | solution.py:754
  28.9 0.6 %second.1 = (f32[16,16,128]{2,1,0:T(8,128)S(1)}, f32[4,16,128]{2,1,0:T(8,128)S(1)}) custom-call(f32[440,128]{1,0:T(8,128)S(1)} %get-tuple-element.79.kp2, f32[16,128]{1,0:T(8,128)S(1)} %get-tuple-element.80.ck2, f32[16,16,128]{2,1,0:T(8,128)S(1)} %get-tuple-element.81.scale2, f32[16,16,128]{2,1,0:T(8,128)S(1)} %get-tuple-element.82.first2, ...), custom_call_target="tpu_custom_call" | custom-call | tf_op jit(solution)/shard_map/second/pallas_call | solution.py:811
  29.5 1.8 %fine.1 = (f32[32,32,128]{2,1,0:T(8,128)S(1)}, f32[4,32,128]{2,1,0:T(8,128)S(1)}) custom-call(f32[1368,128]{1,0:T(8,128)S(1)} %get-tuple-element.73.kp, f32[32,128]{1,0:T(8,128)S(1)} %get-tuple-element.54.rim.ck, f32[32,32,128]{2,1,0:T(8,128)S(1)} %get-tuple-element.74.scale, f32[32,32,128]{2,1,0:T(8,128)S(1)} %get-tuple-element.75.first, ...), custom_call_target="tpu_custom_call" | custom-call | tf_op jit(solution)/shard_map/fine/pallas_call | solution.py:807
  31.4 1.4 %collective-permute-start.10 = (f32[240,128]{1,0:T(8,128)S(1)}, f32[240,128]{1,0:T(8,128)S(1)}, u32[]{:S(2)}, u32[]{:S(2)}) collective-permute-start(f32[240,128]{1,0:T(8,128)S(1)} %get-tuple-element.85), channel_id=1, source_target_pairs={{0,8},{8,16},{16,24},{24,0},{1,9},{9,17},{17,25},{25,1},{2,10},{10... | collective-permute-start | bytes 368648 | tf_op jit(solution)/shard_map/ppermute | solution.py:754
  32.7 1.4 %collective-permute-start.11 = (f32[240,128]{1,0:T(8,128)S(1)}, f32[240,128]{1,0:T(8,128)S(1)}, u32[]{:S(2)}, u32[]{:S(2)}) collective-permute-start(f32[240,128]{1,0:T(8,128)S(1)} %get-tuple-element.86), channel_id=1, source_target_pairs={{0,24},{8,0},{16,8},{24,16},{1,25},{9,1},{17,9},{25,17},{2,26},{10... | collective-permute-start | bytes 368648 | tf_op jit(solution)/shard_map/ppermute | solution.py:754
  34.2 4.4 %collective-permute-start.12 = (f32[3,64,128]{2,1,0:T(8,128)S(1)}, f32[3,64,128]{2,1,0:T(8,128)S(1)}, u32[]{:S(2)}, u32[]{:S(2)}) collective-permute-start(f32[3,64,128]{2,1,0:T(8,128)S(1)} %ring.1), channel_id=1, source_target_pairs={{0,3},{1,4},{2,5},{3,6},{4,7},{5,0},{6,1},{7,2},{8,11},{9,12},{10,... | collective-permute-start | bytes 294920 | tf_op jit(solution)/shard_map/ppermute | solution.py:754
  38.7 1.7 %three.1 = (f32[64,128]{1,0:T(8,128)S(1)}, f32[256,128]{1,0:T(8,128)S(1)}, f32[32,32,128]{2,1,0:T(8,128)S(1)}) custom-call(f32[32,32,128]{2,1,0:T(8,128)S(1)} %copy-done, f32[3,64,128]{2,1,0:T(8,128)S(1)} %get-tuple-element.67.own, f32[112,128]{1,0:T(8,128)S(1)} %collective-permute-done.8.xlo, f32[112,128]{1,0:T(8,128)S(1)} %collective-permute-done.9.xhi, ...), custom_call_target="tpu_custom_call" | custom-call | tf_op jit(solution)/shard_map/three/pallas_call | solution.py:823
  40.4 3.7 %collective-permute-done.13.high = f32[3,64,128]{2,1,0:T(8,128)S(1)} collective-permute-done((f32[3,64,128]{2,1,0:T(8,128)S(1)}, f32[3,64,128]{2,1,0:T(8,128)S(1)}, u32[]{:S(2)}, u32[]{:S(2)}) %collective-permute-start.13) | collective-permute-done | bytes 98336 | tf_op jit(solution)/shard_map/ppermute | solution.py:754
  44.1 2.7 %planes.1.four_in = f32[16,128]{1,0:T(8,128)S(1)} custom-call(s32[3]{0:T(128)S(1)} %pad_add_fusion.place, f32[16,16,128]{2,1,0:T(8,128)S(1)} %all-to-all-done.blocks, f32[3,64,128]{2,1,0:T(8,128)S(1)} %ring.1, f32[3,64,128]{2,1,0:T(8,128)S(1)} %collective-permute-done.12.low, f32[3,64,128]{2,1,0:T(8,128)S(1)} %collective-permute-done.13.high), custom_call_target="tpu_custom_call" | custom-call | tf_op jit(solution)/shard_map/planes/pallas_call | solution.py:827
  46.8 0.9 %finish.1 = f32[32,32,128]{2,1,0:T(8,128)} custom-call(f32[64,128]{1,0:T(8,128)S(1)} %get-tuple-element.89.three_in, f32[256,128]{1,0:T(8,128)S(1)} %get-tuple-element.90.two_in, f32[16,128]{1,0:T(8,128)S(1)} %planes.1.four_in, f32[32,32,128]{2,1,0:T(8,128)S(1)} %get-tuple-element.92.fine_in), custom_call_target="tpu_custom_call" | custom-call | tf_op jit(solution)/shard_map/finish/pallas_call | solution.py:835
  (24 shorter events, 0.7 us)
Async XLA Ops:
  0.0 14.1 %copy-start.1 = (f32[32,32,128]{2,1,0:T(8,128)S(1)}, f32[32,32,128]{2,1,0:T(8,128)}, u32[]{:S(2)}) copy-start(f32[32,32,128]{2,1,0:T(8,128)} %rhs.1) | copy-start | bytes 1572868
  0.0 14.1 %copy-start.2 = (f32[32,32,128]{2,1,0:T(8,128)S(1)}, f32[32,32,128]{2,1,0:T(8,128)}, u32[]{:S(2)}) copy-start(f32[32,32,128]{2,1,0:T(8,128)} %sigma.1) | copy-start | bytes 1572868
  1.6 9.1 %collective-permute-start = (f32[2,32,128]{2,1,0:T(8,128)S(1)}, f32[2,32,128]{2,1,0:T(8,128)S(1)}, u32[]{:S(2)}, u32[]{:S(2)}) collective-permute-start(f32[2,32,128]{2,1,0:T(8,128)S(1)} %get-tuple-element.51), channel_id=1, source_target_pairs={{0,1},{1,2},{2,3},{3,4},{4,5},{5,6},{6,7},{7,0},{8,9},{9,10},{10,1... | collective-permute-start | bytes 98312 | tf_op jit(solution)/shard_map/ppermute | solution.py:754
  4.2 11.7 %collective-permute-start.2 = (f32[3,32,128]{2,1,0:T(8,128)S(1)}, f32[3,32,128]{2,1,0:T(8,128)S(1)}, u32[]{:S(2)}, u32[]{:S(2)}) collective-permute-start(f32[3,32,128]{2,1,0:T(8,128)S(1)} %get-tuple-element.57), channel_id=1, source_target_pairs={{0,32},{32,64},{64,96},{96,0},{1,33},{33,65},{65,97},{97,1},{2,34}... | collective-permute-start | bytes 147464 | tf_op jit(solution)/shard_map/ppermute | solution.py:754
  5.5 10.4 %collective-permute-start.3 = (f32[3,32,128]{2,1,0:T(8,128)S(1)}, f32[3,32,128]{2,1,0:T(8,128)S(1)}, u32[]{:S(2)}, u32[]{:S(2)}) collective-permute-start(f32[3,32,128]{2,1,0:T(8,128)S(1)} %get-tuple-element.58), channel_id=1, source_target_pairs={{0,96},{32,0},{64,32},{96,64},{1,97},{33,1},{65,33},{97,65},{2,98}... | collective-permute-start | bytes 147464 | tf_op jit(solution)/shard_map/ppermute | solution.py:754
  7.0 9.0 %collective-permute-start.4 = (f32[3,32,128]{2,1,0:T(8,128)S(1)}, f32[3,32,128]{2,1,0:T(8,128)S(1)}, u32[]{:S(2)}, u32[]{:S(2)}) collective-permute-start(f32[3,32,128]{2,1,0:T(8,128)S(1)} %get-tuple-element.59), channel_id=1, source_target_pairs={{0,8},{8,16},{16,24},{24,0},{1,9},{9,17},{17,25},{25,1},{2,10},{10... | collective-permute-start | bytes 147464 | tf_op jit(solution)/shard_map/ppermute | solution.py:754
  8.6 7.4 %collective-permute-start.5 = (f32[3,32,128]{2,1,0:T(8,128)S(1)}, f32[3,32,128]{2,1,0:T(8,128)S(1)}, u32[]{:S(2)}, u32[]{:S(2)}) collective-permute-start(f32[3,32,128]{2,1,0:T(8,128)S(1)} %get-tuple-element.60), channel_id=1, source_target_pairs={{0,24},{8,0},{16,8},{24,16},{1,25},{9,1},{17,9},{25,17},{2,26},{10... | collective-permute-start | bytes 147464 | tf_op jit(solution)/shard_map/ppermute | solution.py:754
  10.7 3.3 %collective-permute-start.1 = (f32[2,32,128]{2,1,0:T(8,128)S(1)}, f32[2,32,128]{2,1,0:T(8,128)S(1)}, u32[]{:S(2)}, u32[]{:S(2)}) collective-permute-start(f32[2,32,128]{2,1,0:T(8,128)S(1)} %get-tuple-element.51), channel_id=1, source_target_pairs={{0,7},{1,0},{2,1},{3,2},{4,3},{5,4},{6,5},{7,6},{8,15},{9,8},{10,9... | collective-permute-start | bytes 98312 | tf_op jit(solution)/shard_map/ppermute | solution.py:754
  17.2 1.2 %collective-permute-start.6 = (f32[40,128]{1,0:T(8,128)S(1)}, f32[40,128]{1,0:T(8,128)S(1)}, u32[]{:S(2)}, u32[]{:S(2)}) collective-permute-start(f32[40,128]{1,0:T(8,128)S(1)} %get-tuple-element.61), channel_id=1, source_target_pairs={{0,1},{1,2},{2,3},{3,4},{4,5},{5,6},{6,7},{7,0},{8,9},{9,10},{10,1... | collective-permute-start | bytes 61448 | tf_op jit(solution)/shard_map/ppermute | solution.py:754
  17.2 3.2 %collective-permute-start.7 = (f32[40,128]{1,0:T(8,128)S(1)}, f32[40,128]{1,0:T(8,128)S(1)}, u32[]{:S(2)}, u32[]{:S(2)}) collective-permute-start(f32[40,128]{1,0:T(8,128)S(1)} %get-tuple-element.62), channel_id=1, source_target_pairs={{0,7},{1,0},{2,1},{3,2},{4,3},{5,4},{6,5},{7,6},{8,15},{9,8},{10,9... | collective-permute-start | bytes 61448 | tf_op jit(solution)/shard_map/ppermute | solution.py:754
  21.5 12.6 %all-to-all-start = ((f32[16,16,128]{2,1,0:T(8,128)}), f32[16,16,128]{2,1,0:T(8,128)S(1)}, u32[]{:S(2)}, u32[]{:S(2)}) async-start(f32[16,16,128]{2,1,0:T(8,128)} %get-tuple-element.91), calls=%async_computation | async-start | bytes 262144 | tf_op jit(solution)/shard_map/all_to_all | solution.py:806
  26.1 5.2 %collective-permute-start.8 = (f32[112,128]{1,0:T(8,128)S(1)}, f32[112,128]{1,0:T(8,128)S(1)}, u32[]{:S(2)}, u32[]{:S(2)}) collective-permute-start(f32[112,128]{1,0:T(8,128)S(1)} %get-tuple-element.68.xp), channel_id=1, source_target_pairs={{0,32},{32,64},{64,96},{96,0},{1,33},{33,65},{65,97},{97,1},{2,34}... | collective-permute-start | bytes 172040 | tf_op jit(solution)/shard_map/ppermute | solution.py:754
  27.5 3.8 %collective-permute-start.9 = (f32[112,128]{1,0:T(8,128)S(1)}, f32[112,128]{1,0:T(8,128)S(1)}, u32[]{:S(2)}, u32[]{:S(2)}) collective-permute-start(f32[112,128]{1,0:T(8,128)S(1)} %get-tuple-element.69), channel_id=1, source_target_pairs={{0,96},{32,0},{64,32},{96,64},{1,97},{33,1},{65,33},{97,65},{2,98}... | collective-permute-start | bytes 172040 | tf_op jit(solution)/shard_map/ppermute | solution.py:754
  31.3 7.4 %copy-start = (f32[32,32,128]{2,1,0:T(8,128)S(1)}, f32[32,32,128]{2,1,0:T(8,128)}, u32[]{:S(2)}) copy-start(f32[32,32,128]{2,1,0:T(8,128)} %initial.1) | copy-start | bytes 1572868
  31.4 7.3 %collective-permute-start.10 = (f32[240,128]{1,0:T(8,128)S(1)}, f32[240,128]{1,0:T(8,128)S(1)}, u32[]{:S(2)}, u32[]{:S(2)}) collective-permute-start(f32[240,128]{1,0:T(8,128)S(1)} %get-tuple-element.85), channel_id=1, source_target_pairs={{0,8},{8,16},{16,24},{24,0},{1,9},{9,17},{17,25},{25,1},{2,10},{10... | collective-permute-start | bytes 368648 | tf_op jit(solution)/shard_map/ppermute | solution.py:754
  32.7 5.9 %collective-permute-start.11 = (f32[240,128]{1,0:T(8,128)S(1)}, f32[240,128]{1,0:T(8,128)S(1)}, u32[]{:S(2)}, u32[]{:S(2)}) collective-permute-start(f32[240,128]{1,0:T(8,128)S(1)} %get-tuple-element.86), channel_id=1, source_target_pairs={{0,24},{8,0},{16,8},{24,16},{1,25},{9,1},{17,9},{25,17},{2,26},{10... | collective-permute-start | bytes 368648 | tf_op jit(solution)/shard_map/ppermute | solution.py:754
  34.2 6.2 %collective-permute-start.12 = (f32[3,64,128]{2,1,0:T(8,128)S(1)}, f32[3,64,128]{2,1,0:T(8,128)S(1)}, u32[]{:S(2)}, u32[]{:S(2)}) collective-permute-start(f32[3,64,128]{2,1,0:T(8,128)S(1)} %ring.1), channel_id=1, source_target_pairs={{0,3},{1,4},{2,5},{3,6},{4,7},{5,0},{6,1},{7,2},{8,11},{9,12},{10,... | collective-permute-start | bytes 294920 | tf_op jit(solution)/shard_map/ppermute | solution.py:754
  38.6 5.5 %collective-permute-start.13 = (f32[3,64,128]{2,1,0:T(8,128)S(1)}, f32[3,64,128]{2,1,0:T(8,128)S(1)}, u32[]{:S(2)}, u32[]{:S(2)}) collective-permute-start(f32[3,64,128]{2,1,0:T(8,128)S(1)} %ring.1), channel_id=1, source_target_pairs={{0,5},{1,6},{2,7},{3,0},{4,1},{5,2},{6,3},{7,4},{8,13},{9,14},{10,... | collective-permute-start | bytes 294920 | tf_op jit(solution)/shard_map/ppermute | solution.py:754
